TPU v7x, 32 devices: a whole 2x2x4 slice. The times are simulated.
32 devices in a mesh: dp: 4 (over y, x), tensor: 8 (over z, core).
Axes of the slice: x: 2, y: 2, z: 4, core: 2. Of those that a mesh axis runs over, the one named last changes fastest.
Arguments:
- hidden: bfloat16 [512, 53248], P('dp', 'tensor'), may hold values from -0.29882812 to 0.29882812
- upstream: bfloat16 [512, 8192], P('dp'), may hold values from -6 to 6
- weight: bfloat16 [53248, 8192], P('tensor', 'dp'), may hold values from -0.0625 to 0.0625
- scales: float32 [416, 8192], P('tensor', 'dp'), may hold values from 0.3 to 3
- clip_mask: int32 [416, 8192], P('tensor', 'dp'), may hold values 0 or 1
- rot_block: float32 [52, 52], replicated, may hold values from -0.875 to 0.875
Outputs:
- grad_hidden: bfloat16 [512, 53248], P('dp', 'tensor')
- grad_weight: bfloat16 [53248, 8192], P('tensor', 'dp')
- grad_scales: float32 [416, 8192], P('tensor', 'dp')
All inputs are finite; a program needn't handle non-finite values. No bound on the sum of `clip_mask` on one device may be relied on, other than what follows from the above.
Results may differ from a plain program's by a relative error of at most 0.023.
Values may be sent and summed in bfloat16 or wider, within the bound.
No kernel may reach another device: no remote copies, remote signals or barrier semaphores. Data moves between devices by JAX's collectives and lax.ppermute only.
A program may use at most 192 MiB of HBM per device.

v0:
```python
import functools

import jax
import jax.numpy as jnp
from jax import lax
from jax.experimental import pallas as pl
from jax.experimental.pallas import tpu as pltpu
from jax.sharding import PartitionSpec as P

HB = 128
GROUP = 128
SUB = 16
F32 = jnp.float32
BF16 = jnp.bfloat16


def chunk_plan(groups):
    if groups % 4:
        return (groups,), 1
    units = groups // 4
    count = min(4, units)
    sizes = [units // count + (1 if i < units % count else 0) for i in range(count)]
    return tuple(4 * size for size in sizes), 4


def nt_dot(a, b):
    return lax.dot_general(a, b, (((1,), (1,)), ((), ())), preferred_element_type=F32)


def nn_dot(a, b):
    return lax.dot_general(a, b, (((1,), (0,)), ((), ())), preferred_element_type=F32)


def tn_dot(a, b):
    return lax.dot_general(a, b, (((0,), (0,)), ((), ())), preferred_element_type=F32)


def split2(value):
    high = value.astype(BF16)
    return high, (value - high.astype(F32)).astype(BF16)


def sign_matrix(size):
    both = lax.broadcasted_iota(jnp.int32, (size, size), 0) & lax.broadcasted_iota(
        jnp.int32, (size, size), 1
    )
    parity = jnp.zeros((size, size), jnp.int32)
    for bit in range(size.bit_length() - 1):
        parity = parity ^ ((both >> bit) & 1)
    return (1 - 2 * parity).astype(F32).astype(BF16)


def build_mixing(rot_ref, high_ref, low_ref, sign_ref, transposed):
    blocks = rot_ref.shape[0]
    size = blocks * SUB
    row = lax.broadcasted_iota(jnp.int32, (size, blocks), 0)
    col = lax.broadcasted_iota(jnp.int32, (size, blocks), 1)
    pick = ((row >> 4) == col).astype(F32).astype(BF16)
    rows = lax.broadcasted_iota(jnp.int32, (size, size), 0)
    cols = lax.broadcasted_iota(jnp.int32, (size, size), 1)
    same = (rows & (SUB - 1)) == (cols & (SUB - 1))
    for part, out_ref in zip(split2(rot_ref[...]), (high_ref, low_ref)):
        spread = nt_dot(pick, part) if transposed else nn_dot(pick, part)
        full = nt_dot(spread.astype(BF16), pick)
        out_ref[...] = jnp.where(same, full, 0.0).astype(BF16)
    sign_ref[...] = sign_matrix(HB)


def mix_rows(stacked, high_ref, low_ref, sign_ref):
    mixed = nn_dot(high_ref[...], stacked) + nn_dot(low_ref[...], stacked)
    results = []
    for part in range(stacked.shape[1] // HB):
        high, low = split2(mixed[:, part * HB : (part + 1) * HB])
        both = nn_dot(high, sign_ref[...]) + nn_dot(low, sign_ref[...])
        results.append((both * HB ** (-0.5)).astype(BF16))
    return results


def forward_kernel(sizes, x_ref, rot_ref, *refs):
    outs, (high_ref, low_ref, sign_ref) = refs[: len(sizes)], refs[len(sizes) :]
    blocks = rot_ref.shape[0]

    @pl.when(pl.program_id(0) == 0)
    def _():
        build_mixing(rot_ref, high_ref, low_ref, sign_ref, True)

    parts = x_ref.shape[0] // SUB
    stacked = jnp.concatenate(
        [
            jnp.concatenate(
                [
                    x_ref[j * SUB : (j + 1) * SUB, k * HB : (k + 1) * HB]
                    for k in range(blocks)
                ],
                axis=0,
            )
            for j in range(parts)
        ],
        axis=1,
    )
    for j, result in enumerate(mix_rows(stacked, high_ref, low_ref, sign_ref)):
        start = 0
        for size, out_ref in zip(sizes, outs):
            piece = result[start * SUB : (start + size) * SUB]
            out_ref[:, j * SUB : (j + 1) * SUB, :] = piece.reshape(size, SUB, HB)
            start += size


def backward_kernel(sizes, *refs):
    ins, (rot_ref, out_ref, high_ref, low_ref, sign_ref) = refs[: len(sizes)], refs[len(sizes) :]
    blocks = rot_ref.shape[0]

    @pl.when(pl.program_id(0) == 0)
    def _():
        build_mixing(rot_ref, high_ref, low_ref, sign_ref, False)

    parts = out_ref.shape[0] // SUB
    stacked = jnp.concatenate(
        [
            jnp.concatenate(
                [
                    in_ref[:, j * SUB : (j + 1) * SUB, :].reshape(size * SUB, HB)
                    for size, in_ref in zip(sizes, ins)
                ],
                axis=0,
            )
            for j in range(parts)
        ],
        axis=1,
    )
    for j, result in enumerate(mix_rows(stacked, high_ref, low_ref, sign_ref)):
        for k in range(blocks):
            out_ref[j * SUB : (j + 1) * SUB, k * HB : (k + 1) * HB] = result[
                k * SUB : (k + 1) * SUB
            ]


def local_scratch(blocks):
    return [
        pltpu.VMEM((blocks * SUB, blocks * SUB), BF16),
        pltpu.VMEM((blocks * SUB, blocks * SUB), BF16),
        pltpu.VMEM((HB, HB), BF16),
    ]


def local_cost(rows, blocks):
    size = blocks * SUB
    return pl.CostEstimate(
        flops=4 * size * size * (rows // SUB) * HB,
        bytes_accessed=4 * rows * blocks * HB,
        transcendentals=0,
    )


def local_forward(hidden, rot_block, sizes):
    rows, width = hidden.shape
    blocks = width // HB
    step = 2 * SUB
    return pl.pallas_call(
        functools.partial(forward_kernel, sizes),
        grid=(rows // step,),
        in_specs=[
            pl.BlockSpec((step, width), lambda i: (i, 0)),
            pl.BlockSpec((blocks, blocks), lambda i: (0, 0)),
        ],
        out_specs=[pl.BlockSpec((size, step, HB), lambda i: (0, i, 0)) for size in sizes],
        out_shape=[jax.ShapeDtypeStruct((size, rows, HB), BF16) for size in sizes],
        scratch_shapes=local_scratch(blocks),
        compiler_params=pltpu.CompilerParams(vmem_limit_bytes=32 << 20),
        cost_estimate=local_cost(rows, blocks),
        name="local_forward",
    )(hidden, rot_block)


def local_backward(mixed, rot_block, sizes):
    rows = mixed[0].shape[1]
    blocks = rot_block.shape[0]
    step = 2 * SUB
    return pl.pallas_call(
        functools.partial(backward_kernel, sizes),
        grid=(rows // step,),
        in_specs=[pl.BlockSpec((size, step, HB), lambda i: (0, i, 0)) for size in sizes]
        + [pl.BlockSpec((blocks, blocks), lambda i: (0, 0))],
        out_specs=pl.BlockSpec((step, blocks * HB), lambda i: (i, 0)),
        out_shape=jax.ShapeDtypeStruct((rows, blocks * HB), BF16),
        scratch_shapes=local_scratch(blocks),
        compiler_params=pltpu.CompilerParams(vmem_limit_bytes=32 << 20),
        cost_estimate=local_cost(rows, blocks),
        name="local_backward",
    )(*mixed, rot_block)


def units_kernel(first, per, up_ref, w_ref, s_ref, out_ref, quant_ref):
    base = first + pl.program_id(0) * per
    for g in range(per):
        rows = slice(g * GROUP, (g + 1) * GROUP)
        quant_ref[rows, :] = (w_ref[rows, :].astype(F32) * s_ref[pl.ds(base + g, 1), :]).astype(
            BF16
        )
    result = nt_dot(up_ref[...], quant_ref[...]).astype(BF16)
    tokens = out_ref.shape[2]
    for p in range(out_ref.shape[0]):
        for g in range(per):
            out_ref[p, g] = result[p * tokens : (p + 1) * tokens, g * GROUP : (g + 1) * GROUP]


def unit_grads(up, weight, scales, first, size, per, parts):
    tokens, cols = up.shape
    rows = tokens // parts
    offset = first // per
    return pl.pallas_call(
        functools.partial(units_kernel, first, per),
        grid=(size // per,),
        in_specs=[
            pl.BlockSpec((tokens, cols), lambda i: (0, 0)),
            pl.BlockSpec((per * GROUP, cols), lambda i: (offset + i, 0)),
            pl.BlockSpec(scales.shape, lambda i: (0, 0)),
        ],
        out_specs=pl.BlockSpec((parts, per, rows, HB), lambda i: (0, i, 0, 0)),
        out_shape=jax.ShapeDtypeStruct((parts, size, rows, HB), BF16),
        scratch_shapes=[pltpu.VMEM((per * GROUP, cols), BF16)],
        compiler_params=pltpu.CompilerParams(vmem_limit_bytes=40 << 20),
        cost_estimate=pl.CostEstimate(
            flops=2 * tokens * cols * size * GROUP,
            bytes_accessed=2 * cols * size * GROUP + 2 * tokens * (cols + size * GROUP),
            transcendentals=0,
        ),
        name="unit_grads",
    )(up, weight, scales)


def weights_kernel(first, per, rot_ref, up_ref, w_ref, s_ref, m_ref, *refs):
    gw_ref, gs_ref = refs[-2:]
    step = pl.program_id(0)
    base = first + step * per
    parts = rot_ref.shape[0]
    left = jnp.concatenate(
        [jnp.concatenate([rot_ref[p, g] for p in range(parts)], axis=0) for g in range(per)], axis=1
    )
    cols = up_ref.shape[1]
    tile = min(512, cols)
    for e in range(cols // tile):
        span = slice(e * tile, (e + 1) * tile)
        grad = tn_dot(left, up_ref[:, span])
        for g in range(per):
            rows = slice(g * GROUP, (g + 1) * GROUP)
            piece = grad[rows]
            scale = s_ref[pl.ds(base + g, 1), span]
            kept = m_ref[pl.ds(base + g, 1), span].astype(F32) * scale
            gw_ref[rows, span] = (piece * kept).astype(BF16)
            gs_ref[pl.ds(step * per + g, 1), span] = jnp.sum(
                piece * w_ref[rows, span].astype(F32), axis=0, keepdims=True
            )


def weight_grads(rotated, up, weight, scales, mask, buffer, first, size, per):
    parts, _, rows, _ = rotated.shape
    tokens, cols = up.shape
    offset = first // per
    specs = [
        pl.BlockSpec((parts, per, rows, HB), lambda i: (0, i, 0, 0)),
        pl.BlockSpec((tokens, cols), lambda i: (0, 0)),
        pl.BlockSpec((per * GROUP, cols), lambda i: (offset + i, 0)),
        pl.BlockSpec(scales.shape, lambda i: (0, 0)),
        pl.BlockSpec(scales.shape, lambda i: (0, 0)),
    ]
    args = [rotated, up, weight, scales, mask]
    aliases = {}
    if buffer is not None:
        aliases = {len(args): 0}
        args.append(buffer)
        specs.append(pl.BlockSpec(memory_space=pl.ANY))
    return pl.pallas_call(
        functools.partial(weights_kernel, first, per),
        grid=(size // per,),
        in_specs=specs,
        out_specs=[
            pl.BlockSpec((per * GROUP, cols), lambda i: (offset + i, 0)),
            pl.BlockSpec((size, cols), lambda i: (0, 0)),
        ],
        out_shape=[
            jax.ShapeDtypeStruct(weight.shape, BF16),
            jax.ShapeDtypeStruct((size, cols), F32),
        ],
        input_output_aliases=aliases,
        compiler_params=pltpu.CompilerParams(vmem_limit_bytes=40 << 20),
        cost_estimate=pl.CostEstimate(
            flops=2 * tokens * cols * size * GROUP,
            bytes_accessed=4 * cols * size * GROUP + 2 * tokens * (cols + size * GROUP),
            transcendentals=0,
        ),
        name="weight_grads",
    )(*args)


def partner(value, mask):
    size = lax.axis_size("tensor")
    return lax.ppermute(value, "tensor", [(i, i ^ mask) for i in range(size)])


def mix_across(value, masks):
    size = lax.axis_size("tensor")
    index = lax.axis_index("tensor")
    for place, mask in enumerate(masks):
        other = partner(value, mask).astype(F32)
        sign = jnp.where((index & mask) != 0, -1.0, 1.0).astype(F32)
        total = other + sign * value.astype(F32)
        if place == len(masks) - 1:
            total = total * size ** (-0.5)
        value = total.astype(BF16)
    return value


def gather_upstream(upstream):
    rows = upstream.shape[0]
    parts = lax.axis_size("dp")
    half = rows // 2
    core = lax.axis_index("tensor") & 1
    mine = lax.dynamic_slice_in_dim(upstream, core * half, half, axis=0)
    mine = lax.all_to_all(mine, "dp", split_axis=1, concat_axis=0, tiled=True)
    other = partner(mine, 1)
    cols = mine.shape[1]
    mine = mine.reshape(parts, half, cols)
    other = other.reshape(parts, half, cols)
    low = jnp.where(core == 0, mine, other)
    high = jnp.where(core == 0, other, mine)
    return jnp.concatenate([low, high], axis=1).reshape(parts * rows, cols)


def shards(hidden, upstream, weight, scales, clip_mask, rot_block):
    groups = scales.shape[0]
    parts = lax.axis_size("dp")
    size = lax.axis_size("tensor")
    sizes, per = chunk_plan(groups)
    starts = [sum(sizes[:i]) for i in range(len(sizes))]
    bits = [1 << i for i in range(size.bit_length() - 1)]
    down = bits[::-1]
    up_first = bits[1:] + bits[:1]

    up = gather_upstream(upstream)
    local = local_forward(hidden, rot_block, sizes)
    rotated = [mix_across(value, down) for value in local]
    gathered = [lax.all_gather(value, "dp", axis=0, tiled=False) for value in rotated]

    sums = []
    for start, count in zip(starts, sizes):
        full = unit_grads(up, weight, scales, start, count, per, parts)
        sums.append(
            lax.psum_scatter(full, "dp", scatter_dimension=0, tiled=False)
        )
    mixed = [mix_across(value, up_first) for value in sums]

    buffer = None
    scale_grads = []
    for value, start, count in zip(gathered, starts, sizes):
        buffer, scale_grad = weight_grads(
            value, up, weight, scales, clip_mask, buffer, start, count, per
        )
        scale_grads.append(scale_grad)
    grad_hidden = local_backward(mixed, rot_block, sizes)
    return (grad_hidden, buffer, jnp.concatenate(scale_grads, axis=0))


def solution(mesh):
    return jax.shard_map(
        shards,
        mesh=mesh,
        in_specs=(
            P("dp", "tensor"),
            P("dp", None),
            P("tensor", "dp"),
            P("tensor", "dp"),
            P("tensor", "dp"),
            P(),
        ),
        out_specs=(P("dp", "tensor"), P("tensor", "dp"), P("tensor", "dp")),
        check_vma=False,
    )
```

profile of v0, /device:TPU:0, one launch (start us, length us, event | category | flops | bytes accessed | tf_op | source)
XLA Modules:
  0.0 445.4 jit_solution(12252529555592149987)
XLA Ops:
  9.6 8.1 %local_forward.1 = (bf16[16,128,128]{2,1,0:T(8,128)(2,1)S(1)}, bf16[12,128,128]{2,1,0:T(8,128)(2,1)S(1)}, bf16[12,128,128]{2,1,0:T(8,128)(2,1)S(1)}, bf16[12,128,128]{2,1,0:T(8,128)(2,1)S(1)}) custom-call(bf16[128,6656]{1,0:T(8,128)(2,1)S(1)} %copy-done.14, f32[52,52]{1,0:T(8,128)S(1)} %copy-done.15), custom_call_target="tpu_custom_call" | custom-call | flops 2835349504 | bytes 3407872 | tf_op jit(solution)/shard_map/local_forward/pallas_call | solution.py:159
  18.4 4.0 collective-permute-start.22
  22.4 23.3 %collective-permute-done.22 = bf16[16,128,128]{2,1,0:T(8,128)(2,1)} collective-permute-done((bf16[16,128,128]{2,1,0:T(8,128)(2,1)S(1)}, bf16[16,128,128]{2,1,0:T(8,128)(2,1)}, u32[]{:S(2)}, u32[]{:S(2)}) %collective-permute-start.22) | collective-permute-done | bytes 524320 | tf_op jit(solution)/shard_map/ppermute | solution.py:298
  48.3 12.8 %collective-permute-done.23 = bf16[16,128,128]{2,1,0:T(8,128)(2,1)} collective-permute-done((bf16[16,128,128]{2,1,0:T(8,128)(2,1)}, bf16[16,128,128]{2,1,0:T(8,128)(2,1)}, u32[]{:S(2)}, u32[]{:S(2)}) %collective-permute-start.23) | collective-permute-done | bytes 524320 | tf_op jit(solution)/shard_map/ppermute | solution.py:298
  67.8 3.2 collective-permute-start.19
  71.0 17.8 %collective-permute-done.19 = bf16[12,128,128]{2,1,0:T(8,128)(2,1)S(1)} collective-permute-done((bf16[12,128,128]{2,1,0:T(8,128)(2,1)S(1)}, bf16[12,128,128]{2,1,0:T(8,128)(2,1)S(1)}, u32[]{:S(2)}, u32[]{:S(2)}) %collective-permute-start.19) | collective-permute-done | bytes 393248 | tf_op jit(solution)/shard_map/ppermute | solution.py:298
  89.8 9.9 %collective-permute-done.20 = bf16[12,128,128]{2,1,0:T(8,128)(2,1)S(1)} collective-permute-done((bf16[12,128,128]{2,1,0:T(8,128)(2,1)S(1)}, bf16[12,128,128]{2,1,0:T(8,128)(2,1)S(1)}, u32[]{:S(2)}, u32[]{:S(2)}) %collective-permute-start.20) | collective-permute-done | bytes 393248 | tf_op jit(solution)/shard_map/ppermute | solution.py:298
  99.9 2.8 collective-permute-start.16
  103.7 17.3 %collective-permute-done.16 = bf16[12,128,128]{2,1,0:T(8,128)(2,1)} collective-permute-done((bf16[12,128,128]{2,1,0:T(8,128)(2,1)S(1)}, bf16[12,128,128]{2,1,0:T(8,128)(2,1)}, u32[]{:S(2)}, u32[]{:S(2)}) %collective-permute-start.16) | collective-permute-done | bytes 393248 | tf_op jit(solution)/shard_map/ppermute | solution.py:298
  122.9 10.1 %collective-permute-done.17 = bf16[12,128,128]{2,1,0:T(8,128)(2,1)S(1)} collective-permute-done((bf16[12,128,128]{2,1,0:T(8,128)(2,1)S(1)}, bf16[12,128,128]{2,1,0:T(8,128)(2,1)S(1)}, u32[]{:S(2)}, u32[]{:S(2)}) %collective-permute-start.17) | collective-permute-done | bytes 393248 | tf_op jit(solution)/shard_map/ppermute | solution.py:298
  135.3 3.7 all-to-all-start
  140.1 13.3 %all-to-all-done = bf16[64,4,2048]{2,0,1:T(8,128)(2,1)S(1)} async-done(((bf16[64,4,2048]{2,0,1:T(8,128)(2,1)}), bf16[64,4,2048]{2,0,1:T(8,128)(2,1)S(1)}, u32[]{:S(2)}, u32[]{:S(2)}) %all-to-all-start) | async-done | bytes 1048608 | tf_op jit(solution)/shard_map/all_to_all | solution.py:320
  153.4 2.7 collective-permute-done
  157.2 5.8 %unit_grads.7 = bf16[4,12,128,128]{3,2,1,0:T(8,128)(2,1)S(1)} custom-call(bf16[512,2048]{1,0:T(8,128)(2,1)S(1)} %bitcast.24, bf16[6656,2048]{1,0:T(8,128)(2,1)} %w_ref.15, f32[52,2048]{1,0:T(8,128)S(1)} %copy-done.2), custom_call_target="tpu_custom_call" | custom-call | flops 3221225472 | bytes 9961472 | tf_op jit(solution)/shard_map/unit_grads/pallas_call | solution.py:211
  164.3 2.7 collective-permute-start.13
  167.0 17.8 %collective-permute-done.13 = bf16[12,128,128]{2,1,0:T(8,128)(2,1)S(1)} collective-permute-done((bf16[12,128,128]{2,1,0:T(8,128)(2,1)S(1)}, bf16[12,128,128]{2,1,0:T(8,128)(2,1)S(1)}, u32[]{:S(2)}, u32[]{:S(2)}) %collective-permute-start.13) | collective-permute-done | bytes 393248 | tf_op jit(solution)/shard_map/ppermute | solution.py:298
  185.8 9.6 %collective-permute-done.14 = bf16[12,128,128]{2,1,0:T(8,128)(2,1)S(1)} collective-permute-done((bf16[12,128,128]{2,1,0:T(8,128)(2,1)S(1)}, bf16[12,128,128]{2,1,0:T(8,128)(2,1)S(1)}, u32[]{:S(2)}, u32[]{:S(2)}) %collective-permute-start.14) | collective-permute-done | bytes 393248 | tf_op jit(solution)/shard_map/ppermute | solution.py:298
  198.3 5.9 %unit_grads.6 = bf16[4,12,128,128]{3,2,1,0:T(8,128)(2,1)S(1)} custom-call(bf16[512,2048]{1,0:T(8,128)(2,1)S(1)} %bitcast.25, bf16[6656,2048]{1,0:T(8,128)(2,1)} %w_ref.15, f32[52,2048]{1,0:T(8,128)S(1)} %copy-done.2), custom_call_target="tpu_custom_call" | custom-call | flops 3221225472 | bytes 9961472 | tf_op jit(solution)/shard_map/unit_grads/pallas_call | solution.py:211
  205.4 5.9 %unit_grads.5 = bf16[4,12,128,128]{3,2,1,0:T(8,128)(2,1)S(1)} custom-call(bf16[512,2048]{1,0:T(8,128)(2,1)S(1)} %bitcast.26, bf16[6656,2048]{1,0:T(8,128)(2,1)} %w_ref.15, f32[52,2048]{1,0:T(8,128)S(1)} %copy-done.2), custom_call_target="tpu_custom_call" | custom-call | flops 3221225472 | bytes 9961472 | tf_op jit(solution)/shard_map/unit_grads/pallas_call | solution.py:211
  212.7 7.4 %unit_grads.4 = bf16[4,16,128,128]{3,2,1,0:T(8,128)(2,1)S(1)} custom-call(bf16[512,2048]{1,0:T(8,128)(2,1)S(1)} %bitcast.27, bf16[6656,2048]{1,0:T(8,128)(2,1)} %w_ref.15, f32[52,2048]{1,0:T(8,128)S(1)} %copy-done.2), custom_call_target="tpu_custom_call" | custom-call | flops 4294967296 | bytes 12582912 | tf_op jit(solution)/shard_map/unit_grads/pallas_call | solution.py:211
  224.0 9.7 %weight_grads.4 = (bf16[6656,2048]{1,0:T(8,128)(2,1)}, f32[16,2048]{1,0:T(8,128)S(1)}) custom-call(bf16[4,16,128,128]{3,2,1,0:T(8,128)(2,1)S(1)} %bitcast.32, bf16[512,2048]{1,0:T(8,128)(2,1)S(1)} %bitcast.28, bf16[6656,2048]{1,0:T(8,128)(2,1)} %w_ref.15, f32[52,2048]{1,0:T(8,128)S(1)} %copy-done.2, s32[52,2048]{1,0:T(8,128)S(1)} %copy-done.4), custom_call_target="tpu_custom_call" | custom-call | flops 4294967296 | bytes 20971520 | tf_op jit(solution)/shard_map/weight_grads/pallas_call | solution.py:273
  235.1 8.0 %weight_grads.5 = (bf16[6656,2048]{1,0:T(8,128)(2,1)}, f32[12,2048]{1,0:T(8,128)S(1)}) custom-call(bf16[4,12,128,128]{3,2,1,0:T(8,128)(2,1)S(1)} %bitcast.33, bf16[512,2048]{1,0:T(8,128)(2,1)S(1)} %bitcast.29, bf16[6656,2048]{1,0:T(8,128)(2,1)} %w_ref.15, f32[52,2048]{1,0:T(8,128)S(1)} %copy-done.2, ...), custom_call_target="tpu_custom_call", output_to_operand_aliasing={{0}: (5, {})} | custom-call | flops 3221225472 | bytes 16252928 | tf_op jit(solution)/shard_map/weight_grads/pallas_call | solution.py:273
  244.6 8.1 %weight_grads.6 = (bf16[6656,2048]{1,0:T(8,128)(2,1)}, f32[12,2048]{1,0:T(8,128)S(1)}) custom-call(bf16[4,12,128,128]{3,2,1,0:T(8,128)(2,1)S(1)} %bitcast.34, bf16[512,2048]{1,0:T(8,128)(2,1)S(1)} %bitcast.30, bf16[6656,2048]{1,0:T(8,128)(2,1)} %w_ref.15, f32[52,2048]{1,0:T(8,128)S(1)} %copy-done.2, ...), custom_call_target="tpu_custom_call", output_to_operand_aliasing={{0}: (5, {})} | custom-call | flops 3221225472 | bytes 16252928 | tf_op jit(solution)/shard_map/weight_grads/pallas_call | solution.py:273
  255.5 8.1 %weight_grads.7 = (bf16[6656,2048]{1,0:T(8,128)(2,1)}, f32[12,2048]{1,0:T(8,128)S(1)}) custom-call(bf16[4,12,128,128]{3,2,1,0:T(8,128)(2,1)S(1)} %bitcast.35, bf16[512,2048]{1,0:T(8,128)(2,1)S(1)} %bitcast.31, bf16[6656,2048]{1,0:T(8,128)(2,1)} %w_ref.15, f32[52,2048]{1,0:T(8,128)S(1)} %copy-done.2, ...), custom_call_target="tpu_custom_call", output_to_operand_aliasing={{0}: (5, {})} | custom-call | flops 3221225472 | bytes 16252928 | tf_op jit(solution)/shard_map/weight_grads/pallas_call | solution.py:273
  263.6 12.0 %reduce-scatter.17.cloned.1.call-done = bf16[1,12,128,128]{3,2,1,0:T(8,128)(2,1)} async-done(((bf16[4,12,128,128]{3,2,1,0:T(8,128)(2,1)}), bf16[1,12,128,128]{3,2,1,0:T(8,128)(2,1)}) %reduce-scatter.17.cloned.1.call-update) | async-done | bytes 393232
  277.9 32.2 %reduce-scatter.15.cloned.1.call-done = bf16[1,12,128,128]{3,2,1,0:T(8,128)(2,1)} async-done(((bf16[4,12,128,128]{3,2,1,0:T(8,128)(2,1)}), bf16[1,12,128,128]{3,2,1,0:T(8,128)(2,1)}) %reduce-scatter.15.cloned.1.call-update) | async-done | bytes 393232
  311.6 36.7 %reduce-scatter.13.cloned.1.call-done = bf16[1,16,128,128]{3,2,1,0:T(8,128)(2,1)} async-done(((bf16[4,16,128,128]{3,2,1,0:T(8,128)(2,1)}), bf16[1,16,128,128]{3,2,1,0:T(8,128)(2,1)}) %reduce-scatter.13.cloned.1.call-update) | async-done | bytes 524304
  356.9 15.2 %collective-permute-done.1 = bf16[16,128,128]{2,1,0:T(8,128)(2,1)S(1)} collective-permute-done((bf16[16,128,128]{2,1,0:T(8,128)(2,1)}, bf16[16,128,128]{2,1,0:T(8,128)(2,1)S(1)}, u32[]{:S(2)}, u32[]{:S(2)}) %collective-permute-start.1) | collective-permute-done | bytes 524320 | tf_op jit(solution)/shard_map/ppermute | solution.py:298
  373.2 35.8 %collective-permute-done.8 = bf16[12,128,128]{2,1,0:T(8,128)(2,1)S(1)} collective-permute-done((bf16[12,128,128]{2,1,0:T(8,128)(2,1)S(1)}, bf16[12,128,128]{2,1,0:T(8,128)(2,1)S(1)}, u32[]{:S(2)}, u32[]{:S(2)}) %collective-permute-start.8) | collective-permute-done | bytes 393248 | tf_op jit(solution)/shard_map/ppermute | solution.py:298
  409.2 8.2 %collective-permute-done.5 = bf16[12,128,128]{2,1,0:T(8,128)(2,1)S(1)} collective-permute-done((bf16[12,128,128]{2,1,0:T(8,128)(2,1)S(1)}, bf16[12,128,128]{2,1,0:T(8,128)(2,1)S(1)}, u32[]{:S(2)}, u32[]{:S(2)}) %collective-permute-start.5) | collective-permute-done | bytes 393248 | tf_op jit(solution)/shard_map/ppermute | solution.py:298
  417.7 9.6 %collective-permute-done.2 = bf16[16,128,128]{2,1,0:T(8,128)(2,1)S(1)} collective-permute-done((bf16[16,128,128]{2,1,0:T(8,128)(2,1)S(1)}, bf16[16,128,128]{2,1,0:T(8,128)(2,1)S(1)}, u32[]{:S(2)}, u32[]{:S(2)}) %collective-permute-start.2) | collective-permute-done | bytes 524320 | tf_op jit(solution)/shard_map/ppermute | solution.py:298
  429.6 8.9 %local_backward.1 = bf16[128,6656]{1,0:T(8,128)(2,1)} custom-call(bf16[16,128,128]{2,1,0:T(8,128)(2,1)S(1)} %multiply_convert_fusion.1.refs_0_, bf16[12,128,128]{2,1,0:T(8,128)(2,1)S(1)} %multiply_convert_fusion.7.refs_1_, bf16[12,128,128]{2,1,0:T(8,128)(2,1)S(1)} %multiply_convert_fusion.6.refs_2_, ...), custom_call_target="tpu_custom_call" | custom-call | flops 2835349504 | bytes 3407872 | tf_op jit(solution)/shard_map/local_backward/pallas_call | solution.py:179
  (125 shorter events, 54.1 us)
Async XLA Ops:
  7.2 214.3 %all-gather.15.cloned.1.call-start = ((), (), s32[]{:S(2)}) async-start(), calls=%async_computation.8 | async-start | bytes 2621440 | tf_op jit(solution)/shard_map/all_gather | solution.py:343
  18.4 27.3 %collective-permute-start.22 = (bf16[16,128,128]{2,1,0:T(8,128)(2,1)S(1)}, bf16[16,128,128]{2,1,0:T(8,128)(2,1)}, u32[]{:S(2)}, u32[]{:S(2)}) collective-permute-start(bf16[16,128,128]{2,1,0:T(8,128)(2,1)S(1)} %get-tuple-element.18), channel_id=1, source_target_pairs={{0,4},{1,5},{2,6},{3,7},{4,0},{5,1},{6,2},{7,3},{8,12},{9,13},{10,... | collective-permute-start | bytes 1572872 | tf_op jit(solution)/shard_map/ppermute | solution.py:298
  47.7 13.4 %collective-permute-start.23 = (bf16[16,128,128]{2,1,0:T(8,128)(2,1)}, bf16[16,128,128]{2,1,0:T(8,128)(2,1)}, u32[]{:S(2)}, u32[]{:S(2)}) collective-permute-start(bf16[16,128,128]{2,1,0:T(8,128)(2,1)} %add_convert_fusion.1), channel_id=1, source_target_pairs={{0,2},{1,3},{2,0},{3,1},{4,6},{5,7},{6,4},{7,5},{8,10},{9,11},{10,... | collective-permute-start | bytes 1572872 | tf_op jit(solution)/shard_map/ppermute | solution.py:298
  63.3 2.3 collective-permute-start.24
  67.8 165.9 %all-gather.13.cloned.1.call-start = ((), (), s32[]{:S(2)}) async-start(), calls=%async_computation.7 | async-start | bytes 1966080 | tf_op jit(solution)/shard_map/all_gather | solution.py:343
  67.8 21.0 %collective-permute-start.19 = (bf16[12,128,128]{2,1,0:T(8,128)(2,1)S(1)}, bf16[12,128,128]{2,1,0:T(8,128)(2,1)S(1)}, u32[]{:S(2)}, u32[]{:S(2)}) collective-permute-start(bf16[12,128,128]{2,1,0:T(8,128)(2,1)S(1)} %copy-done.13), channel_id=1, source_target_pairs={{0,4},{1,5},{2,6},{3,7},{4,0},{5,1},{6,2},{7,3},{8,12},{9,13},{10,... | collective-permute-start | bytes 1179656 | tf_op jit(solution)/shard_map/ppermute | solution.py:298
  89.0 10.7 %collective-permute-start.20 = (bf16[12,128,128]{2,1,0:T(8,128)(2,1)S(1)}, bf16[12,128,128]{2,1,0:T(8,128)(2,1)S(1)}, u32[]{:S(2)}, u32[]{:S(2)}) collective-permute-start(bf16[12,128,128]{2,1,0:T(8,128)(2,1)S(1)} %add_convert_fusion.5), channel_id=1, source_target_pairs={{0,2},{1,3},{2,0},{3,1},{4,6},{5,7},{6,4},{7,5},{8,10},{9,11},{10,... | collective-permute-start | bytes 1179656 | tf_op jit(solution)/shard_map/ppermute | solution.py:298
  99.8 2.9 collective-permute-start.21
  99.9 21.1 %collective-permute-start.16 = (bf16[12,128,128]{2,1,0:T(8,128)(2,1)S(1)}, bf16[12,128,128]{2,1,0:T(8,128)(2,1)}, u32[]{:S(2)}, u32[]{:S(2)}) collective-permute-start(bf16[12,128,128]{2,1,0:T(8,128)(2,1)S(1)} %get-tuple-element.16), channel_id=1, source_target_pairs={{0,4},{1,5},{2,6},{3,7},{4,0},{5,1},{6,2},{7,3},{8,12},{9,13},{10,... | collective-permute-start | bytes 1179656 | tf_op jit(solution)/shard_map/ppermute | solution.py:298
  122.1 10.9 %collective-permute-start.17 = (bf16[12,128,128]{2,1,0:T(8,128)(2,1)S(1)}, bf16[12,128,128]{2,1,0:T(8,128)(2,1)S(1)}, u32[]{:S(2)}, u32[]{:S(2)}) collective-permute-start(bf16[12,128,128]{2,1,0:T(8,128)(2,1)S(1)} %add_convert_fusion.7), channel_id=1, source_target_pairs={{0,2},{1,3},{2,0},{3,1},{4,6},{5,7},{6,4},{7,5},{8,10},{9,11},{10,... | collective-permute-start | bytes 1179656 | tf_op jit(solution)/shard_map/ppermute | solution.py:298
  134.1 4.9 %collective-permute-start.18 = (bf16[12,128,128]{2,1,0:T(8,128)(2,1)S(1)}, bf16[12,128,128]{2,1,0:T(8,128)(2,1)S(1)}, u32[]{:S(2)}, u32[]{:S(2)}) collective-permute-start(bf16[12,128,128]{2,1,0:T(8,128)(2,1)S(1)} %add_convert_fusion.6), channel_id=1, source_target_pairs={{0,1},{1,0},{2,3},{3,2},{4,5},{5,4},{6,7},{7,6},{8,9},{9,8},{10,11... | collective-permute-start | bytes 1179656 | tf_op jit(solution)/shard_map/ppermute | solution.py:298
  135.3 18.0 %all-to-all-start = ((bf16[64,4,2048]{2,0,1:T(8,128)(2,1)}), bf16[64,4,2048]{2,0,1:T(8,128)(2,1)S(1)}, u32[]{:S(2)}, u32[]{:S(2)}) async-start(bf16[64,4,2048]{2,0,1:T(8,128)(2,1)} %bitcast.23), calls=%async_computation | async-start | bytes 2097152 | tf_op jit(solution)/shard_map/all_to_all | solution.py:320
  139.1 104.1 %all-gather.11.cloned.1.call-start = ((), (), s32[]{:S(2)}) async-start(), calls=%async_computation.6 | async-start | bytes 1966080 | tf_op jit(solution)/shard_map/all_gather | solution.py:343
  140.0 112.6 %reduce-scatter.19.cloned.1.call-start = ((), (), s32[]{:S(2)}) async-start(), calls=%async_computation.12 | async-start | bytes 1966080
  153.4 2.7 collective-permute-start
  164.3 89.8 %all-gather.9.cloned.1.call-start = ((), (), s32[]{:S(2)}) async-start(), calls=%async_computation.5 | async-start | bytes 1966080 | tf_op jit(solution)/shard_map/all_gather | solution.py:343
  164.3 20.6 %collective-permute-start.13 = (bf16[12,128,128]{2,1,0:T(8,128)(2,1)S(1)}, bf16[12,128,128]{2,1,0:T(8,128)(2,1)S(1)}, u32[]{:S(2)}, u32[]{:S(2)}) collective-permute-start(bf16[12,128,128]{2,1,0:T(8,128)(2,1)S(1)} %get-tuple-element.15), channel_id=1, source_target_pairs={{0,4},{1,5},{2,6},{3,7},{4,0},{5,1},{6,2},{7,3},{8,12},{9,13},{10,... | collective-permute-start | bytes 1179656 | tf_op jit(solution)/shard_map/ppermute | solution.py:298
  185.0 10.4 %collective-permute-start.14 = (bf16[12,128,128]{2,1,0:T(8,128)(2,1)S(1)}, bf16[12,128,128]{2,1,0:T(8,128)(2,1)S(1)}, u32[]{:S(2)}, u32[]{:S(2)}) collective-permute-start(bf16[12,128,128]{2,1,0:T(8,128)(2,1)S(1)} %add_convert_fusion.9), channel_id=1, source_target_pairs={{0,2},{1,3},{2,0},{3,1},{4,6},{5,7},{6,4},{7,5},{8,10},{9,11},{10,... | collective-permute-start | bytes 1179656 | tf_op jit(solution)/shard_map/ppermute | solution.py:298
  198.3 77.3 %reduce-scatter.17.cloned.1.call-start = ((), (), s32[]{:S(2)}) async-start(), calls=%async_computation.11 | async-start | bytes 1966080
  205.4 104.7 %reduce-scatter.15.cloned.1.call-start = ((), (), s32[]{:S(2)}) async-start(), calls=%async_computation.10 | async-start | bytes 1966080
  212.5 135.8 %reduce-scatter.13.cloned.1.call-start = ((), (), s32[]{:S(2)}) async-start(), calls=%async_computation.9 | async-start | bytes 2621440
  252.6 97.2 %collective-permute-start.10 = (bf16[12,128,128]{2,1,0:T(8,128)(2,1)}, bf16[12,128,128]{2,1,0:T(8,128)(2,1)}, u32[]{:S(2)}, u32[]{:S(2)}) collective-permute-start(bf16[12,128,128]{2,1,0:T(8,128)(2,1)} %bitcast.40), channel_id=1, source_target_pairs={{0,2},{1,3},{2,0},{3,1},{4,6},{5,7},{6,4},{7,5},{8,10},{9,11},{10,... | collective-permute-start | bytes 1179656 | tf_op jit(solution)/shard_map/ppermute | solution.py:298
  275.6 77.9 %collective-permute-start.7 = (bf16[12,128,128]{2,1,0:T(8,128)(2,1)}, bf16[12,128,128]{2,1,0:T(8,128)(2,1)S(1)}, u32[]{:S(2)}, u32[]{:S(2)}) collective-permute-start(bf16[12,128,128]{2,1,0:T(8,128)(2,1)} %bitcast.41), channel_id=1, source_target_pairs={{0,2},{1,3},{2,0},{3,1},{4,6},{5,7},{6,4},{7,5},{8,10},{9,11},{10,... | collective-permute-start | bytes 1179656 | tf_op jit(solution)/shard_map/ppermute | solution.py:298
  310.1 44.1 %collective-permute-start.4 = (bf16[12,128,128]{2,1,0:T(8,128)(2,1)}, bf16[12,128,128]{2,1,0:T(8,128)(2,1)S(1)}, u32[]{:S(2)}, u32[]{:S(2)}) collective-permute-start(bf16[12,128,128]{2,1,0:T(8,128)(2,1)} %bitcast.42), channel_id=1, source_target_pairs={{0,2},{1,3},{2,0},{3,1},{4,6},{5,7},{6,4},{7,5},{8,10},{9,11},{10,... | collective-permute-start | bytes 1179656 | tf_op jit(solution)/shard_map/ppermute | solution.py:298
  348.3 23.8 %collective-permute-start.1 = (bf16[16,128,128]{2,1,0:T(8,128)(2,1)}, bf16[16,128,128]{2,1,0:T(8,128)(2,1)S(1)}, u32[]{:S(2)}, u32[]{:S(2)}) collective-permute-start(bf16[16,128,128]{2,1,0:T(8,128)(2,1)} %bitcast.39), channel_id=1, source_target_pairs={{0,2},{1,3},{2,0},{3,1},{4,6},{5,7},{6,4},{7,5},{8,10},{9,11},{10,... | collective-permute-start | bytes 1572872 | tf_op jit(solution)/shard_map/ppermute | solution.py:298
  351.1 21.9 %collective-permute-start.11 = (bf16[12,128,128]{2,1,0:T(8,128)(2,1)S(1)}, bf16[12,128,128]{2,1,0:T(8,128)(2,1)S(1)}, u32[]{:S(2)}, u32[]{:S(2)}) collective-permute-start(bf16[12,128,128]{2,1,0:T(8,128)(2,1)S(1)} %add_convert_fusion.11), channel_id=1, source_target_pairs={{0,4},{1,5},{2,6},{3,7},{4,0},{5,1},{6,2},{7,3},{8,12},{9,13},{10,... | collective-permute-start | bytes 1179656 | tf_op jit(solution)/shard_map/ppermute | solution.py:298
  353.7 55.3 %collective-permute-start.8 = (bf16[12,128,128]{2,1,0:T(8,128)(2,1)S(1)}, bf16[12,128,128]{2,1,0:T(8,128)(2,1)S(1)}, u32[]{:S(2)}, u32[]{:S(2)}) collective-permute-start(bf16[12,128,128]{2,1,0:T(8,128)(2,1)S(1)} %add_convert_fusion.13), channel_id=1, source_target_pairs={{0,4},{1,5},{2,6},{3,7},{4,0},{5,1},{6,2},{7,3},{8,12},{9,13},{10,... | collective-permute-start | bytes 1179656 | tf_op jit(solution)/shard_map/ppermute | solution.py:298
  354.4 63.0 %collective-permute-start.5 = (bf16[12,128,128]{2,1,0:T(8,128)(2,1)S(1)}, bf16[12,128,128]{2,1,0:T(8,128)(2,1)S(1)}, u32[]{:S(2)}, u32[]{:S(2)}) collective-permute-start(bf16[12,128,128]{2,1,0:T(8,128)(2,1)S(1)} %add_convert_fusion.15), channel_id=1, source_target_pairs={{0,4},{1,5},{2,6},{3,7},{4,0},{5,1},{6,2},{7,3},{8,12},{9,13},{10,... | collective-permute-start | bytes 1179656 | tf_op jit(solution)/shard_map/ppermute | solution.py:298
  372.3 55.0 %collective-permute-start.2 = (bf16[16,128,128]{2,1,0:T(8,128)(2,1)S(1)}, bf16[16,128,128]{2,1,0:T(8,128)(2,1)S(1)}, u32[]{:S(2)}, u32[]{:S(2)}) collective-permute-start(bf16[16,128,128]{2,1,0:T(8,128)(2,1)S(1)} %add_convert_fusion.3), channel_id=1, source_target_pairs={{0,4},{1,5},{2,6},{3,7},{4,0},{5,1},{6,2},{7,3},{8,12},{9,13},{10,... | collective-permute-start | bytes 1572872 | tf_op jit(solution)/shard_map/ppermute | solution.py:298
  373.1 54.4 %collective-permute-start.12 = (bf16[12,128,128]{2,1,0:T(8,128)(2,1)S(1)}, bf16[12,128,128]{2,1,0:T(8,128)(2,1)S(1)}, u32[]{:S(2)}, u32[]{:S(2)}) collective-permute-start(bf16[12,128,128]{2,1,0:T(8,128)(2,1)S(1)} %add_convert_fusion.10), channel_id=1, source_target_pairs={{0,1},{1,0},{2,3},{3,2},{4,5},{5,4},{6,7},{7,6},{8,9},{9,8},{10,11... | collective-permute-start | bytes 1179656 | tf_op jit(solution)/shard_map/ppermute | solution.py:298
  409.1 18.6 %collective-permute-start.9 = (bf16[12,128,128]{2,1,0:T(8,128)(2,1)S(1)}, bf16[12,128,128]{2,1,0:T(8,128)(2,1)S(1)}, u32[]{:S(2)}, u32[]{:S(2)}) collective-permute-start(bf16[12,128,128]{2,1,0:T(8,128)(2,1)S(1)} %add_convert_fusion.12), channel_id=1, source_target_pairs={{0,1},{1,0},{2,3},{3,2},{4,5},{5,4},{6,7},{7,6},{8,9},{9,8},{10,11... | collective-permute-start | bytes 1179656 | tf_op jit(solution)/shard_map/ppermute | solution.py:298
  417.6 10.3 %collective-permute-start.6 = (bf16[12,128,128]{2,1,0:T(8,128)(2,1)S(1)}, bf16[12,128,128]{2,1,0:T(8,128)(2,1)S(1)}, u32[]{:S(2)}, u32[]{:S(2)}) collective-permute-start(bf16[12,128,128]{2,1,0:T(8,128)(2,1)S(1)} %add_convert_fusion.14), channel_id=1, source_target_pairs={{0,1},{1,0},{2,3},{3,2},{4,5},{5,4},{6,7},{7,6},{8,9},{9,8},{10,11... | collective-permute-start | bytes 1179656 | tf_op jit(solution)/shard_map/ppermute | solution.py:298
  (23 other events, 324.2 us)
Sparse Core Ops, SparseCore 0:
  67.9 37.2 all-gather.14
  107.0 30.9 all-gather.12
  141.7 32.9 all-gather.10
  177.5 30.9 reduce-scatter.18
  210.8 30.9 all-gather.8
  244.6 30.9 reduce-scatter.16
  279.2 30.9 reduce-scatter.14
  313.1 35.1 reduce-scatter.12
where the time goes:
time: 446 us; the launch traced here: 445 us
  waiting for transfers between devices  290 us (65%)
  Pallas kernels  75.8 us (17%)
  starting transfers between devices  32.4 us (7%)
  local copies, waits for them, and re-layouts  16.6 us (4%)
  other arithmetic  16 us (4%)
  between operations  14.5 us (3%)
    ppermute x25, waiting for transfers between devices, partner(): return lax.ppermute(value, 'tensor', [(i, i ^ mask) for i in range(size)])  196 us
    unnamed x12, waiting for transfers between devices  81.1 us
    pallas_call x4, Pallas kernels, weight_grads(): pl.pallas_call(functools.partial(weights_kernel, first, per), grid=(size...  33.9 us
    ppermute x25, starting transfers between devices, partner(): return lax.ppermute(value, 'tensor', [(i, i ^ mask) for i in range(size)])  28.2 us
    pallas_call x4, Pallas kernels, unit_grads(): pl.pallas_call(functools.partial(units_kernel, first, per), grid=(size //...  24.9 us
    unnamed x42, local copies, waits for them, and re-layouts  15.5 us
    convert_element_type x24, other arithmetic, mix_across(): value = total.astype(BF16)  14.9 us
    all_to_all x1, waiting for transfers between devices, gather_upstream(): mine = lax.all_to_all(mine, 'dp', split_axis=1, concat_axis=0, tiled=True)  13.3 us
  transfers between devices with their start and end apart: 34, of which 20 were waited for; matrix products, arithmetic and copies ran while one was open for 2% of the time, Pallas kernels for 13%

commit v1 on v0

--- a/solution.py
+++ b/solution.py
@@ -12,15 +12,6 @@
 SUB = 16
 F32 = jnp.float32
 BF16 = jnp.bfloat16
-
-
-def chunk_plan(groups):
-    if groups % 4:
-        return (groups,), 1
-    units = groups // 4
-    count = min(4, units)
-    sizes = [units // count + (1 if i < units % count else 0) for i in range(count)]
-    return tuple(4 * size for size in sizes), 4
 
 
 def nt_dot(a, b):
@@ -102,7 +93,7 @@
         start = 0
         for size, out_ref in zip(sizes, outs):
             piece = result[start * SUB : (start + size) * SUB]
-            out_ref[:, j * SUB : (j + 1) * SUB, :] = piece.reshape(size, SUB, HB)
+            out_ref[j] = piece.reshape(size, SUB, HB)
             start += size
 
 
@@ -118,11 +109,7 @@
     stacked = jnp.concatenate(
         [
             jnp.concatenate(
-                [
-                    in_ref[:, j * SUB : (j + 1) * SUB, :].reshape(size * SUB, HB)
-                    for size, in_ref in zip(sizes, ins)
-                ],
-                axis=0,
+                [in_ref[j].reshape(size * SUB, HB) for size, in_ref in zip(sizes, ins)], axis=0
             )
             for j in range(parts)
         ],
@@ -152,19 +139,29 @@
     )
 
 
+ANYWHERE = pl.BlockSpec(memory_space=pl.ANY)
+
+
+def drop_inputs(kernel, start, count):
+    def run(*refs):
+        kernel(*refs[:start], *refs[start + count :])
+
+    return run
+
+
 def local_forward(hidden, rot_block, sizes):
     rows, width = hidden.shape
     blocks = width // HB
-    step = 2 * SUB
+    parts = 2
     return pl.pallas_call(
         functools.partial(forward_kernel, sizes),
-        grid=(rows // step,),
+        grid=(rows // (SUB * parts),),
         in_specs=[
-            pl.BlockSpec((step, width), lambda i: (i, 0)),
+            pl.BlockSpec((SUB * parts, width), lambda i: (i, 0)),
             pl.BlockSpec((blocks, blocks), lambda i: (0, 0)),
         ],
-        out_specs=[pl.BlockSpec((size, step, HB), lambda i: (0, i, 0)) for size in sizes],
-        out_shape=[jax.ShapeDtypeStruct((size, rows, HB), BF16) for size in sizes],
+        out_specs=[pl.BlockSpec((parts, size, SUB, HB), lambda i: (i, 0, 0, 0)) for size in sizes],
+        out_shape=[jax.ShapeDtypeStruct((rows // SUB, size, SUB, HB), BF16) for size in sizes],
         scratch_shapes=local_scratch(blocks),
         compiler_params=pltpu.CompilerParams(vmem_limit_bytes=32 << 20),
         cost_estimate=local_cost(rows, blocks),
@@ -172,25 +169,28 @@
     )(hidden, rot_block)
 
 
-def local_backward(mixed, rot_block, sizes):
-    rows = mixed[0].shape[1]
+def local_backward(mixed, rot_block, sizes, after=()):
+    count = mixed[0].shape[0]
+    rows = count * SUB
     blocks = rot_block.shape[0]
-    step = 2 * SUB
+    parts = 2
     return pl.pallas_call(
-        functools.partial(backward_kernel, sizes),
-        grid=(rows // step,),
-        in_specs=[pl.BlockSpec((size, step, HB), lambda i: (0, i, 0)) for size in sizes]
-        + [pl.BlockSpec((blocks, blocks), lambda i: (0, 0))],
-        out_specs=pl.BlockSpec((step, blocks * HB), lambda i: (i, 0)),
+        drop_inputs(functools.partial(backward_kernel, sizes), len(sizes) + 1, len(after)),
+        grid=(count // parts,),
+        in_specs=[pl.BlockSpec((parts, size, SUB, HB), lambda i: (i, 0, 0, 0)) for size in sizes]
+        + [pl.BlockSpec((blocks, blocks), lambda i: (0, 0))]
+        + [ANYWHERE] * len(after),
+        out_specs=pl.BlockSpec((parts * SUB, blocks * HB), lambda i: (i, 0)),
         out_shape=jax.ShapeDtypeStruct((rows, blocks * HB), BF16),
         scratch_shapes=local_scratch(blocks),
         compiler_params=pltpu.CompilerParams(vmem_limit_bytes=32 << 20),
         cost_estimate=local_cost(rows, blocks),
         name="local_backward",
-    )(*mixed, rot_block)
-
-
-def units_kernel(first, per, up_ref, w_ref, s_ref, out_ref, quant_ref):
+    )(*mixed, rot_block, *after)
+
+
+def units_kernel(first, per, up_ref, w_ref, s_ref, *refs):
+    outs, quant_ref = refs[:-1], refs[-1]
     base = first + pl.program_id(0) * per
     for g in range(per):
         rows = slice(g * GROUP, (g + 1) * GROUP)
@@ -198,26 +198,28 @@
             BF16
         )
     result = nt_dot(up_ref[...], quant_ref[...]).astype(BF16)
-    tokens = out_ref.shape[2]
-    for p in range(out_ref.shape[0]):
-        for g in range(per):
-            out_ref[p, g] = result[p * tokens : (p + 1) * tokens, g * GROUP : (g + 1) * GROUP]
-
-
-def unit_grads(up, weight, scales, first, size, per, parts):
+    token = 0
+    for out_ref in outs:
+        for q in range(out_ref.shape[0]):
+            for g in range(per):
+                out_ref[q, g] = result[token : token + SUB, g * GROUP : (g + 1) * GROUP]
+            token += SUB
+
+
+def unit_grads(up, weight, scales, first, size, per, counts, after=()):
     tokens, cols = up.shape
-    rows = tokens // parts
     offset = first // per
     return pl.pallas_call(
-        functools.partial(units_kernel, first, per),
+        drop_inputs(functools.partial(units_kernel, first, per), 3, len(after)),
         grid=(size // per,),
         in_specs=[
             pl.BlockSpec((tokens, cols), lambda i: (0, 0)),
             pl.BlockSpec((per * GROUP, cols), lambda i: (offset + i, 0)),
             pl.BlockSpec(scales.shape, lambda i: (0, 0)),
-        ],
-        out_specs=pl.BlockSpec((parts, per, rows, HB), lambda i: (0, i, 0, 0)),
-        out_shape=jax.ShapeDtypeStruct((parts, size, rows, HB), BF16),
+        ]
+        + [ANYWHERE] * len(after),
+        out_specs=[pl.BlockSpec((count, per, SUB, HB), lambda i: (0, i, 0, 0)) for count in counts],
+        out_shape=[jax.ShapeDtypeStruct((count, size, SUB, HB), BF16) for count in counts],
         scratch_shapes=[pltpu.VMEM((per * GROUP, cols), BF16)],
         compiler_params=pltpu.CompilerParams(vmem_limit_bytes=40 << 20),
         cost_estimate=pl.CostEstimate(
@@ -226,16 +228,23 @@
             transcendentals=0,
         ),
         name="unit_grads",
-    )(up, weight, scales)
-
-
-def weights_kernel(first, per, rot_ref, up_ref, w_ref, s_ref, m_ref, *refs):
+    )(up, weight, scales, *after)
+
+
+def weights_kernel(first, per, pieces, *refs):
+    rots = refs[:pieces]
+    up_ref, w_ref, s_ref, m_ref = refs[pieces : pieces + 4]
     gw_ref, gs_ref = refs[-2:]
     step = pl.program_id(0)
     base = first + step * per
-    parts = rot_ref.shape[0]
     left = jnp.concatenate(
-        [jnp.concatenate([rot_ref[p, g] for p in range(parts)], axis=0) for g in range(per)], axis=1
+        [
+            jnp.concatenate(
+                [rot_ref[q, g] for rot_ref in rots for q in range(rot_ref.shape[0])], axis=0
+            )
+            for g in range(per)
+        ],
+        axis=1,
     )
     cols = up_ref.shape[1]
     tile = min(512, cols)
@@ -253,27 +262,27 @@
             )
 
 
-def weight_grads(rotated, up, weight, scales, mask, buffer, first, size, per):
-    parts, _, rows, _ = rotated.shape
+def weight_grads(rotated, up, weight, scales, mask, buffer, first, size, per, after=()):
     tokens, cols = up.shape
     offset = first // per
     specs = [
-        pl.BlockSpec((parts, per, rows, HB), lambda i: (0, i, 0, 0)),
+        pl.BlockSpec((piece.shape[0], per, SUB, HB), lambda i: (0, i, 0, 0)) for piece in rotated
+    ] + [
         pl.BlockSpec((tokens, cols), lambda i: (0, 0)),
         pl.BlockSpec((per * GROUP, cols), lambda i: (offset + i, 0)),
         pl.BlockSpec(scales.shape, lambda i: (0, 0)),
         pl.BlockSpec(scales.shape, lambda i: (0, 0)),
     ]
-    args = [rotated, up, weight, scales, mask]
+    args = [*rotated, up, weight, scales, mask]
     aliases = {}
     if buffer is not None:
         aliases = {len(args): 0}
         args.append(buffer)
-        specs.append(pl.BlockSpec(memory_space=pl.ANY))
+        specs.append(ANYWHERE)
     return pl.pallas_call(
-        functools.partial(weights_kernel, first, per),
+        functools.partial(weights_kernel, first, per, len(rotated)),
         grid=(size // per,),
-        in_specs=specs,
+        in_specs=specs + [ANYWHERE] * len(after),
         out_specs=[
             pl.BlockSpec((per * GROUP, cols), lambda i: (offset + i, 0)),
             pl.BlockSpec((size, cols), lambda i: (0, 0)),
@@ -290,19 +299,68 @@
             transcendentals=0,
         ),
         name="weight_grads",
-    )(*args)
-
-
-def partner(value, mask):
-    size = lax.axis_size("tensor")
-    return lax.ppermute(value, "tensor", [(i, i ^ mask) for i in range(size)])
-
-
-def mix_across(value, masks):
+    )(*args, *after)
+
+
+def small_call(kernel, name, ins, outs, steps, after=()):
+    def spec(shape, dim):
+        block = tuple(n // steps if d == dim else n for d, n in enumerate(shape))
+        return pl.BlockSpec(
+            block, lambda i: tuple(i if d == dim else 0 for d in range(len(shape)))
+        )
+
+    return pl.pallas_call(
+        drop_inputs(kernel, len(ins), len(after)),
+        grid=(steps,),
+        in_specs=[spec(value.shape, 1) for value in ins] + [ANYWHERE] * len(after),
+        out_specs=[spec(shape, 1) for shape in outs],
+        out_shape=[jax.ShapeDtypeStruct(shape, BF16) for shape in outs],
+        compiler_params=pltpu.CompilerParams(vmem_limit_bytes=32 << 20),
+        cost_estimate=pl.CostEstimate(
+            flops=0,
+            bytes_accessed=2 * sum(v.size for v in ins) * 2,
+            transcendentals=0,
+        ),
+        name=name,
+    )(*ins, *after)
+
+
+def transform_kernel(x_ref, out_ref):
+    count = x_ref.shape[0]
+    values = [x_ref[t].astype(F32) for t in range(count)]
+    stride = 1
+    while stride < count:
+        for t in range(count):
+            if not t & stride:
+                a, b = values[t], values[t | stride]
+                values[t], values[t | stride] = a + b, a - b
+        stride *= 2
+    for t in range(count):
+        out_ref[t] = (values[t] * count ** (-0.5)).astype(BF16)
+
+
+def transform(value, after=()):
+    steps = 4 if value.shape[1] % 4 == 0 else 1
+    return small_call(
+        transform_kernel, "transform", [value], [value.shape], steps, after
+    )[0]
+
+
+def exchange(value):
+    return lax.all_to_all(value, "tensor", split_axis=0, concat_axis=0, tiled=True)
+
+
+def partner(value, axis, mask):
+    size = lax.axis_size(axis)
+    return lax.ppermute(value, axis, [(i, i ^ mask) for i in range(size)])
+
+
+def mix_across(value):
     size = lax.axis_size("tensor")
     index = lax.axis_index("tensor")
+    masks = [1 << i for i in range(size.bit_length() - 1)]
     for place, mask in enumerate(masks):
-        other = partner(value, mask).astype(F32)
+        other = partner(value, "tensor", mask).astype(F32)
         sign = jnp.where((index & mask) != 0, -1.0, 1.0).astype(F32)
         total = other + sign * value.astype(F32)
         if place == len(masks) - 1:
@@ -312,53 +370,132 @@
 
 
 def gather_upstream(upstream):
-    rows = upstream.shape[0]
+    rows, width = upstream.shape
     parts = lax.axis_size("dp")
+    cols = width // parts
     half = rows // 2
+    index = lax.axis_index("dp")
     core = lax.axis_index("tensor") & 1
-    mine = lax.dynamic_slice_in_dim(upstream, core * half, half, axis=0)
-    mine = lax.all_to_all(mine, "dp", split_axis=1, concat_axis=0, tiled=True)
-    other = partner(mine, 1)
-    cols = mine.shape[1]
-    mine = mine.reshape(parts, half, cols)
-    other = other.reshape(parts, half, cols)
+    own = lax.dynamic_slice(upstream, (0, index * cols), (rows, cols))
+    mine = [
+        partner(
+            lax.dynamic_slice(upstream, (core * half, (index ^ m) * cols), (half, cols)), "dp", m
+        )
+        for m in range(1, parts)
+    ]
+    mine = jnp.stack(mine)
+    other = partner(mine, "tensor", 1)
     low = jnp.where(core == 0, mine, other)
     high = jnp.where(core == 0, other, mine)
-    return jnp.concatenate([low, high], axis=1).reshape(parts * rows, cols)
+    far = jnp.concatenate([low, high], axis=1).reshape((parts - 1) * rows, cols)
+    return jnp.concatenate([own, far], axis=0)
+
+
+def relay_kernel(x_ref, y_ref, a_ref, b_ref, x_out, y_out):
+    half = a_ref.shape[0]
+    x_out[:half] = x_ref[:half]
+    x_out[half:] = (x_ref[half:].astype(F32) + b_ref[...].astype(F32)).astype(BF16)
+    y_out[:half] = (y_ref[:half].astype(F32) + a_ref[...].astype(F32)).astype(BF16)
+    y_out[half:] = y_ref[half:]
+
+
+def total_kernel(own_ref, x_ref, y_ref, out_ref):
+    out_ref[...] = (
+        own_ref[...].astype(F32) + x_ref[...].astype(F32) + y_ref[...].astype(F32)
+    ).astype(BF16)
+
+
+def general_shards(hidden, upstream, weight, scales, clip_mask, rot_block):
+    groups = scales.shape[0]
+    rows = hidden.shape[0]
+    parts = lax.axis_size("dp")
+    subs = rows // SUB
+    index = lax.axis_index("dp")
+
+    up = gather_upstream(upstream)
+    (local,) = local_forward(hidden, rot_block, (groups,))
+    rotated = lax.all_gather(mix_across(local), "dp", axis=0, tiled=False)
+    order = index ^ jnp.arange(parts)
+    rotated = rotated[order].reshape((parts * subs,) + local.shape[1:])
+    per = 4 if groups % 4 == 0 else 1
+    (full,) = unit_grads(up, weight, scales, 0, groups, per, (parts * subs,))
+    full = full.reshape((parts,) + local.shape)[order]
+    mixed = mix_across(lax.psum_scatter(full, "dp", scatter_dimension=0, tiled=False))
+    grad_weight, grad_scales = weight_grads(
+        [rotated], up, weight, scales, clip_mask, None, 0, groups, per
+    )
+    grad_hidden = local_backward([mixed], rot_block, (groups,))
+    return grad_hidden, grad_weight, grad_scales
 
 
 def shards(hidden, upstream, weight, scales, clip_mask, rot_block):
     groups = scales.shape[0]
-    parts = lax.axis_size("dp")
-    size = lax.axis_size("tensor")
-    sizes, per = chunk_plan(groups)
-    starts = [sum(sizes[:i]) for i in range(len(sizes))]
-    bits = [1 << i for i in range(size.bit_length() - 1)]
-    down = bits[::-1]
-    up_first = bits[1:] + bits[:1]
+    subs = hidden.shape[0] // SUB
+    if lax.axis_size("dp") != 4 or lax.axis_size("tensor") != subs or groups % 8 != 4:
+        return general_shards(hidden, upstream, weight, scales, clip_mask, rot_block)
+    per = 4
+    units = groups // per
+    sizes = (per * (units - units // 2), per * (units // 2))
+    starts = (0, sizes[0])
+    half = subs // 2
+    counts = (subs, subs, subs, half, half)
+
+    def scatter_first(parts_of):
+        return partner(parts_of[3], "dp", 1), partner(parts_of[4], "dp", 2)
+
+    def scatter_second(parts_of, received, after):
+        x_part, y_part = small_call(
+            relay_kernel,
+            "relay",
+            [parts_of[1], parts_of[2], *received],
+            [parts_of[1].shape] * 2,
+            2,
+            after,
+        )
+        return partner(x_part, "dp", 1), partner(y_part, "dp", 2)
+
+    def scatter_last(parts_of, received, after):
+        return small_call(
+            total_kernel, "total", [parts_of[0], *received], [parts_of[0].shape], 2, after
+        )[0]
+
+    def gather(value):
+        x_part, y_part = partner(value, "dp", 1), partner(value, "dp", 2)
+        return value, x_part, y_part, partner(y_part[:half], "dp", 1), partner(
+            x_part[half:], "dp", 2
+        )
 
     up = gather_upstream(upstream)
     local = local_forward(hidden, rot_block, sizes)
-    rotated = [mix_across(value, down) for value in local]
-    gathered = [lax.all_gather(value, "dp", axis=0, tiled=False) for value in rotated]
-
-    sums = []
-    for start, count in zip(starts, sizes):
-        full = unit_grads(up, weight, scales, start, count, per, parts)
-        sums.append(
-            lax.psum_scatter(full, "dp", scatter_dimension=0, tiled=False)
-        )
-    mixed = [mix_across(value, up_first) for value in sums]
-
-    buffer = None
-    scale_grads = []
-    for value, start, count in zip(gathered, starts, sizes):
-        buffer, scale_grad = weight_grads(
-            value, up, weight, scales, clip_mask, buffer, start, count, per
-        )
-        scale_grads.append(scale_grad)
-    grad_hidden = local_backward(mixed, rot_block, sizes)
-    return (grad_hidden, buffer, jnp.concatenate(scale_grads, axis=0))
+    forth = [exchange(value) for value in local]
+    unit0 = unit_grads(up, weight, scales, starts[0], sizes[0], per, counts, after=(local[0],))
+    first0 = scatter_first(unit0)
+    turned0 = transform(forth[0], after=(unit0[0],))
+    rotated0 = exchange(turned0)
+    unit1 = unit_grads(up, weight, scales, starts[1], sizes[1], per, counts, after=(turned0,))
+    first1 = scatter_first(unit1)
+    second0 = scatter_second(unit0, first0, after=(unit1[0],))
+    turned1 = transform(forth[1], after=(unit1[0],))
+    rotated1 = exchange(turned1)
+    second1 = scatter_second(unit1, first1, after=(turned1,))
+    sum0 = scatter_last(unit0, second0, after=(turned1,))
+    back0 = exchange(sum0)
+    sum1 = scatter_last(unit1, second1, after=(sum0,))
+    back1 = exchange(sum1)
+    gathered0 = gather(rotated0)
+    gathered1 = gather(rotated1)
+    mixed0 = transform(back0, after=(sum1,))
+    final0 = exchange(mixed0)
+    buffer, scale0 = weight_grads(
+        gathered0, up, weight, scales, clip_mask, None, starts[0], sizes[0], per, after=(mixed0,)
+    )
+    mixed1 = transform(back1, after=(scale0,))
+    final1 = exchange(mixed1)
+    buffer, scale1 = weight_grads(
+        gathered1, up, weight, scales, clip_mask, buffer, starts[1], sizes[1], per, after=(mixed1,)
+    )
+    grad_hidden = local_backward([final0, final1], rot_block, sizes, after=(scale1,))
+    return grad_hidden, buffer, jnp.concatenate([scale0, scale1], axis=0)
 
 
 def solution(mesh):

time: 446 us -> 315 us (0.71)
  waiting for transfers between devices: 290 us -> 113 us
  blocking collectives: 0 us -> 25.9 us
  starting transfers between devices: 32.4 us -> 56.3 us
  between operations: 14.5 us -> 0.93 us
  local copies, waits for them, and re-layouts: 16.6 us -> 29.9 us
  other arithmetic: 16 us -> 3.97 us
  Pallas kernels: 75.8 us -> 82.9 us
    ppermute x25 -> x20, waiting for transfers between devices: 196 us -> 78.3 us  [partner(): return lax.ppermute(value, axis, [(i, i ^ mask) for i in range(size)])]
    unnamed x12 -> x0, waiting for transfers between devices: 81.1 us -> none
    all_to_all x1 -> x7, starting transfers between devices: 3.72 us -> 31.4 us  [exchange(): lax.all_to_all(value, 'tensor', split_axis=0, concat_axis=0, tiled=True)]
    all_to_all x0 -> x1, blocking collectives: none -> 25.9 us  [exchange(): lax.all_to_all(value, 'tensor', split_axis=0, concat_axis=0, tiled=True)]
    all_to_all x1 -> x7, waiting for transfers between devices: 13.3 us -> 34.5 us  [exchange(): lax.all_to_all(value, 'tensor', split_axis=0, concat_axis=0, tiled=True)]
    convert_element_type x24 -> x0, other arithmetic: 14.9 us -> none  [mix_across(): value = total.astype(BF16)]
    unnamed x42 -> x68, local copies, waits for them, and re-layouts: 15.5 us -> 22.7 us
    pallas_call x10 -> x14, Pallas kernels: 75.8 us -> 82.9 us  [the longest x2 31.2 us: weight_grads(): pl.pallas_call(functools.partial(weights_kernel, first, per, len(rotated)...]
  transfers between devices with their start and end apart: 34 -> 27, of which waited for: 20 -> 14; matrix products, arithmetic and copies ran while one was open for 2% -> 3% of each run, Pallas kernels for 13% -> 23%
where the time goes in v1:
time: 315 us; the launch traced here: 313 us
  waiting for transfers between devices  113 us (36%)
  Pallas kernels  82.9 us (26%)
  starting transfers between devices  56.3 us (18%)
  local copies, waits for them, and re-layouts  29.9 us (9%)
  blocking collectives  25.9 us (8%)
  other arithmetic  3.97 us (1%)
    ppermute x20, waiting for transfers between devices, partner(): return lax.ppermute(value, axis, [(i, i ^ mask) for i in range(size)])  78.3 us
    all_to_all x7, waiting for transfers between devices, exchange(): lax.all_to_all(value, 'tensor', split_axis=0, concat_axis=0, tiled=True)  34.5 us
    all_to_all x7, starting transfers between devices, exchange(): lax.all_to_all(value, 'tensor', split_axis=0, concat_axis=0, tiled=True)  31.4 us
    pallas_call x2, Pallas kernels, weight_grads(): pl.pallas_call(functools.partial(weights_kernel, first, per, len(rotated)...  31.2 us
    all_to_all x1, blocking collectives, exchange(): lax.all_to_all(value, 'tensor', split_axis=0, concat_axis=0, tiled=True)  25.9 us
    ppermute x20, starting transfers between devices, partner(): return lax.ppermute(value, axis, [(i, i ^ mask) for i in range(size)])  24.9 us
    unnamed x68, local copies, waits for them, and re-layouts  22.7 us
    pallas_call x2, Pallas kernels, unit_grads(): pl.pallas_call(drop_inputs(functools.partial(units_kernel, first, per), 3...  22.1 us
  transfers between devices with their start and end apart: 27, of which 14 were waited for; matrix products, arithmetic and copies ran while one was open for 3% of the time, Pallas kernels for 23%

profile of v1, /device:TPU:0, one launch (start us, length us, event | category | flops | bytes accessed | tf_op | source)
XLA Modules:
  0.0 312.7 jit_solution(544491403065762009)
XLA Ops:
  1.8 3.0 collective-permute-start
  8.6 8.7 %local_forward.1 = (bf16[8,28,16,128]{3,2,1,0:T(8,128)(2,1)}, bf16[8,24,16,128]{3,2,1,0:T(8,128)(2,1)}) custom-call(bf16[128,6656]{1,0:T(8,128)(2,1)S(1)} %copy-done.27, f32[52,52]{1,0:T(8,128)S(1)} %copy-done.32), custom_call_target="tpu_custom_call" | custom-call | flops 2835349504 | bytes 3407872 | tf_op jit(solution)/shard_map/local_forward/pallas_call | solution.py:156
  17.2 5.3 %all-to-all-start = ((bf16[8,28,16,128]{3,2,1,0:T(8,128)(2,1)}), bf16[8,28,16,128]{3,2,1,0:T(8,128)(2,1)S(1)}, u32[]{:S(2)}, u32[]{:S(2)}) async-start(bf16[8,28,16,128]{3,2,1,0:T(8,128)(2,1)} %get-tuple-element.23.refs_3_), calls=%async_computation | async-start | bytes 1835008 | tf_op jit(solution)/shard_map/all_to_all | solution.py:350
  23.3 1.9 constant_dynamic-slice_fusion
  26.6 19.8 %all-to-all-done.refs_0_ = bf16[8,28,16,128]{3,2,1,0:T(8,128)(2,1)S(1)} async-done(((bf16[8,28,16,128]{3,2,1,0:T(8,128)(2,1)}), bf16[8,28,16,128]{3,2,1,0:T(8,128)(2,1)S(1)}, u32[]{:S(2)}, u32[]{:S(2)}) %all-to-all-start) | async-done | bytes 917536 | tf_op jit(solution)/shard_map/all_to_all | solution.py:350
  46.4 3.5 %all-to-all-start.1 = ((bf16[8,24,16,128]{3,2,1,0:T(8,128)(2,1)}), bf16[8,24,16,128]{3,2,1,0:T(8,128)(2,1)S(1)}, u32[]{:S(2)}, u32[]{:S(2)}) async-start(bf16[8,24,16,128]{3,2,1,0:T(8,128)(2,1)} %get-tuple-element.32), calls=%async_computation.1 | async-start | bytes 1572864 | tf_op jit(solution)/shard_map/all_to_all | solution.py:350
  50.0 1.7 pad_maximum_fusion.refs_0_.refs_5_
  51.7 11.8 %unit_grads.2 = (bf16[8,28,16,128]{3,2,1,0:T(8,128)(2,1)S(1)}, bf16[8,28,16,128]{3,2,1,0:T(8,128)(2,1)S(1)}, bf16[8,28,16,128]{3,2,1,0:T(8,128)(2,1)S(1)}, bf16[...) custom-call(bf16[512,2048]{1,0:T(8,128)(2,1)S(1)} %pad_maximum_fusion.refs_0_.refs_5_, ...), custom_call_target="tpu_custom_call" | custom-call | flops 7516192768 | bytes 20447232 | tf_op jit(solution)/shard_map/unit_grads/pallas_call | solution.py:212
  67.2 10.2 %unit_grads.3 = (bf16[8,24,16,128]{3,2,1,0:T(8,128)(2,1)S(1)}, bf16[8,24,16,128]{3,2,1,0:T(8,128)(2,1)S(1)}, bf16[8,24,16,128]{3,2,1,0:T(8,128)(2,1)S(1)}, bf16[...) custom-call(bf16[512,2048]{1,0:T(8,128)(2,1)S(1)} %pad_maximum_fusion.refs_0_.refs_5_, ...), custom_call_target="tpu_custom_call" | custom-call | flops 6442450944 | bytes 17825792 | tf_op jit(solution)/shard_map/unit_grads/pallas_call | solution.py:212
  86.3 25.9 %all_to_all.40.refs_0_ = bf16[8,24,16,128]{3,2,1,0:T(8,128)(2,1)} all-to-all(bf16[8,24,16,128]{3,2,1,0:T(8,128)(2,1)S(1)} %transform.5.refs_3_.refs_4_), channel_id=1, replica_groups=mesh['dp'=4,'tensor'=8] {'tensor'}, dimensions={0} | all-to-all | bytes 1572864 | tf_op jit(solution)/shard_map/all_to_all | solution.py:350
  112.2 4.2 %all-to-all-start.5 = ((bf16[8,28,16,128]{3,2,1,0:T(8,128)(2,1)}), bf16[8,28,16,128]{3,2,1,0:T(8,128)(2,1)}, u32[]{:S(2)}, u32[]{:S(2)}) async-start(bf16[8,28,16,128]{3,2,1,0:T(8,128)(2,1)} %copy-done.2), calls=%async_computation.5 | async-start | bytes 1835008 | tf_op jit(solution)/shard_map/all_to_all | solution.py:350
  116.4 1.5 collective-permute-start.4
  118.0 1.5 collective-permute-start.5
  119.5 9.9 %collective-permute-done.4.refs_2_ = bf16[4,28,16,128]{3,2,1,0:T(8,128)(2,1)S(1)} collective-permute-done((bf16[4,28,16,128]{3,2,1,0:T(8,128)(2,1)}, bf16[4,28,16,128]{3,2,1,0:T(8,128)(2,1)S(1)}, u32[]{:S(2)}, u32[]{:S(2)}) %collective-permute-start.4) | collective-permute-done | bytes 458784 | tf_op jit(solution)/shard_map/ppermute | solution.py:355
  136.9 19.5 %collective-permute-done.6.refs_1_ = bf16[8,28,16,128]{3,2,1,0:T(8,128)(2,1)S(1)} collective-permute-done((bf16[8,28,16,128]{3,2,1,0:T(8,128)(2,1)S(1)}, bf16[8,28,16,128]{3,2,1,0:T(8,128)(2,1)S(1)}, u32[]{:S(2)}, u32[]{:S(2)}) %collective-permute-start.6) | collective-permute-done | bytes 917536 | tf_op jit(solution)/shard_map/ppermute | solution.py:355
  158.2 4.7 %all-to-all-start.2 = ((bf16[8,28,16,128]{3,2,1,0:T(8,128)(2,1)}), bf16[8,28,16,128]{3,2,1,0:T(8,128)(2,1)}, u32[]{:S(2)}, u32[]{:S(2)}) async-start(bf16[8,28,16,128]{3,2,1,0:T(8,128)(2,1)} %copy-done), calls=%async_computation.2 | async-start | bytes 1835008 | tf_op jit(solution)/shard_map/all_to_all | solution.py:350
  165.8 8.8 %collective-permute-done.8.refs_2_ = bf16[4,24,16,128]{3,2,1,0:T(8,128)(2,1)S(1)} collective-permute-done((bf16[4,24,16,128]{3,2,1,0:T(8,128)(2,1)}, bf16[4,24,16,128]{3,2,1,0:T(8,128)(2,1)S(1)}, u32[]{:S(2)}, u32[]{:S(2)}) %collective-permute-start.8) | collective-permute-done | bytes 393248 | tf_op jit(solution)/shard_map/ppermute | solution.py:355
  180.8 16.6 %collective-permute-done.10.refs_1_ = bf16[8,24,16,128]{3,2,1,0:T(8,128)(2,1)S(1)} collective-permute-done((bf16[8,24,16,128]{3,2,1,0:T(8,128)(2,1)S(1)}, bf16[8,24,16,128]{3,2,1,0:T(8,128)(2,1)S(1)}, u32[]{:S(2)}, u32[]{:S(2)}) %collective-permute-start.10) | collective-permute-done | bytes 786464 | tf_op jit(solution)/shard_map/ppermute | solution.py:355
  199.1 4.4 %all-to-all-start.4 = ((bf16[8,24,16,128]{3,2,1,0:T(8,128)(2,1)}), bf16[8,24,16,128]{3,2,1,0:T(8,128)(2,1)}, u32[]{:S(2)}, u32[]{:S(2)}) async-start(bf16[8,24,16,128]{3,2,1,0:T(8,128)(2,1)} %total.3.refs_1_), calls=%async_computation.4 | async-start | bytes 1572864 | tf_op jit(solution)/shard_map/all_to_all | solution.py:350
  206.4 3.5 %transform.6.refs_9_ = bf16[8,28,16,128]{3,2,1,0:T(8,128)(2,1)} custom-call(bf16[8,28,16,128]{3,2,1,0:T(8,128)(2,1)} %all-to-all-done.2.refs_0_, bf16[8,24,16,128]{3,2,1,0:T(8,128)(2,1)} %total.3.refs_1_), custom_call_target="tpu_custom_call" | custom-call | bytes 1835008 | tf_op jit(solution)/shard_map/transform/pallas_call | solution.py:312
  209.9 14.7 %all-to-all-done.4.refs_0_ = bf16[8,24,16,128]{3,2,1,0:T(8,128)(2,1)} async-done(((bf16[8,24,16,128]{3,2,1,0:T(8,128)(2,1)}), bf16[8,24,16,128]{3,2,1,0:T(8,128)(2,1)}, u32[]{:S(2)}, u32[]{:S(2)}) %all-to-all-start.4) | async-done | bytes 786464 | tf_op jit(solution)/shard_map/all_to_all | solution.py:350
  224.6 4.2 %all-to-all-start.3 = ((bf16[8,28,16,128]{3,2,1,0:T(8,128)(2,1)}), bf16[8,28,16,128]{3,2,1,0:T(8,128)(2,1)}, u32[]{:S(2)}, u32[]{:S(2)}) async-start(bf16[8,28,16,128]{3,2,1,0:T(8,128)(2,1)} %transform.6.refs_9_), calls=%async_computation.3 | async-start | bytes 1835008 | tf_op jit(solution)/shard_map/all_to_all | solution.py:350
  232.4 1.6 collective-permute-start.15
  235.2 8.2 %collective-permute-done.14.refs_3_ = bf16[4,28,16,128]{3,2,1,0:T(8,128)(2,1)S(1)} collective-permute-done((bf16[4,28,16,128]{3,2,1,0:T(8,128)(2,1)S(1)}, bf16[4,28,16,128]{3,2,1,0:T(8,128)(2,1)S(1)}, u32[]{:S(2)}, u32[]{:S(2)}) %collective-permute-start.14) | collective-permute-done | bytes 458784 | tf_op jit(solution)/shard_map/ppermute | solution.py:355
  243.4 2.5 collective-permute-done.15.refs_4_
  245.9 17.3 %weight_grads.2 = (bf16[6656,2048]{1,0:T(8,128)(2,1)}, f32[28,2048]{1,0:T(8,128)S(1)}) custom-call(bf16[8,28,16,128]{3,2,1,0:T(8,128)(2,1)} %all-to-all-done.5.refs_0_, bf16[8,28,16,128]{3,2,1,0:T(8,128)(2,1)} %collective-permute-done.12.refs_1_, bf16[8,28,16,128]{3,2,1,0:T(8,128)(2,1)} %collective-permute-done.13.refs_2_, ...), custom_call_target="tpu_custom_call" | custom-call | flops 7516192768 | bytes 35127296 | tf_op jit(solution)/shard_map/weight_grads/pallas_call | solution.py:282
  263.2 3.4 %transform.7.refs_10_ = bf16[8,24,16,128]{3,2,1,0:T(8,128)(2,1)} custom-call(bf16[8,24,16,128]{3,2,1,0:T(8,128)(2,1)} %all-to-all-done.4.refs_0_, f32[28,2048]{1,0:T(8,128)S(1)} %get-tuple-element.39.refs_1_), custom_call_target="tpu_custom_call" | custom-call | bytes 1572864 | tf_op jit(solution)/shard_map/transform/pallas_call | solution.py:312
  267.3 5.0 %all-to-all-start.6 = ((bf16[8,24,16,128]{3,2,1,0:T(8,128)(2,1)}), bf16[8,24,16,128]{3,2,1,0:T(8,128)(2,1)}, u32[]{:S(2)}, u32[]{:S(2)}) async-start(bf16[8,24,16,128]{3,2,1,0:T(8,128)(2,1)} %transform.7.refs_10_), calls=%async_computation.6 | async-start | bytes 1572864 | tf_op jit(solution)/shard_map/all_to_all | solution.py:350
  275.1 1.6 collective-permute-start.19
  276.7 8.2 %collective-permute-done.18.refs_3_ = bf16[4,24,16,128]{3,2,1,0:T(8,128)(2,1)S(1)} collective-permute-done((bf16[4,24,16,128]{3,2,1,0:T(8,128)(2,1)S(1)}, bf16[4,24,16,128]{3,2,1,0:T(8,128)(2,1)S(1)}, u32[]{:S(2)}, u32[]{:S(2)}) %collective-permute-start.18) | collective-permute-done | bytes 393248 | tf_op jit(solution)/shard_map/ppermute | solution.py:355
  287.4 13.9 %weight_grads.3 = (bf16[6656,2048]{1,0:T(8,128)(2,1)}, f32[24,2048]{1,0:T(8,128)S(1)}) custom-call(bf16[8,24,16,128]{3,2,1,0:T(8,128)(2,1)S(1)} %copy-done.12, bf16[8,24,16,128]{3,2,1,0:T(8,128)(2,1)} %collective-permute-done.16.refs_1_, bf16[8,24,16,128]{3,2,1,0:T(8,128)(2,1)} %collective-permute-done.17.refs_2_, ...), custom_call_target="tpu_custom_call", output_to_operand_aliasing={{0}: (9, {})} | custom-call | flops 6442450944 | bytes 30408704 | tf_op jit(solution)/shard_map/weight_grads/pallas_call | solution.py:282
  302.9 9.8 %local_backward.1 = bf16[128,6656]{1,0:T(8,128)(2,1)} custom-call(bf16[8,28,16,128]{3,2,1,0:T(8,128)(2,1)} %all-to-all-done.3.refs_0_, bf16[8,24,16,128]{3,2,1,0:T(8,128)(2,1)} %all-to-all-done.6.refs_1_, f32[52,52]{1,0:T(8,128)S(1)} %copy-done.33, f32[24,2048]{1,0:T(8,128)S(1)} %get-tuple-element.41.refs_3_), custom_call_target="tpu_custom_call" | custom-call | flops 2835349504 | bytes 3407872 | tf_op jit(solution)/shard_map/local_backward/pallas_call | solution.py:177
  (116 shorter events, 54.7 us)
Async XLA Ops:
  1.8 20.8 %collective-permute-start = (bf16[64,2048]{1,0:T(8,128)(2,1)S(1)}, bf16[64,2048]{1,0:T(8,128)(2,1)S(1)}, u32[]{:S(2)}, u32[]{:S(2)}) collective-permute-start(bf16[64,2048]{1,0:T(8,128)(2,1)S(1)} %get-tuple-element.43), channel_id=1, source_target_pairs={{0,8},{8,0},{16,24},{24,16},{1,9},{9,1},{17,25},{25,17},{2,10},{10... | collective-permute-start | bytes 786440 | tf_op jit(solution)/shard_map/ppermute | solution.py:355
  4.8 17.8 %collective-permute-start.2 = (bf16[64,2048]{1,0:T(8,128)(2,1)S(1)}, bf16[64,2048]{1,0:T(8,128)(2,1)S(1)}, u32[]{:S(2)}, u32[]{:S(2)}) collective-permute-start(bf16[64,2048]{1,0:T(8,128)(2,1)S(1)} %get-tuple-element.44), channel_id=1, source_target_pairs={{0,24},{8,16},{16,8},{24,0},{1,25},{9,17},{17,9},{25,1},{2,26},{10... | collective-permute-start | bytes 786440 | tf_op jit(solution)/shard_map/ppermute | solution.py:355
  6.3 16.3 %collective-permute-start.1 = (bf16[64,2048]{1,0:T(8,128)(2,1)S(1)}, bf16[64,2048]{1,0:T(8,128)(2,1)S(1)}, u32[]{:S(2)}, u32[]{:S(2)}) collective-permute-start(bf16[64,2048]{1,0:T(8,128)(2,1)S(1)} %get-tuple-element.45), channel_id=1, source_target_pairs={{0,16},{8,24},{16,0},{24,8},{1,17},{9,25},{17,1},{25,9},{2,18},{10... | collective-permute-start | bytes 786440 | tf_op jit(solution)/shard_map/ppermute | solution.py:355
  17.2 29.1 %all-to-all-start = ((bf16[8,28,16,128]{3,2,1,0:T(8,128)(2,1)}), bf16[8,28,16,128]{3,2,1,0:T(8,128)(2,1)S(1)}, u32[]{:S(2)}, u32[]{:S(2)}) async-start(bf16[8,28,16,128]{3,2,1,0:T(8,128)(2,1)} %get-tuple-element.23.refs_3_), calls=%async_computation | async-start | bytes 1835008 | tf_op jit(solution)/shard_map/all_to_all | solution.py:350
  22.7 2.5 collective-permute-start.3
  46.4 36.2 %all-to-all-start.1 = ((bf16[8,24,16,128]{3,2,1,0:T(8,128)(2,1)}), bf16[8,24,16,128]{3,2,1,0:T(8,128)(2,1)S(1)}, u32[]{:S(2)}, u32[]{:S(2)}) async-start(bf16[8,24,16,128]{3,2,1,0:T(8,128)(2,1)} %get-tuple-element.32), calls=%async_computation.1 | async-start | bytes 1572864 | tf_op jit(solution)/shard_map/all_to_all | solution.py:350
  112.2 46.0 %all-to-all-start.5 = ((bf16[8,28,16,128]{3,2,1,0:T(8,128)(2,1)}), bf16[8,28,16,128]{3,2,1,0:T(8,128)(2,1)}, u32[]{:S(2)}, u32[]{:S(2)}) async-start(bf16[8,28,16,128]{3,2,1,0:T(8,128)(2,1)} %copy-done.2), calls=%async_computation.5 | async-start | bytes 1835008 | tf_op jit(solution)/shard_map/all_to_all | solution.py:350
  116.4 13.0 %collective-permute-start.4 = (bf16[4,28,16,128]{3,2,1,0:T(8,128)(2,1)}, bf16[4,28,16,128]{3,2,1,0:T(8,128)(2,1)S(1)}, u32[]{:S(2)}, u32[]{:S(2)}) collective-permute-start(bf16[4,28,16,128]{3,2,1,0:T(8,128)(2,1)} %copy-done.29), channel_id=1, source_target_pairs={{0,8},{8,0},{16,24},{24,16},{1,9},{9,1},{17,25},{25,17},{2,10},{10... | collective-permute-start | bytes 1376264 | tf_op jit(solution)/shard_map/ppermute | solution.py:355
  118.0 12.7 %collective-permute-start.5 = (bf16[4,28,16,128]{3,2,1,0:T(8,128)(2,1)}, bf16[4,28,16,128]{3,2,1,0:T(8,128)(2,1)S(1)}, u32[]{:S(2)}, u32[]{:S(2)}) collective-permute-start(bf16[4,28,16,128]{3,2,1,0:T(8,128)(2,1)} %copy-done.28), channel_id=1, source_target_pairs={{0,16},{8,24},{16,0},{24,8},{1,17},{9,25},{17,1},{25,9},{2,18},{10... | collective-permute-start | bytes 1376264 | tf_op jit(solution)/shard_map/ppermute | solution.py:355
  134.1 22.5 %copy-start.11 = (bf16[8,28,16,128]{3,2,1,0:T(8,128)(2,1)S(1)}, bf16[8,28,16,128]{3,2,1,0:T(8,128)(2,1)}, u32[]{:S(2)}) copy-start(bf16[8,28,16,128]{3,2,1,0:T(8,128)(2,1)} %copy-done.10) | copy-start | bytes 2752516
  134.8 21.6 %collective-permute-start.6 = (bf16[8,28,16,128]{3,2,1,0:T(8,128)(2,1)S(1)}, bf16[8,28,16,128]{3,2,1,0:T(8,128)(2,1)S(1)}, u32[]{:S(2)}, u32[]{:S(2)}) collective-permute-start(bf16[8,28,16,128]{3,2,1,0:T(8,128)(2,1)S(1)} %get-tuple-element.30), channel_id=1, source_target_pairs={{0,8},{8,0},{16,24},{24,16},{1,9},{9,1},{17,25},{25,17},{2,10},{10... | collective-permute-start | bytes 2752520 | tf_op jit(solution)/shard_map/ppermute | solution.py:355
  135.4 21.2 %collective-permute-start.7 = (bf16[8,28,16,128]{3,2,1,0:T(8,128)(2,1)S(1)}, bf16[8,28,16,128]{3,2,1,0:T(8,128)(2,1)S(1)}, u32[]{:S(2)}, u32[]{:S(2)}) collective-permute-start(bf16[8,28,16,128]{3,2,1,0:T(8,128)(2,1)S(1)} %get-tuple-element.31), channel_id=1, source_target_pairs={{0,16},{8,24},{16,0},{24,8},{1,17},{9,25},{17,1},{25,9},{2,18},{10... | collective-permute-start | bytes 2752520 | tf_op jit(solution)/shard_map/ppermute | solution.py:355
  158.2 40.9 %all-to-all-start.2 = ((bf16[8,28,16,128]{3,2,1,0:T(8,128)(2,1)}), bf16[8,28,16,128]{3,2,1,0:T(8,128)(2,1)}, u32[]{:S(2)}, u32[]{:S(2)}) async-start(bf16[8,28,16,128]{3,2,1,0:T(8,128)(2,1)} %copy-done), calls=%async_computation.2 | async-start | bytes 1835008 | tf_op jit(solution)/shard_map/all_to_all | solution.py:350
  162.8 35.0 %copy-start.1 = (bf16[8,28,16,128]{3,2,1,0:T(8,128)(2,1)S(1)}, bf16[8,28,16,128]{3,2,1,0:T(8,128)(2,1)}, u32[]{:S(2)}) copy-start(bf16[8,28,16,128]{3,2,1,0:T(8,128)(2,1)} %copy-done) | copy-start | bytes 2752516
  162.9 35.0 %copy-start.7 = (bf16[8,24,16,128]{3,2,1,0:T(8,128)(2,1)S(1)}, bf16[8,24,16,128]{3,2,1,0:T(8,128)(2,1)}, u32[]{:S(2)}) copy-start(bf16[8,24,16,128]{3,2,1,0:T(8,128)(2,1)} %copy-done.4) | copy-start | bytes 2359300
  162.9 11.7 %collective-permute-start.8 = (bf16[4,24,16,128]{3,2,1,0:T(8,128)(2,1)}, bf16[4,24,16,128]{3,2,1,0:T(8,128)(2,1)S(1)}, u32[]{:S(2)}, u32[]{:S(2)}) collective-permute-start(bf16[4,24,16,128]{3,2,1,0:T(8,128)(2,1)} %copy-done.31), channel_id=1, source_target_pairs={{0,8},{8,0},{16,24},{24,16},{1,9},{9,1},{17,25},{25,17},{2,10},{10... | collective-permute-start | bytes 1179656 | tf_op jit(solution)/shard_map/ppermute | solution.py:355
  164.3 11.4 %collective-permute-start.9 = (bf16[4,24,16,128]{3,2,1,0:T(8,128)(2,1)}, bf16[4,24,16,128]{3,2,1,0:T(8,128)(2,1)S(1)}, u32[]{:S(2)}, u32[]{:S(2)}) collective-permute-start(bf16[4,24,16,128]{3,2,1,0:T(8,128)(2,1)} %copy-done.30), channel_id=1, source_target_pairs={{0,16},{8,24},{16,0},{24,8},{1,17},{9,25},{17,1},{25,9},{2,18},{10... | collective-permute-start | bytes 1179656 | tf_op jit(solution)/shard_map/ppermute | solution.py:355
  178.5 18.8 %collective-permute-start.10 = (bf16[8,24,16,128]{3,2,1,0:T(8,128)(2,1)S(1)}, bf16[8,24,16,128]{3,2,1,0:T(8,128)(2,1)S(1)}, u32[]{:S(2)}, u32[]{:S(2)}) collective-permute-start(bf16[8,24,16,128]{3,2,1,0:T(8,128)(2,1)S(1)} %get-tuple-element.37), channel_id=1, source_target_pairs={{0,8},{8,0},{16,24},{24,16},{1,9},{9,1},{17,25},{25,17},{2,10},{10... | collective-permute-start | bytes 2359304 | tf_op jit(solution)/shard_map/ppermute | solution.py:355
  179.2 18.6 %collective-permute-start.11 = (bf16[8,24,16,128]{3,2,1,0:T(8,128)(2,1)S(1)}, bf16[8,24,16,128]{3,2,1,0:T(8,128)(2,1)S(1)}, u32[]{:S(2)}, u32[]{:S(2)}) collective-permute-start(bf16[8,24,16,128]{3,2,1,0:T(8,128)(2,1)S(1)} %get-tuple-element.38), channel_id=1, source_target_pairs={{0,16},{8,24},{16,0},{24,8},{1,17},{9,25},{17,1},{25,9},{2,18},{10... | collective-permute-start | bytes 2359304 | tf_op jit(solution)/shard_map/ppermute | solution.py:355
  199.1 25.5 %all-to-all-start.4 = ((bf16[8,24,16,128]{3,2,1,0:T(8,128)(2,1)}), bf16[8,24,16,128]{3,2,1,0:T(8,128)(2,1)}, u32[]{:S(2)}, u32[]{:S(2)}) async-start(bf16[8,24,16,128]{3,2,1,0:T(8,128)(2,1)} %total.3.refs_1_), calls=%async_computation.4 | async-start | bytes 1572864 | tf_op jit(solution)/shard_map/all_to_all | solution.py:350
  203.5 25.3 %collective-permute-start.13 = (bf16[8,28,16,128]{3,2,1,0:T(8,128)(2,1)}, bf16[8,28,16,128]{3,2,1,0:T(8,128)(2,1)}, u32[]{:S(2)}, u32[]{:S(2)}) collective-permute-start(bf16[8,28,16,128]{3,2,1,0:T(8,128)(2,1)} %all-to-all-done.5.refs_0_), channel_id=1, source_target_pairs={{0,16},{8,24},{16,0},{24,8},{1,17},{9,25},{17,1},{25,9},{2,18},{10... | collective-permute-start | bytes 2752520 | tf_op jit(solution)/shard_map/ppermute | solution.py:355
  205.0 26.4 %collective-permute-start.12 = (bf16[8,28,16,128]{3,2,1,0:T(8,128)(2,1)}, bf16[8,28,16,128]{3,2,1,0:T(8,128)(2,1)}, u32[]{:S(2)}, u32[]{:S(2)}) collective-permute-start(bf16[8,28,16,128]{3,2,1,0:T(8,128)(2,1)} %all-to-all-done.5.refs_0_), channel_id=1, source_target_pairs={{0,8},{8,0},{16,24},{24,16},{1,9},{9,1},{17,25},{25,17},{2,10},{10... | collective-permute-start | bytes 2752520 | tf_op jit(solution)/shard_map/ppermute | solution.py:355
  209.9 24.2 %copy-start.12 = (bf16[8,24,16,128]{3,2,1,0:T(8,128)(2,1)S(1)}, bf16[8,24,16,128]{3,2,1,0:T(8,128)(2,1)}, u32[]{:S(2)}) copy-start(bf16[8,24,16,128]{3,2,1,0:T(8,128)(2,1)} %all_to_all.40.refs_0_) | copy-start | bytes 2359300
  224.6 42.7 %all-to-all-start.3 = ((bf16[8,28,16,128]{3,2,1,0:T(8,128)(2,1)}), bf16[8,28,16,128]{3,2,1,0:T(8,128)(2,1)}, u32[]{:S(2)}, u32[]{:S(2)}) async-start(bf16[8,28,16,128]{3,2,1,0:T(8,128)(2,1)} %transform.6.refs_9_), calls=%async_computation.3 | async-start | bytes 1835008 | tf_op jit(solution)/shard_map/all_to_all | solution.py:350
  228.8 17.1 %copy-start.15 = (s32[52,2048]{1,0:T(8,128)S(1)}, s32[52,2048]{1,0:T(8,128)}, u32[]{:S(2)}) copy-start(s32[52,2048]{1,0:T(8,128)} %refs_8_.3) | copy-start | bytes 1277956
  229.9 13.4 %collective-permute-start.14 = (bf16[4,28,16,128]{3,2,1,0:T(8,128)(2,1)S(1)}, bf16[4,28,16,128]{3,2,1,0:T(8,128)(2,1)S(1)}, u32[]{:S(2)}, u32[]{:S(2)}) collective-permute-start(bf16[4,28,16,128]{3,2,1,0:T(8,128)(2,1)S(1)} %slice.16), channel_id=1, source_target_pairs={{0,8},{8,0},{16,24},{24,16},{1,9},{9,1},{17,25},{25,17},{2,10},{10... | collective-permute-start | bytes 1376264 | tf_op jit(solution)/shard_map/ppermute | solution.py:355
  232.4 13.4 %collective-permute-start.15 = (bf16[4,28,16,128]{3,2,1,0:T(8,128)(2,1)S(1)}, bf16[4,28,16,128]{3,2,1,0:T(8,128)(2,1)S(1)}, u32[]{:S(2)}, u32[]{:S(2)}) collective-permute-start(bf16[4,28,16,128]{3,2,1,0:T(8,128)(2,1)S(1)} %slice.17), channel_id=1, source_target_pairs={{0,16},{8,24},{16,0},{24,8},{1,17},{9,25},{17,1},{25,9},{2,18},{10... | collective-permute-start | bytes 1376264 | tf_op jit(solution)/shard_map/ppermute | solution.py:355
  234.0 38.3 %collective-permute-start.17 = (bf16[8,24,16,128]{3,2,1,0:T(8,128)(2,1)S(1)}, bf16[8,24,16,128]{3,2,1,0:T(8,128)(2,1)}, u32[]{:S(2)}, u32[]{:S(2)}) collective-permute-start(bf16[8,24,16,128]{3,2,1,0:T(8,128)(2,1)S(1)} %copy-done.12), channel_id=1, source_target_pairs={{0,16},{8,24},{16,0},{24,8},{1,17},{9,25},{17,1},{25,9},{2,18},{10... | collective-permute-start | bytes 2359304 | tf_op jit(solution)/shard_map/ppermute | solution.py:355
  234.5 39.5 %collective-permute-start.16 = (bf16[8,24,16,128]{3,2,1,0:T(8,128)(2,1)S(1)}, bf16[8,24,16,128]{3,2,1,0:T(8,128)(2,1)}, u32[]{:S(2)}, u32[]{:S(2)}) collective-permute-start(bf16[8,24,16,128]{3,2,1,0:T(8,128)(2,1)S(1)} %copy-done.12), channel_id=1, source_target_pairs={{0,8},{8,0},{16,24},{24,16},{1,9},{9,1},{17,25},{25,17},{2,10},{10... | collective-permute-start | bytes 2359304 | tf_op jit(solution)/shard_map/ppermute | solution.py:355
  267.3 34.9 %all-to-all-start.6 = ((bf16[8,24,16,128]{3,2,1,0:T(8,128)(2,1)}), bf16[8,24,16,128]{3,2,1,0:T(8,128)(2,1)}, u32[]{:S(2)}, u32[]{:S(2)}) async-start(bf16[8,24,16,128]{3,2,1,0:T(8,128)(2,1)} %transform.7.refs_10_), calls=%async_computation.6 | async-start | bytes 1572864 | tf_op jit(solution)/shard_map/all_to_all | solution.py:350
  273.4 11.6 %collective-permute-start.18 = (bf16[4,24,16,128]{3,2,1,0:T(8,128)(2,1)S(1)}, bf16[4,24,16,128]{3,2,1,0:T(8,128)(2,1)S(1)}, u32[]{:S(2)}, u32[]{:S(2)}) collective-permute-start(bf16[4,24,16,128]{3,2,1,0:T(8,128)(2,1)S(1)} %slice.18), channel_id=1, source_target_pairs={{0,8},{8,0},{16,24},{24,16},{1,9},{9,1},{17,25},{25,17},{2,10},{10... | collective-permute-start | bytes 1179656 | tf_op jit(solution)/shard_map/ppermute | solution.py:355
  275.1 11.3 %collective-permute-start.19 = (bf16[4,24,16,128]{3,2,1,0:T(8,128)(2,1)S(1)}, bf16[4,24,16,128]{3,2,1,0:T(8,128)(2,1)S(1)}, u32[]{:S(2)}, u32[]{:S(2)}) collective-permute-start(bf16[4,24,16,128]{3,2,1,0:T(8,128)(2,1)S(1)} %slice.19), channel_id=1, source_target_pairs={{0,16},{8,24},{16,0},{24,8},{1,17},{9,25},{17,1},{25,9},{2,18},{10... | collective-permute-start | bytes 1179656 | tf_op jit(solution)/shard_map/ppermute | solution.py:355
  (29 other events, 57.0 us)

commit v2 on v1

--- a/solution.py
+++ b/solution.py
@@ -130,16 +130,18 @@
     ]
 
 
-def local_cost(rows, blocks):
-    size = blocks * SUB
+FREE = pl.CostEstimate(flops=0, bytes_accessed=0, transcendentals=0)
+
+
+def cost(size, cols):
     return pl.CostEstimate(
-        flops=4 * size * size * (rows // SUB) * HB,
-        bytes_accessed=4 * rows * blocks * HB,
-        transcendentals=0,
-    )
-
-
+        flops=0, bytes_accessed=4 * size * GROUP * cols, transcendentals=0
+    )
 ANYWHERE = pl.BlockSpec(memory_space=pl.ANY)
+
+
+def in_hbm(*values):
+    return [pltpu.with_memory_space_constraint(value, pltpu.HBM) for value in values]
 
 
 def drop_inputs(kernel, start, count):
@@ -163,10 +165,10 @@
         out_specs=[pl.BlockSpec((parts, size, SUB, HB), lambda i: (i, 0, 0, 0)) for size in sizes],
         out_shape=[jax.ShapeDtypeStruct((rows // SUB, size, SUB, HB), BF16) for size in sizes],
         scratch_shapes=local_scratch(blocks),
-        compiler_params=pltpu.CompilerParams(vmem_limit_bytes=32 << 20),
-        cost_estimate=local_cost(rows, blocks),
+        compiler_params=pltpu.CompilerParams(vmem_limit_bytes=16 << 20),
+        cost_estimate=FREE,
         name="local_forward",
-    )(hidden, rot_block)
+    )(*in_hbm(hidden), rot_block)
 
 
 def local_backward(mixed, rot_block, sizes, after=()):
@@ -181,10 +183,10 @@
         + [pl.BlockSpec((blocks, blocks), lambda i: (0, 0))]
         + [ANYWHERE] * len(after),
         out_specs=pl.BlockSpec((parts * SUB, blocks * HB), lambda i: (i, 0)),
-        out_shape=jax.ShapeDtypeStruct((rows, blocks * HB), BF16),
+        out_shape=pltpu.HBM((rows, blocks * HB), BF16),
         scratch_shapes=local_scratch(blocks),
-        compiler_params=pltpu.CompilerParams(vmem_limit_bytes=32 << 20),
-        cost_estimate=local_cost(rows, blocks),
+        compiler_params=pltpu.CompilerParams(vmem_limit_bytes=16 << 20),
+        cost_estimate=FREE,
         name="local_backward",
     )(*mixed, rot_block, *after)
 
@@ -221,14 +223,10 @@
         out_specs=[pl.BlockSpec((count, per, SUB, HB), lambda i: (0, i, 0, 0)) for count in counts],
         out_shape=[jax.ShapeDtypeStruct((count, size, SUB, HB), BF16) for count in counts],
         scratch_shapes=[pltpu.VMEM((per * GROUP, cols), BF16)],
-        compiler_params=pltpu.CompilerParams(vmem_limit_bytes=40 << 20),
-        cost_estimate=pl.CostEstimate(
-            flops=2 * tokens * cols * size * GROUP,
-            bytes_accessed=2 * cols * size * GROUP + 2 * tokens * (cols + size * GROUP),
-            transcendentals=0,
-        ),
+        compiler_params=pltpu.CompilerParams(vmem_limit_bytes=26 << 20),
+        cost_estimate=FREE,
         name="unit_grads",
-    )(up, weight, scales, *after)
+    )(up, *in_hbm(weight, scales), *after)
 
 
 def weights_kernel(first, per, pieces, *refs):
@@ -266,14 +264,15 @@
     tokens, cols = up.shape
     offset = first // per
     specs = [
-        pl.BlockSpec((piece.shape[0], per, SUB, HB), lambda i: (0, i, 0, 0)) for piece in rotated
+        pl.BlockSpec((piece.shape[0], per, SUB, HB), lambda i: (0, offset + i, 0, 0))
+        for piece in rotated
     ] + [
         pl.BlockSpec((tokens, cols), lambda i: (0, 0)),
         pl.BlockSpec((per * GROUP, cols), lambda i: (offset + i, 0)),
         pl.BlockSpec(scales.shape, lambda i: (0, 0)),
         pl.BlockSpec(scales.shape, lambda i: (0, 0)),
     ]
-    args = [*rotated, up, weight, scales, mask]
+    args = [*rotated, up, *in_hbm(weight, scales, mask)]
     aliases = {}
     if buffer is not None:
         aliases = {len(args): 0}
@@ -288,16 +287,12 @@
             pl.BlockSpec((size, cols), lambda i: (0, 0)),
         ],
         out_shape=[
-            jax.ShapeDtypeStruct(weight.shape, BF16),
+            pltpu.HBM(weight.shape, BF16),
             jax.ShapeDtypeStruct((size, cols), F32),
         ],
         input_output_aliases=aliases,
-        compiler_params=pltpu.CompilerParams(vmem_limit_bytes=40 << 20),
-        cost_estimate=pl.CostEstimate(
-            flops=2 * tokens * cols * size * GROUP,
-            bytes_accessed=4 * cols * size * GROUP + 2 * tokens * (cols + size * GROUP),
-            transcendentals=0,
-        ),
+        compiler_params=pltpu.CompilerParams(vmem_limit_bytes=26 << 20),
+        cost_estimate=FREE,
         name="weight_grads",
     )(*args, *after)
 
@@ -315,12 +310,8 @@
         in_specs=[spec(value.shape, 1) for value in ins] + [ANYWHERE] * len(after),
         out_specs=[spec(shape, 1) for shape in outs],
         out_shape=[jax.ShapeDtypeStruct(shape, BF16) for shape in outs],
-        compiler_params=pltpu.CompilerParams(vmem_limit_bytes=32 << 20),
-        cost_estimate=pl.CostEstimate(
-            flops=0,
-            bytes_accessed=2 * sum(v.size for v in ins) * 2,
-            transcendentals=0,
-        ),
+        compiler_params=pltpu.CompilerParams(vmem_limit_bytes=16 << 20),
+        cost_estimate=FREE,
         name=name,
     )(*ins, *after)
 
@@ -399,10 +390,33 @@
     y_out[half:] = y_ref[half:]
 
 
-def total_kernel(own_ref, x_ref, y_ref, out_ref):
-    out_ref[...] = (
+def total_kernel(own_ref, x_ref, y_ref, *refs):
+    refs[-1][...] = (
         own_ref[...].astype(F32) + x_ref[...].astype(F32) + y_ref[...].astype(F32)
     ).astype(BF16)
+
+
+def total(ins, buffer, first, groups, per, after=()):
+    count, size = ins[0].shape[:2]
+    offset = first // per
+    args = list(ins)
+    specs = [pl.BlockSpec((count, per, SUB, HB), lambda i: (0, i, 0, 0))] * 3
+    aliases = {}
+    if buffer is not None:
+        aliases = {3: 0}
+        args.append(buffer)
+        specs.append(ANYWHERE)
+    return pl.pallas_call(
+        total_kernel,
+        grid=(size // per,),
+        in_specs=specs + [ANYWHERE] * len(after),
+        out_specs=pl.BlockSpec((count, per, SUB, HB), lambda i: (0, offset + i, 0, 0)),
+        out_shape=jax.ShapeDtypeStruct((count, groups, SUB, HB), BF16),
+        input_output_aliases=aliases,
+        compiler_params=pltpu.CompilerParams(vmem_limit_bytes=16 << 20),
+        cost_estimate=FREE,
+        name="total",
+    )(*args, *after)
 
 
 def general_shards(hidden, upstream, weight, scales, clip_mask, rot_block):
@@ -452,12 +466,7 @@
             2,
             after,
         )
-        return partner(x_part, "dp", 1), partner(y_part, "dp", 2)
-
-    def scatter_last(parts_of, received, after):
-        return small_call(
-            total_kernel, "total", [parts_of[0], *received], [parts_of[0].shape], 2, after
-        )[0]
+        return x_part, partner(x_part, "dp", 1), partner(y_part, "dp", 2)
 
     def gather(value):
         x_part, y_part = partner(value, "dp", 1), partner(value, "dp", 2)
@@ -466,35 +475,29 @@
         )
 
     up = gather_upstream(upstream)
-    local = local_forward(hidden, rot_block, sizes)
-    forth = [exchange(value) for value in local]
-    unit0 = unit_grads(up, weight, scales, starts[0], sizes[0], per, counts, after=(local[0],))
+    (local,) = local_forward(hidden, rot_block, (groups,))
+    forth = exchange(local)
+    unit0 = unit_grads(up, weight, scales, starts[0], sizes[0], per, counts, after=(local,))
     first0 = scatter_first(unit0)
-    turned0 = transform(forth[0], after=(unit0[0],))
-    rotated0 = exchange(turned0)
-    unit1 = unit_grads(up, weight, scales, starts[1], sizes[1], per, counts, after=(turned0,))
+    unit1 = unit_grads(up, weight, scales, starts[1], sizes[1], per, counts, after=(unit0[0],))
     first1 = scatter_first(unit1)
-    second0 = scatter_second(unit0, first0, after=(unit1[0],))
-    turned1 = transform(forth[1], after=(unit1[0],))
-    rotated1 = exchange(turned1)
-    second1 = scatter_second(unit1, first1, after=(turned1,))
-    sum0 = scatter_last(unit0, second0, after=(turned1,))
-    back0 = exchange(sum0)
-    sum1 = scatter_last(unit1, second1, after=(sum0,))
-    back1 = exchange(sum1)
-    gathered0 = gather(rotated0)
-    gathered1 = gather(rotated1)
-    mixed0 = transform(back0, after=(sum1,))
-    final0 = exchange(mixed0)
+    relayed0, *second0 = scatter_second(unit0, first0, after=(unit1[0],))
+    turned = transform(forth, after=(relayed0,))
+    rotated = exchange(turned)
+    relayed1, *second1 = scatter_second(unit1, first1, after=(turned,))
+    summed = total((unit0[0], *second0), None, starts[0], groups, per, after=(turned,))
+    summed = total((unit1[0], *second1), summed, starts[1], groups, per, after=(rotated,))
+    back = exchange(summed)
+    gathered = gather(rotated)
+    mixed = transform(back, after=gathered[1:3])
+    final = exchange(mixed)
     buffer, scale0 = weight_grads(
-        gathered0, up, weight, scales, clip_mask, None, starts[0], sizes[0], per, after=(mixed0,)
-    )
-    mixed1 = transform(back1, after=(scale0,))
-    final1 = exchange(mixed1)
+        gathered, up, weight, scales, clip_mask, None, starts[0], sizes[0], per, after=(mixed,)
+    )
     buffer, scale1 = weight_grads(
-        gathered1, up, weight, scales, clip_mask, buffer, starts[1], sizes[1], per, after=(mixed1,)
-    )
-    grad_hidden = local_backward([final0, final1], rot_block, sizes, after=(scale1,))
+        gathered, up, weight, scales, clip_mask, buffer, starts[1], sizes[1], per
+    )
+    grad_hidden = local_backward([final], rot_block, (groups,), after=(scale1,))
     return grad_hidden, buffer, jnp.concatenate([scale0, scale1], axis=0)
 
 

time: 315 us -> 263 us (0.83)
  blocking collectives: 25.9 us -> 0 us
  starting transfers between devices: 56.3 us -> 37.8 us
  waiting for transfers between devices: 113 us -> 108 us
  Pallas kernels: 82.9 us -> 79.7 us
    all_to_all x7 -> x4, waiting for transfers between devices: 34.5 us -> 0.01 us  [exchange(): lax.all_to_all(value, 'tensor', split_axis=0, concat_axis=0, tiled=True)]
    ppermute x20 -> x16, waiting for transfers between devices: 78.3 us -> 108 us  [partner(): return lax.ppermute(value, axis, [(i, i ^ mask) for i in range(size)])]
    all_to_all x1 -> x0, blocking collectives: 25.9 us -> none  [exchange(): lax.all_to_all(value, 'tensor', split_axis=0, concat_axis=0, tiled=True)]
    all_to_all x7 -> x4, starting transfers between devices: 31.4 us -> 20.7 us  [exchange(): lax.all_to_all(value, 'tensor', split_axis=0, concat_axis=0, tiled=True)]
    ppermute x20 -> x16, starting transfers between devices: 24.9 us -> 17.1 us  [partner(): return lax.ppermute(value, axis, [(i, i ^ mask) for i in range(size)])]
    unnamed x68 -> x62, local copies, waits for them, and re-layouts: 22.7 us -> 29.1 us
    pallas_call x8 -> x4, Pallas kernels: 11.1 us -> 6.75 us  [small_call(): pl.pallas_call(drop_inputs(kernel, len(ins), len(after)), grid=(steps,),...]
  transfers between devices with their start and end apart: 27 -> 20, of which waited for: 14 -> 11; matrix products, arithmetic and copies ran while one was open for 3% -> 2% of each run, Pallas kernels for 23% -> 21%
where the time goes in v2:
time: 263 us; the launch traced here: 262 us
  waiting for transfers between devices  108 us (41%)
  Pallas kernels  79.7 us (30%)
  starting transfers between devices  37.8 us (14%)
  local copies, waits for them, and re-layouts  31.9 us (12%)
  other arithmetic  3.44 us (1%)
    ppermute x16, waiting for transfers between devices, partner(): return lax.ppermute(value, axis, [(i, i ^ mask) for i in range(size)])  108 us
    pallas_call x2, Pallas kernels, weight_grads(): pl.pallas_call(functools.partial(weights_kernel, first, per, len(rotated)...  29.9 us
    unnamed x62, local copies, waits for them, and re-layouts  29.1 us
    pallas_call x2, Pallas kernels, unit_grads(): pl.pallas_call(drop_inputs(functools.partial(units_kernel, first, per), 3...  22.2 us
    all_to_all x4, starting transfers between devices, exchange(): lax.all_to_all(value, 'tensor', split_axis=0, concat_axis=0, tiled=True)  20.7 us
    ppermute x16, starting transfers between devices, partner(): return lax.ppermute(value, axis, [(i, i ^ mask) for i in range(size)])  17.1 us
    pallas_call x1, Pallas kernels, local_backward(): pl.pallas_call(drop_inputs(functools.partial(backward_kernel, sizes), len...  9.76 us
    pallas_call x1, Pallas kernels, local_forward(): pl.pallas_call(functools.partial(forward_kernel, sizes), grid=(rows // (S...  9.75 us
  transfers between devices with their start and end apart: 20, of which 11 were waited for; matrix products, arithmetic and copies ran while one was open for 2% of the time, Pallas kernels for 21%

profile of v2, /device:TPU:0, one launch (start us, length us, event | category | flops | bytes accessed | tf_op | source)
XLA Modules:
  0.0 261.8 jit_solution(10378002644866986249)
XLA Ops:
  1.4 9.7 %local_forward.1.refs_3_ = bf16[8,52,16,128]{3,2,1,0:T(8,128)(2,1)} custom-call(bf16[128,6656]{1,0:T(8,128)(2,1)} %x_ref.1, f32[52,52]{1,0:T(8,128)S(1)} %copy-done.26), custom_call_target="tpu_custom_call" | custom-call | tf_op jit(solution)/shard_map/local_forward/pallas_call | solution.py:158
  11.1 6.5 %all-to-all-start = ((bf16[8,52,16,128]{3,2,1,0:T(8,128)(2,1)}), bf16[8,52,16,128]{3,2,1,0:T(8,128)(2,1)}, u32[]{:S(2)}, u32[]{:S(2)}) async-start(bf16[8,52,16,128]{3,2,1,0:T(8,128)(2,1)} %local_forward.1.refs_3_), calls=%async_computation | async-start | bytes 3407872 | tf_op jit(solution)/shard_map/all_to_all | solution.py:341
  17.7 1.6 collective-permute-start
  19.2 1.5 collective-permute-start.2
  21.2 5.6 %collective-permute-done = bf16[64,2048]{1,0:T(8,128)(2,1)S(1)} collective-permute-done((bf16[64,2048]{1,0:T(8,128)(2,1)S(1)}, bf16[64,2048]{1,0:T(8,128)(2,1)S(1)}, u32[]{:S(2)}, u32[]{:S(2)}) %collective-permute-start) | collective-permute-done | bytes 262176 | tf_op jit(solution)/shard_map/ppermute | solution.py:346
  26.8 6.3 %collective-permute-done.2 = bf16[64,2048]{1,0:T(8,128)(2,1)S(1)} collective-permute-done((bf16[64,2048]{1,0:T(8,128)(2,1)S(1)}, bf16[64,2048]{1,0:T(8,128)(2,1)S(1)}, u32[]{:S(2)}, u32[]{:S(2)}) %collective-permute-start.2) | collective-permute-done | bytes 262176 | tf_op jit(solution)/shard_map/ppermute | solution.py:346
  35.5 2.6 collective-permute-done.3
  39.8 11.8 %unit_grads.2 = (bf16[8,28,16,128]{3,2,1,0:T(8,128)(2,1)S(1)}, bf16[8,28,16,128]{3,2,1,0:T(8,128)(2,1)S(1)}, bf16[8,28,16,128]{3,2,1,0:T(8,128)(2,1)S(1)}, bf16[...) custom-call(bf16[512,2048]{1,0:T(8,128)(2,1)S(1)} %pad_maximum_fusion.refs_0_.refs_5_, ...), custom_call_target="tpu_custom_call" | custom-call | tf_op jit(solution)/shard_map/unit_grads/pallas_call | solution.py:214
  51.6 1.5 collective-permute-start.6
  53.7 10.3 %unit_grads.3 = (bf16[8,24,16,128]{3,2,1,0:T(8,128)(2,1)S(1)}, bf16[8,24,16,128]{3,2,1,0:T(8,128)(2,1)S(1)}, bf16[8,24,16,128]{3,2,1,0:T(8,128)(2,1)S(1)}, bf16[...) custom-call(bf16[512,2048]{1,0:T(8,128)(2,1)S(1)} %pad_maximum_fusion.refs_0_.refs_5_, ...), custom_call_target="tpu_custom_call" | custom-call | tf_op jit(solution)/shard_map/unit_grads/pallas_call | solution.py:214
  71.1 2.8 %transform.2.refs_4_.refs_0_ = bf16[8,52,16,128]{3,2,1,0:T(8,128)(2,1)S(1)} custom-call(bf16[8,52,16,128]{3,2,1,0:T(8,128)(2,1)} %all-to-all-done.refs_0_, bf16[8,28,16,128]{3,2,1,0:T(8,128)(2,1)S(1)} %copy-done.17), custom_call_target="tpu_custom_call" | custom-call | tf_op jit(solution)/shard_map/transform/pallas_call | solution.py:307
  75.1 4.7 %all-to-all-start.1 = ((bf16[8,52,16,128]{3,2,1,0:T(8,128)(2,1)}), bf16[8,52,16,128]{3,2,1,0:T(8,128)(2,1)}, u32[]{:S(2)}, u32[]{:S(2)}) async-start(bf16[8,52,16,128]{3,2,1,0:T(8,128)(2,1)} %copy-done), calls=%async_computation.1 | async-start | bytes 3407872 | tf_op jit(solution)/shard_map/all_to_all | solution.py:341
  80.4 1.5 collective-permute-start.5
  82.4 1.5 collective-permute-start.10
  83.9 8.1 %collective-permute-done.4.refs_2_ = bf16[4,24,16,128]{3,2,1,0:T(8,128)(2,1)S(1)} collective-permute-done((bf16[4,24,16,128]{3,2,1,0:T(8,128)(2,1)}, bf16[4,24,16,128]{3,2,1,0:T(8,128)(2,1)S(1)}, u32[]{:S(2)}, u32[]{:S(2)}) %collective-permute-start.4) | collective-permute-done | bytes 393248 | tf_op jit(solution)/shard_map/ppermute | solution.py:346
  96.6 1.6 collective-permute-start.8
  98.2 1.5 collective-permute-start.9
  99.7 12.3 %collective-permute-done.11.y_ref = bf16[8,28,16,128]{3,2,1,0:T(8,128)(2,1)S(1)} collective-permute-done((bf16[8,28,16,128]{3,2,1,0:T(8,128)(2,1)}, bf16[8,28,16,128]{3,2,1,0:T(8,128)(2,1)S(1)}, u32[]{:S(2)}, u32[]{:S(2)}) %collective-permute-start.11) | collective-permute-done | bytes 917536 | tf_op jit(solution)/shard_map/ppermute | solution.py:346
  113.9 14.2 %collective-permute-done.8.x_ref = bf16[8,24,16,128]{3,2,1,0:T(8,128)(2,1)S(1)} collective-permute-done((bf16[8,24,16,128]{3,2,1,0:T(8,128)(2,1)S(1)}, bf16[8,24,16,128]{3,2,1,0:T(8,128)(2,1)S(1)}, u32[]{:S(2)}, u32[]{:S(2)}) %collective-permute-start.8) | collective-permute-done | bytes 786464 | tf_op jit(solution)/shard_map/ppermute | solution.py:346
  136.6 4.7 %all-to-all-start.2 = ((bf16[8,52,16,128]{3,2,1,0:T(8,128)(2,1)}), bf16[8,52,16,128]{3,2,1,0:T(8,128)(2,1)}, u32[]{:S(2)}, u32[]{:S(2)}) async-start(bf16[8,52,16,128]{3,2,1,0:T(8,128)(2,1)} %copy-done.11), calls=%async_computation.2 | async-start | bytes 3407872 | tf_op jit(solution)/shard_map/all_to_all | solution.py:341
  141.3 1.5 collective-permute-start.13
  143.5 37.7 %collective-permute-done.13.refs_2_ = bf16[8,52,16,128]{3,2,1,0:T(8,128)(2,1)S(1)} collective-permute-done((bf16[8,52,16,128]{3,2,1,0:T(8,128)(2,1)}, bf16[8,52,16,128]{3,2,1,0:T(8,128)(2,1)S(1)}, u32[]{:S(2)}, u32[]{:S(2)}) %collective-permute-start.13) | collective-permute-done | bytes 1703968 | tf_op jit(solution)/shard_map/ppermute | solution.py:346
  186.5 2.8 %transform.3.refs_9_ = bf16[8,52,16,128]{3,2,1,0:T(8,128)(2,1)S(1)} custom-call(bf16[8,52,16,128]{3,2,1,0:T(8,128)(2,1)} %all-to-all-done.2.refs_0_, bf16[8,52,16,128]{3,2,1,0:T(8,128)(2,1)S(1)} %copy-done.7, bf16[8,52,16,128]{3,2,1,0:T(8,128)(2,1)S(1)} %copy-done.4), custom_call_target="tpu_custom_call" | custom-call | tf_op jit(solution)/shard_map/transform/pallas_call | solution.py:307
  190.5 4.7 %all-to-all-start.3 = ((bf16[8,52,16,128]{3,2,1,0:T(8,128)(2,1)}), bf16[8,52,16,128]{3,2,1,0:T(8,128)(2,1)}, u32[]{:S(2)}, u32[]{:S(2)}) async-start(bf16[8,52,16,128]{3,2,1,0:T(8,128)(2,1)} %copy-done.12), calls=%async_computation.3 | async-start | bytes 3407872 | tf_op jit(solution)/shard_map/all_to_all | solution.py:341
  195.3 1.5 slice.8
  198.7 1.6 collective-permute-start.15
  200.3 17.8 %collective-permute-done.14.refs_3_ = bf16[4,52,16,128]{3,2,1,0:T(8,128)(2,1)S(1)} collective-permute-done((bf16[4,52,16,128]{3,2,1,0:T(8,128)(2,1)S(1)}, bf16[4,52,16,128]{3,2,1,0:T(8,128)(2,1)S(1)}, u32[]{:S(2)}, u32[]{:S(2)}) %collective-permute-start.14) | collective-permute-done | bytes 852000 | tf_op jit(solution)/shard_map/ppermute | solution.py:346
  218.1 1.7 collective-permute-done.15.refs_4_
  219.9 1.5 copy-done.13
  221.3 16.0 %weight_grads.2 = (bf16[6656,2048]{1,0:T(8,128)(2,1)}, f32[28,2048]{1,0:T(8,128)S(1)}) custom-call(bf16[8,52,16,128]{3,2,1,0:T(8,128)(2,1)} %all-to-all-done.1.refs_1_.refs_0_, bf16[8,52,16,128]{3,2,1,0:T(8,128)(2,1)S(1)} %copy-done.8, bf16[8,52,16,128]{3,2,1,0:T(8,128)(2,1)S(1)} %copy-done.5, bf16[4,52,16,128]{3,2,1,0:T(8,128)(2,1)S(1)} %collective-permute-done.14.refs_3_, ...), custom_call_target="tpu_custom_call" | custom-call | tf_op jit(solution)/shard_map/weight_grads/pallas_call | solution.py:281
  237.3 13.9 %weight_grads.3 = (bf16[6656,2048]{1,0:T(8,128)(2,1)}, f32[24,2048]{1,0:T(8,128)S(1)}) custom-call(bf16[8,52,16,128]{3,2,1,0:T(8,128)(2,1)} %all-to-all-done.1.refs_1_.refs_0_, bf16[8,52,16,128]{3,2,1,0:T(8,128)(2,1)S(1)} %copy-done.8, bf16[8,52,16,128]{3,2,1,0:T(8,128)(2,1)S(1)} %copy-done.5, ...), custom_call_target="tpu_custom_call", output_to_operand_aliasing={{0}: (9, {})} | custom-call | tf_op jit(solution)/shard_map/weight_grads/pallas_call | solution.py:281
  252.1 9.8 %local_backward.1 = bf16[128,6656]{1,0:T(8,128)(2,1)} custom-call(bf16[8,52,16,128]{3,2,1,0:T(8,128)(2,1)} %all-to-all-done.3.refs_0_, f32[52,52]{1,0:T(8,128)S(1)} %copy-done.27, f32[24,2048]{1,0:T(8,128)S(1)} %get-tuple-element.36.refs_2_), custom_call_target="tpu_custom_call" | custom-call | tf_op jit(solution)/shard_map/local_backward/pallas_call | solution.py:179
  (91 shorter events, 40.1 us)
Async XLA Ops:
  11.1 6.5 %copy-start.30 = (bf16[128,8192]{1,0:T(8,128)(2,1)S(1)}, bf16[128,8192]{1,0:T(8,128)(2,1)}, u32[]{:S(2)}) copy-start(bf16[128,8192]{1,0:T(8,128)(2,1)} %param.7) | copy-start | bytes 6291460
  11.1 58.8 %all-to-all-start = ((bf16[8,52,16,128]{3,2,1,0:T(8,128)(2,1)}), bf16[8,52,16,128]{3,2,1,0:T(8,128)(2,1)}, u32[]{:S(2)}, u32[]{:S(2)}) async-start(bf16[8,52,16,128]{3,2,1,0:T(8,128)(2,1)} %local_forward.1.refs_3_), calls=%async_computation | async-start | bytes 3407872 | tf_op jit(solution)/shard_map/all_to_all | solution.py:341
  17.7 9.2 %collective-permute-start = (bf16[64,2048]{1,0:T(8,128)(2,1)S(1)}, bf16[64,2048]{1,0:T(8,128)(2,1)S(1)}, u32[]{:S(2)}, u32[]{:S(2)}) collective-permute-start(bf16[64,2048]{1,0:T(8,128)(2,1)S(1)} %get-tuple-element.39), channel_id=1, source_target_pairs={{0,8},{8,0},{16,24},{24,16},{1,9},{9,1},{17,25},{25,17},{2,10},{10... | collective-permute-start | bytes 786440 | tf_op jit(solution)/shard_map/ppermute | solution.py:346
  19.2 13.9 %collective-permute-start.2 = (bf16[64,2048]{1,0:T(8,128)(2,1)S(1)}, bf16[64,2048]{1,0:T(8,128)(2,1)S(1)}, u32[]{:S(2)}, u32[]{:S(2)}) collective-permute-start(bf16[64,2048]{1,0:T(8,128)(2,1)S(1)} %get-tuple-element.40), channel_id=1, source_target_pairs={{0,24},{8,16},{16,8},{24,0},{1,25},{9,17},{17,9},{25,1},{2,26},{10... | collective-permute-start | bytes 786440 | tf_op jit(solution)/shard_map/ppermute | solution.py:346
  20.7 13.8 %collective-permute-start.1 = (bf16[64,2048]{1,0:T(8,128)(2,1)S(1)}, bf16[64,2048]{1,0:T(8,128)(2,1)S(1)}, u32[]{:S(2)}, u32[]{:S(2)}) collective-permute-start(bf16[64,2048]{1,0:T(8,128)(2,1)S(1)} %get-tuple-element.41), channel_id=1, source_target_pairs={{0,16},{8,24},{16,0},{24,8},{1,17},{9,25},{17,1},{25,9},{2,18},{10... | collective-permute-start | bytes 786440 | tf_op jit(solution)/shard_map/ppermute | solution.py:346
  35.5 2.6 %collective-permute-start.3 = (bf16[3,64,2048]{2,1,0:T(8,128)(2,1)}, bf16[3,64,2048]{2,1,0:T(8,128)(2,1)}, u32[]{:S(2)}, u32[]{:S(2)}) collective-permute-start(bf16[3,64,2048]{2,1,0:T(8,128)(2,1)} %pad_maximum_fusion.2), channel_id=1, source_target_pairs={{0,1},{1,0},{2,3},{3,2},{4,5},{5,4},{6,7},{7,6},{8,9},{9,8},{10,11... | collective-permute-start | bytes 2359304 | tf_op jit(solution)/shard_map/ppermute | solution.py:346
  51.6 15.0 %collective-permute-start.6 = (bf16[4,28,16,128]{3,2,1,0:T(8,128)(2,1)S(1)}, bf16[4,28,16,128]{3,2,1,0:T(8,128)(2,1)S(1)}, u32[]{:S(2)}, u32[]{:S(2)}) collective-permute-start(bf16[4,28,16,128]{3,2,1,0:T(8,128)(2,1)S(1)} %get-tuple-element.29), channel_id=1, source_target_pairs={{0,8},{8,0},{16,24},{24,16},{1,9},{9,1},{17,25},{25,17},{2,10},{10... | collective-permute-start | bytes 1376264 | tf_op jit(solution)/shard_map/ppermute | solution.py:346
  53.2 13.4 %collective-permute-start.7 = (bf16[4,28,16,128]{3,2,1,0:T(8,128)(2,1)S(1)}, bf16[4,28,16,128]{3,2,1,0:T(8,128)(2,1)S(1)}, u32[]{:S(2)}, u32[]{:S(2)}) collective-permute-start(bf16[4,28,16,128]{3,2,1,0:T(8,128)(2,1)S(1)} %get-tuple-element.30), channel_id=1, source_target_pairs={{0,16},{8,24},{16,0},{24,8},{1,17},{9,25},{17,1},{25,9},{2,18},{10... | collective-permute-start | bytes 1376264 | tf_op jit(solution)/shard_map/ppermute | solution.py:346
  73.9 1.2 copy-start
  75.1 54.8 %all-to-all-start.1 = ((bf16[8,52,16,128]{3,2,1,0:T(8,128)(2,1)}), bf16[8,52,16,128]{3,2,1,0:T(8,128)(2,1)}, u32[]{:S(2)}, u32[]{:S(2)}) async-start(bf16[8,52,16,128]{3,2,1,0:T(8,128)(2,1)} %copy-done), calls=%async_computation.1 | async-start | bytes 3407872 | tf_op jit(solution)/shard_map/all_to_all | solution.py:341
  79.9 12.1 %collective-permute-start.4 = (bf16[4,24,16,128]{3,2,1,0:T(8,128)(2,1)}, bf16[4,24,16,128]{3,2,1,0:T(8,128)(2,1)S(1)}, u32[]{:S(2)}, u32[]{:S(2)}) collective-permute-start(bf16[4,24,16,128]{3,2,1,0:T(8,128)(2,1)} %copy-done.29), channel_id=1, source_target_pairs={{0,8},{8,0},{16,24},{24,16},{1,9},{9,1},{17,25},{25,17},{2,10},{10... | collective-permute-start | bytes 1179656 | tf_op jit(solution)/shard_map/ppermute | solution.py:346
  80.4 11.9 %collective-permute-start.5 = (bf16[4,24,16,128]{3,2,1,0:T(8,128)(2,1)S(1)}, bf16[4,24,16,128]{3,2,1,0:T(8,128)(2,1)S(1)}, u32[]{:S(2)}, u32[]{:S(2)}) collective-permute-start(bf16[4,24,16,128]{3,2,1,0:T(8,128)(2,1)S(1)} %get-tuple-element.26), channel_id=1, source_target_pairs={{0,16},{8,24},{16,0},{24,8},{1,17},{9,25},{17,1},{25,9},{2,18},{10... | collective-permute-start | bytes 1179656 | tf_op jit(solution)/shard_map/ppermute | solution.py:346
  81.9 30.1 %collective-permute-start.11 = (bf16[8,28,16,128]{3,2,1,0:T(8,128)(2,1)}, bf16[8,28,16,128]{3,2,1,0:T(8,128)(2,1)S(1)}, u32[]{:S(2)}, u32[]{:S(2)}) collective-permute-start(bf16[8,28,16,128]{3,2,1,0:T(8,128)(2,1)} %copy-done.28), channel_id=1, source_target_pairs={{0,16},{8,24},{16,0},{24,8},{1,17},{9,25},{17,1},{25,9},{2,18},{10... | collective-permute-start | bytes 2752520 | tf_op jit(solution)/shard_map/ppermute | solution.py:346
  82.4 29.6 %collective-permute-start.10 = (bf16[8,28,16,128]{3,2,1,0:T(8,128)(2,1)}, bf16[8,28,16,128]{3,2,1,0:T(8,128)(2,1)S(1)}, u32[]{:S(2)}, u32[]{:S(2)}) collective-permute-start(bf16[8,28,16,128]{3,2,1,0:T(8,128)(2,1)} %copy-done.16), channel_id=1, source_target_pairs={{0,8},{8,0},{16,24},{24,16},{1,9},{9,1},{17,25},{25,17},{2,10},{10... | collective-permute-start | bytes 2752520 | tf_op jit(solution)/shard_map/ppermute | solution.py:346
  92.3 1.5 copy-start.1
  96.1 15.9 %copy-start.2 = (bf16[8,52,16,128]{3,2,1,0:T(8,128)(2,1)S(1)}, bf16[8,52,16,128]{3,2,1,0:T(8,128)(2,1)}, u32[]{:S(2)}) copy-start(bf16[8,52,16,128]{3,2,1,0:T(8,128)(2,1)} %copy-done) | copy-start | bytes 5111812
  96.6 31.5 %collective-permute-start.8 = (bf16[8,24,16,128]{3,2,1,0:T(8,128)(2,1)S(1)}, bf16[8,24,16,128]{3,2,1,0:T(8,128)(2,1)S(1)}, u32[]{:S(2)}, u32[]{:S(2)}) collective-permute-start(bf16[8,24,16,128]{3,2,1,0:T(8,128)(2,1)S(1)} %get-tuple-element.32), channel_id=1, source_target_pairs={{0,8},{8,0},{16,24},{24,16},{1,9},{9,1},{17,25},{25,17},{2,10},{10... | collective-permute-start | bytes 2359304 | tf_op jit(solution)/shard_map/ppermute | solution.py:346
  98.2 30.8 %collective-permute-start.9 = (bf16[8,24,16,128]{3,2,1,0:T(8,128)(2,1)S(1)}, bf16[8,24,16,128]{3,2,1,0:T(8,128)(2,1)S(1)}, u32[]{:S(2)}, u32[]{:S(2)}) collective-permute-start(bf16[8,24,16,128]{3,2,1,0:T(8,128)(2,1)S(1)} %get-tuple-element.33), channel_id=1, source_target_pairs={{0,16},{8,24},{16,0},{24,8},{1,17},{9,25},{17,1},{25,9},{2,18},{10... | collective-permute-start | bytes 2359304 | tf_op jit(solution)/shard_map/ppermute | solution.py:346
  129.9 1.5 copy-start.10
  136.6 47.0 %all-to-all-start.2 = ((bf16[8,52,16,128]{3,2,1,0:T(8,128)(2,1)}), bf16[8,52,16,128]{3,2,1,0:T(8,128)(2,1)}, u32[]{:S(2)}, u32[]{:S(2)}) async-start(bf16[8,52,16,128]{3,2,1,0:T(8,128)(2,1)} %copy-done.11), calls=%async_computation.2 | async-start | bytes 3407872 | tf_op jit(solution)/shard_map/all_to_all | solution.py:341
  141.3 39.8 %collective-permute-start.13 = (bf16[8,52,16,128]{3,2,1,0:T(8,128)(2,1)}, bf16[8,52,16,128]{3,2,1,0:T(8,128)(2,1)S(1)}, u32[]{:S(2)}, u32[]{:S(2)}) collective-permute-start(bf16[8,52,16,128]{3,2,1,0:T(8,128)(2,1)} %all-to-all-done.1.refs_1_.refs_0_), channel_id=1, source_target_pairs={{0,16},{8,24},{16,0},{24,8},{1,17},{9,25},{17,1},{25,9},{2,18},{10... | collective-permute-start | bytes 5111816 | tf_op jit(solution)/shard_map/ppermute | solution.py:346
  142.8 39.6 %collective-permute-start.12 = (bf16[8,52,16,128]{3,2,1,0:T(8,128)(2,1)}, bf16[8,52,16,128]{3,2,1,0:T(8,128)(2,1)S(1)}, u32[]{:S(2)}, u32[]{:S(2)}) collective-permute-start(bf16[8,52,16,128]{3,2,1,0:T(8,128)(2,1)} %all-to-all-done.1.refs_1_.refs_0_), channel_id=1, source_target_pairs={{0,8},{8,0},{16,24},{24,16},{1,9},{9,1},{17,25},{25,17},{2,10},{10... | collective-permute-start | bytes 5111816 | tf_op jit(solution)/shard_map/ppermute | solution.py:346
  181.2 1.2 copy-start.3
  183.6 1.5 copy-start.4
  185.0 1.5 copy-start.7
  190.5 61.5 %all-to-all-start.3 = ((bf16[8,52,16,128]{3,2,1,0:T(8,128)(2,1)}), bf16[8,52,16,128]{3,2,1,0:T(8,128)(2,1)}, u32[]{:S(2)}, u32[]{:S(2)}) async-start(bf16[8,52,16,128]{3,2,1,0:T(8,128)(2,1)} %copy-done.12), calls=%async_computation.3 | async-start | bytes 3407872 | tf_op jit(solution)/shard_map/all_to_all | solution.py:341
  195.2 24.6 %copy-start.5 = (bf16[8,52,16,128]{3,2,1,0:T(8,128)(2,1)S(1)}, bf16[8,52,16,128]{3,2,1,0:T(8,128)(2,1)}, u32[]{:S(2)}) copy-start(bf16[8,52,16,128]{3,2,1,0:T(8,128)(2,1)} %copy-done.3) | copy-start | bytes 5111812
  195.2 24.6 %copy-start.8 = (bf16[8,52,16,128]{3,2,1,0:T(8,128)(2,1)S(1)}, bf16[8,52,16,128]{3,2,1,0:T(8,128)(2,1)}, u32[]{:S(2)}) copy-start(bf16[8,52,16,128]{3,2,1,0:T(8,128)(2,1)} %copy-done.6) | copy-start | bytes 5111812
  196.7 21.4 %collective-permute-start.14 = (bf16[4,52,16,128]{3,2,1,0:T(8,128)(2,1)S(1)}, bf16[4,52,16,128]{3,2,1,0:T(8,128)(2,1)S(1)}, u32[]{:S(2)}, u32[]{:S(2)}) collective-permute-start(bf16[4,52,16,128]{3,2,1,0:T(8,128)(2,1)S(1)} %slice.8), channel_id=1, source_target_pairs={{0,8},{8,0},{16,24},{24,16},{1,9},{9,1},{17,25},{25,17},{2,10},{10... | collective-permute-start | bytes 2555912 | tf_op jit(solution)/shard_map/ppermute | solution.py:346
  198.7 21.1 %collective-permute-start.15 = (bf16[4,52,16,128]{3,2,1,0:T(8,128)(2,1)S(1)}, bf16[4,52,16,128]{3,2,1,0:T(8,128)(2,1)S(1)}, u32[]{:S(2)}, u32[]{:S(2)}) collective-permute-start(bf16[4,52,16,128]{3,2,1,0:T(8,128)(2,1)S(1)} %slice.9), channel_id=1, source_target_pairs={{0,16},{8,24},{16,0},{24,8},{1,17},{9,25},{17,1},{25,9},{2,18},{10... | collective-permute-start | bytes 2555912 | tf_op jit(solution)/shard_map/ppermute | solution.py:346
  219.9 1.5 copy-start.13
  237.3 14.7 %copy-start.27 = (f32[52,52]{1,0:T(8,128)S(1)}, f32[52,52]{1,0:T(8,128)}, u32[]{:S(2)}) copy-start(f32[52,52]{1,0:T(8,128)} %refs_1_.5) | copy-start | bytes 32452
  (19 other events, 19.4 us)

commit v3 on v2

--- a/solution.py
+++ b/solution.py
@@ -10,6 +10,7 @@
 HB = 128
 GROUP = 128
 SUB = 16
+ROWS = 8
 F32 = jnp.float32
 BF16 = jnp.bfloat16
 
@@ -43,13 +44,13 @@
 
 def build_mixing(rot_ref, high_ref, low_ref, sign_ref, transposed):
     blocks = rot_ref.shape[0]
-    size = blocks * SUB
+    size = blocks * ROWS
     row = lax.broadcasted_iota(jnp.int32, (size, blocks), 0)
     col = lax.broadcasted_iota(jnp.int32, (size, blocks), 1)
-    pick = ((row >> 4) == col).astype(F32).astype(BF16)
+    pick = ((row >> 3) == col).astype(F32).astype(BF16)
     rows = lax.broadcasted_iota(jnp.int32, (size, size), 0)
     cols = lax.broadcasted_iota(jnp.int32, (size, size), 1)
-    same = (rows & (SUB - 1)) == (cols & (SUB - 1))
+    same = (rows & (ROWS - 1)) == (cols & (ROWS - 1))
     for part, out_ref in zip(split2(rot_ref[...]), (high_ref, low_ref)):
         spread = nt_dot(pick, part) if transposed else nn_dot(pick, part)
         full = nt_dot(spread.astype(BF16), pick)
@@ -57,13 +58,14 @@
     sign_ref[...] = sign_matrix(HB)
 
 
-def mix_rows(stacked, high_ref, low_ref, sign_ref):
+def mix_rows(tiles, high_ref, low_ref, sign_ref):
+    blocks = len(tiles[0])
+    stacked = jnp.concatenate([jnp.concatenate(one, axis=0).astype(BF16) for one in tiles], axis=1)
     mixed = nn_dot(high_ref[...], stacked) + nn_dot(low_ref[...], stacked)
     results = []
-    for part in range(stacked.shape[1] // HB):
-        high, low = split2(mixed[:, part * HB : (part + 1) * HB])
-        both = nn_dot(high, sign_ref[...]) + nn_dot(low, sign_ref[...])
-        results.append((both * HB ** (-0.5)).astype(BF16))
+    for j in range(len(tiles)):
+        part = nn_dot(mixed[:, j * HB : (j + 1) * HB].astype(BF16), sign_ref[...])
+        results.append((part * HB ** (-0.5)).reshape(blocks, ROWS, HB))
     return results
 
 
@@ -75,25 +77,15 @@
     def _():
         build_mixing(rot_ref, high_ref, low_ref, sign_ref, True)
 
-    parts = x_ref.shape[0] // SUB
-    stacked = jnp.concatenate(
-        [
-            jnp.concatenate(
-                [
-                    x_ref[j * SUB : (j + 1) * SUB, k * HB : (k + 1) * HB]
-                    for k in range(blocks)
-                ],
-                axis=0,
-            )
-            for j in range(parts)
-        ],
-        axis=1,
-    )
-    for j, result in enumerate(mix_rows(stacked, high_ref, low_ref, sign_ref)):
+    rows = x_ref.shape[0]
+    wide = [x_ref[:, k * HB : (k + 1) * HB].astype(F32) for k in range(blocks)]
+    tiles = [[one[j : j + ROWS] for one in wide] for j in range(0, rows, ROWS)]
+    results = mix_rows(tiles, high_ref, low_ref, sign_ref)
+    for j in range(rows // SUB):
+        both = jnp.concatenate([results[2 * j], results[2 * j + 1]], axis=1).astype(BF16)
         start = 0
         for size, out_ref in zip(sizes, outs):
-            piece = result[start * SUB : (start + size) * SUB]
-            out_ref[j] = piece.reshape(size, SUB, HB)
+            out_ref[j] = both[start : start + size]
             start += size
 
 
@@ -105,27 +97,24 @@
     def _():
         build_mixing(rot_ref, high_ref, low_ref, sign_ref, False)
 
-    parts = out_ref.shape[0] // SUB
-    stacked = jnp.concatenate(
-        [
-            jnp.concatenate(
-                [in_ref[j].reshape(size * SUB, HB) for size, in_ref in zip(sizes, ins)], axis=0
-            )
-            for j in range(parts)
-        ],
-        axis=1,
-    )
-    for j, result in enumerate(mix_rows(stacked, high_ref, low_ref, sign_ref)):
+    rows = out_ref.shape[0]
+    tiles = []
+    for j in range(rows // SUB):
+        wide = [
+            in_ref[j, c].astype(F32) for size, in_ref in zip(sizes, ins) for c in range(size)
+        ]
+        tiles += [[one[:ROWS] for one in wide], [one[ROWS:] for one in wide]]
+    results = mix_rows(tiles, high_ref, low_ref, sign_ref)
+    for j in range(rows // SUB):
+        both = jnp.concatenate([results[2 * j], results[2 * j + 1]], axis=1).astype(BF16)
         for k in range(blocks):
-            out_ref[j * SUB : (j + 1) * SUB, k * HB : (k + 1) * HB] = result[
-                k * SUB : (k + 1) * SUB
-            ]
+            out_ref[j * SUB : (j + 1) * SUB, k * HB : (k + 1) * HB] = both[k]
 
 
 def local_scratch(blocks):
     return [
-        pltpu.VMEM((blocks * SUB, blocks * SUB), BF16),
-        pltpu.VMEM((blocks * SUB, blocks * SUB), BF16),
+        pltpu.VMEM((blocks * ROWS, blocks * ROWS), BF16),
+        pltpu.VMEM((blocks * ROWS, blocks * ROWS), BF16),
         pltpu.VMEM((HB, HB), BF16),
     ]
 
@@ -165,7 +154,7 @@
         out_specs=[pl.BlockSpec((parts, size, SUB, HB), lambda i: (i, 0, 0, 0)) for size in sizes],
         out_shape=[jax.ShapeDtypeStruct((rows // SUB, size, SUB, HB), BF16) for size in sizes],
         scratch_shapes=local_scratch(blocks),
-        compiler_params=pltpu.CompilerParams(vmem_limit_bytes=16 << 20),
+        compiler_params=pltpu.CompilerParams(vmem_limit_bytes=60 << 20),
         cost_estimate=FREE,
         name="local_forward",
     )(*in_hbm(hidden), rot_block)
@@ -185,7 +174,7 @@
         out_specs=pl.BlockSpec((parts * SUB, blocks * HB), lambda i: (i, 0)),
         out_shape=pltpu.HBM((rows, blocks * HB), BF16),
         scratch_shapes=local_scratch(blocks),
-        compiler_params=pltpu.CompilerParams(vmem_limit_bytes=16 << 20),
+        compiler_params=pltpu.CompilerParams(vmem_limit_bytes=60 << 20),
         cost_estimate=FREE,
         name="local_backward",
     )(*mixed, rot_block, *after)
@@ -310,7 +299,7 @@
         in_specs=[spec(value.shape, 1) for value in ins] + [ANYWHERE] * len(after),
         out_specs=[spec(shape, 1) for shape in outs],
         out_shape=[jax.ShapeDtypeStruct(shape, BF16) for shape in outs],
-        compiler_params=pltpu.CompilerParams(vmem_limit_bytes=16 << 20),
+        compiler_params=pltpu.CompilerParams(vmem_limit_bytes=60 << 20),
         cost_estimate=FREE,
         name=name,
     )(*ins, *after)
@@ -413,7 +402,7 @@
         out_specs=pl.BlockSpec((count, per, SUB, HB), lambda i: (0, offset + i, 0, 0)),
         out_shape=jax.ShapeDtypeStruct((count, groups, SUB, HB), BF16),
         input_output_aliases=aliases,
-        compiler_params=pltpu.CompilerParams(vmem_limit_bytes=16 << 20),
+        compiler_params=pltpu.CompilerParams(vmem_limit_bytes=60 << 20),
         cost_estimate=FREE,
         name="total",
     )(*args, *after)
@@ -449,7 +438,7 @@
         return general_shards(hidden, upstream, weight, scales, clip_mask, rot_block)
     per = 4
     units = groups // per
-    sizes = (per * (units - units // 2), per * (units // 2))
+    sizes = (per * (units - 2 * units // 5), per * (2 * units // 5))
     starts = (0, sizes[0])
     half = subs // 2
     counts = (subs, subs, subs, half, half)
@@ -479,12 +468,12 @@
     forth = exchange(local)
     unit0 = unit_grads(up, weight, scales, starts[0], sizes[0], per, counts, after=(local,))
     first0 = scatter_first(unit0)
-    unit1 = unit_grads(up, weight, scales, starts[1], sizes[1], per, counts, after=(unit0[0],))
+    turned = transform(forth, after=(unit0[0],))
+    rotated = exchange(turned)
+    unit1 = unit_grads(up, weight, scales, starts[1], sizes[1], per, counts, after=(turned,))
     first1 = scatter_first(unit1)
     relayed0, *second0 = scatter_second(unit0, first0, after=(unit1[0],))
-    turned = transform(forth, after=(relayed0,))
-    rotated = exchange(turned)
-    relayed1, *second1 = scatter_second(unit1, first1, after=(turned,))
+    relayed1, *second1 = scatter_second(unit1, first1, after=(relayed0,))
     summed = total((unit0[0], *second0), None, starts[0], groups, per, after=(turned,))
     summed = total((unit1[0], *second1), summed, starts[1], groups, per, after=(rotated,))
     back = exchange(summed)

time: 263 us -> 259 us (0.985)
  local copies, waits for them, and re-layouts: 31.9 us -> 15.1 us
  Pallas kernels: 79.7 us -> 89.5 us
  waiting for transfers between devices: 108 us -> 111 us
    unnamed x62 -> x32, local copies, waits for them, and re-layouts: 29.1 us -> 12.2 us
    pallas_call x2, Pallas kernels: 1.34 us -> 9.96 us  [total(): pl.pallas_call(total_kernel, grid=(size // per,), in_specs=specs + [ANYWH...]
    pallas_call x4, Pallas kernels: 6.75 us -> 13.4 us  [small_call(): pl.pallas_call(drop_inputs(kernel, len(ins), len(after)), grid=(steps,),...]
    pallas_call x1, Pallas kernels: 9.76 us -> 5.99 us  [local_backward(): pl.pallas_call(drop_inputs(functools.partial(backward_kernel, sizes), len...]
    pallas_call x1, Pallas kernels: 9.75 us -> 5.99 us  [local_forward(): pl.pallas_call(functools.partial(forward_kernel, sizes), grid=(rows // (S...]
  transfers between devices with their start and end apart: 20 -> 20, of which waited for: 11 -> 12; matrix products, arithmetic and copies ran while one was open for 2% -> 2% of each run, Pallas kernels for 21% -> 25%
where the time goes in v3:
time: 259 us; the launch traced here: 258 us
  waiting for transfers between devices  111 us (43%)
  Pallas kernels  89.5 us (35%)
  starting transfers between devices  38.3 us (15%)
  local copies, waits for them, and re-layouts  15.1 us (6%)
  other arithmetic  3.46 us (1%)
    ppermute x16, waiting for transfers between devices, partner(): return lax.ppermute(value, axis, [(i, i ^ mask) for i in range(size)])  109 us
    pallas_call x2, Pallas kernels, weight_grads(): pl.pallas_call(functools.partial(weights_kernel, first, per, len(rotated)...  32.1 us
    pallas_call x2, Pallas kernels, unit_grads(): pl.pallas_call(drop_inputs(functools.partial(units_kernel, first, per), 3...  22.2 us
    all_to_all x4, starting transfers between devices, exchange(): lax.all_to_all(value, 'tensor', split_axis=0, concat_axis=0, tiled=True)  20.2 us
    ppermute x16, starting transfers between devices, partner(): return lax.ppermute(value, axis, [(i, i ^ mask) for i in range(size)])  18.1 us
    pallas_call x4, Pallas kernels, small_call(): pl.pallas_call(drop_inputs(kernel, len(ins), len(after)), grid=(steps,),...  13.4 us
    unnamed x32, local copies, waits for them, and re-layouts  12.2 us
    pallas_call x2, Pallas kernels, total(): pl.pallas_call(total_kernel, grid=(size // per,), in_specs=specs + [ANYWH...  9.96 us
  transfers between devices with their start and end apart: 20, of which 12 were waited for; matrix products, arithmetic and copies ran while one was open for 2% of the time, Pallas kernels for 25%

profile of v3, /device:TPU:0, one launch (start us, length us, event | category | flops | bytes accessed | tf_op | source)
XLA Modules:
  0.0 257.6 jit_solution(15812289848103880219)
XLA Ops:
  0.6 6.0 %local_forward.1.refs_3_ = bf16[8,52,16,128]{3,2,1,0:T(8,128)(2,1)} custom-call(bf16[128,6656]{1,0:T(8,128)(2,1)} %x_ref.1, f32[52,52]{1,0:T(8,128)} %refs_1_.5), custom_call_target="tpu_custom_call" | custom-call | tf_op jit(solution)/shard_map/local_forward/pallas_call | solution.py:147
  6.6 6.5 %all-to-all-start = ((bf16[8,52,16,128]{3,2,1,0:T(8,128)(2,1)}), bf16[8,52,16,128]{3,2,1,0:T(8,128)(2,1)}, u32[]{:S(2)}, u32[]{:S(2)}) async-start(bf16[8,52,16,128]{3,2,1,0:T(8,128)(2,1)} %local_forward.1.refs_3_), calls=%async_computation | async-start | bytes 3407872 | tf_op jit(solution)/shard_map/all_to_all | solution.py:330
  13.2 1.6 collective-permute-start
  14.7 1.5 collective-permute-start.2
  16.7 5.6 %collective-permute-done = bf16[64,2048]{1,0:T(8,128)(2,1)S(1)} collective-permute-done((bf16[64,2048]{1,0:T(8,128)(2,1)S(1)}, bf16[64,2048]{1,0:T(8,128)(2,1)S(1)}, u32[]{:S(2)}, u32[]{:S(2)}) %collective-permute-start) | collective-permute-done | bytes 262176 | tf_op jit(solution)/shard_map/ppermute | solution.py:335
  22.3 6.3 %collective-permute-done.2 = bf16[64,2048]{1,0:T(8,128)(2,1)S(1)} collective-permute-done((bf16[64,2048]{1,0:T(8,128)(2,1)S(1)}, bf16[64,2048]{1,0:T(8,128)(2,1)S(1)}, u32[]{:S(2)}, u32[]{:S(2)}) %collective-permute-start.2) | collective-permute-done | bytes 262176 | tf_op jit(solution)/shard_map/ppermute | solution.py:335
  31.0 2.6 %collective-permute-done.3 = bf16[3,64,2048]{2,1,0:T(8,128)(2,1)} collective-permute-done((bf16[3,64,2048]{2,1,0:T(8,128)(2,1)}, bf16[3,64,2048]{2,1,0:T(8,128)(2,1)}, u32[]{:S(2)}, u32[]{:S(2)}) %collective-permute-start.3) | collective-permute-done | bytes 786464 | tf_op jit(solution)/shard_map/ppermute | solution.py:335
  36.5 13.3 %unit_grads.2 = (bf16[8,32,16,128]{3,2,1,0:T(8,128)(2,1)S(1)}, bf16[8,32,16,128]{3,2,1,0:T(8,128)(2,1)S(1)}, bf16[8,32,16,128]{3,2,1,0:T(8,128)(2,1)S(1)}, bf16[...) custom-call(bf16[512,2048]{1,0:T(8,128)(2,1)S(1)} %pad_maximum_fusion.refs_0_.refs_5_, ...), custom_call_target="tpu_custom_call" | custom-call | tf_op jit(solution)/shard_map/unit_grads/pallas_call | solution.py:203
  53.8 4.0 %transform.2.refs_3_.refs_0_ = bf16[8,52,16,128]{3,2,1,0:T(8,128)(2,1)} custom-call(bf16[8,52,16,128]{3,2,1,0:T(8,128)(2,1)} %all-to-all-done.refs_0_, bf16[8,32,16,128]{3,2,1,0:T(8,128)(2,1)} %copy-done.3), custom_call_target="tpu_custom_call" | custom-call | tf_op jit(solution)/shard_map/transform/pallas_call | solution.py:296
  57.8 4.3 %all-to-all-start.1 = ((bf16[8,52,16,128]{3,2,1,0:T(8,128)(2,1)}), bf16[8,52,16,128]{3,2,1,0:T(8,128)(2,1)}, u32[]{:S(2)}, u32[]{:S(2)}) async-start(bf16[8,52,16,128]{3,2,1,0:T(8,128)(2,1)} %transform.2.refs_3_.refs_0_), calls=%async_computation.1 | async-start | bytes 3407872 | tf_op jit(solution)/shard_map/all_to_all | solution.py:330
  62.1 1.6 collective-permute-start.6
  63.7 1.5 collective-permute-start.7
  66.6 8.9 %unit_grads.3 = (bf16[8,20,16,128]{3,2,1,0:T(8,128)(2,1)S(1)}, bf16[8,20,16,128]{3,2,1,0:T(8,128)(2,1)S(1)}, bf16[8,20,16,128]{3,2,1,0:T(8,128)(2,1)S(1)}, bf16[...) custom-call(bf16[512,2048]{1,0:T(8,128)(2,1)S(1)} %pad_maximum_fusion.refs_0_.refs_5_, ...), custom_call_target="tpu_custom_call" | custom-call | tf_op jit(solution)/shard_map/unit_grads/pallas_call | solution.py:203
  79.8 3.0 %relay.2 = (bf16[8,32,16,128]{3,2,1,0:T(8,128)(2,1)}, bf16[8,32,16,128]{3,2,1,0:T(8,128)(2,1)}) custom-call(bf16[8,32,16,128]{3,2,1,0:T(8,128)(2,1)} %copy-done.5, bf16[8,32,16,128]{3,2,1,0:T(8,128)(2,1)} %copy-done.6, bf16[4,32,16,128]{3,2,1,0:T(8,128)(2,1)} %copy-done.12, bf16[4,32,16,128]{3,2,1,0:T(8,128)(2,1)} %copy-done.13, ...), custom_call_target="tpu_custom_call" | custom-call | tf_op jit(solution)/shard_map/relay/pallas_call | solution.py:296
  85.3 1.5 collective-permute-start.5
  86.8 28.2 %collective-permute-done.4.refs_2_ = bf16[4,20,16,128]{3,2,1,0:T(8,128)(2,1)S(1)} collective-permute-done((bf16[4,20,16,128]{3,2,1,0:T(8,128)(2,1)S(1)}, bf16[4,20,16,128]{3,2,1,0:T(8,128)(2,1)S(1)}, u32[]{:S(2)}, u32[]{:S(2)}) %collective-permute-start.4) | collective-permute-done | bytes 327712 | tf_op jit(solution)/shard_map/ppermute | solution.py:335
  116.5 2.4 relay.3
  121.9 5.9 %total.2.refs_0_ = bf16[8,52,16,128]{3,2,1,0:T(8,128)(2,1)} custom-call(bf16[8,32,16,128]{3,2,1,0:T(8,128)(2,1)} %copy-done.3, bf16[8,32,16,128]{3,2,1,0:T(8,128)(2,1)} %collective-permute-done.10.x_ref, bf16[8,32,16,128]{3,2,1,0:T(8,128)(2,1)} %copy-done.10, bf16[8,52,16,128]{3,2,1,0:T(8,128)(2,1)} %transform.2.refs_3_.refs_0_), custom_call_target="tpu_custom_call" | custom-call | tf_op jit(solution)/shard_map/total/pallas_call | solution.py:398
  127.8 6.6 %collective-permute-done.8.x_ref = bf16[8,20,16,128]{3,2,1,0:T(8,128)(2,1)} collective-permute-done((bf16[8,20,16,128]{3,2,1,0:T(8,128)(2,1)}, bf16[8,20,16,128]{3,2,1,0:T(8,128)(2,1)}, u32[]{:S(2)}, u32[]{:S(2)}) %collective-permute-start.8) | collective-permute-done | bytes 655392 | tf_op jit(solution)/shard_map/ppermute | solution.py:335
  134.5 4.1 %total.3 = bf16[8,52,16,128]{3,2,1,0:T(8,128)(2,1)} custom-call(bf16[8,20,16,128]{3,2,1,0:T(8,128)(2,1)} %copy-done.4, bf16[8,20,16,128]{3,2,1,0:T(8,128)(2,1)} %collective-permute-done.8.x_ref, bf16[8,20,16,128]{3,2,1,0:T(8,128)(2,1)} %collective-permute-done.9.y_ref, bf16[8,52,16,128]{3,2,1,0:T(8,128)(2,1)} %total.2.refs_0_, ...), custom_call_target="tpu_custom_call", output_to_operand_aliasing={{}: (3, {})} | custom-call | tf_op jit(solution)/shard_map/total/pallas_call | solution.py:398
  138.7 4.7 %all-to-all-start.2 = ((bf16[8,52,16,128]{3,2,1,0:T(8,128)(2,1)}), bf16[8,52,16,128]{3,2,1,0:T(8,128)(2,1)}, u32[]{:S(2)}, u32[]{:S(2)}) async-start(bf16[8,52,16,128]{3,2,1,0:T(8,128)(2,1)} %total.3), calls=%async_computation.2 | async-start | bytes 3407872 | tf_op jit(solution)/shard_map/all_to_all | solution.py:330
  143.4 1.5 collective-permute-start.13
  144.9 1.5 collective-permute-start.12
  146.4 36.9 %collective-permute-done.13.refs_2_ = bf16[8,52,16,128]{3,2,1,0:T(8,128)(2,1)} collective-permute-done((bf16[8,52,16,128]{3,2,1,0:T(8,128)(2,1)}, bf16[8,52,16,128]{3,2,1,0:T(8,128)(2,1)}, u32[]{:S(2)}, u32[]{:S(2)}) %collective-permute-start.13) | collective-permute-done | bytes 1703968 | tf_op jit(solution)/shard_map/ppermute | solution.py:335
  184.5 4.0 %transform.3.refs_9_ = bf16[8,52,16,128]{3,2,1,0:T(8,128)(2,1)} custom-call(bf16[8,52,16,128]{3,2,1,0:T(8,128)(2,1)} %all-to-all-done.2.refs_0_, bf16[8,52,16,128]{3,2,1,0:T(8,128)(2,1)} %collective-permute-done.12.refs_1_, bf16[8,52,16,128]{3,2,1,0:T(8,128)(2,1)} %collective-permute-done.13.refs_2_), custom_call_target="tpu_custom_call" | custom-call | tf_op jit(solution)/shard_map/transform/pallas_call | solution.py:296
  188.5 4.7 %all-to-all-start.3 = ((bf16[8,52,16,128]{3,2,1,0:T(8,128)(2,1)}), bf16[8,52,16,128]{3,2,1,0:T(8,128)(2,1)}, u32[]{:S(2)}, u32[]{:S(2)}) async-start(bf16[8,52,16,128]{3,2,1,0:T(8,128)(2,1)} %transform.3.refs_9_), calls=%async_computation.3 | async-start | bytes 3407872 | tf_op jit(solution)/shard_map/all_to_all | solution.py:330
  194.7 1.6 collective-permute-start.14
  198.3 17.8 %collective-permute-done.14.refs_3_ = bf16[4,52,16,128]{3,2,1,0:T(8,128)(2,1)S(1)} collective-permute-done((bf16[4,52,16,128]{3,2,1,0:T(8,128)(2,1)S(1)}, bf16[4,52,16,128]{3,2,1,0:T(8,128)(2,1)S(1)}, u32[]{:S(2)}, u32[]{:S(2)}) %collective-permute-start.14) | collective-permute-done | bytes 852000 | tf_op jit(solution)/shard_map/ppermute | solution.py:335
  216.1 2.6 %collective-permute-done.15.refs_4_ = bf16[4,52,16,128]{3,2,1,0:T(8,128)(2,1)S(1)} collective-permute-done((bf16[4,52,16,128]{3,2,1,0:T(8,128)(2,1)S(1)}, bf16[4,52,16,128]{3,2,1,0:T(8,128)(2,1)S(1)}, u32[]{:S(2)}, u32[]{:S(2)}) %collective-permute-start.15) | collective-permute-done | bytes 852000 | tf_op jit(solution)/shard_map/ppermute | solution.py:335
  218.7 18.9 %weight_grads.2 = (bf16[6656,2048]{1,0:T(8,128)(2,1)}, f32[32,2048]{1,0:T(8,128)S(1)}) custom-call(bf16[8,52,16,128]{3,2,1,0:T(8,128)(2,1)} %all-to-all-done.1.refs_1_.refs_0_, bf16[8,52,16,128]{3,2,1,0:T(8,128)(2,1)} %collective-permute-done.12.refs_1_, bf16[8,52,16,128]{3,2,1,0:T(8,128)(2,1)} %collective-permute-done.13.refs_2_, ...), custom_call_target="tpu_custom_call" | custom-call | tf_op jit(solution)/shard_map/weight_grads/pallas_call | solution.py:270
  237.6 13.2 %weight_grads.3 = (bf16[6656,2048]{1,0:T(8,128)(2,1)}, f32[20,2048]{1,0:T(8,128)S(1)}) custom-call(bf16[8,52,16,128]{3,2,1,0:T(8,128)(2,1)} %all-to-all-done.1.refs_1_.refs_0_, bf16[8,52,16,128]{3,2,1,0:T(8,128)(2,1)} %collective-permute-done.12.refs_1_, bf16[8,52,16,128]{3,2,1,0:T(8,128)(2,1)} %collective-permute-done.13.refs_2_, ...), custom_call_target="tpu_custom_call", output_to_operand_aliasing={{0}: (9, {})} | custom-call | tf_op jit(solution)/shard_map/weight_grads/pallas_call | solution.py:270
  251.6 6.0 %local_backward.1 = bf16[128,6656]{1,0:T(8,128)(2,1)} custom-call(bf16[8,52,16,128]{3,2,1,0:T(8,128)(2,1)} %all-to-all-done.3.refs_0_, f32[52,52]{1,0:T(8,128)} %refs_1_.5, f32[20,2048]{1,0:T(8,128)} %copy-done.7), custom_call_target="tpu_custom_call" | custom-call | tf_op jit(solution)/shard_map/local_backward/pallas_call | solution.py:168
  (61 shorter events, 28.3 us)
Async XLA Ops:
  6.6 6.5 %copy-start.11 = (bf16[128,8192]{1,0:T(8,128)(2,1)S(1)}, bf16[128,8192]{1,0:T(8,128)(2,1)}, u32[]{:S(2)}) copy-start(bf16[128,8192]{1,0:T(8,128)(2,1)} %param.7) | copy-start | bytes 6291460
  6.6 47.2 %all-to-all-start = ((bf16[8,52,16,128]{3,2,1,0:T(8,128)(2,1)}), bf16[8,52,16,128]{3,2,1,0:T(8,128)(2,1)}, u32[]{:S(2)}, u32[]{:S(2)}) async-start(bf16[8,52,16,128]{3,2,1,0:T(8,128)(2,1)} %local_forward.1.refs_3_), calls=%async_computation | async-start | bytes 3407872 | tf_op jit(solution)/shard_map/all_to_all | solution.py:330
  13.2 9.2 %collective-permute-start = (bf16[64,2048]{1,0:T(8,128)(2,1)S(1)}, bf16[64,2048]{1,0:T(8,128)(2,1)S(1)}, u32[]{:S(2)}, u32[]{:S(2)}) collective-permute-start(bf16[64,2048]{1,0:T(8,128)(2,1)S(1)} %get-tuple-element.39), channel_id=1, source_target_pairs={{0,8},{8,0},{16,24},{24,16},{1,9},{9,1},{17,25},{25,17},{2,10},{10... | collective-permute-start | bytes 786440 | tf_op jit(solution)/shard_map/ppermute | solution.py:335
  14.7 13.9 %collective-permute-start.2 = (bf16[64,2048]{1,0:T(8,128)(2,1)S(1)}, bf16[64,2048]{1,0:T(8,128)(2,1)S(1)}, u32[]{:S(2)}, u32[]{:S(2)}) collective-permute-start(bf16[64,2048]{1,0:T(8,128)(2,1)S(1)} %get-tuple-element.40), channel_id=1, source_target_pairs={{0,24},{8,16},{16,8},{24,0},{1,25},{9,17},{17,9},{25,1},{2,26},{10... | collective-permute-start | bytes 786440 | tf_op jit(solution)/shard_map/ppermute | solution.py:335
  16.2 13.8 %collective-permute-start.1 = (bf16[64,2048]{1,0:T(8,128)(2,1)S(1)}, bf16[64,2048]{1,0:T(8,128)(2,1)S(1)}, u32[]{:S(2)}, u32[]{:S(2)}) collective-permute-start(bf16[64,2048]{1,0:T(8,128)(2,1)S(1)} %get-tuple-element.41), channel_id=1, source_target_pairs={{0,16},{8,24},{16,0},{24,8},{1,17},{9,25},{17,1},{25,9},{2,18},{10... | collective-permute-start | bytes 786440 | tf_op jit(solution)/shard_map/ppermute | solution.py:335
  30.9 2.6 %collective-permute-start.3 = (bf16[3,64,2048]{2,1,0:T(8,128)(2,1)}, bf16[3,64,2048]{2,1,0:T(8,128)(2,1)}, u32[]{:S(2)}, u32[]{:S(2)}) collective-permute-start(bf16[3,64,2048]{2,1,0:T(8,128)(2,1)} %pad_maximum_fusion.2), channel_id=1, source_target_pairs={{0,1},{1,0},{2,3},{3,2},{4,5},{5,4},{6,7},{7,6},{8,9},{9,8},{10,11... | collective-permute-start | bytes 2359304 | tf_op jit(solution)/shard_map/ppermute | solution.py:335
  35.0 1.5 copy-start.2
  49.7 1.0 copy-start.3
  50.7 1.0 copy-start.5
  51.7 1.0 copy-start.6
  57.8 76.8 %all-to-all-start.1 = ((bf16[8,52,16,128]{3,2,1,0:T(8,128)(2,1)}), bf16[8,52,16,128]{3,2,1,0:T(8,128)(2,1)}, u32[]{:S(2)}, u32[]{:S(2)}) async-start(bf16[8,52,16,128]{3,2,1,0:T(8,128)(2,1)} %transform.2.refs_3_.refs_0_), calls=%async_computation.1 | async-start | bytes 3407872 | tf_op jit(solution)/shard_map/all_to_all | solution.py:330
  62.1 16.0 %collective-permute-start.6 = (bf16[4,32,16,128]{3,2,1,0:T(8,128)(2,1)S(1)}, bf16[4,32,16,128]{3,2,1,0:T(8,128)(2,1)S(1)}, u32[]{:S(2)}, u32[]{:S(2)}) collective-permute-start(bf16[4,32,16,128]{3,2,1,0:T(8,128)(2,1)S(1)} %get-tuple-element.29), channel_id=1, source_target_pairs={{0,8},{8,0},{16,24},{24,16},{1,9},{9,1},{17,25},{25,17},{2,10},{10... | collective-permute-start | bytes 1572872 | tf_op jit(solution)/shard_map/ppermute | solution.py:335
  63.7 14.4 %collective-permute-start.7 = (bf16[4,32,16,128]{3,2,1,0:T(8,128)(2,1)S(1)}, bf16[4,32,16,128]{3,2,1,0:T(8,128)(2,1)S(1)}, u32[]{:S(2)}, u32[]{:S(2)}) collective-permute-start(bf16[4,32,16,128]{3,2,1,0:T(8,128)(2,1)S(1)} %get-tuple-element.30), channel_id=1, source_target_pairs={{0,16},{8,24},{16,0},{24,8},{1,17},{9,25},{17,1},{25,9},{2,18},{10... | collective-permute-start | bytes 1572872 | tf_op jit(solution)/shard_map/ppermute | solution.py:335
  65.2 1.5 copy-start
  75.5 0.9 copy-start.4
  77.2 0.9 copy-start.9
  78.1 0.8 copy-start.12
  82.7 38.2 %collective-permute-start.11 = (bf16[8,32,16,128]{3,2,1,0:T(8,128)(2,1)}, bf16[8,32,16,128]{3,2,1,0:T(8,128)(2,1)S(1)}, u32[]{:S(2)}, u32[]{:S(2)}) collective-permute-start(bf16[8,32,16,128]{3,2,1,0:T(8,128)(2,1)} %get-tuple-element.34), channel_id=1, source_target_pairs={{0,16},{8,24},{16,0},{24,8},{1,17},{9,25},{17,1},{25,9},{2,18},{10... | collective-permute-start | bytes 3145736 | tf_op jit(solution)/shard_map/ppermute | solution.py:335
  83.2 37.7 %collective-permute-start.10 = (bf16[8,32,16,128]{3,2,1,0:T(8,128)(2,1)}, bf16[8,32,16,128]{3,2,1,0:T(8,128)(2,1)}, u32[]{:S(2)}, u32[]{:S(2)}) collective-permute-start(bf16[8,32,16,128]{3,2,1,0:T(8,128)(2,1)} %get-tuple-element.31.refs_4_), channel_id=1, source_target_pairs={{0,8},{8,0},{16,24},{24,16},{1,9},{9,1},{17,25},{25,17},{2,10},{10... | collective-permute-start | bytes 3145736 | tf_op jit(solution)/shard_map/ppermute | solution.py:335
  83.9 31.1 %collective-permute-start.4 = (bf16[4,20,16,128]{3,2,1,0:T(8,128)(2,1)S(1)}, bf16[4,20,16,128]{3,2,1,0:T(8,128)(2,1)S(1)}, u32[]{:S(2)}, u32[]{:S(2)}) collective-permute-start(bf16[4,20,16,128]{3,2,1,0:T(8,128)(2,1)S(1)} %get-tuple-element.25), channel_id=1, source_target_pairs={{0,8},{8,0},{16,24},{24,16},{1,9},{9,1},{17,25},{25,17},{2,10},{10... | collective-permute-start | bytes 983048 | tf_op jit(solution)/shard_map/ppermute | solution.py:335
  85.3 29.7 %collective-permute-start.5 = (bf16[4,20,16,128]{3,2,1,0:T(8,128)(2,1)S(1)}, bf16[4,20,16,128]{3,2,1,0:T(8,128)(2,1)S(1)}, u32[]{:S(2)}, u32[]{:S(2)}) collective-permute-start(bf16[4,20,16,128]{3,2,1,0:T(8,128)(2,1)S(1)} %get-tuple-element.26), channel_id=1, source_target_pairs={{0,16},{8,24},{16,0},{24,8},{1,17},{9,25},{17,1},{25,9},{2,18},{10... | collective-permute-start | bytes 983048 | tf_op jit(solution)/shard_map/ppermute | solution.py:335
  118.9 15.5 %collective-permute-start.8 = (bf16[8,20,16,128]{3,2,1,0:T(8,128)(2,1)}, bf16[8,20,16,128]{3,2,1,0:T(8,128)(2,1)}, u32[]{:S(2)}, u32[]{:S(2)}) collective-permute-start(bf16[8,20,16,128]{3,2,1,0:T(8,128)(2,1)} %get-tuple-element.32), channel_id=1, source_target_pairs={{0,8},{8,0},{16,24},{24,16},{1,9},{9,1},{17,25},{25,17},{2,10},{10... | collective-permute-start | bytes 1966088 | tf_op jit(solution)/shard_map/ppermute | solution.py:335
  119.5 15.1 %collective-permute-start.9 = (bf16[8,20,16,128]{3,2,1,0:T(8,128)(2,1)}, bf16[8,20,16,128]{3,2,1,0:T(8,128)(2,1)}, u32[]{:S(2)}, u32[]{:S(2)}) collective-permute-start(bf16[8,20,16,128]{3,2,1,0:T(8,128)(2,1)} %get-tuple-element.33), channel_id=1, source_target_pairs={{0,16},{8,24},{16,0},{24,8},{1,17},{9,25},{17,1},{25,9},{2,18},{10... | collective-permute-start | bytes 1966088 | tf_op jit(solution)/shard_map/ppermute | solution.py:335
  120.9 1.0 copy-start.10
  138.7 45.9 %all-to-all-start.2 = ((bf16[8,52,16,128]{3,2,1,0:T(8,128)(2,1)}), bf16[8,52,16,128]{3,2,1,0:T(8,128)(2,1)}, u32[]{:S(2)}, u32[]{:S(2)}) async-start(bf16[8,52,16,128]{3,2,1,0:T(8,128)(2,1)} %total.3), calls=%async_computation.2 | async-start | bytes 3407872 | tf_op jit(solution)/shard_map/all_to_all | solution.py:330
  143.4 39.9 %collective-permute-start.13 = (bf16[8,52,16,128]{3,2,1,0:T(8,128)(2,1)}, bf16[8,52,16,128]{3,2,1,0:T(8,128)(2,1)}, u32[]{:S(2)}, u32[]{:S(2)}) collective-permute-start(bf16[8,52,16,128]{3,2,1,0:T(8,128)(2,1)} %all-to-all-done.1.refs_1_.refs_0_), channel_id=1, source_target_pairs={{0,16},{8,24},{16,0},{24,8},{1,17},{9,25},{17,1},{25,9},{2,18},{10... | collective-permute-start | bytes 5111816 | tf_op jit(solution)/shard_map/ppermute | solution.py:335
  144.9 39.6 %collective-permute-start.12 = (bf16[8,52,16,128]{3,2,1,0:T(8,128)(2,1)}, bf16[8,52,16,128]{3,2,1,0:T(8,128)(2,1)}, u32[]{:S(2)}, u32[]{:S(2)}) collective-permute-start(bf16[8,52,16,128]{3,2,1,0:T(8,128)(2,1)} %all-to-all-done.1.refs_1_.refs_0_), channel_id=1, source_target_pairs={{0,8},{8,0},{16,24},{24,16},{1,9},{9,1},{17,25},{25,17},{2,10},{10... | collective-permute-start | bytes 5111816 | tf_op jit(solution)/shard_map/ppermute | solution.py:335
  188.5 63.1 %all-to-all-start.3 = ((bf16[8,52,16,128]{3,2,1,0:T(8,128)(2,1)}), bf16[8,52,16,128]{3,2,1,0:T(8,128)(2,1)}, u32[]{:S(2)}, u32[]{:S(2)}) async-start(bf16[8,52,16,128]{3,2,1,0:T(8,128)(2,1)} %transform.3.refs_9_), calls=%async_computation.3 | async-start | bytes 3407872 | tf_op jit(solution)/shard_map/all_to_all | solution.py:330
  193.3 25.4 %copy-start.1 = (bf16[8,52,16,128]{3,2,1,0:T(8,128)(2,1)S(1)}, bf16[8,52,16,128]{3,2,1,0:T(8,128)(2,1)}, u32[]{:S(2)}) copy-start(bf16[8,52,16,128]{3,2,1,0:T(8,128)(2,1)} %transform.3.refs_9_) | copy-start | bytes 5111812
  194.7 21.4 %collective-permute-start.14 = (bf16[4,52,16,128]{3,2,1,0:T(8,128)(2,1)S(1)}, bf16[4,52,16,128]{3,2,1,0:T(8,128)(2,1)S(1)}, u32[]{:S(2)}, u32[]{:S(2)}) collective-permute-start(bf16[4,52,16,128]{3,2,1,0:T(8,128)(2,1)S(1)} %slice.8), channel_id=1, source_target_pairs={{0,8},{8,0},{16,24},{24,16},{1,9},{9,1},{17,25},{25,17},{2,10},{10... | collective-permute-start | bytes 2555912 | tf_op jit(solution)/shard_map/ppermute | solution.py:335
  197.6 21.1 %collective-permute-start.15 = (bf16[4,52,16,128]{3,2,1,0:T(8,128)(2,1)S(1)}, bf16[4,52,16,128]{3,2,1,0:T(8,128)(2,1)S(1)}, u32[]{:S(2)}, u32[]{:S(2)}) collective-permute-start(bf16[4,52,16,128]{3,2,1,0:T(8,128)(2,1)S(1)} %slice.9), channel_id=1, source_target_pairs={{0,16},{8,24},{16,0},{24,8},{1,17},{9,25},{17,1},{25,9},{2,18},{10... | collective-permute-start | bytes 2555912 | tf_op jit(solution)/shard_map/ppermute | solution.py:335
  250.8 0.8 copy-start.7
  (4 other events, 3.1 us)

commit v4 on v3

--- a/solution.py
+++ b/solution.py
@@ -120,12 +120,9 @@
 
 
 FREE = pl.CostEstimate(flops=0, bytes_accessed=0, transcendentals=0)
-
-
-def cost(size, cols):
-    return pl.CostEstimate(
-        flops=0, bytes_accessed=4 * size * GROUP * cols, transcendentals=0
-    )
+LONG = pl.CostEstimate(flops=10**12, bytes_accessed=0, transcendentals=0)
+SMALL = 12 << 20
+
 ANYWHERE = pl.BlockSpec(memory_space=pl.ANY)
 
 
@@ -152,7 +149,7 @@
             pl.BlockSpec((blocks, blocks), lambda i: (0, 0)),
         ],
         out_specs=[pl.BlockSpec((parts, size, SUB, HB), lambda i: (i, 0, 0, 0)) for size in sizes],
-        out_shape=[jax.ShapeDtypeStruct((rows // SUB, size, SUB, HB), BF16) for size in sizes],
+        out_shape=[pltpu.HBM((rows // SUB, size, SUB, HB), BF16) for size in sizes],
         scratch_shapes=local_scratch(blocks),
         compiler_params=pltpu.CompilerParams(vmem_limit_bytes=60 << 20),
         cost_estimate=FREE,
@@ -177,24 +174,29 @@
         compiler_params=pltpu.CompilerParams(vmem_limit_bytes=60 << 20),
         cost_estimate=FREE,
         name="local_backward",
-    )(*mixed, rot_block, *after)
-
-
-def units_kernel(first, per, up_ref, w_ref, s_ref, *refs):
-    outs, quant_ref = refs[:-1], refs[-1]
+    )(*mixed, rot_block, *in_hbm(*after))
+
+
+def units_kernel(first, per, up_ref, w_ref, s_ref, *outs):
     base = first + pl.program_id(0) * per
-    for g in range(per):
-        rows = slice(g * GROUP, (g + 1) * GROUP)
-        quant_ref[rows, :] = (w_ref[rows, :].astype(F32) * s_ref[pl.ds(base + g, 1), :]).astype(
-            BF16
+    pair = 2 if per % 2 == 0 else 1
+    for start in range(0, per, pair):
+        quant = jnp.concatenate(
+            [
+                (
+                    w_ref[g * GROUP : (g + 1) * GROUP, :].astype(F32) * s_ref[pl.ds(base + g, 1), :]
+                ).astype(BF16)
+                for g in range(start, start + pair)
+            ],
+            axis=0,
         )
-    result = nt_dot(up_ref[...], quant_ref[...]).astype(BF16)
-    token = 0
-    for out_ref in outs:
-        for q in range(out_ref.shape[0]):
-            for g in range(per):
-                out_ref[q, g] = result[token : token + SUB, g * GROUP : (g + 1) * GROUP]
-            token += SUB
+        result = nt_dot(up_ref[...], quant).astype(BF16)
+        token = 0
+        for out_ref in outs:
+            for q in range(out_ref.shape[0]):
+                for g in range(pair):
+                    out_ref[q, start + g] = result[token : token + SUB, g * GROUP : (g + 1) * GROUP]
+                token += SUB
 
 
 def unit_grads(up, weight, scales, first, size, per, counts, after=()):
@@ -210,12 +212,11 @@
         ]
         + [ANYWHERE] * len(after),
         out_specs=[pl.BlockSpec((count, per, SUB, HB), lambda i: (0, i, 0, 0)) for count in counts],
-        out_shape=[jax.ShapeDtypeStruct((count, size, SUB, HB), BF16) for count in counts],
-        scratch_shapes=[pltpu.VMEM((per * GROUP, cols), BF16)],
+        out_shape=[pltpu.HBM((count, size, SUB, HB), BF16) for count in counts],
         compiler_params=pltpu.CompilerParams(vmem_limit_bytes=26 << 20),
         cost_estimate=FREE,
         name="unit_grads",
-    )(up, *in_hbm(weight, scales), *after)
+    )(up, *in_hbm(weight, scales), *in_hbm(*after))
 
 
 def weights_kernel(first, per, pieces, *refs):
@@ -234,7 +235,7 @@
         axis=1,
     )
     cols = up_ref.shape[1]
-    tile = min(512, cols)
+    tile = min(256, cols)
     for e in range(cols // tile):
         span = slice(e * tile, (e + 1) * tile)
         grad = tn_dot(left, up_ref[:, span])
@@ -281,12 +282,12 @@
         ],
         input_output_aliases=aliases,
         compiler_params=pltpu.CompilerParams(vmem_limit_bytes=26 << 20),
-        cost_estimate=FREE,
+        cost_estimate=LONG,
         name="weight_grads",
-    )(*args, *after)
-
-
-def small_call(kernel, name, ins, outs, steps, after=()):
+    )(*args, *in_hbm(*after))
+
+
+def small_call(kernel, name, ins, outs, steps, after=(), cost=FREE):
     def spec(shape, dim):
         block = tuple(n // steps if d == dim else n for d, n in enumerate(shape))
         return pl.BlockSpec(
@@ -298,11 +299,11 @@
         grid=(steps,),
         in_specs=[spec(value.shape, 1) for value in ins] + [ANYWHERE] * len(after),
         out_specs=[spec(shape, 1) for shape in outs],
-        out_shape=[jax.ShapeDtypeStruct(shape, BF16) for shape in outs],
-        compiler_params=pltpu.CompilerParams(vmem_limit_bytes=60 << 20),
-        cost_estimate=FREE,
+        out_shape=[pltpu.HBM(shape, BF16) for shape in outs],
+        compiler_params=pltpu.CompilerParams(vmem_limit_bytes=SMALL),
+        cost_estimate=cost,
         name=name,
-    )(*ins, *after)
+    )(*ins, *in_hbm(*after))
 
 
 def transform_kernel(x_ref, out_ref):
@@ -319,10 +320,10 @@
         out_ref[t] = (values[t] * count ** (-0.5)).astype(BF16)
 
 
-def transform(value, after=()):
+def transform(value, after=(), cost=FREE):
     steps = 4 if value.shape[1] % 4 == 0 else 1
     return small_call(
-        transform_kernel, "transform", [value], [value.shape], steps, after
+        transform_kernel, "transform", [value], [value.shape], steps, after, cost
     )[0]
 
 
@@ -379,33 +380,34 @@
     y_out[half:] = y_ref[half:]
 
 
-def total_kernel(own_ref, x_ref, y_ref, *refs):
-    refs[-1][...] = (
-        own_ref[...].astype(F32) + x_ref[...].astype(F32) + y_ref[...].astype(F32)
-    ).astype(BF16)
-
-
-def total(ins, buffer, first, groups, per, after=()):
-    count, size = ins[0].shape[:2]
-    offset = first // per
-    args = list(ins)
-    specs = [pl.BlockSpec((count, per, SUB, HB), lambda i: (0, i, 0, 0))] * 3
-    aliases = {}
-    if buffer is not None:
-        aliases = {3: 0}
-        args.append(buffer)
-        specs.append(ANYWHERE)
+def total_kernel(count, *refs):
+    out_ref = refs[-1]
+    start = 0
+    for i in range(count):
+        own_ref, x_ref, y_ref = refs[3 * i : 3 * i + 3]
+        size = own_ref.shape[1]
+        out_ref[:, start : start + size] = (
+            own_ref[...].astype(F32) + x_ref[...].astype(F32) + y_ref[...].astype(F32)
+        ).astype(BF16)
+        start += size
+
+
+def total(chunks, after=()):
+    ins = [value for own, *far in chunks for value in (*in_hbm(own), *far)]
+    subs = ins[0].shape[0]
+    groups = sum(chunk[0].shape[1] for chunk in chunks)
+    step = 2
     return pl.pallas_call(
-        total_kernel,
-        grid=(size // per,),
-        in_specs=specs + [ANYWHERE] * len(after),
-        out_specs=pl.BlockSpec((count, per, SUB, HB), lambda i: (0, offset + i, 0, 0)),
-        out_shape=jax.ShapeDtypeStruct((count, groups, SUB, HB), BF16),
-        input_output_aliases=aliases,
-        compiler_params=pltpu.CompilerParams(vmem_limit_bytes=60 << 20),
+        drop_inputs(functools.partial(total_kernel, len(chunks)), len(ins), len(after)),
+        grid=(subs // step,),
+        in_specs=[pl.BlockSpec((step,) + v.shape[1:], lambda i: (i, 0, 0, 0)) for v in ins]
+        + [ANYWHERE] * len(after),
+        out_specs=pl.BlockSpec((step, groups, SUB, HB), lambda i: (i, 0, 0, 0)),
+        out_shape=pltpu.HBM((subs, groups, SUB, HB), BF16),
+        compiler_params=pltpu.CompilerParams(vmem_limit_bytes=SMALL),
         cost_estimate=FREE,
         name="total",
-    )(*args, *after)
+    )(*ins, *in_hbm(*after))
 
 
 def general_shards(hidden, upstream, weight, scales, clip_mask, rot_block):
@@ -438,7 +440,7 @@
         return general_shards(hidden, upstream, weight, scales, clip_mask, rot_block)
     per = 4
     units = groups // per
-    sizes = (per * (units - 2 * units // 5), per * (2 * units // 5))
+    sizes = (per * (units - units // 2), per * (units // 2))
     starts = (0, sizes[0])
     half = subs // 2
     counts = (subs, subs, subs, half, half)
@@ -446,14 +448,15 @@
     def scatter_first(parts_of):
         return partner(parts_of[3], "dp", 1), partner(parts_of[4], "dp", 2)
 
-    def scatter_second(parts_of, received, after):
+    def scatter_second(parts_of, received, after, cost=FREE):
         x_part, y_part = small_call(
             relay_kernel,
             "relay",
-            [parts_of[1], parts_of[2], *received],
+            [*in_hbm(parts_of[1], parts_of[2]), *received],
             [parts_of[1].shape] * 2,
             2,
             after,
+            cost,
         )
         return x_part, partner(x_part, "dp", 1), partner(y_part, "dp", 2)
 
@@ -468,17 +471,16 @@
     forth = exchange(local)
     unit0 = unit_grads(up, weight, scales, starts[0], sizes[0], per, counts, after=(local,))
     first0 = scatter_first(unit0)
-    turned = transform(forth, after=(unit0[0],))
-    rotated = exchange(turned)
-    unit1 = unit_grads(up, weight, scales, starts[1], sizes[1], per, counts, after=(turned,))
+    unit1 = unit_grads(up, weight, scales, starts[1], sizes[1], per, counts, after=(unit0[0],))
     first1 = scatter_first(unit1)
     relayed0, *second0 = scatter_second(unit0, first0, after=(unit1[0],))
-    relayed1, *second1 = scatter_second(unit1, first1, after=(relayed0,))
-    summed = total((unit0[0], *second0), None, starts[0], groups, per, after=(turned,))
-    summed = total((unit1[0], *second1), summed, starts[1], groups, per, after=(rotated,))
+    turned = transform(forth, after=(relayed0,), cost=LONG)
+    rotated = exchange(turned)
+    relayed1, *second1 = scatter_second(unit1, first1, after=(turned,), cost=LONG)
+    summed = total(((unit0[0], *second0), (unit1[0], *second1)), after=(rotated,))
     back = exchange(summed)
     gathered = gather(rotated)
-    mixed = transform(back, after=gathered[1:3])
+    mixed = transform(back, cost=LONG)
     final = exchange(mixed)
     buffer, scale0 = weight_grads(
         gathered, up, weight, scales, clip_mask, None, starts[0], sizes[0], per, after=(mixed,)

time: 259 us -> 230 us (0.89)
  waiting for transfers between devices: 111 us -> 99.8 us
  Pallas kernels: 89.5 us -> 81.9 us
  local copies, waits for them, and re-layouts: 15.1 us -> 7.89 us
  starting transfers between devices: 38.3 us -> 35.6 us
    ppermute x16, waiting for transfers between devices: 109 us -> 93 us  [partner(): return lax.ppermute(value, axis, [(i, i ^ mask) for i in range(size)])]
    unnamed x32 -> x14, local copies, waits for them, and re-layouts: 12.2 us -> 3.21 us
    all_to_all x4, waiting for transfers between devices: 1.15 us -> 6.86 us  [exchange(): lax.all_to_all(value, 'tensor', split_axis=0, concat_axis=0, tiled=True)]
    pallas_call x2 -> x1, Pallas kernels: 9.96 us -> 4.3 us  [total(): pl.pallas_call(drop_inputs(functools.partial(total_kernel, len(chunks)),...]
    pallas_call x4, Pallas kernels: 13.4 us -> 9.78 us  [small_call(): pl.pallas_call(drop_inputs(kernel, len(ins), len(after)), grid=(steps,),...]
    pallas_call x2, Pallas kernels: 22.2 us -> 25.4 us  [unit_grads(): pl.pallas_call(drop_inputs(functools.partial(units_kernel, first, per), 3...]
  transfers between devices with their start and end apart: 20 -> 20, of which waited for: 12 -> 11; matrix products, arithmetic and copies ran while one was open for 2% -> 3% of each run, Pallas kernels for 25% -> 29%
where the time goes in v4:
time: 230 us; the launch traced here: 228 us
  waiting for transfers between devices  99.8 us (43%)
  Pallas kernels  81.9 us (36%)
  starting transfers between devices  35.6 us (15%)
  local copies, waits for them, and re-layouts  7.89 us (3%)
  other arithmetic  2.48 us (1%)
    ppermute x16, waiting for transfers between devices, partner(): return lax.ppermute(value, axis, [(i, i ^ mask) for i in range(size)])  93 us
    pallas_call x2, Pallas kernels, weight_grads(): pl.pallas_call(functools.partial(weights_kernel, first, per, len(rotated)...  30.5 us
    pallas_call x2, Pallas kernels, unit_grads(): pl.pallas_call(drop_inputs(functools.partial(units_kernel, first, per), 3...  25.4 us
    all_to_all x4, starting transfers between devices, exchange(): lax.all_to_all(value, 'tensor', split_axis=0, concat_axis=0, tiled=True)  19.6 us
    ppermute x16, starting transfers between devices, partner(): return lax.ppermute(value, axis, [(i, i ^ mask) for i in range(size)])  16 us
    pallas_call x4, Pallas kernels, small_call(): pl.pallas_call(drop_inputs(kernel, len(ins), len(after)), grid=(steps,),...  9.78 us
    all_to_all x4, waiting for transfers between devices, exchange(): lax.all_to_all(value, 'tensor', split_axis=0, concat_axis=0, tiled=True)  6.86 us
    pallas_call x1, Pallas kernels, local_forward(): pl.pallas_call(functools.partial(forward_kernel, sizes), grid=(rows // (S...  5.99 us
  transfers between devices with their start and end apart: 20, of which 11 were waited for; matrix products, arithmetic and copies ran while one was open for 3% of the time, Pallas kernels for 29%

profile of v4, /device:TPU:0, one launch (start us, length us, event | category | flops | bytes accessed | tf_op | source)
XLA Modules:
  0.0 228.4 jit_solution(10471695502459523644)
XLA Ops:
  0.6 6.0 %local_forward.1.refs_3_ = bf16[8,52,16,128]{3,2,1,0:T(8,128)(2,1)} custom-call(bf16[128,6656]{1,0:T(8,128)(2,1)} %x_ref.1, f32[52,52]{1,0:T(8,128)} %refs_1_.5), custom_call_target="tpu_custom_call" | custom-call | tf_op jit(solution)/shard_map/local_forward/pallas_call | solution.py:144
  6.6 6.3 %all-to-all-start = ((bf16[8,52,16,128]{3,2,1,0:T(8,128)(2,1)}), bf16[8,52,16,128]{3,2,1,0:T(8,128)(2,1)S(1)}, u32[]{:S(2)}, u32[]{:S(2)}) async-start(bf16[8,52,16,128]{3,2,1,0:T(8,128)(2,1)} %local_forward.1.refs_3_), calls=%async_computation | async-start | bytes 3407872 | tf_op jit(solution)/shard_map/all_to_all | solution.py:331
  14.1 1.6 collective-permute-start
  15.7 1.5 collective-permute-start.2
  17.7 5.6 %collective-permute-done = bf16[64,2048]{1,0:T(8,128)(2,1)S(1)} collective-permute-done((bf16[64,2048]{1,0:T(8,128)(2,1)S(1)}, bf16[64,2048]{1,0:T(8,128)(2,1)S(1)}, u32[]{:S(2)}, u32[]{:S(2)}) %collective-permute-start) | collective-permute-done | bytes 262176 | tf_op jit(solution)/shard_map/ppermute | solution.py:336
  23.3 6.3 %collective-permute-done.2 = bf16[64,2048]{1,0:T(8,128)(2,1)S(1)} collective-permute-done((bf16[64,2048]{1,0:T(8,128)(2,1)S(1)}, bf16[64,2048]{1,0:T(8,128)(2,1)S(1)}, u32[]{:S(2)}, u32[]{:S(2)}) %collective-permute-start.2) | collective-permute-done | bytes 262176 | tf_op jit(solution)/shard_map/ppermute | solution.py:336
  35.1 13.8 %unit_grads.2 = (bf16[8,28,16,128]{3,2,1,0:T(8,128)(2,1)}, bf16[8,28,16,128]{3,2,1,0:T(8,128)(2,1)}, bf16[8,28,16,128]{3,2,1,0:T(8,128)(2,1)}, bf16[4,28,16,128]{3,2,1,0:T(8,128)(2,1)}, bf16[4,28,16,128]{3,2,1,0:T(8,128)(2,1)}) custom-call(bf16[512,2048]{1,0:T(8,128)(2,1)S(1)} %pad_maximum_fusion.refs_0_.refs_5_, bf16[6656,2048]{1,0:T(8,128)(2,1)} %refs_6_.3, ...), custom_call_target="tpu_custom_call" | custom-call | tf_op jit(solution)/shard_map/unit_grads/pallas_call | solution.py:205
  48.9 1.5 collective-permute-start.4
  50.9 11.6 %unit_grads.3 = (bf16[8,24,16,128]{3,2,1,0:T(8,128)(2,1)}, bf16[8,24,16,128]{3,2,1,0:T(8,128)(2,1)}, bf16[8,24,16,128]{3,2,1,0:T(8,128)(2,1)}, bf16[4,24,16,128]{3,2,1,0:T(8,128)(2,1)}, bf16[4,24,16,128]{3,2,1,0:T(8,128)(2,1)}) custom-call(bf16[512,2048]{1,0:T(8,128)(2,1)S(1)} %pad_maximum_fusion.refs_0_.refs_5_, bf16[6656,2048]{1,0:T(8,128)(2,1)} %refs_6_.3, ...), custom_call_target="tpu_custom_call" | custom-call | tf_op jit(solution)/shard_map/unit_grads/pallas_call | solution.py:205
  63.0 1.5 collective-permute-start.9
  64.6 2.6 %relay.2 = (bf16[8,28,16,128]{3,2,1,0:T(8,128)(2,1)}, bf16[8,28,16,128]{3,2,1,0:T(8,128)(2,1)}) custom-call(bf16[8,28,16,128]{3,2,1,0:T(8,128)(2,1)} %get-tuple-element.22.refs_0_, bf16[8,28,16,128]{3,2,1,0:T(8,128)(2,1)} %get-tuple-element.23.refs_1_, bf16[4,28,16,128]{3,2,1,0:T(8,128)(2,1)S(1)} %collective-permute-done.4.refs_2_, ...), custom_call_target="tpu_custom_call" | custom-call | tf_op jit(solution)/shard_map/relay/pallas_call | solution.py:297
  67.7 1.5 collective-permute-start.6
  69.2 2.3 transform.2.refs_4_
  71.4 4.7 %all-to-all-start.1 = ((bf16[8,52,16,128]{3,2,1,0:T(8,128)(2,1)}), bf16[8,52,16,128]{3,2,1,0:T(8,128)(2,1)}, u32[]{:S(2)}, u32[]{:S(2)}) async-start(bf16[8,52,16,128]{3,2,1,0:T(8,128)(2,1)} %transform.2.refs_4_), calls=%async_computation.1 | async-start | bytes 3407872 | tf_op jit(solution)/shard_map/all_to_all | solution.py:331
  76.2 2.6 %relay.3 = (bf16[8,24,16,128]{3,2,1,0:T(8,128)(2,1)}, bf16[8,24,16,128]{3,2,1,0:T(8,128)(2,1)}) custom-call(bf16[8,24,16,128]{3,2,1,0:T(8,128)(2,1)} %get-tuple-element.29.refs_0_, bf16[8,24,16,128]{3,2,1,0:T(8,128)(2,1)} %get-tuple-element.30.refs_1_, bf16[4,24,16,128]{3,2,1,0:T(8,128)(2,1)} %collective-permute-done.8.refs_2_, ...), custom_call_target="tpu_custom_call" | custom-call | flops 999999995904 | tf_op jit(solution)/shard_map/relay/pallas_call | solution.py:297
  79.5 1.5 collective-permute-start.11
  81.0 14.0 %collective-permute-done.7.refs_2_ = bf16[8,28,16,128]{3,2,1,0:T(8,128)(2,1)} collective-permute-done((bf16[8,28,16,128]{3,2,1,0:T(8,128)(2,1)}, bf16[8,28,16,128]{3,2,1,0:T(8,128)(2,1)}, u32[]{:S(2)}, u32[]{:S(2)}) %collective-permute-start.7) | collective-permute-done | bytes 917536 | tf_op jit(solution)/shard_map/ppermute | solution.py:336
  95.1 14.8 %collective-permute-done.10.refs_4_ = bf16[8,24,16,128]{3,2,1,0:T(8,128)(2,1)S(1)} collective-permute-done((bf16[8,24,16,128]{3,2,1,0:T(8,128)(2,1)}, bf16[8,24,16,128]{3,2,1,0:T(8,128)(2,1)S(1)}, u32[]{:S(2)}, u32[]{:S(2)}) %collective-permute-start.10) | collective-permute-done | bytes 786464 | tf_op jit(solution)/shard_map/ppermute | solution.py:336
  110.1 6.9 %all-to-all-done.1.refs_6_.refs_0_ = bf16[8,52,16,128]{3,2,1,0:T(8,128)(2,1)} async-done(((bf16[8,52,16,128]{3,2,1,0:T(8,128)(2,1)}), bf16[8,52,16,128]{3,2,1,0:T(8,128)(2,1)}, u32[]{:S(2)}, u32[]{:S(2)}) %all-to-all-start.1) | async-done | bytes 1703968 | tf_op jit(solution)/shard_map/all_to_all | solution.py:331
  116.9 4.3 %total.1 = bf16[8,52,16,128]{3,2,1,0:T(8,128)(2,1)} custom-call(bf16[8,28,16,128]{3,2,1,0:T(8,128)(2,1)} %get-tuple-element.21.refs_3_.refs_0_, bf16[8,28,16,128]{3,2,1,0:T(8,128)(2,1)} %collective-permute-done.6.refs_1_, bf16[8,28,16,128]{3,2,1,0:T(8,128)(2,1)} %collective-permute-done.7.refs_2_, ...), custom_call_target="tpu_custom_call" | custom-call | tf_op jit(solution)/shard_map/total/pallas_call | solution.py:400
  121.2 3.6 %all-to-all-start.2 = ((bf16[8,52,16,128]{3,2,1,0:T(8,128)(2,1)}), bf16[8,52,16,128]{3,2,1,0:T(8,128)(2,1)S(1)}, u32[]{:S(2)}, u32[]{:S(2)}) async-start(bf16[8,52,16,128]{3,2,1,0:T(8,128)(2,1)} %total.1), calls=%async_computation.2 | async-start | bytes 3407872 | tf_op jit(solution)/shard_map/all_to_all | solution.py:331
  124.8 1.6 collective-permute-start.13
  126.9 37.6 %collective-permute-done.13.refs_2_ = bf16[8,52,16,128]{3,2,1,0:T(8,128)(2,1)S(1)} collective-permute-done((bf16[8,52,16,128]{3,2,1,0:T(8,128)(2,1)}, bf16[8,52,16,128]{3,2,1,0:T(8,128)(2,1)S(1)}, u32[]{:S(2)}, u32[]{:S(2)}) %collective-permute-start.13) | collective-permute-done | bytes 1703968 | tf_op jit(solution)/shard_map/ppermute | solution.py:336
  167.8 1.5 collective-permute-start.15
  169.3 2.3 transform.3.refs_9_
  171.6 4.9 %all-to-all-start.3 = ((bf16[8,52,16,128]{3,2,1,0:T(8,128)(2,1)}), bf16[8,52,16,128]{3,2,1,0:T(8,128)(2,1)}, u32[]{:S(2)}, u32[]{:S(2)}) async-start(bf16[8,52,16,128]{3,2,1,0:T(8,128)(2,1)} %transform.3.refs_9_), calls=%async_computation.3 | async-start | bytes 3407872 | tf_op jit(solution)/shard_map/all_to_all | solution.py:331
  176.5 10.0 %collective-permute-done.14.refs_3_ = bf16[4,52,16,128]{3,2,1,0:T(8,128)(2,1)} collective-permute-done((bf16[4,52,16,128]{3,2,1,0:T(8,128)(2,1)}, bf16[4,52,16,128]{3,2,1,0:T(8,128)(2,1)}, u32[]{:S(2)}, u32[]{:S(2)}) %collective-permute-start.14) | collective-permute-done | bytes 852000 | tf_op jit(solution)/shard_map/ppermute | solution.py:336
  186.5 1.8 collective-permute-done.15.refs_4_
  188.2 1.5 copy-done.4
  191.1 16.3 %weight_grads.2 = (bf16[6656,2048]{1,0:T(8,128)(2,1)}, f32[28,2048]{1,0:T(8,128)S(1)}) custom-call(bf16[8,52,16,128]{3,2,1,0:T(8,128)(2,1)} %all-to-all-done.1.refs_6_.refs_0_, bf16[8,52,16,128]{3,2,1,0:T(8,128)(2,1)S(1)} %copy-done.6, bf16[8,52,16,128]{3,2,1,0:T(8,128)(2,1)S(1)} %copy-done.4, bf16[4,52,16,128]{3,2,1,0:T(8,128)(2,1)} %collective-permute-done.14.refs_3_, ...), custom_call_target="tpu_custom_call" | custom-call | flops 999999995904 | tf_op jit(solution)/shard_map/weight_grads/pallas_call | solution.py:271
  207.5 14.1 %weight_grads.3 = (bf16[6656,2048]{1,0:T(8,128)(2,1)}, f32[24,2048]{1,0:T(8,128)S(1)}) custom-call(bf16[8,52,16,128]{3,2,1,0:T(8,128)(2,1)} %all-to-all-done.1.refs_6_.refs_0_, bf16[8,52,16,128]{3,2,1,0:T(8,128)(2,1)S(1)} %copy-done.6, bf16[8,52,16,128]{3,2,1,0:T(8,128)(2,1)S(1)} %copy-done.4, ...), custom_call_target="tpu_custom_call", output_to_operand_aliasing={{0}: (9, {})} | custom-call | flops 999999995904 | tf_op jit(solution)/shard_map/weight_grads/pallas_call | solution.py:271
  222.4 6.0 %local_backward.1 = bf16[128,6656]{1,0:T(8,128)(2,1)} custom-call(bf16[8,52,16,128]{3,2,1,0:T(8,128)(2,1)} %all-to-all-done.3.refs_0_, f32[52,52]{1,0:T(8,128)} %refs_1_.5, f32[24,2048]{1,0:T(8,128)} %copy-done.2), custom_call_target="tpu_custom_call" | custom-call | tf_op jit(solution)/shard_map/local_backward/pallas_call | solution.py:165
  (42 shorter events, 15.7 us)
Async XLA Ops:
  6.6 62.5 %all-to-all-start = ((bf16[8,52,16,128]{3,2,1,0:T(8,128)(2,1)}), bf16[8,52,16,128]{3,2,1,0:T(8,128)(2,1)S(1)}, u32[]{:S(2)}, u32[]{:S(2)}) async-start(bf16[8,52,16,128]{3,2,1,0:T(8,128)(2,1)} %local_forward.1.refs_3_), calls=%async_computation | async-start | bytes 3407872 | tf_op jit(solution)/shard_map/all_to_all | solution.py:331
  14.1 9.2 %collective-permute-start = (bf16[64,2048]{1,0:T(8,128)(2,1)S(1)}, bf16[64,2048]{1,0:T(8,128)(2,1)S(1)}, u32[]{:S(2)}, u32[]{:S(2)}) collective-permute-start(bf16[64,2048]{1,0:T(8,128)(2,1)S(1)} %get-tuple-element.39), channel_id=1, source_target_pairs={{0,8},{8,0},{16,24},{24,16},{1,9},{9,1},{17,25},{25,17},{2,10},{10... | collective-permute-start | bytes 786440 | tf_op jit(solution)/shard_map/ppermute | solution.py:336
  15.7 13.9 %collective-permute-start.2 = (bf16[64,2048]{1,0:T(8,128)(2,1)S(1)}, bf16[64,2048]{1,0:T(8,128)(2,1)S(1)}, u32[]{:S(2)}, u32[]{:S(2)}) collective-permute-start(bf16[64,2048]{1,0:T(8,128)(2,1)S(1)} %get-tuple-element.40), channel_id=1, source_target_pairs={{0,24},{8,16},{16,8},{24,0},{1,25},{9,17},{17,9},{25,1},{2,26},{10... | collective-permute-start | bytes 786440 | tf_op jit(solution)/shard_map/ppermute | solution.py:336
  17.2 13.8 %collective-permute-start.1 = (bf16[64,2048]{1,0:T(8,128)(2,1)S(1)}, bf16[64,2048]{1,0:T(8,128)(2,1)S(1)}, u32[]{:S(2)}, u32[]{:S(2)}) collective-permute-start(bf16[64,2048]{1,0:T(8,128)(2,1)S(1)} %get-tuple-element.41), channel_id=1, source_target_pairs={{0,16},{8,24},{16,0},{24,8},{1,17},{9,25},{17,1},{25,9},{2,18},{10... | collective-permute-start | bytes 786440 | tf_op jit(solution)/shard_map/ppermute | solution.py:336
  31.0 2.5 %collective-permute-start.3 = (bf16[3,64,2048]{2,1,0:T(8,128)(2,1)S(1)}, bf16[3,64,2048]{2,1,0:T(8,128)(2,1)}, u32[]{:S(2)}, u32[]{:S(2)}) collective-permute-start(bf16[3,64,2048]{2,1,0:T(8,128)(2,1)S(1)} %pad_maximum_fusion.2), channel_id=1, source_target_pairs={{0,1},{1,0},{2,3},{3,2},{4,5},{5,4},{6,7},{7,6},{8,9},{9,8},{10,11... | collective-permute-start | bytes 2359304 | tf_op jit(solution)/shard_map/ppermute | solution.py:336
  35.1 15.8 %copy-start = (bf16[512,2048]{1,0:T(8,128)(2,1)}, bf16[512,2048]{1,0:T(8,128)(2,1)S(1)}, u32[]{:S(2)}) copy-start(bf16[512,2048]{1,0:T(8,128)(2,1)S(1)} %pad_maximum_fusion.refs_0_.refs_5_) | copy-start | bytes 6291460
  48.9 15.6 %collective-permute-start.4 = (bf16[4,28,16,128]{3,2,1,0:T(8,128)(2,1)}, bf16[4,28,16,128]{3,2,1,0:T(8,128)(2,1)S(1)}, u32[]{:S(2)}, u32[]{:S(2)}) collective-permute-start(bf16[4,28,16,128]{3,2,1,0:T(8,128)(2,1)} %get-tuple-element.24), channel_id=1, source_target_pairs={{0,8},{8,0},{16,24},{24,16},{1,9},{9,1},{17,25},{25,17},{2,10},{10... | collective-permute-start | bytes 1376264 | tf_op jit(solution)/shard_map/ppermute | solution.py:336
  50.4 14.1 %collective-permute-start.5 = (bf16[4,28,16,128]{3,2,1,0:T(8,128)(2,1)}, bf16[4,28,16,128]{3,2,1,0:T(8,128)(2,1)S(1)}, u32[]{:S(2)}, u32[]{:S(2)}) collective-permute-start(bf16[4,28,16,128]{3,2,1,0:T(8,128)(2,1)} %get-tuple-element.25), channel_id=1, source_target_pairs={{0,16},{8,24},{16,0},{24,8},{1,17},{9,25},{17,1},{25,9},{2,18},{10... | collective-permute-start | bytes 1376264 | tf_op jit(solution)/shard_map/ppermute | solution.py:336
  62.5 13.7 %collective-permute-start.8 = (bf16[4,24,16,128]{3,2,1,0:T(8,128)(2,1)}, bf16[4,24,16,128]{3,2,1,0:T(8,128)(2,1)}, u32[]{:S(2)}, u32[]{:S(2)}) collective-permute-start(bf16[4,24,16,128]{3,2,1,0:T(8,128)(2,1)} %get-tuple-element.31), channel_id=1, source_target_pairs={{0,8},{8,0},{16,24},{24,16},{1,9},{9,1},{17,25},{25,17},{2,10},{10... | collective-permute-start | bytes 1179656 | tf_op jit(solution)/shard_map/ppermute | solution.py:336
  63.0 13.2 %collective-permute-start.9 = (bf16[4,24,16,128]{3,2,1,0:T(8,128)(2,1)}, bf16[4,24,16,128]{3,2,1,0:T(8,128)(2,1)}, u32[]{:S(2)}, u32[]{:S(2)}) collective-permute-start(bf16[4,24,16,128]{3,2,1,0:T(8,128)(2,1)} %get-tuple-element.32), channel_id=1, source_target_pairs={{0,16},{8,24},{16,0},{24,8},{1,17},{9,25},{17,1},{25,9},{2,18},{10... | collective-permute-start | bytes 1179656 | tf_op jit(solution)/shard_map/ppermute | solution.py:336
  67.2 27.9 %collective-permute-start.7 = (bf16[8,28,16,128]{3,2,1,0:T(8,128)(2,1)}, bf16[8,28,16,128]{3,2,1,0:T(8,128)(2,1)}, u32[]{:S(2)}, u32[]{:S(2)}) collective-permute-start(bf16[8,28,16,128]{3,2,1,0:T(8,128)(2,1)} %get-tuple-element.28), channel_id=1, source_target_pairs={{0,16},{8,24},{16,0},{24,8},{1,17},{9,25},{17,1},{25,9},{2,18},{10... | collective-permute-start | bytes 2752520 | tf_op jit(solution)/shard_map/ppermute | solution.py:336
  67.7 27.4 %collective-permute-start.6 = (bf16[8,28,16,128]{3,2,1,0:T(8,128)(2,1)}, bf16[8,28,16,128]{3,2,1,0:T(8,128)(2,1)}, u32[]{:S(2)}, u32[]{:S(2)}) collective-permute-start(bf16[8,28,16,128]{3,2,1,0:T(8,128)(2,1)} %get-tuple-element.27.refs_1_), channel_id=1, source_target_pairs={{0,8},{8,0},{16,24},{24,16},{1,9},{9,1},{17,25},{25,17},{2,10},{10... | collective-permute-start | bytes 2752520 | tf_op jit(solution)/shard_map/ppermute | solution.py:336
  71.4 45.5 %all-to-all-start.1 = ((bf16[8,52,16,128]{3,2,1,0:T(8,128)(2,1)}), bf16[8,52,16,128]{3,2,1,0:T(8,128)(2,1)}, u32[]{:S(2)}, u32[]{:S(2)}) async-start(bf16[8,52,16,128]{3,2,1,0:T(8,128)(2,1)} %transform.2.refs_4_), calls=%async_computation.1 | async-start | bytes 3407872 | tf_op jit(solution)/shard_map/all_to_all | solution.py:331
  78.8 31.0 %collective-permute-start.10 = (bf16[8,24,16,128]{3,2,1,0:T(8,128)(2,1)}, bf16[8,24,16,128]{3,2,1,0:T(8,128)(2,1)S(1)}, u32[]{:S(2)}, u32[]{:S(2)}) collective-permute-start(bf16[8,24,16,128]{3,2,1,0:T(8,128)(2,1)} %get-tuple-element.33), channel_id=1, source_target_pairs={{0,8},{8,0},{16,24},{24,16},{1,9},{9,1},{17,25},{25,17},{2,10},{10... | collective-permute-start | bytes 2359304 | tf_op jit(solution)/shard_map/ppermute | solution.py:336
  79.5 30.6 %collective-permute-start.11 = (bf16[8,24,16,128]{3,2,1,0:T(8,128)(2,1)}, bf16[8,24,16,128]{3,2,1,0:T(8,128)(2,1)S(1)}, u32[]{:S(2)}, u32[]{:S(2)}) collective-permute-start(bf16[8,24,16,128]{3,2,1,0:T(8,128)(2,1)} %get-tuple-element.34), channel_id=1, source_target_pairs={{0,16},{8,24},{16,0},{24,8},{1,17},{9,25},{17,1},{25,9},{2,18},{10... | collective-permute-start | bytes 2359304 | tf_op jit(solution)/shard_map/ppermute | solution.py:336
  121.2 48.1 %all-to-all-start.2 = ((bf16[8,52,16,128]{3,2,1,0:T(8,128)(2,1)}), bf16[8,52,16,128]{3,2,1,0:T(8,128)(2,1)S(1)}, u32[]{:S(2)}, u32[]{:S(2)}) async-start(bf16[8,52,16,128]{3,2,1,0:T(8,128)(2,1)} %total.1), calls=%async_computation.2 | async-start | bytes 3407872 | tf_op jit(solution)/shard_map/all_to_all | solution.py:331
  124.8 39.7 %collective-permute-start.13 = (bf16[8,52,16,128]{3,2,1,0:T(8,128)(2,1)}, bf16[8,52,16,128]{3,2,1,0:T(8,128)(2,1)S(1)}, u32[]{:S(2)}, u32[]{:S(2)}) collective-permute-start(bf16[8,52,16,128]{3,2,1,0:T(8,128)(2,1)} %all-to-all-done.1.refs_6_.refs_0_), channel_id=1, source_target_pairs={{0,16},{8,24},{16,0},{24,8},{1,17},{9,25},{17,1},{25,9},{2,18},{10... | collective-permute-start | bytes 5111816 | tf_op jit(solution)/shard_map/ppermute | solution.py:336
  126.4 39.9 %collective-permute-start.12 = (bf16[8,52,16,128]{3,2,1,0:T(8,128)(2,1)}, bf16[8,52,16,128]{3,2,1,0:T(8,128)(2,1)S(1)}, u32[]{:S(2)}, u32[]{:S(2)}) collective-permute-start(bf16[8,52,16,128]{3,2,1,0:T(8,128)(2,1)} %all-to-all-done.1.refs_6_.refs_0_), channel_id=1, source_target_pairs={{0,8},{8,0},{16,24},{24,16},{1,9},{9,1},{17,25},{25,17},{2,10},{10... | collective-permute-start | bytes 5111816 | tf_op jit(solution)/shard_map/ppermute | solution.py:336
  164.5 3.0 %copy-start.3 = (bf16[8,52,16,128]{3,2,1,0:T(8,128)(2,1)}, bf16[8,52,16,128]{3,2,1,0:T(8,128)(2,1)S(1)}, u32[]{:S(2)}) copy-start(bf16[8,52,16,128]{3,2,1,0:T(8,128)(2,1)S(1)} %collective-permute-done.13.refs_2_) | copy-start | bytes 5111812
  165.8 20.7 %collective-permute-start.14 = (bf16[4,52,16,128]{3,2,1,0:T(8,128)(2,1)}, bf16[4,52,16,128]{3,2,1,0:T(8,128)(2,1)}, u32[]{:S(2)}, u32[]{:S(2)}) collective-permute-start(bf16[4,52,16,128]{3,2,1,0:T(8,128)(2,1)} %slice.8), channel_id=1, source_target_pairs={{0,8},{8,0},{16,24},{24,16},{1,9},{9,1},{17,25},{25,17},{2,10},{10... | collective-permute-start | bytes 2555912 | tf_op jit(solution)/shard_map/ppermute | solution.py:336
  166.3 1.5 copy-start.5
  167.8 20.4 %collective-permute-start.15 = (bf16[4,52,16,128]{3,2,1,0:T(8,128)(2,1)}, bf16[4,52,16,128]{3,2,1,0:T(8,128)(2,1)}, u32[]{:S(2)}, u32[]{:S(2)}) collective-permute-start(bf16[4,52,16,128]{3,2,1,0:T(8,128)(2,1)} %slice.9), channel_id=1, source_target_pairs={{0,16},{8,24},{16,0},{24,8},{1,17},{9,25},{17,1},{25,9},{2,18},{10... | collective-permute-start | bytes 2555912 | tf_op jit(solution)/shard_map/ppermute | solution.py:336
  171.6 16.6 %copy-start.1 = (bf16[512,2048]{1,0:T(8,128)(2,1)S(1)}, bf16[512,2048]{1,0:T(8,128)(2,1)}, u32[]{:S(2)}) copy-start(bf16[512,2048]{1,0:T(8,128)(2,1)} %copy-done) | copy-start | bytes 6291460
  171.6 50.8 %all-to-all-start.3 = ((bf16[8,52,16,128]{3,2,1,0:T(8,128)(2,1)}), bf16[8,52,16,128]{3,2,1,0:T(8,128)(2,1)}, u32[]{:S(2)}, u32[]{:S(2)}) async-start(bf16[8,52,16,128]{3,2,1,0:T(8,128)(2,1)} %transform.3.refs_9_), calls=%async_computation.3 | async-start | bytes 3407872 | tf_op jit(solution)/shard_map/all_to_all | solution.py:331
  188.2 1.5 copy-start.4
  189.7 1.5 copy-start.6
  221.6 0.8 copy-start.2

commit v5 on v4

--- a/solution.py
+++ b/solution.py
@@ -121,6 +121,7 @@
 
 FREE = pl.CostEstimate(flops=0, bytes_accessed=0, transcendentals=0)
 LONG = pl.CostEstimate(flops=10**12, bytes_accessed=0, transcendentals=0)
+SOME = pl.CostEstimate(flops=5_000_000_000, bytes_accessed=0, transcendentals=0)
 SMALL = 12 << 20
 
 ANYWHERE = pl.BlockSpec(memory_space=pl.ANY)
@@ -177,29 +178,24 @@
     )(*mixed, rot_block, *in_hbm(*after))
 
 
-def units_kernel(first, per, up_ref, w_ref, s_ref, *outs):
+def units_kernel(first, per, up_ref, w_ref, s_ref, *refs):
+    outs, quant_ref = refs[:-1], refs[-1]
     base = first + pl.program_id(0) * per
-    pair = 2 if per % 2 == 0 else 1
-    for start in range(0, per, pair):
-        quant = jnp.concatenate(
-            [
-                (
-                    w_ref[g * GROUP : (g + 1) * GROUP, :].astype(F32) * s_ref[pl.ds(base + g, 1), :]
-                ).astype(BF16)
-                for g in range(start, start + pair)
-            ],
-            axis=0,
+    for g in range(per):
+        rows = slice(g * GROUP, (g + 1) * GROUP)
+        quant_ref[rows, :] = (w_ref[rows, :].astype(F32) * s_ref[pl.ds(base + g, 1), :]).astype(
+            BF16
         )
-        result = nt_dot(up_ref[...], quant).astype(BF16)
-        token = 0
-        for out_ref in outs:
-            for q in range(out_ref.shape[0]):
-                for g in range(pair):
-                    out_ref[q, start + g] = result[token : token + SUB, g * GROUP : (g + 1) * GROUP]
-                token += SUB
-
-
-def unit_grads(up, weight, scales, first, size, per, counts, after=()):
+    result = nt_dot(up_ref[...], quant_ref[...]).astype(BF16)
+    token = 0
+    for out_ref in outs:
+        for q in range(out_ref.shape[0]):
+            for g in range(per):
+                out_ref[q, g] = result[token : token + SUB, g * GROUP : (g + 1) * GROUP]
+            token += SUB
+
+
+def unit_grads(up, weight, scales, first, size, per, counts, after=(), cost=FREE):
     tokens, cols = up.shape
     offset = first // per
     return pl.pallas_call(
@@ -213,8 +209,9 @@
         + [ANYWHERE] * len(after),
         out_specs=[pl.BlockSpec((count, per, SUB, HB), lambda i: (0, i, 0, 0)) for count in counts],
         out_shape=[pltpu.HBM((count, size, SUB, HB), BF16) for count in counts],
+        scratch_shapes=[pltpu.VMEM((per * GROUP, cols), BF16)],
         compiler_params=pltpu.CompilerParams(vmem_limit_bytes=26 << 20),
-        cost_estimate=FREE,
+        cost_estimate=cost,
         name="unit_grads",
     )(up, *in_hbm(weight, scales), *in_hbm(*after))
 
@@ -304,6 +301,18 @@
         cost_estimate=cost,
         name=name,
     )(*ins, *in_hbm(*after))
+
+
+def gate(value, after):
+    return pl.pallas_call(
+        drop_inputs(lambda x_ref, out_ref: None, 1, len(after)),
+        in_specs=[ANYWHERE] * (1 + len(after)),
+        out_specs=ANYWHERE,
+        out_shape=pltpu.HBM(value.shape, value.dtype),
+        input_output_aliases={0: 0},
+        cost_estimate=FREE,
+        name="gate",
+    )(*in_hbm(value, *after))
 
 
 def transform_kernel(x_ref, out_ref):
@@ -469,7 +478,9 @@
     up = gather_upstream(upstream)
     (local,) = local_forward(hidden, rot_block, (groups,))
     forth = exchange(local)
-    unit0 = unit_grads(up, weight, scales, starts[0], sizes[0], per, counts, after=(local,))
+    unit0 = unit_grads(
+        up, weight, scales, starts[0], sizes[0], per, counts, after=(local,), cost=SOME
+    )
     first0 = scatter_first(unit0)
     unit1 = unit_grads(up, weight, scales, starts[1], sizes[1], per, counts, after=(unit0[0],))
     first1 = scatter_first(unit1)
@@ -477,7 +488,7 @@
     turned = transform(forth, after=(relayed0,), cost=LONG)
     rotated = exchange(turned)
     relayed1, *second1 = scatter_second(unit1, first1, after=(turned,), cost=LONG)
-    summed = total(((unit0[0], *second0), (unit1[0], *second1)), after=(rotated,))
+    summed = gate(total(((unit0[0], *second0), (unit1[0], *second1))), after=(rotated,))
     back = exchange(summed)
     gathered = gather(rotated)
     mixed = transform(back, cost=LONG)

time: 230 us -> 215 us (0.935)
  waiting for transfers between devices: 99.8 us -> 82.9 us
    ppermute x16, waiting for transfers between devices: 93 us -> 79.1 us  [partner(): return lax.ppermute(value, axis, [(i, i ^ mask) for i in range(size)])]
    ppermute x16, starting transfers between devices: 16 us -> 19.8 us  [partner(): return lax.ppermute(value, axis, [(i, i ^ mask) for i in range(size)])]
    all_to_all x4, waiting for transfers between devices: 6.86 us -> 3.72 us  [exchange(): lax.all_to_all(value, 'tensor', split_axis=0, concat_axis=0, tiled=True)]
  transfers between devices with their start and end apart: 20 -> 20, of which waited for: 11 -> 11; matrix products, arithmetic and copies ran while one was open for 3% -> 3% of each run, Pallas kernels for 29% -> 35%
where the time goes in v5:
time: 215 us; the launch traced here: 214 us
  waiting for transfers between devices  82.9 us (39%)
  Pallas kernels  81.8 us (38%)
  starting transfers between devices  37.9 us (18%)
  local copies, waits for them, and re-layouts  7.89 us (4%)
  other arithmetic  2.48 us (1%)
    ppermute x16, waiting for transfers between devices, partner(): return lax.ppermute(value, axis, [(i, i ^ mask) for i in range(size)])  79.1 us
    pallas_call x2, Pallas kernels, weight_grads(): pl.pallas_call(functools.partial(weights_kernel, first, per, len(rotated)...  30.4 us
    pallas_call x2, Pallas kernels, unit_grads(): pl.pallas_call(drop_inputs(functools.partial(units_kernel, first, per), 3...  25.3 us
    ppermute x16, starting transfers between devices, partner(): return lax.ppermute(value, axis, [(i, i ^ mask) for i in range(size)])  19.8 us
    all_to_all x4, starting transfers between devices, exchange(): lax.all_to_all(value, 'tensor', split_axis=0, concat_axis=0, tiled=True)  18.1 us
    pallas_call x4, Pallas kernels, small_call(): pl.pallas_call(drop_inputs(kernel, len(ins), len(after)), grid=(steps,),...  9.77 us
    pallas_call x1, Pallas kernels, local_backward(): pl.pallas_call(drop_inputs(functools.partial(backward_kernel, sizes), len...  5.99 us
    pallas_call x1, Pallas kernels, local_forward(): pl.pallas_call(functools.partial(forward_kernel, sizes), grid=(rows // (S...  5.97 us
  transfers between devices with their start and end apart: 20, of which 11 were waited for; matrix products, arithmetic and copies ran while one was open for 3% of the time, Pallas kernels for 35%

profile of v5, /device:TPU:0, one launch (start us, length us, event | category | flops | bytes accessed | tf_op | source)
XLA Modules:
  0.0 213.7 jit_solution(14757531376591637450)
XLA Ops:
  1.8 3.0 %collective-permute-start = (bf16[64,2048]{1,0:T(8,128)(2,1)S(1)}, bf16[64,2048]{1,0:T(8,128)(2,1)S(1)}, u32[]{:S(2)}, u32[]{:S(2)}) collective-permute-start(bf16[64,2048]{1,0:T(8,128)(2,1)S(1)} %get-tuple-element.39), channel_id=1, source_target_pairs={{0,8},{8,0},{16,24},{24,16},{1,9},{9,1},{17,25},{25,17},{2,10},{10... | collective-permute-start | bytes 786440 | tf_op jit(solution)/shard_map/ppermute | solution.py:345
  4.8 1.5 collective-permute-start.2
  6.4 6.0 %local_forward.1.refs_3_ = bf16[8,52,16,128]{3,2,1,0:T(8,128)(2,1)} custom-call(bf16[128,6656]{1,0:T(8,128)(2,1)} %x_ref.1, f32[52,52]{1,0:T(8,128)} %refs_1_.5), custom_call_target="tpu_custom_call" | custom-call | tf_op jit(solution)/shard_map/local_forward/pallas_call | solution.py:145
  12.3 5.3 %all-to-all-start = ((bf16[8,52,16,128]{3,2,1,0:T(8,128)(2,1)}), bf16[8,52,16,128]{3,2,1,0:T(8,128)(2,1)S(1)}, u32[]{:S(2)}, u32[]{:S(2)}) async-start(bf16[8,52,16,128]{3,2,1,0:T(8,128)(2,1)} %local_forward.1.refs_3_), calls=%async_computation | async-start | bytes 3407872 | tf_op jit(solution)/shard_map/all_to_all | solution.py:340
  23.6 13.8 %unit_grads.2 = (bf16[8,28,16,128]{3,2,1,0:T(8,128)(2,1)}, bf16[8,28,16,128]{3,2,1,0:T(8,128)(2,1)}, bf16[8,28,16,128]{3,2,1,0:T(8,128)(2,1)}, bf16[4,28,16,128]{3,2,1,0:T(8,128)(2,1)}, bf16[4,28,16,128]{3,2,1,0:T(8,128)(2,1)}) custom-call(bf16[512,2048]{1,0:T(8,128)(2,1)S(1)} %pad_maximum_fusion.refs_0_.refs_5_, bf16[6656,2048]{1,0:T(8,128)(2,1)} %refs_6_.3, ...), custom_call_target="tpu_custom_call" | custom-call | flops 5000000000 | tf_op jit(solution)/shard_map/unit_grads/pallas_call | solution.py:201
  37.4 1.5 collective-permute-start.4
  39.4 11.5 %unit_grads.3 = (bf16[8,24,16,128]{3,2,1,0:T(8,128)(2,1)}, bf16[8,24,16,128]{3,2,1,0:T(8,128)(2,1)}, bf16[8,24,16,128]{3,2,1,0:T(8,128)(2,1)}, bf16[4,24,16,128]{3,2,1,0:T(8,128)(2,1)}, bf16[4,24,16,128]{3,2,1,0:T(8,128)(2,1)}) custom-call(bf16[512,2048]{1,0:T(8,128)(2,1)S(1)} %pad_maximum_fusion.refs_0_.refs_5_, bf16[6656,2048]{1,0:T(8,128)(2,1)} %refs_6_.3, ...), custom_call_target="tpu_custom_call" | custom-call | tf_op jit(solution)/shard_map/unit_grads/pallas_call | solution.py:201
  51.2 1.7 collective-permute-start.9
  52.9 2.6 %relay.2 = (bf16[8,28,16,128]{3,2,1,0:T(8,128)(2,1)}, bf16[8,28,16,128]{3,2,1,0:T(8,128)(2,1)}) custom-call(bf16[8,28,16,128]{3,2,1,0:T(8,128)(2,1)} %get-tuple-element.22.refs_0_, bf16[8,28,16,128]{3,2,1,0:T(8,128)(2,1)} %get-tuple-element.23.refs_1_, bf16[4,28,16,128]{3,2,1,0:T(8,128)(2,1)S(1)} %collective-permute-done.4.refs_2_, ...), custom_call_target="tpu_custom_call" | custom-call | tf_op jit(solution)/shard_map/relay/pallas_call | solution.py:294
  55.9 1.7 collective-permute-start.6
  58.3 2.3 %transform.2.refs_4_ = bf16[8,52,16,128]{3,2,1,0:T(8,128)(2,1)} custom-call(bf16[8,52,16,128]{3,2,1,0:T(8,128)(2,1)S(1)} %all-to-all-done.refs_0_, bf16[8,28,16,128]{3,2,1,0:T(8,128)(2,1)} %get-tuple-element.27.refs_1_), custom_call_target="tpu_custom_call" | custom-call | flops 999999995904 | tf_op jit(solution)/shard_map/transform/pallas_call | solution.py:294
  60.6 4.3 %all-to-all-start.1 = ((bf16[8,52,16,128]{3,2,1,0:T(8,128)(2,1)}), bf16[8,52,16,128]{3,2,1,0:T(8,128)(2,1)}, u32[]{:S(2)}, u32[]{:S(2)}) async-start(bf16[8,52,16,128]{3,2,1,0:T(8,128)(2,1)} %transform.2.refs_4_), calls=%async_computation.1 | async-start | bytes 3407872 | tf_op jit(solution)/shard_map/all_to_all | solution.py:340
  64.9 2.6 %relay.3 = (bf16[8,24,16,128]{3,2,1,0:T(8,128)(2,1)}, bf16[8,24,16,128]{3,2,1,0:T(8,128)(2,1)}) custom-call(bf16[8,24,16,128]{3,2,1,0:T(8,128)(2,1)} %get-tuple-element.29.refs_0_, bf16[8,24,16,128]{3,2,1,0:T(8,128)(2,1)} %get-tuple-element.30.refs_1_, bf16[4,24,16,128]{3,2,1,0:T(8,128)(2,1)} %collective-permute-done.8.refs_2_, ...), custom_call_target="tpu_custom_call" | custom-call | flops 999999995904 | tf_op jit(solution)/shard_map/relay/pallas_call | solution.py:294
  67.5 1.5 collective-permute-start.10
  69.0 1.5 collective-permute-start.11
  70.6 12.7 %collective-permute-done.7.refs_2_ = bf16[8,28,16,128]{3,2,1,0:T(8,128)(2,1)} collective-permute-done((bf16[8,28,16,128]{3,2,1,0:T(8,128)(2,1)}, bf16[8,28,16,128]{3,2,1,0:T(8,128)(2,1)}, u32[]{:S(2)}, u32[]{:S(2)}) %collective-permute-start.7) | collective-permute-done | bytes 917536 | tf_op jit(solution)/shard_map/ppermute | solution.py:345
  83.3 14.9 %collective-permute-done.10.refs_4_ = bf16[8,24,16,128]{3,2,1,0:T(8,128)(2,1)S(1)} collective-permute-done((bf16[8,24,16,128]{3,2,1,0:T(8,128)(2,1)}, bf16[8,24,16,128]{3,2,1,0:T(8,128)(2,1)S(1)}, u32[]{:S(2)}, u32[]{:S(2)}) %collective-permute-start.10) | collective-permute-done | bytes 786464 | tf_op jit(solution)/shard_map/ppermute | solution.py:345
  98.3 4.3 %total.1.refs_0_ = bf16[8,52,16,128]{3,2,1,0:T(8,128)(2,1)} custom-call(bf16[8,28,16,128]{3,2,1,0:T(8,128)(2,1)} %get-tuple-element.21.refs_3_.refs_0_, bf16[8,28,16,128]{3,2,1,0:T(8,128)(2,1)} %collective-permute-done.6.refs_1_, bf16[8,28,16,128]{3,2,1,0:T(8,128)(2,1)} %collective-permute-done.7.refs_2_, ...), custom_call_target="tpu_custom_call" | custom-call | tf_op jit(solution)/shard_map/total/pallas_call | solution.py:409
  102.6 2.9 %all-to-all-done.1.refs_1_.refs_0_ = bf16[8,52,16,128]{3,2,1,0:T(8,128)(2,1)} async-done(((bf16[8,52,16,128]{3,2,1,0:T(8,128)(2,1)}), bf16[8,52,16,128]{3,2,1,0:T(8,128)(2,1)}, u32[]{:S(2)}, u32[]{:S(2)}) %all-to-all-start.1) | async-done | bytes 1703968 | tf_op jit(solution)/shard_map/all_to_all | solution.py:340
  105.5 3.6 %all-to-all-start.2 = ((bf16[8,52,16,128]{3,2,1,0:T(8,128)(2,1)}), bf16[8,52,16,128]{3,2,1,0:T(8,128)(2,1)S(1)}, u32[]{:S(2)}, u32[]{:S(2)}) async-start(bf16[8,52,16,128]{3,2,1,0:T(8,128)(2,1)} %gate.1), calls=%async_computation.2 | async-start | bytes 3407872 | tf_op jit(solution)/shard_map/all_to_all | solution.py:340
  109.1 1.6 collective-permute-start.13
  110.7 1.5 collective-permute-start.12
  112.2 36.6 %collective-permute-done.13.refs_2_ = bf16[8,52,16,128]{3,2,1,0:T(8,128)(2,1)S(1)} collective-permute-done((bf16[8,52,16,128]{3,2,1,0:T(8,128)(2,1)}, bf16[8,52,16,128]{3,2,1,0:T(8,128)(2,1)S(1)}, u32[]{:S(2)}, u32[]{:S(2)}) %collective-permute-start.13) | collective-permute-done | bytes 1703968 | tf_op jit(solution)/shard_map/ppermute | solution.py:345
  150.1 1.5 collective-permute-start.14
  153.1 1.5 collective-permute-start.15
  154.6 2.3 %transform.3.refs_9_ = bf16[8,52,16,128]{3,2,1,0:T(8,128)(2,1)} custom-call(bf16[8,52,16,128]{3,2,1,0:T(8,128)(2,1)S(1)} %all-to-all-done.2.refs_0_), custom_call_target="tpu_custom_call" | custom-call | flops 999999995904 | tf_op jit(solution)/shard_map/transform/pallas_call | solution.py:294
  156.9 4.9 %all-to-all-start.3 = ((bf16[8,52,16,128]{3,2,1,0:T(8,128)(2,1)}), bf16[8,52,16,128]{3,2,1,0:T(8,128)(2,1)}, u32[]{:S(2)}, u32[]{:S(2)}) async-start(bf16[8,52,16,128]{3,2,1,0:T(8,128)(2,1)} %transform.3.refs_9_), calls=%async_computation.3 | async-start | bytes 3407872 | tf_op jit(solution)/shard_map/all_to_all | solution.py:340
  161.8 9.0 %collective-permute-done.14.refs_3_ = bf16[4,52,16,128]{3,2,1,0:T(8,128)(2,1)} collective-permute-done((bf16[4,52,16,128]{3,2,1,0:T(8,128)(2,1)}, bf16[4,52,16,128]{3,2,1,0:T(8,128)(2,1)}, u32[]{:S(2)}, u32[]{:S(2)}) %collective-permute-start.14) | collective-permute-done | bytes 852000 | tf_op jit(solution)/shard_map/ppermute | solution.py:345
  170.8 2.7 %collective-permute-done.15.refs_4_ = bf16[4,52,16,128]{3,2,1,0:T(8,128)(2,1)} collective-permute-done((bf16[4,52,16,128]{3,2,1,0:T(8,128)(2,1)}, bf16[4,52,16,128]{3,2,1,0:T(8,128)(2,1)}, u32[]{:S(2)}, u32[]{:S(2)}) %collective-permute-start.15) | collective-permute-done | bytes 852000 | tf_op jit(solution)/shard_map/ppermute | solution.py:345
  176.4 16.3 %weight_grads.2 = (bf16[6656,2048]{1,0:T(8,128)(2,1)}, f32[28,2048]{1,0:T(8,128)S(1)}) custom-call(bf16[8,52,16,128]{3,2,1,0:T(8,128)(2,1)} %all-to-all-done.1.refs_1_.refs_0_, bf16[8,52,16,128]{3,2,1,0:T(8,128)(2,1)S(1)} %copy-done.6, bf16[8,52,16,128]{3,2,1,0:T(8,128)(2,1)S(1)} %copy-done.4, bf16[4,52,16,128]{3,2,1,0:T(8,128)(2,1)} %collective-permute-done.14.refs_3_, ...), custom_call_target="tpu_custom_call" | custom-call | flops 999999995904 | tf_op jit(solution)/shard_map/weight_grads/pallas_call | solution.py:268
  192.7 14.1 %weight_grads.3 = (bf16[6656,2048]{1,0:T(8,128)(2,1)}, f32[24,2048]{1,0:T(8,128)S(1)}) custom-call(bf16[8,52,16,128]{3,2,1,0:T(8,128)(2,1)} %all-to-all-done.1.refs_1_.refs_0_, bf16[8,52,16,128]{3,2,1,0:T(8,128)(2,1)S(1)} %copy-done.6, bf16[8,52,16,128]{3,2,1,0:T(8,128)(2,1)S(1)} %copy-done.4, ...), custom_call_target="tpu_custom_call", output_to_operand_aliasing={{0}: (9, {})} | custom-call | flops 999999995904 | tf_op jit(solution)/shard_map/weight_grads/pallas_call | solution.py:268
  207.7 6.0 %local_backward.1 = bf16[128,6656]{1,0:T(8,128)(2,1)} custom-call(bf16[8,52,16,128]{3,2,1,0:T(8,128)(2,1)} %all-to-all-done.3.refs_0_, f32[52,52]{1,0:T(8,128)} %refs_1_.5, f32[24,2048]{1,0:T(8,128)} %copy-done.2), custom_call_target="tpu_custom_call" | custom-call | tf_op jit(solution)/shard_map/local_backward/pallas_call | solution.py:166
  (43 shorter events, 15.6 us)
Async XLA Ops:
  1.8 15.9 %collective-permute-start = (bf16[64,2048]{1,0:T(8,128)(2,1)S(1)}, bf16[64,2048]{1,0:T(8,128)(2,1)S(1)}, u32[]{:S(2)}, u32[]{:S(2)}) collective-permute-start(bf16[64,2048]{1,0:T(8,128)(2,1)S(1)} %get-tuple-element.39), channel_id=1, source_target_pairs={{0,8},{8,0},{16,24},{24,16},{1,9},{9,1},{17,25},{25,17},{2,10},{10... | collective-permute-start | bytes 786440 | tf_op jit(solution)/shard_map/ppermute | solution.py:345
  4.8 13.2 %collective-permute-start.2 = (bf16[64,2048]{1,0:T(8,128)(2,1)S(1)}, bf16[64,2048]{1,0:T(8,128)(2,1)S(1)}, u32[]{:S(2)}, u32[]{:S(2)}) collective-permute-start(bf16[64,2048]{1,0:T(8,128)(2,1)S(1)} %get-tuple-element.40), channel_id=1, source_target_pairs={{0,24},{8,16},{16,8},{24,0},{1,25},{9,17},{17,9},{25,1},{2,26},{10... | collective-permute-start | bytes 786440 | tf_op jit(solution)/shard_map/ppermute | solution.py:345
  6.3 13.1 %collective-permute-start.1 = (bf16[64,2048]{1,0:T(8,128)(2,1)S(1)}, bf16[64,2048]{1,0:T(8,128)(2,1)S(1)}, u32[]{:S(2)}, u32[]{:S(2)}) collective-permute-start(bf16[64,2048]{1,0:T(8,128)(2,1)S(1)} %get-tuple-element.41), channel_id=1, source_target_pairs={{0,16},{8,24},{16,0},{24,8},{1,17},{9,25},{17,1},{25,9},{2,18},{10... | collective-permute-start | bytes 786440 | tf_op jit(solution)/shard_map/ppermute | solution.py:345
  12.3 46.0 %all-to-all-start = ((bf16[8,52,16,128]{3,2,1,0:T(8,128)(2,1)}), bf16[8,52,16,128]{3,2,1,0:T(8,128)(2,1)S(1)}, u32[]{:S(2)}, u32[]{:S(2)}) async-start(bf16[8,52,16,128]{3,2,1,0:T(8,128)(2,1)} %local_forward.1.refs_3_), calls=%async_computation | async-start | bytes 3407872 | tf_op jit(solution)/shard_map/all_to_all | solution.py:340
  19.5 2.5 %collective-permute-start.3 = (bf16[3,64,2048]{2,1,0:T(8,128)(2,1)S(1)}, bf16[3,64,2048]{2,1,0:T(8,128)(2,1)}, u32[]{:S(2)}, u32[]{:S(2)}) collective-permute-start(bf16[3,64,2048]{2,1,0:T(8,128)(2,1)S(1)} %pad_maximum_fusion.2), channel_id=1, source_target_pairs={{0,1},{1,0},{2,3},{3,2},{4,5},{5,4},{6,7},{7,6},{8,9},{9,8},{10,11... | collective-permute-start | bytes 2359304 | tf_op jit(solution)/shard_map/ppermute | solution.py:345
  23.6 15.8 %copy-start = (bf16[512,2048]{1,0:T(8,128)(2,1)}, bf16[512,2048]{1,0:T(8,128)(2,1)S(1)}, u32[]{:S(2)}) copy-start(bf16[512,2048]{1,0:T(8,128)(2,1)S(1)} %pad_maximum_fusion.refs_0_.refs_5_) | copy-start | bytes 6291460
  37.4 15.5 %collective-permute-start.4 = (bf16[4,28,16,128]{3,2,1,0:T(8,128)(2,1)}, bf16[4,28,16,128]{3,2,1,0:T(8,128)(2,1)S(1)}, u32[]{:S(2)}, u32[]{:S(2)}) collective-permute-start(bf16[4,28,16,128]{3,2,1,0:T(8,128)(2,1)} %get-tuple-element.24), channel_id=1, source_target_pairs={{0,8},{8,0},{16,24},{24,16},{1,9},{9,1},{17,25},{25,17},{2,10},{10... | collective-permute-start | bytes 1376264 | tf_op jit(solution)/shard_map/ppermute | solution.py:345
  38.9 14.0 %collective-permute-start.5 = (bf16[4,28,16,128]{3,2,1,0:T(8,128)(2,1)}, bf16[4,28,16,128]{3,2,1,0:T(8,128)(2,1)S(1)}, u32[]{:S(2)}, u32[]{:S(2)}) collective-permute-start(bf16[4,28,16,128]{3,2,1,0:T(8,128)(2,1)} %get-tuple-element.25), channel_id=1, source_target_pairs={{0,16},{8,24},{16,0},{24,8},{1,17},{9,25},{17,1},{25,9},{2,18},{10... | collective-permute-start | bytes 1376264 | tf_op jit(solution)/shard_map/ppermute | solution.py:345
  50.9 14.0 %collective-permute-start.8 = (bf16[4,24,16,128]{3,2,1,0:T(8,128)(2,1)}, bf16[4,24,16,128]{3,2,1,0:T(8,128)(2,1)}, u32[]{:S(2)}, u32[]{:S(2)}) collective-permute-start(bf16[4,24,16,128]{3,2,1,0:T(8,128)(2,1)} %get-tuple-element.31), channel_id=1, source_target_pairs={{0,8},{8,0},{16,24},{24,16},{1,9},{9,1},{17,25},{25,17},{2,10},{10... | collective-permute-start | bytes 1179656 | tf_op jit(solution)/shard_map/ppermute | solution.py:345
  51.2 13.7 %collective-permute-start.9 = (bf16[4,24,16,128]{3,2,1,0:T(8,128)(2,1)}, bf16[4,24,16,128]{3,2,1,0:T(8,128)(2,1)}, u32[]{:S(2)}, u32[]{:S(2)}) collective-permute-start(bf16[4,24,16,128]{3,2,1,0:T(8,128)(2,1)} %get-tuple-element.32), channel_id=1, source_target_pairs={{0,16},{8,24},{16,0},{24,8},{1,17},{9,25},{17,1},{25,9},{2,18},{10... | collective-permute-start | bytes 1179656 | tf_op jit(solution)/shard_map/ppermute | solution.py:345
  55.6 27.7 %collective-permute-start.7 = (bf16[8,28,16,128]{3,2,1,0:T(8,128)(2,1)}, bf16[8,28,16,128]{3,2,1,0:T(8,128)(2,1)}, u32[]{:S(2)}, u32[]{:S(2)}) collective-permute-start(bf16[8,28,16,128]{3,2,1,0:T(8,128)(2,1)} %get-tuple-element.28), channel_id=1, source_target_pairs={{0,16},{8,24},{16,0},{24,8},{1,17},{9,25},{17,1},{25,9},{2,18},{10... | collective-permute-start | bytes 2752520 | tf_op jit(solution)/shard_map/ppermute | solution.py:345
  55.9 27.4 %collective-permute-start.6 = (bf16[8,28,16,128]{3,2,1,0:T(8,128)(2,1)}, bf16[8,28,16,128]{3,2,1,0:T(8,128)(2,1)}, u32[]{:S(2)}, u32[]{:S(2)}) collective-permute-start(bf16[8,28,16,128]{3,2,1,0:T(8,128)(2,1)} %get-tuple-element.27.refs_1_), channel_id=1, source_target_pairs={{0,8},{8,0},{16,24},{24,16},{1,9},{9,1},{17,25},{25,17},{2,10},{10... | collective-permute-start | bytes 2752520 | tf_op jit(solution)/shard_map/ppermute | solution.py:345
  60.6 44.9 %all-to-all-start.1 = ((bf16[8,52,16,128]{3,2,1,0:T(8,128)(2,1)}), bf16[8,52,16,128]{3,2,1,0:T(8,128)(2,1)}, u32[]{:S(2)}, u32[]{:S(2)}) async-start(bf16[8,52,16,128]{3,2,1,0:T(8,128)(2,1)} %transform.2.refs_4_), calls=%async_computation.1 | async-start | bytes 3407872 | tf_op jit(solution)/shard_map/all_to_all | solution.py:340
  67.5 30.7 %collective-permute-start.10 = (bf16[8,24,16,128]{3,2,1,0:T(8,128)(2,1)}, bf16[8,24,16,128]{3,2,1,0:T(8,128)(2,1)S(1)}, u32[]{:S(2)}, u32[]{:S(2)}) collective-permute-start(bf16[8,24,16,128]{3,2,1,0:T(8,128)(2,1)} %get-tuple-element.33), channel_id=1, source_target_pairs={{0,8},{8,0},{16,24},{24,16},{1,9},{9,1},{17,25},{25,17},{2,10},{10... | collective-permute-start | bytes 2359304 | tf_op jit(solution)/shard_map/ppermute | solution.py:345
  69.0 29.2 %collective-permute-start.11 = (bf16[8,24,16,128]{3,2,1,0:T(8,128)(2,1)}, bf16[8,24,16,128]{3,2,1,0:T(8,128)(2,1)S(1)}, u32[]{:S(2)}, u32[]{:S(2)}) collective-permute-start(bf16[8,24,16,128]{3,2,1,0:T(8,128)(2,1)} %get-tuple-element.34), channel_id=1, source_target_pairs={{0,16},{8,24},{16,0},{24,8},{1,17},{9,25},{17,1},{25,9},{2,18},{10... | collective-permute-start | bytes 2359304 | tf_op jit(solution)/shard_map/ppermute | solution.py:345
  105.5 49.1 %all-to-all-start.2 = ((bf16[8,52,16,128]{3,2,1,0:T(8,128)(2,1)}), bf16[8,52,16,128]{3,2,1,0:T(8,128)(2,1)S(1)}, u32[]{:S(2)}, u32[]{:S(2)}) async-start(bf16[8,52,16,128]{3,2,1,0:T(8,128)(2,1)} %gate.1), calls=%async_computation.2 | async-start | bytes 3407872 | tf_op jit(solution)/shard_map/all_to_all | solution.py:340
  109.1 39.7 %collective-permute-start.13 = (bf16[8,52,16,128]{3,2,1,0:T(8,128)(2,1)}, bf16[8,52,16,128]{3,2,1,0:T(8,128)(2,1)S(1)}, u32[]{:S(2)}, u32[]{:S(2)}) collective-permute-start(bf16[8,52,16,128]{3,2,1,0:T(8,128)(2,1)} %all-to-all-done.1.refs_1_.refs_0_), channel_id=1, source_target_pairs={{0,16},{8,24},{16,0},{24,8},{1,17},{9,25},{17,1},{25,9},{2,18},{10... | collective-permute-start | bytes 5111816 | tf_op jit(solution)/shard_map/ppermute | solution.py:345
  110.7 40.8 %collective-permute-start.12 = (bf16[8,52,16,128]{3,2,1,0:T(8,128)(2,1)}, bf16[8,52,16,128]{3,2,1,0:T(8,128)(2,1)S(1)}, u32[]{:S(2)}, u32[]{:S(2)}) collective-permute-start(bf16[8,52,16,128]{3,2,1,0:T(8,128)(2,1)} %all-to-all-done.1.refs_1_.refs_0_), channel_id=1, source_target_pairs={{0,8},{8,0},{16,24},{24,16},{1,9},{9,1},{17,25},{25,17},{2,10},{10... | collective-permute-start | bytes 5111816 | tf_op jit(solution)/shard_map/ppermute | solution.py:345
  148.9 3.9 %copy-start.3 = (bf16[8,52,16,128]{3,2,1,0:T(8,128)(2,1)}, bf16[8,52,16,128]{3,2,1,0:T(8,128)(2,1)S(1)}, u32[]{:S(2)}) copy-start(bf16[8,52,16,128]{3,2,1,0:T(8,128)(2,1)S(1)} %collective-permute-done.13.refs_2_) | copy-start | bytes 5111812
  150.1 20.7 %collective-permute-start.14 = (bf16[4,52,16,128]{3,2,1,0:T(8,128)(2,1)}, bf16[4,52,16,128]{3,2,1,0:T(8,128)(2,1)}, u32[]{:S(2)}, u32[]{:S(2)}) collective-permute-start(bf16[4,52,16,128]{3,2,1,0:T(8,128)(2,1)} %slice.8), channel_id=1, source_target_pairs={{0,8},{8,0},{16,24},{24,16},{1,9},{9,1},{17,25},{25,17},{2,10},{10... | collective-permute-start | bytes 2555912 | tf_op jit(solution)/shard_map/ppermute | solution.py:345
  151.6 1.5 copy-start.5
  153.1 20.4 %collective-permute-start.15 = (bf16[4,52,16,128]{3,2,1,0:T(8,128)(2,1)}, bf16[4,52,16,128]{3,2,1,0:T(8,128)(2,1)}, u32[]{:S(2)}, u32[]{:S(2)}) collective-permute-start(bf16[4,52,16,128]{3,2,1,0:T(8,128)(2,1)} %slice.9), channel_id=1, source_target_pairs={{0,16},{8,24},{16,0},{24,8},{1,17},{9,25},{17,1},{25,9},{2,18},{10... | collective-permute-start | bytes 2555912 | tf_op jit(solution)/shard_map/ppermute | solution.py:345
  156.9 16.6 %copy-start.1 = (bf16[512,2048]{1,0:T(8,128)(2,1)S(1)}, bf16[512,2048]{1,0:T(8,128)(2,1)}, u32[]{:S(2)}) copy-start(bf16[512,2048]{1,0:T(8,128)(2,1)} %copy-done) | copy-start | bytes 6291460
  156.9 50.8 %all-to-all-start.3 = ((bf16[8,52,16,128]{3,2,1,0:T(8,128)(2,1)}), bf16[8,52,16,128]{3,2,1,0:T(8,128)(2,1)}, u32[]{:S(2)}, u32[]{:S(2)}) async-start(bf16[8,52,16,128]{3,2,1,0:T(8,128)(2,1)} %transform.3.refs_9_), calls=%async_computation.3 | async-start | bytes 3407872 | tf_op jit(solution)/shard_map/all_to_all | solution.py:340
  173.5 1.5 copy-start.4
  175.0 1.5 copy-start.6
  206.9 0.8 copy-start.2

commit v6 on v5

--- a/solution.py
+++ b/solution.py
@@ -11,6 +11,7 @@
 GROUP = 128
 SUB = 16
 ROWS = 8
+SIDE = 8
 F32 = jnp.float32
 BF16 = jnp.bfloat16
 
@@ -247,11 +248,11 @@
             )
 
 
-def weight_grads(rotated, up, weight, scales, mask, buffer, first, size, per, after=()):
+def weight_grads(rotated, up, weight, scales, mask, buffer, first, size, per, after=(), cost=FREE):
     tokens, cols = up.shape
     offset = first // per
     specs = [
-        pl.BlockSpec((piece.shape[0], per, SUB, HB), lambda i: (0, offset + i, 0, 0))
+        pl.BlockSpec((piece.shape[0], per, SUB, HB), lambda i: (0, i, 0, 0))
         for piece in rotated
     ] + [
         pl.BlockSpec((tokens, cols), lambda i: (0, 0)),
@@ -279,7 +280,7 @@
         ],
         input_output_aliases=aliases,
         compiler_params=pltpu.CompilerParams(vmem_limit_bytes=26 << 20),
-        cost_estimate=LONG,
+        cost_estimate=cost,
         name="weight_grads",
     )(*args, *in_hbm(*after))
 
@@ -312,7 +313,7 @@
         input_output_aliases={0: 0},
         cost_estimate=FREE,
         name="gate",
-    )(*in_hbm(value, *after))
+    )(*in_hbm(value), *after)
 
 
 def transform_kernel(x_ref, out_ref):
@@ -390,33 +391,60 @@
 
 
 def total_kernel(count, *refs):
-    out_ref = refs[-1]
-    start = 0
+    outs = refs[3 * count :]
+    place = 0
     for i in range(count):
         own_ref, x_ref, y_ref = refs[3 * i : 3 * i + 3]
+        value = own_ref[...].astype(F32) + x_ref[...].astype(F32) + y_ref[...].astype(F32)
+        value = value.astype(BF16)
         size = own_ref.shape[1]
-        out_ref[:, start : start + size] = (
-            own_ref[...].astype(F32) + x_ref[...].astype(F32) + y_ref[...].astype(F32)
-        ).astype(BF16)
-        start += size
-
-
-def total(chunks, after=()):
+        start = 0
+        for out_ref in outs:
+            first, last = max(place, start), min(place + size, start + out_ref.shape[1])
+            if first < last:
+                out_ref[:, first - start : last - start] = value[:, first - place : last - place]
+            start += out_ref.shape[1]
+        place += size
+
+
+def total(chunks, sizes, after=()):
     ins = [value for own, *far in chunks for value in (*in_hbm(own), *far)]
     subs = ins[0].shape[0]
-    groups = sum(chunk[0].shape[1] for chunk in chunks)
     step = 2
     return pl.pallas_call(
         drop_inputs(functools.partial(total_kernel, len(chunks)), len(ins), len(after)),
         grid=(subs // step,),
         in_specs=[pl.BlockSpec((step,) + v.shape[1:], lambda i: (i, 0, 0, 0)) for v in ins]
         + [ANYWHERE] * len(after),
-        out_specs=pl.BlockSpec((step, groups, SUB, HB), lambda i: (i, 0, 0, 0)),
-        out_shape=pltpu.HBM((subs, groups, SUB, HB), BF16),
+        out_specs=[pl.BlockSpec((step, size, SUB, HB), lambda i: (i, 0, 0, 0)) for size in sizes],
+        out_shape=[pltpu.HBM((subs, size, SUB, HB), BF16) for size in sizes],
         compiler_params=pltpu.CompilerParams(vmem_limit_bytes=SMALL),
         cost_estimate=FREE,
         name="total",
     )(*ins, *in_hbm(*after))
+
+
+def butterfly_kernel(scale, x_ref, other_ref, sign_ref, out_ref):
+    value = other_ref[...].astype(F32) + sign_ref[0] * x_ref[...].astype(F32)
+    out_ref[...] = (value * scale).astype(BF16)
+
+
+def butterfly(value, mask, scale, after):
+    other = partner(value, "tensor", mask)
+    sign = jnp.where((lax.axis_index("tensor") & mask) != 0, -1.0, 1.0).astype(F32).reshape(1)
+    count = value.shape[0]
+    step = min(4, count)
+    spec = pl.BlockSpec((step,) + value.shape[1:], lambda i: (i, 0, 0, 0))
+    return pl.pallas_call(
+        drop_inputs(functools.partial(butterfly_kernel, scale), 3, len(after)),
+        grid=(count // step,),
+        in_specs=[spec, spec, pl.BlockSpec(memory_space=pltpu.SMEM)] + [ANYWHERE] * len(after),
+        out_specs=spec,
+        out_shape=pltpu.HBM(value.shape, BF16),
+        compiler_params=pltpu.CompilerParams(vmem_limit_bytes=SMALL),
+        cost_estimate=FREE,
+        name="butterfly",
+    )(*in_hbm(value), other, sign, *in_hbm(*after))
 
 
 def general_shards(hidden, upstream, weight, scales, clip_mask, rot_block):
@@ -445,7 +473,7 @@
 def shards(hidden, upstream, weight, scales, clip_mask, rot_block):
     groups = scales.shape[0]
     subs = hidden.shape[0] // SUB
-    if lax.axis_size("dp") != 4 or lax.axis_size("tensor") != subs or groups % 8 != 4:
+    if lax.axis_size("dp") != 4 or lax.axis_size("tensor") != subs or groups % 8 != 4 or subs != 8:
         return general_shards(hidden, upstream, weight, scales, clip_mask, rot_block)
     per = 4
     units = groups // per
@@ -469,8 +497,10 @@
         )
         return x_part, partner(x_part, "dp", 1), partner(y_part, "dp", 2)
 
-    def gather(value):
-        x_part, y_part = partner(value, "dp", 1), partner(value, "dp", 2)
+    def gather_first(value):
+        return value, partner(value, "dp", 1), partner(value, "dp", 2)
+
+    def gather_second(value, x_part, y_part):
         return value, x_part, y_part, partner(y_part[:half], "dp", 1), partner(
             x_part[half:], "dp", 2
         )
@@ -488,18 +518,37 @@
     turned = transform(forth, after=(relayed0,), cost=LONG)
     rotated = exchange(turned)
     relayed1, *second1 = scatter_second(unit1, first1, after=(turned,), cost=LONG)
-    summed = gate(total(((unit0[0], *second0), (unit1[0], *second1))), after=(rotated,))
+    side, summed = total(
+        ((unit0[0], *second0), (unit1[0], *second1)), (SIDE, groups - SIDE)
+    )
+    summed = gate(summed, after=(rotated,))
     back = exchange(summed)
-    gathered = gather(rotated)
+    gathered0 = gather_second(*gather_first(rotated[:, : sizes[0]]))
+    near = gather_first(gate(rotated, after=gathered0[1:3])[:, sizes[0] :])
     mixed = transform(back, cost=LONG)
     final = exchange(mixed)
     buffer, scale0 = weight_grads(
-        gathered, up, weight, scales, clip_mask, None, starts[0], sizes[0], per, after=(mixed,)
-    )
+        gathered0,
+        up,
+        weight,
+        scales,
+        clip_mask,
+        None,
+        starts[0],
+        sizes[0],
+        per,
+        after=(mixed,),
+        cost=LONG,
+    )
+    gathered1 = gather_second(near[0], *(gate(value, after=(scale0,)) for value in near[1:]))
+    side = gate(side, after=gathered0[1:3])
+    side = butterfly(side, 4, 1.0, after=(scale0,))
+    side = butterfly(side, 2, 1.0, after=())
     buffer, scale1 = weight_grads(
-        gathered, up, weight, scales, clip_mask, buffer, starts[1], sizes[1], per
-    )
-    grad_hidden = local_backward([final], rot_block, (groups,), after=(scale1,))
+        gathered1, up, weight, scales, clip_mask, buffer, starts[1], sizes[1], per, after=(side,)
+    )
+    side = butterfly(side, 1, subs ** (-0.5), after=(scale1,))
+    grad_hidden = local_backward([side, final], rot_block, (SIDE, groups - SIDE))
     return grad_hidden, buffer, jnp.concatenate([scale0, scale1], axis=0)
 
 

time: 215 us -> 228 us (1.060)
  local copies, waits for them, and re-layouts: 7.89 us -> 17.4 us
  waiting for transfers between devices: 82.9 us -> 73.4 us
  starting transfers between devices: 37.9 us -> 45.2 us
  Pallas kernels: 81.8 us -> 87 us
    ppermute x16 -> x23, waiting for transfers between devices: 79.1 us -> 69.1 us  [partner(): return lax.ppermute(value, axis, [(i, i ^ mask) for i in range(size)])]
    ppermute x16 -> x23, starting transfers between devices: 19.8 us -> 27.4 us  [partner(): return lax.ppermute(value, axis, [(i, i ^ mask) for i in range(size)])]
    slice x2 -> x6, local copies, waits for them, and re-layouts: 2.42 us -> 8.98 us  [the longest x2 2.84 us: gather_second(): y_part[:half]]
    pallas_call x0 -> x3, Pallas kernels: none -> 5.11 us  [butterfly(): pl.pallas_call(drop_inputs(functools.partial(butterfly_kernel, scale), 3,...]
    unnamed x14 -> x24, local copies, waits for them, and re-layouts: 3.21 us -> 6.16 us
  transfers between devices with their start and end apart: 20 -> 27, of which waited for: 11 -> 12; matrix products, arithmetic and copies ran while one was open for 3% -> 6% of each run, Pallas kernels for 35% -> 36%
where the time goes in v6:
time: 228 us; the launch traced here: 226 us
  Pallas kernels  87 us (38%)
  waiting for transfers between devices  73.4 us (32%)
  starting transfers between devices  45.2 us (20%)
  local copies, waits for them, and re-layouts  17.4 us (8%)
  other arithmetic  2.48 us (1%)
    ppermute x23, waiting for transfers between devices, partner(): return lax.ppermute(value, axis, [(i, i ^ mask) for i in range(size)])  69.1 us
    pallas_call x2, Pallas kernels, weight_grads(): pl.pallas_call(functools.partial(weights_kernel, first, per, len(rotated)...  30.7 us
    ppermute x23, starting transfers between devices, partner(): return lax.ppermute(value, axis, [(i, i ^ mask) for i in range(size)])  27.4 us
    pallas_call x2, Pallas kernels, unit_grads(): pl.pallas_call(drop_inputs(functools.partial(units_kernel, first, per), 3...  25.3 us
    all_to_all x4, starting transfers between devices, exchange(): lax.all_to_all(value, 'tensor', split_axis=0, concat_axis=0, tiled=True)  17.8 us
    pallas_call x4, Pallas kernels, small_call(): pl.pallas_call(drop_inputs(kernel, len(ins), len(after)), grid=(steps,),...  9.55 us
    unnamed x24, local copies, waits for them, and re-layouts  6.16 us
    pallas_call x1, Pallas kernels, local_backward(): pl.pallas_call(drop_inputs(functools.partial(backward_kernel, sizes), len...  6.03 us
  transfers between devices with their start and end apart: 27, of which 12 were waited for; matrix products, arithmetic and copies ran while one was open for 6% of the time, Pallas kernels for 36%

profile of v6, /device:TPU:0, one launch (start us, length us, event | category | flops | bytes accessed | tf_op | source)
XLA Modules:
  0.0 226.3 jit_solution(7266725023358290278)
XLA Ops:
  1.8 3.0 %collective-permute-start = (bf16[64,2048]{1,0:T(8,128)(2,1)S(1)}, bf16[64,2048]{1,0:T(8,128)(2,1)S(1)}, u32[]{:S(2)}, u32[]{:S(2)}) collective-permute-start(bf16[64,2048]{1,0:T(8,128)(2,1)S(1)} %get-tuple-element.43), channel_id=1, source_target_pairs={{0,8},{8,0},{16,24},{24,16},{1,9},{9,1},{17,25},{25,17},{2,10},{10... | collective-permute-start | bytes 786440 | tf_op jit(solution)/shard_map/ppermute | solution.py:346
  4.8 1.5 collective-permute-start.1
  6.4 6.0 %local_forward.1.refs_3_ = bf16[8,52,16,128]{3,2,1,0:T(8,128)(2,1)} custom-call(bf16[128,6656]{1,0:T(8,128)(2,1)} %x_ref.1, f32[52,52]{1,0:T(8,128)} %refs_2_.5), custom_call_target="tpu_custom_call" | custom-call | tf_op jit(solution)/shard_map/local_forward/pallas_call | solution.py:146
  12.4 5.3 %all-to-all-start = ((bf16[8,52,16,128]{3,2,1,0:T(8,128)(2,1)}), bf16[8,52,16,128]{3,2,1,0:T(8,128)(2,1)S(1)}, u32[]{:S(2)}, u32[]{:S(2)}) async-start(bf16[8,52,16,128]{3,2,1,0:T(8,128)(2,1)} %local_forward.1.refs_3_), calls=%async_computation | async-start | bytes 3407872 | tf_op jit(solution)/shard_map/all_to_all | solution.py:341
  22.4 13.8 %unit_grads.2 = (bf16[8,28,16,128]{3,2,1,0:T(8,128)(2,1)}, bf16[8,28,16,128]{3,2,1,0:T(8,128)(2,1)}, bf16[8,28,16,128]{3,2,1,0:T(8,128)(2,1)}, bf16[4,28,16,128]{3,2,1,0:T(8,128)(2,1)}, bf16[4,28,16,128]{3,2,1,0:T(8,128)(2,1)}) custom-call(bf16[512,2048]{1,0:T(8,128)(2,1)S(1)} %pad_maximum_fusion.refs_0_.refs_5_, bf16[6656,2048]{1,0:T(8,128)(2,1)} %refs_6_.3, ...), custom_call_target="tpu_custom_call" | custom-call | flops 5000000000 | tf_op jit(solution)/shard_map/unit_grads/pallas_call | solution.py:202
  38.9 11.5 %unit_grads.3 = (bf16[8,24,16,128]{3,2,1,0:T(8,128)(2,1)}, bf16[8,24,16,128]{3,2,1,0:T(8,128)(2,1)}, bf16[8,24,16,128]{3,2,1,0:T(8,128)(2,1)}, bf16[4,24,16,128]{3,2,1,0:T(8,128)(2,1)}, bf16[4,24,16,128]{3,2,1,0:T(8,128)(2,1)}) custom-call(bf16[512,2048]{1,0:T(8,128)(2,1)S(1)} %pad_maximum_fusion.refs_0_.refs_5_, bf16[6656,2048]{1,0:T(8,128)(2,1)} %refs_6_.3, ...), custom_call_target="tpu_custom_call" | custom-call | tf_op jit(solution)/shard_map/unit_grads/pallas_call | solution.py:202
  51.8 2.5 %relay.2 = (bf16[8,28,16,128]{3,2,1,0:T(8,128)(2,1)}, bf16[8,28,16,128]{3,2,1,0:T(8,128)(2,1)}) custom-call(bf16[8,28,16,128]{3,2,1,0:T(8,128)(2,1)} %get-tuple-element.24.refs_0_, bf16[8,28,16,128]{3,2,1,0:T(8,128)(2,1)} %get-tuple-element.25.refs_1_, bf16[4,28,16,128]{3,2,1,0:T(8,128)(2,1)S(1)} %collective-permute-done.4.refs_2_, ...), custom_call_target="tpu_custom_call" | custom-call | tf_op jit(solution)/shard_map/relay/pallas_call | solution.py:295
  58.3 2.3 %transform.2.refs_4_ = bf16[8,52,16,128]{3,2,1,0:T(8,128)(2,1)} custom-call(bf16[8,52,16,128]{3,2,1,0:T(8,128)(2,1)S(1)} %all-to-all-done.refs_0_, bf16[8,28,16,128]{3,2,1,0:T(8,128)(2,1)} %get-tuple-element.29.refs_1_), custom_call_target="tpu_custom_call" | custom-call | flops 999999995904 | tf_op jit(solution)/shard_map/transform/pallas_call | solution.py:295
  60.6 4.3 %all-to-all-start.1 = ((bf16[8,52,16,128]{3,2,1,0:T(8,128)(2,1)}), bf16[8,52,16,128]{3,2,1,0:T(8,128)(2,1)}, u32[]{:S(2)}, u32[]{:S(2)}) async-start(bf16[8,52,16,128]{3,2,1,0:T(8,128)(2,1)} %transform.2.refs_4_), calls=%async_computation.1 | async-start | bytes 3407872 | tf_op jit(solution)/shard_map/all_to_all | solution.py:341
  64.9 2.6 %relay.3 = (bf16[8,24,16,128]{3,2,1,0:T(8,128)(2,1)}, bf16[8,24,16,128]{3,2,1,0:T(8,128)(2,1)}) custom-call(bf16[8,24,16,128]{3,2,1,0:T(8,128)(2,1)} %get-tuple-element.31.refs_0_, bf16[8,24,16,128]{3,2,1,0:T(8,128)(2,1)} %get-tuple-element.32.refs_1_, bf16[4,24,16,128]{3,2,1,0:T(8,128)(2,1)} %collective-permute-done.8.refs_2_, ...), custom_call_target="tpu_custom_call" | custom-call | flops 999999995904 | tf_op jit(solution)/shard_map/relay/pallas_call | solution.py:295
  70.6 11.8 %collective-permute-done.6.refs_1_ = bf16[8,28,16,128]{3,2,1,0:T(8,128)(2,1)} collective-permute-done((bf16[8,28,16,128]{3,2,1,0:T(8,128)(2,1)}, bf16[8,28,16,128]{3,2,1,0:T(8,128)(2,1)}, u32[]{:S(2)}, u32[]{:S(2)}) %collective-permute-start.6) | collective-permute-done | bytes 917536 | tf_op jit(solution)/shard_map/ppermute | solution.py:346
  83.3 14.6 %collective-permute-done.10.refs_4_ = bf16[8,24,16,128]{3,2,1,0:T(8,128)(2,1)S(1)} collective-permute-done((bf16[8,24,16,128]{3,2,1,0:T(8,128)(2,1)}, bf16[8,24,16,128]{3,2,1,0:T(8,128)(2,1)S(1)}, u32[]{:S(2)}, u32[]{:S(2)}) %collective-permute-start.10) | collective-permute-done | bytes 786464 | tf_op jit(solution)/shard_map/ppermute | solution.py:346
  98.3 4.3 %total.1 = (bf16[8,8,16,128]{3,2,1,0:T(8,128)(2,1)}, bf16[8,44,16,128]{3,2,1,0:T(8,128)(2,1)}) custom-call(bf16[8,28,16,128]{3,2,1,0:T(8,128)(2,1)} %get-tuple-element.23.refs_3_.refs_0_, bf16[8,28,16,128]{3,2,1,0:T(8,128)(2,1)} %collective-permute-done.6.refs_1_, bf16[8,28,16,128]{3,2,1,0:T(8,128)(2,1)} %collective-permute-done.7.refs_2_, ...), custom_call_target="tpu_custom_call" | custom-call | tf_op jit(solution)/shard_map/total/pallas_call | solution.py:414
  102.6 3.0 %all-to-all-done.1.refs_1_.refs_0_ = bf16[8,52,16,128]{3,2,1,0:T(8,128)(2,1)} async-done(((bf16[8,52,16,128]{3,2,1,0:T(8,128)(2,1)}), bf16[8,52,16,128]{3,2,1,0:T(8,128)(2,1)}, u32[]{:S(2)}, u32[]{:S(2)}) %all-to-all-start.1) | async-done | bytes 1703968 | tf_op jit(solution)/shard_map/all_to_all | solution.py:341
  105.6 3.6 %all-to-all-start.2 = ((bf16[8,44,16,128]{3,2,1,0:T(8,128)(2,1)}), bf16[8,44,16,128]{3,2,1,0:T(8,128)(2,1)S(1)}, u32[]{:S(2)}, u32[]{:S(2)}) async-start(bf16[8,44,16,128]{3,2,1,0:T(8,128)(2,1)} %gate.6), calls=%async_computation.2 | async-start | bytes 2883584 | tf_op jit(solution)/shard_map/all_to_all | solution.py:341
  110.5 1.6 collective-permute-start.12
  114.5 18.7 %collective-permute-done.12.refs_1_ = bf16[8,28,16,128]{3,2,1,0:T(8,128)(2,1)S(1)} collective-permute-done((bf16[8,28,16,128]{3,2,1,0:T(8,128)(2,1)S(1)}, bf16[8,28,16,128]{3,2,1,0:T(8,128)(2,1)S(1)}, u32[]{:S(2)}, u32[]{:S(2)}) %collective-permute-start.12) | collective-permute-done | bytes 917536 | tf_op jit(solution)/shard_map/ppermute | solution.py:346
  135.4 2.2 slice.27.refs_0_
  140.4 1.8 slice.25
  144.3 2.6 %collective-permute-start.14 = (bf16[8,8,16,128]{3,2,1,0:T(8,128)(2,1)}, bf16[8,8,16,128]{3,2,1,0:T(8,128)(2,1)}, u32[]{:S(2)}, u32[]{:S(2)}) collective-permute-start(bf16[8,8,16,128]{3,2,1,0:T(8,128)(2,1)} %gate.5.refs_0_), channel_id=1, source_target_pairs={{0,4},{1,5},{2,6},{3,7},{4,0},{5,1},{6,2},{7,3},{8,12},{9,13},{10,... | collective-permute-start | bytes 786440 | tf_op jit(solution)/shard_map/ppermute | solution.py:346
  146.9 2.1 transform.3.refs_9_
  149.0 4.6 %all-to-all-start.3 = ((bf16[8,44,16,128]{3,2,1,0:T(8,128)(2,1)}), bf16[8,44,16,128]{3,2,1,0:T(8,128)(2,1)}, u32[]{:S(2)}, u32[]{:S(2)}) async-start(bf16[8,44,16,128]{3,2,1,0:T(8,128)(2,1)} %transform.3.refs_9_), calls=%async_computation.3 | async-start | bytes 2883584 | tf_op jit(solution)/shard_map/all_to_all | solution.py:341
  153.6 14.3 %collective-permute-done.15.refs_3_ = bf16[4,28,16,128]{3,2,1,0:T(8,128)(2,1)} collective-permute-done((bf16[4,28,16,128]{3,2,1,0:T(8,128)(2,1)}, bf16[4,28,16,128]{3,2,1,0:T(8,128)(2,1)}, u32[]{:S(2)}, u32[]{:S(2)}) %collective-permute-start.15) | collective-permute-done | bytes 458784 | tf_op jit(solution)/shard_map/ppermute | solution.py:346
  171.4 16.1 %weight_grads.2 = (bf16[6656,2048]{1,0:T(8,128)(2,1)}, f32[28,2048]{1,0:T(8,128)S(1)}) custom-call(bf16[8,28,16,128]{3,2,1,0:T(8,128)(2,1)S(1)} %copy-done.10, bf16[8,28,16,128]{3,2,1,0:T(8,128)(2,1)S(1)} %copy-done.4, bf16[8,28,16,128]{3,2,1,0:T(8,128)(2,1)S(1)} %copy-done.6, bf16[4,28,16,128]{3,2,1,0:T(8,128)(2,1)} %collective-permute-done.15.refs_3_, ...), custom_call_target="tpu_custom_call" | custom-call | flops 999999995904 | tf_op jit(solution)/shard_map/weight_grads/pallas_call | solution.py:269
  189.2 1.6 collective-permute-start.21
  190.8 1.8 slice.29
  193.1 1.8 butterfly.3.refs_0_
  196.2 5.3 %collective-permute-done.17.refs_1_ = bf16[8,8,16,128]{3,2,1,0:T(8,128)(2,1)S(1)} collective-permute-done((bf16[8,8,16,128]{3,2,1,0:T(8,128)(2,1)}, bf16[8,8,16,128]{3,2,1,0:T(8,128)(2,1)S(1)}, u32[]{:S(2)}, u32[]{:S(2)}) %collective-permute-start.17) | collective-permute-done | bytes 262176 | tf_op jit(solution)/shard_map/ppermute | solution.py:346
  201.5 1.7 butterfly.4.refs_10_.refs_0_
  203.1 14.6 %weight_grads.3 = (bf16[6656,2048]{1,0:T(8,128)(2,1)}, f32[24,2048]{1,0:T(8,128)S(1)}) custom-call(bf16[8,24,16,128]{3,2,1,0:T(8,128)(2,1)} %slice.27.refs_0_, bf16[8,24,16,128]{3,2,1,0:T(8,128)(2,1)} %gate.8.refs_1_, bf16[8,24,16,128]{3,2,1,0:T(8,128)(2,1)} %gate.9.refs_2_, ...), custom_call_target="tpu_custom_call", output_to_operand_aliasing={{0}: (9, {})} | custom-call | tf_op jit(solution)/shard_map/weight_grads/pallas_call | solution.py:269
  218.6 1.7 butterfly.5.refs_0_
  220.3 6.0 %local_backward.1 = bf16[128,6656]{1,0:T(8,128)(2,1)} custom-call(bf16[8,8,16,128]{3,2,1,0:T(8,128)(2,1)} %butterfly.5.refs_0_, bf16[8,44,16,128]{3,2,1,0:T(8,128)(2,1)} %all-to-all-done.3.refs_1_, f32[52,52]{1,0:T(8,128)} %refs_2_.5), custom_call_target="tpu_custom_call" | custom-call | tf_op jit(solution)/shard_map/local_backward/pallas_call | solution.py:167
  (78 shorter events, 37.1 us)
Async XLA Ops:
  1.8 15.9 %collective-permute-start = (bf16[64,2048]{1,0:T(8,128)(2,1)S(1)}, bf16[64,2048]{1,0:T(8,128)(2,1)S(1)}, u32[]{:S(2)}, u32[]{:S(2)}) collective-permute-start(bf16[64,2048]{1,0:T(8,128)(2,1)S(1)} %get-tuple-element.43), channel_id=1, source_target_pairs={{0,8},{8,0},{16,24},{24,16},{1,9},{9,1},{17,25},{25,17},{2,10},{10... | collective-permute-start | bytes 786440 | tf_op jit(solution)/shard_map/ppermute | solution.py:346
  4.8 13.4 %collective-permute-start.1 = (bf16[64,2048]{1,0:T(8,128)(2,1)S(1)}, bf16[64,2048]{1,0:T(8,128)(2,1)S(1)}, u32[]{:S(2)}, u32[]{:S(2)}) collective-permute-start(bf16[64,2048]{1,0:T(8,128)(2,1)S(1)} %get-tuple-element.45), channel_id=1, source_target_pairs={{0,16},{8,24},{16,0},{24,8},{1,17},{9,25},{17,1},{25,9},{2,18},{10... | collective-permute-start | bytes 786440 | tf_op jit(solution)/shard_map/ppermute | solution.py:346
  6.4 11.9 %collective-permute-start.2 = (bf16[64,2048]{1,0:T(8,128)(2,1)S(1)}, bf16[64,2048]{1,0:T(8,128)(2,1)S(1)}, u32[]{:S(2)}, u32[]{:S(2)}) collective-permute-start(bf16[64,2048]{1,0:T(8,128)(2,1)S(1)} %get-tuple-element.44), channel_id=1, source_target_pairs={{0,24},{8,16},{16,8},{24,0},{1,25},{9,17},{17,9},{25,1},{2,26},{10... | collective-permute-start | bytes 786440 | tf_op jit(solution)/shard_map/ppermute | solution.py:346
  12.4 46.0 %all-to-all-start = ((bf16[8,52,16,128]{3,2,1,0:T(8,128)(2,1)}), bf16[8,52,16,128]{3,2,1,0:T(8,128)(2,1)S(1)}, u32[]{:S(2)}, u32[]{:S(2)}) async-start(bf16[8,52,16,128]{3,2,1,0:T(8,128)(2,1)} %local_forward.1.refs_3_), calls=%async_computation | async-start | bytes 3407872 | tf_op jit(solution)/shard_map/all_to_all | solution.py:341
  18.3 2.5 %collective-permute-start.3 = (bf16[3,64,2048]{2,1,0:T(8,128)(2,1)S(1)}, bf16[3,64,2048]{2,1,0:T(8,128)(2,1)}, u32[]{:S(2)}, u32[]{:S(2)}) collective-permute-start(bf16[3,64,2048]{2,1,0:T(8,128)(2,1)S(1)} %pad_maximum_fusion.2), channel_id=1, source_target_pairs={{0,1},{1,0},{2,3},{3,2},{4,5},{5,4},{6,7},{7,6},{8,9},{9,8},{10,11... | collective-permute-start | bytes 2359304 | tf_op jit(solution)/shard_map/ppermute | solution.py:346
  22.4 16.5 %copy-start = (bf16[512,2048]{1,0:T(8,128)(2,1)}, bf16[512,2048]{1,0:T(8,128)(2,1)S(1)}, u32[]{:S(2)}) copy-start(bf16[512,2048]{1,0:T(8,128)(2,1)S(1)} %pad_maximum_fusion.refs_0_.refs_5_) | copy-start | bytes 6291460
  36.2 15.5 %collective-permute-start.4 = (bf16[4,28,16,128]{3,2,1,0:T(8,128)(2,1)}, bf16[4,28,16,128]{3,2,1,0:T(8,128)(2,1)S(1)}, u32[]{:S(2)}, u32[]{:S(2)}) collective-permute-start(bf16[4,28,16,128]{3,2,1,0:T(8,128)(2,1)} %get-tuple-element.26), channel_id=1, source_target_pairs={{0,8},{8,0},{16,24},{24,16},{1,9},{9,1},{17,25},{25,17},{2,10},{10... | collective-permute-start | bytes 1376264 | tf_op jit(solution)/shard_map/ppermute | solution.py:346
  37.5 14.3 %collective-permute-start.5 = (bf16[4,28,16,128]{3,2,1,0:T(8,128)(2,1)}, bf16[4,28,16,128]{3,2,1,0:T(8,128)(2,1)S(1)}, u32[]{:S(2)}, u32[]{:S(2)}) collective-permute-start(bf16[4,28,16,128]{3,2,1,0:T(8,128)(2,1)} %get-tuple-element.27), channel_id=1, source_target_pairs={{0,16},{8,24},{16,0},{24,8},{1,17},{9,25},{17,1},{25,9},{2,18},{10... | collective-permute-start | bytes 1376264 | tf_op jit(solution)/shard_map/ppermute | solution.py:346
  50.4 14.5 %collective-permute-start.8 = (bf16[4,24,16,128]{3,2,1,0:T(8,128)(2,1)}, bf16[4,24,16,128]{3,2,1,0:T(8,128)(2,1)}, u32[]{:S(2)}, u32[]{:S(2)}) collective-permute-start(bf16[4,24,16,128]{3,2,1,0:T(8,128)(2,1)} %get-tuple-element.33), channel_id=1, source_target_pairs={{0,8},{8,0},{16,24},{24,16},{1,9},{9,1},{17,25},{25,17},{2,10},{10... | collective-permute-start | bytes 1179656 | tf_op jit(solution)/shard_map/ppermute | solution.py:346
  51.3 13.7 %collective-permute-start.9 = (bf16[4,24,16,128]{3,2,1,0:T(8,128)(2,1)}, bf16[4,24,16,128]{3,2,1,0:T(8,128)(2,1)}, u32[]{:S(2)}, u32[]{:S(2)}) collective-permute-start(bf16[4,24,16,128]{3,2,1,0:T(8,128)(2,1)} %get-tuple-element.34), channel_id=1, source_target_pairs={{0,16},{8,24},{16,0},{24,8},{1,17},{9,25},{17,1},{25,9},{2,18},{10... | collective-permute-start | bytes 1179656 | tf_op jit(solution)/shard_map/ppermute | solution.py:346
  54.3 28.0 %collective-permute-start.6 = (bf16[8,28,16,128]{3,2,1,0:T(8,128)(2,1)}, bf16[8,28,16,128]{3,2,1,0:T(8,128)(2,1)}, u32[]{:S(2)}, u32[]{:S(2)}) collective-permute-start(bf16[8,28,16,128]{3,2,1,0:T(8,128)(2,1)} %get-tuple-element.29.refs_1_), channel_id=1, source_target_pairs={{0,8},{8,0},{16,24},{24,16},{1,9},{9,1},{17,25},{25,17},{2,10},{10... | collective-permute-start | bytes 2752520 | tf_op jit(solution)/shard_map/ppermute | solution.py:346
  55.6 27.7 %collective-permute-start.7 = (bf16[8,28,16,128]{3,2,1,0:T(8,128)(2,1)}, bf16[8,28,16,128]{3,2,1,0:T(8,128)(2,1)}, u32[]{:S(2)}, u32[]{:S(2)}) collective-permute-start(bf16[8,28,16,128]{3,2,1,0:T(8,128)(2,1)} %get-tuple-element.30), channel_id=1, source_target_pairs={{0,16},{8,24},{16,0},{24,8},{1,17},{9,25},{17,1},{25,9},{2,18},{10... | collective-permute-start | bytes 2752520 | tf_op jit(solution)/shard_map/ppermute | solution.py:346
  60.6 45.0 %all-to-all-start.1 = ((bf16[8,52,16,128]{3,2,1,0:T(8,128)(2,1)}), bf16[8,52,16,128]{3,2,1,0:T(8,128)(2,1)}, u32[]{:S(2)}, u32[]{:S(2)}) async-start(bf16[8,52,16,128]{3,2,1,0:T(8,128)(2,1)} %transform.2.refs_4_), calls=%async_computation.1 | async-start | bytes 3407872 | tf_op jit(solution)/shard_map/all_to_all | solution.py:341
  67.6 30.4 %collective-permute-start.10 = (bf16[8,24,16,128]{3,2,1,0:T(8,128)(2,1)}, bf16[8,24,16,128]{3,2,1,0:T(8,128)(2,1)S(1)}, u32[]{:S(2)}, u32[]{:S(2)}) collective-permute-start(bf16[8,24,16,128]{3,2,1,0:T(8,128)(2,1)} %get-tuple-element.35), channel_id=1, source_target_pairs={{0,8},{8,0},{16,24},{24,16},{1,9},{9,1},{17,25},{25,17},{2,10},{10... | collective-permute-start | bytes 2359304 | tf_op jit(solution)/shard_map/ppermute | solution.py:346
  69.1 29.3 %collective-permute-start.11 = (bf16[8,24,16,128]{3,2,1,0:T(8,128)(2,1)}, bf16[8,24,16,128]{3,2,1,0:T(8,128)(2,1)S(1)}, u32[]{:S(2)}, u32[]{:S(2)}) collective-permute-start(bf16[8,24,16,128]{3,2,1,0:T(8,128)(2,1)} %get-tuple-element.36), channel_id=1, source_target_pairs={{0,16},{8,24},{16,0},{24,8},{1,17},{9,25},{17,1},{25,9},{2,18},{10... | collective-permute-start | bytes 2359304 | tf_op jit(solution)/shard_map/ppermute | solution.py:346
  105.6 41.3 %all-to-all-start.2 = ((bf16[8,44,16,128]{3,2,1,0:T(8,128)(2,1)}), bf16[8,44,16,128]{3,2,1,0:T(8,128)(2,1)S(1)}, u32[]{:S(2)}, u32[]{:S(2)}) async-start(bf16[8,44,16,128]{3,2,1,0:T(8,128)(2,1)} %gate.6), calls=%async_computation.2 | async-start | bytes 2883584 | tf_op jit(solution)/shard_map/all_to_all | solution.py:341
  110.5 22.7 %collective-permute-start.12 = (bf16[8,28,16,128]{3,2,1,0:T(8,128)(2,1)S(1)}, bf16[8,28,16,128]{3,2,1,0:T(8,128)(2,1)S(1)}, u32[]{:S(2)}, u32[]{:S(2)}) collective-permute-start(bf16[8,28,16,128]{3,2,1,0:T(8,128)(2,1)S(1)} %slice.24.refs_0_), channel_id=1, source_target_pairs={{0,8},{8,0},{16,24},{24,16},{1,9},{9,1},{17,25},{25,17},{2,10},{10... | collective-permute-start | bytes 2752520 | tf_op jit(solution)/shard_map/ppermute | solution.py:346
  112.0 22.4 %collective-permute-start.13 = (bf16[8,28,16,128]{3,2,1,0:T(8,128)(2,1)S(1)}, bf16[8,28,16,128]{3,2,1,0:T(8,128)(2,1)S(1)}, u32[]{:S(2)}, u32[]{:S(2)}) collective-permute-start(bf16[8,28,16,128]{3,2,1,0:T(8,128)(2,1)S(1)} %slice.24.refs_0_), channel_id=1, source_target_pairs={{0,16},{8,24},{16,0},{24,8},{1,17},{9,25},{17,1},{25,9},{2,18},{10... | collective-permute-start | bytes 2752520 | tf_op jit(solution)/shard_map/ppermute | solution.py:346
  133.2 1.2 copy-start.2
  135.4 7.6 %copy-start.3 = (bf16[8,28,16,128]{3,2,1,0:T(8,128)(2,1)S(1)}, bf16[8,28,16,128]{3,2,1,0:T(8,128)(2,1)}, u32[]{:S(2)}) copy-start(bf16[8,28,16,128]{3,2,1,0:T(8,128)(2,1)} %copy-done.2) | copy-start | bytes 2752516
  137.6 50.6 %collective-permute-start.20 = (bf16[8,24,16,128]{3,2,1,0:T(8,128)(2,1)}, bf16[8,24,16,128]{3,2,1,0:T(8,128)(2,1)}, u32[]{:S(2)}, u32[]{:S(2)}) collective-permute-start(bf16[8,24,16,128]{3,2,1,0:T(8,128)(2,1)} %slice.27.refs_0_), channel_id=1, source_target_pairs={{0,16},{8,24},{16,0},{24,8},{1,17},{9,25},{17,1},{25,9},{2,18},{10... | collective-permute-start | bytes 2359304 | tf_op jit(solution)/shard_map/ppermute | solution.py:346
  139.1 51.7 %collective-permute-start.19 = (bf16[8,24,16,128]{3,2,1,0:T(8,128)(2,1)}, bf16[8,24,16,128]{3,2,1,0:T(8,128)(2,1)}, u32[]{:S(2)}, u32[]{:S(2)}) collective-permute-start(bf16[8,24,16,128]{3,2,1,0:T(8,128)(2,1)} %slice.27.refs_0_), channel_id=1, source_target_pairs={{0,8},{8,0},{16,24},{24,16},{1,9},{9,1},{17,25},{25,17},{2,10},{10... | collective-permute-start | bytes 2359304 | tf_op jit(solution)/shard_map/ppermute | solution.py:346
  142.2 25.6 %collective-permute-start.15 = (bf16[4,28,16,128]{3,2,1,0:T(8,128)(2,1)}, bf16[4,28,16,128]{3,2,1,0:T(8,128)(2,1)}, u32[]{:S(2)}, u32[]{:S(2)}) collective-permute-start(bf16[4,28,16,128]{3,2,1,0:T(8,128)(2,1)} %slice.25), channel_id=1, source_target_pairs={{0,8},{8,0},{16,24},{24,16},{1,9},{9,1},{17,25},{25,17},{2,10},{10... | collective-permute-start | bytes 1376264 | tf_op jit(solution)/shard_map/ppermute | solution.py:346
  143.8 24.1 %collective-permute-start.16 = (bf16[4,28,16,128]{3,2,1,0:T(8,128)(2,1)}, bf16[4,28,16,128]{3,2,1,0:T(8,128)(2,1)}, u32[]{:S(2)}, u32[]{:S(2)}) collective-permute-start(bf16[4,28,16,128]{3,2,1,0:T(8,128)(2,1)} %slice.26), channel_id=1, source_target_pairs={{0,16},{8,24},{16,0},{24,8},{1,17},{9,25},{17,1},{25,9},{2,18},{10... | collective-permute-start | bytes 1376264 | tf_op jit(solution)/shard_map/ppermute | solution.py:346
  144.3 48.8 %collective-permute-start.14 = (bf16[8,8,16,128]{3,2,1,0:T(8,128)(2,1)}, bf16[8,8,16,128]{3,2,1,0:T(8,128)(2,1)}, u32[]{:S(2)}, u32[]{:S(2)}) collective-permute-start(bf16[8,8,16,128]{3,2,1,0:T(8,128)(2,1)} %gate.5.refs_0_), channel_id=1, source_target_pairs={{0,4},{1,5},{2,6},{3,7},{4,0},{5,1},{6,2},{7,3},{8,12},{9,13},{10,... | collective-permute-start | bytes 786440 | tf_op jit(solution)/shard_map/ppermute | solution.py:346
  149.0 18.9 %copy-start.1 = (bf16[512,2048]{1,0:T(8,128)(2,1)S(1)}, bf16[512,2048]{1,0:T(8,128)(2,1)}, u32[]{:S(2)}) copy-start(bf16[512,2048]{1,0:T(8,128)(2,1)} %copy-done) | copy-start | bytes 6291460
  149.0 71.3 %all-to-all-start.3 = ((bf16[8,44,16,128]{3,2,1,0:T(8,128)(2,1)}), bf16[8,44,16,128]{3,2,1,0:T(8,128)(2,1)}, u32[]{:S(2)}, u32[]{:S(2)}) async-start(bf16[8,44,16,128]{3,2,1,0:T(8,128)(2,1)} %transform.3.refs_9_), calls=%async_computation.3 | async-start | bytes 2883584 | tf_op jit(solution)/shard_map/all_to_all | solution.py:341
  189.2 13.9 %collective-permute-start.21 = (bf16[4,24,16,128]{3,2,1,0:T(8,128)(2,1)S(1)}, bf16[4,24,16,128]{3,2,1,0:T(8,128)(2,1)S(1)}, u32[]{:S(2)}, u32[]{:S(2)}) collective-permute-start(bf16[4,24,16,128]{3,2,1,0:T(8,128)(2,1)S(1)} %slice.28), channel_id=1, source_target_pairs={{0,8},{8,0},{16,24},{24,16},{1,9},{9,1},{17,25},{25,17},{2,10},{10... | collective-permute-start | bytes 1179656 | tf_op jit(solution)/shard_map/ppermute | solution.py:346
  192.6 10.5 %collective-permute-start.22 = (bf16[4,24,16,128]{3,2,1,0:T(8,128)(2,1)}, bf16[4,24,16,128]{3,2,1,0:T(8,128)(2,1)S(1)}, u32[]{:S(2)}, u32[]{:S(2)}) collective-permute-start(bf16[4,24,16,128]{3,2,1,0:T(8,128)(2,1)} %slice.29), channel_id=1, source_target_pairs={{0,16},{8,24},{16,0},{24,8},{1,17},{9,25},{17,1},{25,9},{2,18},{10... | collective-permute-start | bytes 1179656 | tf_op jit(solution)/shard_map/ppermute | solution.py:346
  194.9 6.6 %collective-permute-start.17 = (bf16[8,8,16,128]{3,2,1,0:T(8,128)(2,1)}, bf16[8,8,16,128]{3,2,1,0:T(8,128)(2,1)S(1)}, u32[]{:S(2)}, u32[]{:S(2)}) collective-permute-start(bf16[8,8,16,128]{3,2,1,0:T(8,128)(2,1)} %butterfly.3.refs_0_), channel_id=1, source_target_pairs={{0,2},{1,3},{2,0},{3,1},{4,6},{5,7},{6,4},{7,5},{8,10},{9,11},{10,... | collective-permute-start | bytes 786440 | tf_op jit(solution)/shard_map/ppermute | solution.py:346
  203.1 15.5 %collective-permute-start.18 = (bf16[8,8,16,128]{3,2,1,0:T(8,128)(2,1)}, bf16[8,8,16,128]{3,2,1,0:T(8,128)(2,1)S(1)}, u32[]{:S(2)}, u32[]{:S(2)}) collective-permute-start(bf16[8,8,16,128]{3,2,1,0:T(8,128)(2,1)} %butterfly.4.refs_10_.refs_0_), channel_id=1, source_target_pairs={{0,1},{1,0},{2,3},{3,2},{4,5},{5,4},{6,7},{7,6},{8,9},{9,8},{10,11... | collective-permute-start | bytes 786440 | tf_op jit(solution)/shard_map/ppermute | solution.py:346
  203.1 14.6 %copy-start.8 = (f32[28,2048]{1,0:T(8,128)S(1)}, f32[28,2048]{1,0:T(8,128)}, u32[]{:S(2)}) copy-start(f32[28,2048]{1,0:T(8,128)} %copy-done.7) | copy-start | bytes 688132
  (7 other events, 7.0 us)

commit v7 on v6

--- a/solution.py
+++ b/solution.py
@@ -122,7 +122,8 @@
 
 FREE = pl.CostEstimate(flops=0, bytes_accessed=0, transcendentals=0)
 LONG = pl.CostEstimate(flops=10**12, bytes_accessed=0, transcendentals=0)
-SOME = pl.CostEstimate(flops=5_000_000_000, bytes_accessed=0, transcendentals=0)
+SOME = pl.CostEstimate(flops=2_000_000_000, bytes_accessed=0, transcendentals=0)
+MORE = pl.CostEstimate(flops=26_000_000_000, bytes_accessed=0, transcendentals=0)
 SMALL = 12 << 20
 
 ANYWHERE = pl.BlockSpec(memory_space=pl.ANY)
@@ -180,14 +181,21 @@
 
 
 def units_kernel(first, per, up_ref, w_ref, s_ref, *refs):
-    outs, quant_ref = refs[:-1], refs[-1]
+    outs, (turned_ref, quant_ref) = refs[:-2], refs[-2:]
     base = first + pl.program_id(0) * per
+
+    @pl.when(pl.program_id(0) == 0)
+    def _():
+        tile = 256
+        for e in range(0, up_ref.shape[1], tile):
+            turned_ref[e : e + tile, :] = up_ref[:, e : e + tile].T
+
     for g in range(per):
         rows = slice(g * GROUP, (g + 1) * GROUP)
         quant_ref[rows, :] = (w_ref[rows, :].astype(F32) * s_ref[pl.ds(base + g, 1), :]).astype(
             BF16
         )
-    result = nt_dot(up_ref[...], quant_ref[...]).astype(BF16)
+    result = nn_dot(quant_ref[...], turned_ref[...]).astype(BF16).T
     token = 0
     for out_ref in outs:
         for q in range(out_ref.shape[0]):
@@ -210,7 +218,7 @@
         + [ANYWHERE] * len(after),
         out_specs=[pl.BlockSpec((count, per, SUB, HB), lambda i: (0, i, 0, 0)) for count in counts],
         out_shape=[pltpu.HBM((count, size, SUB, HB), BF16) for count in counts],
-        scratch_shapes=[pltpu.VMEM((per * GROUP, cols), BF16)],
+        scratch_shapes=[pltpu.VMEM((cols, tokens), BF16), pltpu.VMEM((per * GROUP, cols), BF16)],
         compiler_params=pltpu.CompilerParams(vmem_limit_bytes=26 << 20),
         cost_estimate=cost,
         name="unit_grads",
@@ -260,7 +268,7 @@
         pl.BlockSpec(scales.shape, lambda i: (0, 0)),
         pl.BlockSpec(scales.shape, lambda i: (0, 0)),
     ]
-    args = [*rotated, up, *in_hbm(weight, scales, mask)]
+    args = [*in_hbm(*rotated), up, *in_hbm(weight, scales, mask)]
     aliases = {}
     if buffer is not None:
         aliases = {len(args): 0}
@@ -479,6 +487,7 @@
     units = groups // per
     sizes = (per * (units - units // 2), per * (units // 2))
     starts = (0, sizes[0])
+    cuts = (per * (units - 2 * units // 5), per * (2 * units // 5))
     half = subs // 2
     counts = (subs, subs, subs, half, half)
 
@@ -506,7 +515,7 @@
         )
 
     up = gather_upstream(upstream)
-    (local,) = local_forward(hidden, rot_block, (groups,))
+    side, local = local_forward(hidden, rot_block, (SIDE, groups - SIDE))
     forth = exchange(local)
     unit0 = unit_grads(
         up, weight, scales, starts[0], sizes[0], per, counts, after=(local,), cost=SOME
@@ -517,16 +526,18 @@
     relayed0, *second0 = scatter_second(unit0, first0, after=(unit1[0],))
     turned = transform(forth, after=(relayed0,), cost=LONG)
     rotated = exchange(turned)
-    relayed1, *second1 = scatter_second(unit1, first1, after=(turned,), cost=LONG)
-    side, summed = total(
-        ((unit0[0], *second0), (unit1[0], *second1)), (SIDE, groups - SIDE)
-    )
+    side = butterfly(gate(side, after=(relayed0,)), 4, 1.0, after=(turned,))
+    relayed1, *second1 = scatter_second(unit1, first1, after=(side,), cost=LONG)
+    side = butterfly(side, 2, 1.0, after=(relayed1,))
+    side = butterfly(side, 1, subs ** (-0.5), after=())
+    (summed,) = total(((unit0[0], *second0), (unit1[0], *second1)), (groups,), after=(side,))
     summed = gate(summed, after=(rotated,))
     back = exchange(summed)
-    gathered0 = gather_second(*gather_first(rotated[:, : sizes[0]]))
-    near = gather_first(gate(rotated, after=gathered0[1:3])[:, sizes[0] :])
+    low = jnp.concatenate([side, rotated[:, : cuts[0] - SIDE]], axis=1)
+    gathered0 = gather_second(*gather_first(low))
     mixed = transform(back, cost=LONG)
     final = exchange(mixed)
+    near = gather_first(gate(rotated, after=(*gathered0[3:5], mixed))[:, cuts[0] - SIDE :])
     buffer, scale0 = weight_grads(
         gathered0,
         up,
@@ -534,21 +545,17 @@
         scales,
         clip_mask,
         None,
-        starts[0],
-        sizes[0],
+        0,
+        cuts[0],
         per,
         after=(mixed,),
-        cost=LONG,
+        cost=MORE,
     )
     gathered1 = gather_second(near[0], *(gate(value, after=(scale0,)) for value in near[1:]))
-    side = gate(side, after=gathered0[1:3])
-    side = butterfly(side, 4, 1.0, after=(scale0,))
-    side = butterfly(side, 2, 1.0, after=())
     buffer, scale1 = weight_grads(
-        gathered1, up, weight, scales, clip_mask, buffer, starts[1], sizes[1], per, after=(side,)
-    )
-    side = butterfly(side, 1, subs ** (-0.5), after=(scale1,))
-    grad_hidden = local_backward([side, final], rot_block, (SIDE, groups - SIDE))
+        gathered1, up, weight, scales, clip_mask, buffer, cuts[0], cuts[1], per
+    )
+    grad_hidden = local_backward([final], rot_block, (groups,), after=(scale1,))
     return grad_hidden, buffer, jnp.concatenate([scale0, scale1], axis=0)
 
 

time: 228 us -> 223 us (0.978)
  waiting for transfers between devices: 73.4 us -> 64.5 us
  Pallas kernels: 87 us -> 92.4 us
  local copies, waits for them, and re-layouts: 17.4 us -> 12.3 us
  starting transfers between devices: 45.2 us -> 48.5 us
    ppermute x23, waiting for transfers between devices: 69.1 us -> 54.8 us  [partner(): return lax.ppermute(value, axis, [(i, i ^ mask) for i in range(size)])]
    all_to_all x4, waiting for transfers between devices: 4.34 us -> 9.64 us  [exchange(): lax.all_to_all(value, 'tensor', split_axis=0, concat_axis=0, tiled=True)]
    unnamed x24, local copies, waits for them, and re-layouts: 6.16 us -> 2.96 us
    pallas_call x2, Pallas kernels: 30.7 us -> 33.3 us  [weight_grads(): pl.pallas_call(functools.partial(weights_kernel, first, per, len(rotated)...]
  transfers between devices with their start and end apart: 27 -> 27, of which waited for: 12 -> 10; matrix products, arithmetic and copies ran while one was open for 6% -> 5% of each run, Pallas kernels for 36% -> 39%
where the time goes in v7:
time: 223 us; the launch traced here: 221 us
  Pallas kernels  92.4 us (41%)
  waiting for transfers between devices  64.5 us (29%)
  starting transfers between devices  48.5 us (22%)
  local copies, waits for them, and re-layouts  12.3 us (6%)
  other arithmetic  2.57 us (1%)
    ppermute x23, waiting for transfers between devices, partner(): return lax.ppermute(value, axis, [(i, i ^ mask) for i in range(size)])  54.8 us
    pallas_call x2, Pallas kernels, weight_grads(): pl.pallas_call(functools.partial(weights_kernel, first, per, len(rotated)...  33.3 us
    ppermute x23, starting transfers between devices, partner(): return lax.ppermute(value, axis, [(i, i ^ mask) for i in range(size)])  28.5 us
    pallas_call x2, Pallas kernels, unit_grads(): pl.pallas_call(drop_inputs(functools.partial(units_kernel, first, per), 3...  26 us
    all_to_all x4, starting transfers between devices, exchange(): lax.all_to_all(value, 'tensor', split_axis=0, concat_axis=0, tiled=True)  20 us
    pallas_call x4, Pallas kernels, small_call(): pl.pallas_call(drop_inputs(kernel, len(ins), len(after)), grid=(steps,),...  11.6 us
    all_to_all x4, waiting for transfers between devices, exchange(): lax.all_to_all(value, 'tensor', split_axis=0, concat_axis=0, tiled=True)  9.64 us
    pallas_call x1, Pallas kernels, local_backward(): pl.pallas_call(drop_inputs(functools.partial(backward_kernel, sizes), len...  5.98 us
  transfers between devices with their start and end apart: 27, of which 10 were waited for; matrix products, arithmetic and copies ran while one was open for 5% of the time, Pallas kernels for 39%

profile of v7, /device:TPU:0, one launch (start us, length us, event | category | flops | bytes accessed | tf_op | source)
XLA Modules:
  0.0 221.2 jit_solution(17921185617487294524)
XLA Ops:
  1.8 3.0 %collective-permute-start = (bf16[64,2048]{1,0:T(8,128)(2,1)S(1)}, bf16[64,2048]{1,0:T(8,128)(2,1)S(1)}, u32[]{:S(2)}, u32[]{:S(2)}) collective-permute-start(bf16[64,2048]{1,0:T(8,128)(2,1)S(1)} %get-tuple-element.43), channel_id=1, source_target_pairs={{0,8},{8,0},{16,24},{24,16},{1,9},{9,1},{17,25},{25,17},{2,10},{10... | collective-permute-start | bytes 786440 | tf_op jit(solution)/shard_map/ppermute | solution.py:354
  6.4 5.9 %local_forward.1 = (bf16[8,8,16,128]{3,2,1,0:T(8,128)(2,1)}, bf16[8,44,16,128]{3,2,1,0:T(8,128)(2,1)}) custom-call(bf16[128,6656]{1,0:T(8,128)(2,1)} %x_ref.1, f32[52,52]{1,0:T(8,128)} %refs_1_.5), custom_call_target="tpu_custom_call" | custom-call | tf_op jit(solution)/shard_map/local_forward/pallas_call | solution.py:147
  12.3 5.3 %all-to-all-start = ((bf16[8,44,16,128]{3,2,1,0:T(8,128)(2,1)}), bf16[8,44,16,128]{3,2,1,0:T(8,128)(2,1)S(1)}, u32[]{:S(2)}, u32[]{:S(2)}) async-start(bf16[8,44,16,128]{3,2,1,0:T(8,128)(2,1)} %get-tuple-element.23.refs_3_), calls=%async_computation | async-start | bytes 2883584 | tf_op jit(solution)/shard_map/all_to_all | solution.py:349
  23.6 13.8 %unit_grads.2 = (bf16[8,28,16,128]{3,2,1,0:T(8,128)(2,1)}, bf16[8,28,16,128]{3,2,1,0:T(8,128)(2,1)}, bf16[8,28,16,128]{3,2,1,0:T(8,128)(2,1)}, bf16[4,28,16,128]{3,2,1,0:T(8,128)(2,1)}, bf16[4,28,16,128]{3,2,1,0:T(8,128)(2,1)}) custom-call(bf16[512,2048]{1,0:T(8,128)(2,1)S(1)} %pad_maximum_fusion.refs_0_.refs_5_, bf16[6656,2048]{1,0:T(8,128)(2,1)} %refs_6_.3, ...), custom_call_target="tpu_custom_call" | custom-call | flops 2000000000 | tf_op jit(solution)/shard_map/unit_grads/pallas_call | solution.py:210
  39.4 12.2 %unit_grads.3 = (bf16[8,24,16,128]{3,2,1,0:T(8,128)(2,1)}, bf16[8,24,16,128]{3,2,1,0:T(8,128)(2,1)}, bf16[8,24,16,128]{3,2,1,0:T(8,128)(2,1)}, bf16[4,24,16,128]{3,2,1,0:T(8,128)(2,1)}, bf16[4,24,16,128]{3,2,1,0:T(8,128)(2,1)}) custom-call(bf16[512,2048]{1,0:T(8,128)(2,1)S(1)} %pad_maximum_fusion.refs_0_.refs_5_, bf16[6656,2048]{1,0:T(8,128)(2,1)} %refs_6_.3, ...), custom_call_target="tpu_custom_call" | custom-call | tf_op jit(solution)/shard_map/unit_grads/pallas_call | solution.py:210
  52.0 1.7 collective-permute-start.9
  53.7 2.8 %relay.2 = (bf16[8,28,16,128]{3,2,1,0:T(8,128)(2,1)}, bf16[8,28,16,128]{3,2,1,0:T(8,128)(2,1)}) custom-call(bf16[8,28,16,128]{3,2,1,0:T(8,128)(2,1)} %get-tuple-element.25.refs_0_, bf16[8,28,16,128]{3,2,1,0:T(8,128)(2,1)} %get-tuple-element.26.refs_1_, bf16[4,28,16,128]{3,2,1,0:T(8,128)(2,1)} %collective-permute-done.4.refs_2_, ...), custom_call_target="tpu_custom_call" | custom-call | tf_op jit(solution)/shard_map/relay/pallas_call | solution.py:303
  58.0 2.6 %collective-permute-start.10 = (bf16[8,8,16,128]{3,2,1,0:T(8,128)(2,1)}, bf16[8,8,16,128]{3,2,1,0:T(8,128)(2,1)}, u32[]{:S(2)}, u32[]{:S(2)}) collective-permute-start(bf16[8,8,16,128]{3,2,1,0:T(8,128)(2,1)} %gate.5.refs_0_), channel_id=1, source_target_pairs={{0,4},{1,5},{2,6},{3,7},{4,0},{5,1},{6,2},{7,3},{8,12},{9,13},{10,... | collective-permute-start | bytes 786440 | tf_op jit(solution)/shard_map/ppermute | solution.py:354
  61.1 2.1 transform.2.refs_3_
  63.2 4.3 %all-to-all-start.1 = ((bf16[8,44,16,128]{3,2,1,0:T(8,128)(2,1)}), bf16[8,44,16,128]{3,2,1,0:T(8,128)(2,1)}, u32[]{:S(2)}, u32[]{:S(2)}) async-start(bf16[8,44,16,128]{3,2,1,0:T(8,128)(2,1)} %transform.2.refs_3_), calls=%async_computation.1 | async-start | bytes 2883584 | tf_op jit(solution)/shard_map/all_to_all | solution.py:349
  67.5 4.4 %collective-permute-done.10.refs_1_ = bf16[8,8,16,128]{3,2,1,0:T(8,128)(2,1)} collective-permute-done((bf16[8,8,16,128]{3,2,1,0:T(8,128)(2,1)}, bf16[8,8,16,128]{3,2,1,0:T(8,128)(2,1)}, u32[]{:S(2)}, u32[]{:S(2)}) %collective-permute-start.10) | collective-permute-done | bytes 262176 | tf_op jit(solution)/shard_map/ppermute | solution.py:354
  72.0 1.8 butterfly.3.refs_4_.refs_0_
  73.8 2.6 %relay.3 = (bf16[8,24,16,128]{3,2,1,0:T(8,128)(2,1)}, bf16[8,24,16,128]{3,2,1,0:T(8,128)(2,1)}) custom-call(bf16[8,24,16,128]{3,2,1,0:T(8,128)(2,1)} %get-tuple-element.32.refs_0_, bf16[8,24,16,128]{3,2,1,0:T(8,128)(2,1)} %get-tuple-element.33.refs_1_, bf16[4,24,16,128]{3,2,1,0:T(8,128)(2,1)} %collective-permute-done.8.refs_2_, ...), custom_call_target="tpu_custom_call" | custom-call | flops 999999995904 | tf_op jit(solution)/shard_map/relay/pallas_call | solution.py:303
  77.2 6.2 %collective-permute-start.13 = (bf16[8,8,16,128]{3,2,1,0:T(8,128)(2,1)S(1)}, bf16[8,8,16,128]{3,2,1,0:T(8,128)(2,1)S(1)}, u32[]{:S(2)}, u32[]{:S(2)}) collective-permute-start(bf16[8,8,16,128]{3,2,1,0:T(8,128)(2,1)S(1)} %copy-done.6), channel_id=1, source_target_pairs={{0,2},{1,3},{2,0},{3,1},{4,6},{5,7},{6,4},{7,5},{8,10},{9,11},{10,... | collective-permute-start | bytes 786440 | tf_op jit(solution)/shard_map/ppermute | solution.py:354
  83.4 13.9 %collective-permute-done.13.refs_1_ = bf16[8,8,16,128]{3,2,1,0:T(8,128)(2,1)S(1)} collective-permute-done((bf16[8,8,16,128]{3,2,1,0:T(8,128)(2,1)S(1)}, bf16[8,8,16,128]{3,2,1,0:T(8,128)(2,1)S(1)}, u32[]{:S(2)}, u32[]{:S(2)}) %collective-permute-start.13) | collective-permute-done | bytes 262176 | tf_op jit(solution)/shard_map/ppermute | solution.py:354
  97.4 1.7 butterfly.4.refs_0_
  99.0 1.7 collective-permute-done.14.refs_1_
  100.8 1.7 butterfly.5.refs_6_
  102.5 4.4 %total.1.refs_0_ = bf16[8,52,16,128]{3,2,1,0:T(8,128)(2,1)} custom-call(bf16[8,28,16,128]{3,2,1,0:T(8,128)(2,1)} %get-tuple-element.24.refs_3_.refs_0_, bf16[8,28,16,128]{3,2,1,0:T(8,128)(2,1)} %collective-permute-done.6.refs_1_, bf16[8,28,16,128]{3,2,1,0:T(8,128)(2,1)} %collective-permute-done.7.refs_2_, ...), custom_call_target="tpu_custom_call" | custom-call | tf_op jit(solution)/shard_map/total/pallas_call | solution.py:422
  106.9 5.9 %all-to-all-start.2 = ((bf16[8,52,16,128]{3,2,1,0:T(8,128)(2,1)}), bf16[8,52,16,128]{3,2,1,0:T(8,128)(2,1)}, u32[]{:S(2)}, u32[]{:S(2)}) async-start(bf16[8,52,16,128]{3,2,1,0:T(8,128)(2,1)} %gate.6), calls=%async_computation.2 | async-start | bytes 3407872 | tf_op jit(solution)/shard_map/all_to_all | solution.py:349
  115.2 1.5 collective-permute-start.15
  116.7 23.1 %collective-permute-done.17.refs_1_ = bf16[8,32,16,128]{3,2,1,0:T(8,128)(2,1)S(1)} collective-permute-done((bf16[8,32,16,128]{3,2,1,0:T(8,128)(2,1)S(1)}, bf16[8,32,16,128]{3,2,1,0:T(8,128)(2,1)S(1)}, u32[]{:S(2)}, u32[]{:S(2)}) %collective-permute-start.17) | collective-permute-done | bytes 1048608 | tf_op jit(solution)/shard_map/ppermute | solution.py:354
  140.8 1.5 collective-permute-start.18
  144.0 9.6 %all-to-all-done.2.refs_0_ = bf16[8,52,16,128]{3,2,1,0:T(8,128)(2,1)} async-done(((bf16[8,52,16,128]{3,2,1,0:T(8,128)(2,1)}), bf16[8,52,16,128]{3,2,1,0:T(8,128)(2,1)}, u32[]{:S(2)}, u32[]{:S(2)}) %all-to-all-start.2) | async-done | bytes 1703968 | tf_op jit(solution)/shard_map/all_to_all | solution.py:349
  153.6 4.0 %transform.3.refs_3_.refs_9_ = bf16[8,52,16,128]{3,2,1,0:T(8,128)(2,1)} custom-call(bf16[8,52,16,128]{3,2,1,0:T(8,128)(2,1)} %all-to-all-done.2.refs_0_), custom_call_target="tpu_custom_call" | custom-call | flops 999999995904 | tf_op jit(solution)/shard_map/transform/pallas_call | solution.py:303
  157.6 4.5 %all-to-all-start.3 = ((bf16[8,52,16,128]{3,2,1,0:T(8,128)(2,1)}), bf16[8,52,16,128]{3,2,1,0:T(8,128)(2,1)}, u32[]{:S(2)}, u32[]{:S(2)}) async-start(bf16[8,52,16,128]{3,2,1,0:T(8,128)(2,1)} %transform.3.refs_3_.refs_9_), calls=%async_computation.3 | async-start | bytes 3407872 | tf_op jit(solution)/shard_map/all_to_all | solution.py:349
  162.1 2.1 slice.27.refs_0_
  166.2 19.6 %weight_grads.2 = (bf16[6656,2048]{1,0:T(8,128)(2,1)}, f32[32,2048]{1,0:T(8,128)S(1)}) custom-call(bf16[8,32,16,128]{3,2,1,0:T(8,128)(2,1)} %copy-done.5, bf16[8,32,16,128]{3,2,1,0:T(8,128)(2,1)} %copy-done.10, bf16[8,32,16,128]{3,2,1,0:T(8,128)(2,1)} %copy-done.11, bf16[4,32,16,128]{3,2,1,0:T(8,128)(2,1)} %collective-permute-done.16.refs_1_.refs_3_, ...), custom_call_target="tpu_custom_call" | custom-call | flops 25999998976 | tf_op jit(solution)/shard_map/weight_grads/pallas_call | solution.py:277
  189.4 1.6 collective-permute-start.21
  191.4 7.2 %collective-permute-done.21.refs_3_ = bf16[4,20,16,128]{3,2,1,0:T(8,128)(2,1)S(1)} collective-permute-done((bf16[4,20,16,128]{3,2,1,0:T(8,128)(2,1)S(1)}, bf16[4,20,16,128]{3,2,1,0:T(8,128)(2,1)S(1)}, u32[]{:S(2)}, u32[]{:S(2)}) %collective-permute-start.21) | collective-permute-done | bytes 327712 | tf_op jit(solution)/shard_map/ppermute | solution.py:354
  200.6 13.7 %weight_grads.3 = (bf16[6656,2048]{1,0:T(8,128)(2,1)}, f32[20,2048]{1,0:T(8,128)S(1)}) custom-call(bf16[8,20,16,128]{3,2,1,0:T(8,128)(2,1)} %slice.27.refs_0_, bf16[8,20,16,128]{3,2,1,0:T(8,128)(2,1)} %gate.8.refs_1_, bf16[8,20,16,128]{3,2,1,0:T(8,128)(2,1)} %gate.9.refs_2_, bf16[4,20,16,128]{3,2,1,0:T(8,128)(2,1)} %copy-done.8, ...), custom_call_target="tpu_custom_call", output_to_operand_aliasing={{0}: (9, {})} | custom-call | tf_op jit(solution)/shard_map/weight_grads/pallas_call | solution.py:277
  215.2 6.0 %local_backward.1 = bf16[128,6656]{1,0:T(8,128)(2,1)} custom-call(bf16[8,52,16,128]{3,2,1,0:T(8,128)(2,1)} %all-to-all-done.3.refs_0_, f32[52,52]{1,0:T(8,128)} %refs_1_.5, f32[20,2048]{1,0:T(8,128)} %copy-done.2), custom_call_target="tpu_custom_call" | custom-call | tf_op jit(solution)/shard_map/local_backward/pallas_call | solution.py:168
  (79 shorter events, 27.6 us)
Async XLA Ops:
  1.8 15.8 %collective-permute-start = (bf16[64,2048]{1,0:T(8,128)(2,1)S(1)}, bf16[64,2048]{1,0:T(8,128)(2,1)S(1)}, u32[]{:S(2)}, u32[]{:S(2)}) collective-permute-start(bf16[64,2048]{1,0:T(8,128)(2,1)S(1)} %get-tuple-element.43), channel_id=1, source_target_pairs={{0,8},{8,0},{16,24},{24,16},{1,9},{9,1},{17,25},{25,17},{2,10},{10... | collective-permute-start | bytes 786440 | tf_op jit(solution)/shard_map/ppermute | solution.py:354
  4.9 13.2 %collective-permute-start.2 = (bf16[64,2048]{1,0:T(8,128)(2,1)S(1)}, bf16[64,2048]{1,0:T(8,128)(2,1)S(1)}, u32[]{:S(2)}, u32[]{:S(2)}) collective-permute-start(bf16[64,2048]{1,0:T(8,128)(2,1)S(1)} %get-tuple-element.44), channel_id=1, source_target_pairs={{0,24},{8,16},{16,8},{24,0},{1,25},{9,17},{17,9},{25,1},{2,26},{10... | collective-permute-start | bytes 786440 | tf_op jit(solution)/shard_map/ppermute | solution.py:354
  6.3 13.1 %collective-permute-start.1 = (bf16[64,2048]{1,0:T(8,128)(2,1)S(1)}, bf16[64,2048]{1,0:T(8,128)(2,1)S(1)}, u32[]{:S(2)}, u32[]{:S(2)}) collective-permute-start(bf16[64,2048]{1,0:T(8,128)(2,1)S(1)} %get-tuple-element.45), channel_id=1, source_target_pairs={{0,16},{8,24},{16,0},{24,8},{1,17},{9,25},{17,1},{25,9},{2,18},{10... | collective-permute-start | bytes 786440 | tf_op jit(solution)/shard_map/ppermute | solution.py:354
  12.3 48.8 %all-to-all-start = ((bf16[8,44,16,128]{3,2,1,0:T(8,128)(2,1)}), bf16[8,44,16,128]{3,2,1,0:T(8,128)(2,1)S(1)}, u32[]{:S(2)}, u32[]{:S(2)}) async-start(bf16[8,44,16,128]{3,2,1,0:T(8,128)(2,1)} %get-tuple-element.23.refs_3_), calls=%async_computation | async-start | bytes 2883584 | tf_op jit(solution)/shard_map/all_to_all | solution.py:349
  19.4 1.3 copy-start.7
  19.5 2.5 %collective-permute-start.3 = (bf16[3,64,2048]{2,1,0:T(8,128)(2,1)S(1)}, bf16[3,64,2048]{2,1,0:T(8,128)(2,1)}, u32[]{:S(2)}, u32[]{:S(2)}) collective-permute-start(bf16[3,64,2048]{2,1,0:T(8,128)(2,1)S(1)} %pad_maximum_fusion.3), channel_id=1, source_target_pairs={{0,1},{1,0},{2,3},{3,2},{4,5},{5,4},{6,7},{7,6},{8,9},{9,8},{10,11... | collective-permute-start | bytes 2359304 | tf_op jit(solution)/shard_map/ppermute | solution.py:354
  37.4 16.3 %collective-permute-start.4 = (bf16[4,28,16,128]{3,2,1,0:T(8,128)(2,1)}, bf16[4,28,16,128]{3,2,1,0:T(8,128)(2,1)}, u32[]{:S(2)}, u32[]{:S(2)}) collective-permute-start(bf16[4,28,16,128]{3,2,1,0:T(8,128)(2,1)} %get-tuple-element.27), channel_id=1, source_target_pairs={{0,8},{8,0},{16,24},{24,16},{1,9},{9,1},{17,25},{25,17},{2,10},{10... | collective-permute-start | bytes 1376264 | tf_op jit(solution)/shard_map/ppermute | solution.py:354
  38.9 14.8 %collective-permute-start.5 = (bf16[4,28,16,128]{3,2,1,0:T(8,128)(2,1)}, bf16[4,28,16,128]{3,2,1,0:T(8,128)(2,1)}, u32[]{:S(2)}, u32[]{:S(2)}) collective-permute-start(bf16[4,28,16,128]{3,2,1,0:T(8,128)(2,1)} %get-tuple-element.28), channel_id=1, source_target_pairs={{0,16},{8,24},{16,0},{24,8},{1,17},{9,25},{17,1},{25,9},{2,18},{10... | collective-permute-start | bytes 1376264 | tf_op jit(solution)/shard_map/ppermute | solution.py:354
  51.6 22.1 %collective-permute-start.8 = (bf16[4,24,16,128]{3,2,1,0:T(8,128)(2,1)}, bf16[4,24,16,128]{3,2,1,0:T(8,128)(2,1)}, u32[]{:S(2)}, u32[]{:S(2)}) collective-permute-start(bf16[4,24,16,128]{3,2,1,0:T(8,128)(2,1)} %get-tuple-element.34), channel_id=1, source_target_pairs={{0,8},{8,0},{16,24},{24,16},{1,9},{9,1},{17,25},{25,17},{2,10},{10... | collective-permute-start | bytes 1179656 | tf_op jit(solution)/shard_map/ppermute | solution.py:354
  52.0 21.7 %collective-permute-start.9 = (bf16[4,24,16,128]{3,2,1,0:T(8,128)(2,1)}, bf16[4,24,16,128]{3,2,1,0:T(8,128)(2,1)}, u32[]{:S(2)}, u32[]{:S(2)}) collective-permute-start(bf16[4,24,16,128]{3,2,1,0:T(8,128)(2,1)} %get-tuple-element.35), channel_id=1, source_target_pairs={{0,16},{8,24},{16,0},{24,8},{1,17},{9,25},{17,1},{25,9},{2,18},{10... | collective-permute-start | bytes 1179656 | tf_op jit(solution)/shard_map/ppermute | solution.py:354
  56.5 46.0 %collective-permute-start.6 = (bf16[8,28,16,128]{3,2,1,0:T(8,128)(2,1)}, bf16[8,28,16,128]{3,2,1,0:T(8,128)(2,1)}, u32[]{:S(2)}, u32[]{:S(2)}) collective-permute-start(bf16[8,28,16,128]{3,2,1,0:T(8,128)(2,1)} %get-tuple-element.30.refs_1_), channel_id=1, source_target_pairs={{0,8},{8,0},{16,24},{24,16},{1,9},{9,1},{17,25},{25,17},{2,10},{10... | collective-permute-start | bytes 2752520 | tf_op jit(solution)/shard_map/ppermute | solution.py:354
  58.0 13.9 %collective-permute-start.10 = (bf16[8,8,16,128]{3,2,1,0:T(8,128)(2,1)}, bf16[8,8,16,128]{3,2,1,0:T(8,128)(2,1)}, u32[]{:S(2)}, u32[]{:S(2)}) collective-permute-start(bf16[8,8,16,128]{3,2,1,0:T(8,128)(2,1)} %gate.5.refs_0_), channel_id=1, source_target_pairs={{0,4},{1,5},{2,6},{3,7},{4,0},{5,1},{6,2},{7,3},{8,12},{9,13},{10,... | collective-permute-start | bytes 786440 | tf_op jit(solution)/shard_map/ppermute | solution.py:354
  60.6 41.9 %collective-permute-start.7 = (bf16[8,28,16,128]{3,2,1,0:T(8,128)(2,1)}, bf16[8,28,16,128]{3,2,1,0:T(8,128)(2,1)}, u32[]{:S(2)}, u32[]{:S(2)}) collective-permute-start(bf16[8,28,16,128]{3,2,1,0:T(8,128)(2,1)} %get-tuple-element.31), channel_id=1, source_target_pairs={{0,16},{8,24},{16,0},{24,8},{1,17},{9,25},{17,1},{25,9},{2,18},{10... | collective-permute-start | bytes 2752520 | tf_op jit(solution)/shard_map/ppermute | solution.py:354
  63.2 43.7 %all-to-all-start.1 = ((bf16[8,44,16,128]{3,2,1,0:T(8,128)(2,1)}), bf16[8,44,16,128]{3,2,1,0:T(8,128)(2,1)}, u32[]{:S(2)}, u32[]{:S(2)}) async-start(bf16[8,44,16,128]{3,2,1,0:T(8,128)(2,1)} %transform.2.refs_3_), calls=%async_computation.1 | async-start | bytes 2883584 | tf_op jit(solution)/shard_map/all_to_all | solution.py:349
  73.8 3.5 %copy-start.6 = (bf16[8,8,16,128]{3,2,1,0:T(8,128)(2,1)S(1)}, bf16[8,8,16,128]{3,2,1,0:T(8,128)(2,1)}, u32[]{:S(2)}) copy-start(bf16[8,8,16,128]{3,2,1,0:T(8,128)(2,1)} %butterfly.3.refs_4_.refs_0_) | copy-start | bytes 786436
  76.4 26.1 %collective-permute-start.12 = (bf16[8,24,16,128]{3,2,1,0:T(8,128)(2,1)}, bf16[8,24,16,128]{3,2,1,0:T(8,128)(2,1)S(1)}, u32[]{:S(2)}, u32[]{:S(2)}) collective-permute-start(bf16[8,24,16,128]{3,2,1,0:T(8,128)(2,1)} %get-tuple-element.38), channel_id=1, source_target_pairs={{0,16},{8,24},{16,0},{24,8},{1,17},{9,25},{17,1},{25,9},{2,18},{10... | collective-permute-start | bytes 2359304 | tf_op jit(solution)/shard_map/ppermute | solution.py:354
  76.7 25.7 %collective-permute-start.11 = (bf16[8,24,16,128]{3,2,1,0:T(8,128)(2,1)}, bf16[8,24,16,128]{3,2,1,0:T(8,128)(2,1)}, u32[]{:S(2)}, u32[]{:S(2)}) collective-permute-start(bf16[8,24,16,128]{3,2,1,0:T(8,128)(2,1)} %get-tuple-element.37.refs_3_), channel_id=1, source_target_pairs={{0,8},{8,0},{16,24},{24,16},{1,9},{9,1},{17,25},{25,17},{2,10},{10... | collective-permute-start | bytes 2359304 | tf_op jit(solution)/shard_map/ppermute | solution.py:354
  77.2 20.2 %collective-permute-start.13 = (bf16[8,8,16,128]{3,2,1,0:T(8,128)(2,1)S(1)}, bf16[8,8,16,128]{3,2,1,0:T(8,128)(2,1)S(1)}, u32[]{:S(2)}, u32[]{:S(2)}) collective-permute-start(bf16[8,8,16,128]{3,2,1,0:T(8,128)(2,1)S(1)} %copy-done.6), channel_id=1, source_target_pairs={{0,2},{1,3},{2,0},{3,1},{4,6},{5,7},{6,4},{7,5},{8,10},{9,11},{10,... | collective-permute-start | bytes 786440 | tf_op jit(solution)/shard_map/ppermute | solution.py:354
  99.0 1.7 collective-permute-start.14
  106.9 7.2 %copy-start.4 = (bf16[8,8,16,128]{3,2,1,0:T(8,128)(2,1)S(1)}, bf16[8,8,16,128]{3,2,1,0:T(8,128)(2,1)}, u32[]{:S(2)}) copy-start(bf16[8,8,16,128]{3,2,1,0:T(8,128)(2,1)} %butterfly.5.refs_6_) | copy-start | bytes 786436
  106.9 46.7 %all-to-all-start.2 = ((bf16[8,52,16,128]{3,2,1,0:T(8,128)(2,1)}), bf16[8,52,16,128]{3,2,1,0:T(8,128)(2,1)}, u32[]{:S(2)}, u32[]{:S(2)}) async-start(bf16[8,52,16,128]{3,2,1,0:T(8,128)(2,1)} %gate.6), calls=%async_computation.2 | async-start | bytes 3407872 | tf_op jit(solution)/shard_map/all_to_all | solution.py:349
  114.2 25.6 %collective-permute-start.17 = (bf16[8,32,16,128]{3,2,1,0:T(8,128)(2,1)S(1)}, bf16[8,32,16,128]{3,2,1,0:T(8,128)(2,1)S(1)}, u32[]{:S(2)}, u32[]{:S(2)}) collective-permute-start(bf16[8,32,16,128]{3,2,1,0:T(8,128)(2,1)S(1)} %pad_maximum_fusion.2.refs_0_), channel_id=1, source_target_pairs={{0,8},{8,0},{16,24},{24,16},{1,9},{9,1},{17,25},{25,17},{2,10},{10... | collective-permute-start | bytes 3145736 | tf_op jit(solution)/shard_map/ppermute | solution.py:354
  115.2 27.1 %collective-permute-start.15 = (bf16[8,32,16,128]{3,2,1,0:T(8,128)(2,1)S(1)}, bf16[8,32,16,128]{3,2,1,0:T(8,128)(2,1)S(1)}, u32[]{:S(2)}, u32[]{:S(2)}) collective-permute-start(bf16[8,32,16,128]{3,2,1,0:T(8,128)(2,1)S(1)} %pad_maximum_fusion.2.refs_0_), channel_id=1, source_target_pairs={{0,16},{8,24},{16,0},{24,8},{1,17},{9,25},{17,1},{25,9},{2,18},{10... | collective-permute-start | bytes 3145736 | tf_op jit(solution)/shard_map/ppermute | solution.py:354
  139.9 2.4 %copy-start.10 = (bf16[8,32,16,128]{3,2,1,0:T(8,128)(2,1)}, bf16[8,32,16,128]{3,2,1,0:T(8,128)(2,1)S(1)}, u32[]{:S(2)}) copy-start(bf16[8,32,16,128]{3,2,1,0:T(8,128)(2,1)S(1)} %collective-permute-done.17.refs_1_) | copy-start | bytes 3145732
  140.8 21.3 %collective-permute-start.18 = (bf16[4,32,16,128]{3,2,1,0:T(8,128)(2,1)}, bf16[4,32,16,128]{3,2,1,0:T(8,128)(2,1)}, u32[]{:S(2)}, u32[]{:S(2)}) collective-permute-start(bf16[4,32,16,128]{3,2,1,0:T(8,128)(2,1)} %slice.26), channel_id=1, source_target_pairs={{0,16},{8,24},{16,0},{24,8},{1,17},{9,25},{17,1},{25,9},{2,18},{10... | collective-permute-start | bytes 1572872 | tf_op jit(solution)/shard_map/ppermute | solution.py:354
  143.4 18.6 %collective-permute-start.16 = (bf16[4,32,16,128]{3,2,1,0:T(8,128)(2,1)}, bf16[4,32,16,128]{3,2,1,0:T(8,128)(2,1)}, u32[]{:S(2)}, u32[]{:S(2)}) collective-permute-start(bf16[4,32,16,128]{3,2,1,0:T(8,128)(2,1)} %slice.25), channel_id=1, source_target_pairs={{0,8},{8,0},{16,24},{24,16},{1,9},{9,1},{17,25},{25,17},{2,10},{10... | collective-permute-start | bytes 1572872 | tf_op jit(solution)/shard_map/ppermute | solution.py:354
  157.6 57.6 %all-to-all-start.3 = ((bf16[8,52,16,128]{3,2,1,0:T(8,128)(2,1)}), bf16[8,52,16,128]{3,2,1,0:T(8,128)(2,1)}, u32[]{:S(2)}, u32[]{:S(2)}) async-start(bf16[8,52,16,128]{3,2,1,0:T(8,128)(2,1)} %transform.3.refs_3_.refs_9_), calls=%async_computation.3 | async-start | bytes 3407872 | tf_op jit(solution)/shard_map/all_to_all | solution.py:349
  164.2 23.4 %collective-permute-start.20 = (bf16[8,20,16,128]{3,2,1,0:T(8,128)(2,1)}, bf16[8,20,16,128]{3,2,1,0:T(8,128)(2,1)S(1)}, u32[]{:S(2)}, u32[]{:S(2)}) collective-permute-start(bf16[8,20,16,128]{3,2,1,0:T(8,128)(2,1)} %slice.27.refs_0_), channel_id=1, source_target_pairs={{0,16},{8,24},{16,0},{24,8},{1,17},{9,25},{17,1},{25,9},{2,18},{10... | collective-permute-start | bytes 1966088 | tf_op jit(solution)/shard_map/ppermute | solution.py:354
  165.7 20.8 %collective-permute-start.19 = (bf16[8,20,16,128]{3,2,1,0:T(8,128)(2,1)}, bf16[8,20,16,128]{3,2,1,0:T(8,128)(2,1)}, u32[]{:S(2)}, u32[]{:S(2)}) collective-permute-start(bf16[8,20,16,128]{3,2,1,0:T(8,128)(2,1)} %slice.27.refs_0_), channel_id=1, source_target_pairs={{0,8},{8,0},{16,24},{24,16},{1,9},{9,1},{17,25},{25,17},{2,10},{10... | collective-permute-start | bytes 1966088 | tf_op jit(solution)/shard_map/ppermute | solution.py:354
  189.4 9.3 %collective-permute-start.21 = (bf16[4,20,16,128]{3,2,1,0:T(8,128)(2,1)S(1)}, bf16[4,20,16,128]{3,2,1,0:T(8,128)(2,1)S(1)}, u32[]{:S(2)}, u32[]{:S(2)}) collective-permute-start(bf16[4,20,16,128]{3,2,1,0:T(8,128)(2,1)S(1)} %slice.28), channel_id=1, source_target_pairs={{0,8},{8,0},{16,24},{24,16},{1,9},{9,1},{17,25},{25,17},{2,10},{10... | collective-permute-start | bytes 983048 | tf_op jit(solution)/shard_map/ppermute | solution.py:354
  190.9 9.0 %collective-permute-start.22 = (bf16[4,20,16,128]{3,2,1,0:T(8,128)(2,1)S(1)}, bf16[4,20,16,128]{3,2,1,0:T(8,128)(2,1)S(1)}, u32[]{:S(2)}, u32[]{:S(2)}) collective-permute-start(bf16[4,20,16,128]{3,2,1,0:T(8,128)(2,1)S(1)} %slice.29), channel_id=1, source_target_pairs={{0,16},{8,24},{16,0},{24,8},{1,17},{9,25},{17,1},{25,9},{2,18},{10... | collective-permute-start | bytes 983048 | tf_op jit(solution)/shard_map/ppermute | solution.py:354
  200.6 13.7 %copy-start.1 = (f32[32,2048]{1,0:T(8,128)S(1)}, f32[32,2048]{1,0:T(8,128)}, u32[]{:S(2)}) copy-start(f32[32,2048]{1,0:T(8,128)} %copy-done) | copy-start | bytes 786436
  (7 other events, 6.5 us)

commit v8 on v5

--- a/solution.py
+++ b/solution.py
@@ -21,10 +21,6 @@
 
 def nn_dot(a, b):
     return lax.dot_general(a, b, (((1,), (0,)), ((), ())), preferred_element_type=F32)
-
-
-def tn_dot(a, b):
-    return lax.dot_general(a, b, (((0,), (0,)), ((), ())), preferred_element_type=F32)
 
 
 def split2(value):
@@ -90,13 +86,8 @@
 
 
 def backward_kernel(sizes, *refs):
-    ins, (rot_ref, out_ref, high_ref, low_ref, sign_ref) = refs[: len(sizes)], refs[len(sizes) :]
-    blocks = rot_ref.shape[0]
-
-    @pl.when(pl.program_id(0) == 0)
-    def _():
-        build_mixing(rot_ref, high_ref, low_ref, sign_ref, False)
-
+    ins, (high_ref, low_ref, sign_ref, out_ref) = refs[: len(sizes)], refs[len(sizes) :]
+    blocks = sum(sizes)
     rows = out_ref.shape[0]
     tiles = []
     for j in range(rows // SUB):
@@ -122,7 +113,7 @@
 FREE = pl.CostEstimate(flops=0, bytes_accessed=0, transcendentals=0)
 LONG = pl.CostEstimate(flops=10**12, bytes_accessed=0, transcendentals=0)
 SOME = pl.CostEstimate(flops=5_000_000_000, bytes_accessed=0, transcendentals=0)
-SMALL = 12 << 20
+SMALL = 16 << 20
 
 ANYWHERE = pl.BlockSpec(memory_space=pl.ANY)
 
@@ -158,24 +149,39 @@
     )(*in_hbm(hidden), rot_block)
 
 
-def local_backward(mixed, rot_block, sizes, after=()):
+def backward_matrices(rot_block, after=()):
+    size = rot_block.shape[0] * ROWS
+    shapes = [(size, size), (size, size), (HB, HB)]
+    return pl.pallas_call(
+        drop_inputs(
+            lambda rot_ref, *refs: build_mixing(rot_ref, *refs, False), 1, len(after)
+        ),
+        in_specs=[pl.BlockSpec(memory_space=pltpu.VMEM)] + [ANYWHERE] * len(after),
+        out_specs=[pl.BlockSpec(memory_space=pltpu.VMEM)] * 3,
+        out_shape=[pltpu.HBM(shape, BF16) for shape in shapes],
+        compiler_params=pltpu.CompilerParams(vmem_limit_bytes=SMALL),
+        cost_estimate=FREE,
+        name="backward_matrices",
+    )(rot_block, *after)
+
+
+def local_backward(mixed, matrices, sizes, after=()):
     count = mixed[0].shape[0]
     rows = count * SUB
-    blocks = rot_block.shape[0]
+    blocks = sum(sizes)
     parts = 2
     return pl.pallas_call(
-        drop_inputs(functools.partial(backward_kernel, sizes), len(sizes) + 1, len(after)),
+        drop_inputs(functools.partial(backward_kernel, sizes), len(sizes) + 3, len(after)),
         grid=(count // parts,),
         in_specs=[pl.BlockSpec((parts, size, SUB, HB), lambda i: (i, 0, 0, 0)) for size in sizes]
-        + [pl.BlockSpec((blocks, blocks), lambda i: (0, 0))]
+        + [pl.BlockSpec(value.shape, lambda i: (0, 0)) for value in matrices]
         + [ANYWHERE] * len(after),
         out_specs=pl.BlockSpec((parts * SUB, blocks * HB), lambda i: (i, 0)),
         out_shape=pltpu.HBM((rows, blocks * HB), BF16),
-        scratch_shapes=local_scratch(blocks),
-        compiler_params=pltpu.CompilerParams(vmem_limit_bytes=60 << 20),
+        compiler_params=pltpu.CompilerParams(vmem_limit_bytes=24 << 20),
         cost_estimate=FREE,
         name="local_backward",
-    )(*mixed, rot_block, *in_hbm(*after))
+    )(*mixed, *in_hbm(*matrices, *after))
 
 
 def units_kernel(first, per, up_ref, w_ref, s_ref, *refs):
@@ -230,12 +236,12 @@
             for g in range(per)
         ],
         axis=1,
-    )
+    ).T
     cols = up_ref.shape[1]
     tile = min(256, cols)
     for e in range(cols // tile):
         span = slice(e * tile, (e + 1) * tile)
-        grad = tn_dot(left, up_ref[:, span])
+        grad = nn_dot(left, up_ref[:, span])
         for g in range(per):
             rows = slice(g * GROUP, (g + 1) * GROUP)
             piece = grad[rows]
@@ -251,8 +257,12 @@
     tokens, cols = up.shape
     offset = first // per
     specs = [
-        pl.BlockSpec((piece.shape[0], per, SUB, HB), lambda i: (0, offset + i, 0, 0))
+        pl.BlockSpec(
+            (piece.shape[0], per, SUB, HB),
+            functools.partial(lambda place, i: (0, place + i, 0, 0), place),
+        )
         for piece in rotated
+        for place in ((0 if piece.shape[1] == size else offset),)
     ] + [
         pl.BlockSpec((tokens, cols), lambda i: (0, 0)),
         pl.BlockSpec((per * GROUP, cols), lambda i: (offset + i, 0)),
@@ -301,6 +311,32 @@
         cost_estimate=cost,
         name=name,
     )(*ins, *in_hbm(*after))
+
+
+def cut_kernel(start, x_ref, y_ref, x_out, y_out):
+    size = x_out.shape[1]
+    x_out[...] = x_ref[:, start : start + size]
+    y_out[...] = y_ref[:, start : start + size]
+
+
+def cut(x_part, y_part, start, size, after):
+    subs, groups = x_part.shape[:2]
+    half = subs // 2
+    out = pl.BlockSpec((2, size, SUB, HB), lambda i: (i, 0, 0, 0))
+    return pl.pallas_call(
+        drop_inputs(functools.partial(cut_kernel, start), 2, len(after)),
+        grid=(half // 2,),
+        in_specs=[
+            pl.BlockSpec((2, groups, SUB, HB), lambda i: (half // 2 + i, 0, 0, 0)),
+            pl.BlockSpec((2, groups, SUB, HB), lambda i: (i, 0, 0, 0)),
+        ]
+        + [ANYWHERE] * len(after),
+        out_specs=[out, out],
+        out_shape=[pltpu.HBM((half, size, SUB, HB), BF16)] * 2,
+        compiler_params=pltpu.CompilerParams(vmem_limit_bytes=SMALL),
+        cost_estimate=FREE,
+        name="cut",
+    )(x_part, y_part, *in_hbm(*after))
 
 
 def gate(value, after):
@@ -438,7 +474,7 @@
     grad_weight, grad_scales = weight_grads(
         [rotated], up, weight, scales, clip_mask, None, 0, groups, per
     )
-    grad_hidden = local_backward([mixed], rot_block, (groups,))
+    grad_hidden = local_backward([mixed], backward_matrices(rot_block), (groups,))
     return grad_hidden, grad_weight, grad_scales
 
 
@@ -469,11 +505,9 @@
         )
         return x_part, partner(x_part, "dp", 1), partner(y_part, "dp", 2)
 
-    def gather(value):
-        x_part, y_part = partner(value, "dp", 1), partner(value, "dp", 2)
-        return value, x_part, y_part, partner(y_part[:half], "dp", 1), partner(
-            x_part[half:], "dp", 2
-        )
+    def gather_rest(near, chunk, after):
+        x_half, y_half = cut(near[1], near[2], starts[chunk], sizes[chunk], after)
+        return *near, partner(y_half, "dp", 1), partner(x_half, "dp", 2)
 
     up = gather_upstream(upstream)
     (local,) = local_forward(hidden, rot_block, (groups,))
@@ -489,17 +523,20 @@
     rotated = exchange(turned)
     relayed1, *second1 = scatter_second(unit1, first1, after=(turned,), cost=LONG)
     summed = gate(total(((unit0[0], *second0), (unit1[0], *second1))), after=(rotated,))
+    matrices = backward_matrices(rot_block, after=(relayed1,))
     back = exchange(summed)
-    gathered = gather(rotated)
+    near = (rotated, partner(rotated, "dp", 1), partner(rotated, "dp", 2))
+    gathered0 = gather_rest(near, 0, ())
     mixed = transform(back, cost=LONG)
     final = exchange(mixed)
+    gathered1 = gather_rest(near, 1, (mixed,))
     buffer, scale0 = weight_grads(
-        gathered, up, weight, scales, clip_mask, None, starts[0], sizes[0], per, after=(mixed,)
+        gathered0, up, weight, scales, clip_mask, None, starts[0], sizes[0], per, after=(mixed,)
     )
     buffer, scale1 = weight_grads(
-        gathered, up, weight, scales, clip_mask, buffer, starts[1], sizes[1], per
+        gathered1, up, weight, scales, clip_mask, buffer, starts[1], sizes[1], per
     )
-    grad_hidden = local_backward([final], rot_block, (groups,), after=(scale1,))
+    grad_hidden = local_backward([final], matrices, (groups,), after=(scale1,))
     return grad_hidden, buffer, jnp.concatenate([scale0, scale1], axis=0)
 
 

time: 215 us -> 209 us (0.972)
  waiting for transfers between devices: 82.9 us -> 76.3 us
  local copies, waits for them, and re-layouts: 7.89 us -> 3.44 us
  Pallas kernels: 81.8 us -> 84.8 us
    ppermute x16 -> x18, waiting for transfers between devices: 79.1 us -> 66.4 us  [partner(): return lax.ppermute(value, axis, [(i, i ^ mask) for i in range(size)])]
    all_to_all x4, waiting for transfers between devices: 3.72 us -> 9.88 us  [exchange(): lax.all_to_all(value, 'tensor', split_axis=0, concat_axis=0, tiled=True)]
    pallas_call x0 -> x3, Pallas kernels: none -> 3.37 us  [the longest x2 1.97 us: cut(): pl.pallas_call(drop_inputs(functools.partial(cut_kernel, start), 2, len(a...]
    slice x2 -> x0, local copies, waits for them, and re-layouts: 2.42 us -> none  [the longest x1 1.22 us: gather(): x_part[half:]]
    ppermute x16 -> x18, starting transfers between devices: 19.8 us -> 21.5 us  [partner(): return lax.ppermute(value, axis, [(i, i ^ mask) for i in range(size)])]
  transfers between devices with their start and end apart: 20 -> 22, of which waited for: 11 -> 12; matrix products, arithmetic and copies ran while one was open for 3% -> 2% of each run, Pallas kernels for 35% -> 38%
where the time goes in v8:
time: 209 us; the launch traced here: 208 us
  Pallas kernels  84.8 us (41%)
  waiting for transfers between devices  76.3 us (37%)
  starting transfers between devices  39.9 us (19%)
  local copies, waits for them, and re-layouts  3.44 us (2%)
  other arithmetic  2.45 us (1%)
    ppermute x18, waiting for transfers between devices, partner(): return lax.ppermute(value, axis, [(i, i ^ mask) for i in range(size)])  66.4 us
    pallas_call x2, Pallas kernels, weight_grads(): pl.pallas_call(functools.partial(weights_kernel, first, per, len(rotated)...  30.5 us
    pallas_call x2, Pallas kernels, unit_grads(): pl.pallas_call(drop_inputs(functools.partial(units_kernel, first, per), 3...  25.3 us
    ppermute x18, starting transfers between devices, partner(): return lax.ppermute(value, axis, [(i, i ^ mask) for i in range(size)])  21.5 us
    all_to_all x4, starting transfers between devices, exchange(): lax.all_to_all(value, 'tensor', split_axis=0, concat_axis=0, tiled=True)  18.4 us
    all_to_all x4, waiting for transfers between devices, exchange(): lax.all_to_all(value, 'tensor', split_axis=0, concat_axis=0, tiled=True)  9.88 us
    pallas_call x4, Pallas kernels, small_call(): pl.pallas_call(drop_inputs(kernel, len(ins), len(after)), grid=(steps,),...  9.71 us
    pallas_call x1, Pallas kernels, local_forward(): pl.pallas_call(functools.partial(forward_kernel, sizes), grid=(rows // (S...  5.97 us
  transfers between devices with their start and end apart: 22, of which 12 were waited for; matrix products, arithmetic and copies ran while one was open for 2% of the time, Pallas kernels for 38%

profile of v8, /device:TPU:0, one launch (start us, length us, event | category | flops | bytes accessed | tf_op | source)
XLA Modules:
  0.0 207.7 jit_solution(7674121084447161067)
XLA Ops:
  1.8 3.0 %collective-permute-start = (bf16[64,2048]{1,0:T(8,128)(2,1)S(1)}, bf16[64,2048]{1,0:T(8,128)(2,1)S(1)}, u32[]{:S(2)}, u32[]{:S(2)}) collective-permute-start(bf16[64,2048]{1,0:T(8,128)(2,1)S(1)} %get-tuple-element.53), channel_id=1, source_target_pairs={{0,8},{8,0},{16,24},{24,16},{1,9},{9,1},{17,25},{25,17},{2,10},{10... | collective-permute-start | bytes 786440 | tf_op jit(solution)/shard_map/ppermute | solution.py:381
  4.8 1.5 collective-permute-start.1
  6.4 6.0 %local_forward.1.refs_3_ = bf16[8,52,16,128]{3,2,1,0:T(8,128)(2,1)} custom-call(bf16[128,6656]{1,0:T(8,128)(2,1)} %x_ref.1, f32[52,52]{1,0:T(8,128)} %refs_0_.1), custom_call_target="tpu_custom_call" | custom-call | tf_op jit(solution)/shard_map/local_forward/pallas_call | solution.py:136
  12.3 5.3 %all-to-all-start = ((bf16[8,52,16,128]{3,2,1,0:T(8,128)(2,1)}), bf16[8,52,16,128]{3,2,1,0:T(8,128)(2,1)S(1)}, u32[]{:S(2)}, u32[]{:S(2)}) async-start(bf16[8,52,16,128]{3,2,1,0:T(8,128)(2,1)} %local_forward.1.refs_3_), calls=%async_computation | async-start | bytes 3407872 | tf_op jit(solution)/shard_map/all_to_all | solution.py:376
  19.5 1.3 collective-permute-done.3
  22.4 13.8 %unit_grads.2 = (bf16[8,28,16,128]{3,2,1,0:T(8,128)(2,1)}, bf16[8,28,16,128]{3,2,1,0:T(8,128)(2,1)}, bf16[8,28,16,128]{3,2,1,0:T(8,128)(2,1)}, bf16[4,28,16,128]{3,2,1,0:T(8,128)(2,1)}, bf16[4,28,16,128]{3,2,1,0:T(8,128)(2,1)}) custom-call(bf16[512,2048]{1,0:T(8,128)(2,1)S(1)} %pad_maximum_fusion.refs_0_.refs_5_, bf16[6656,2048]{1,0:T(8,128)(2,1)} %refs_6_.3, ...), custom_call_target="tpu_custom_call" | custom-call | flops 5000000000 | tf_op jit(solution)/shard_map/unit_grads/pallas_call | solution.py:207
  37.4 1.4 collective-permute-start.5
  38.9 11.5 %unit_grads.3 = (bf16[8,24,16,128]{3,2,1,0:T(8,128)(2,1)}, bf16[8,24,16,128]{3,2,1,0:T(8,128)(2,1)}, bf16[8,24,16,128]{3,2,1,0:T(8,128)(2,1)}, bf16[4,24,16,128]{3,2,1,0:T(8,128)(2,1)}, bf16[4,24,16,128]{3,2,1,0:T(8,128)(2,1)}) custom-call(bf16[512,2048]{1,0:T(8,128)(2,1)S(1)} %pad_maximum_fusion.refs_0_.refs_5_, bf16[6656,2048]{1,0:T(8,128)(2,1)} %refs_6_.3, ...), custom_call_target="tpu_custom_call" | custom-call | tf_op jit(solution)/shard_map/unit_grads/pallas_call | solution.py:207
  51.8 2.5 %relay.2 = (bf16[8,28,16,128]{3,2,1,0:T(8,128)(2,1)}, bf16[8,28,16,128]{3,2,1,0:T(8,128)(2,1)}) custom-call(bf16[8,28,16,128]{3,2,1,0:T(8,128)(2,1)} %get-tuple-element.29.refs_0_, bf16[8,28,16,128]{3,2,1,0:T(8,128)(2,1)} %get-tuple-element.30.refs_1_, bf16[4,28,16,128]{3,2,1,0:T(8,128)(2,1)S(1)} %collective-permute-done.4.refs_2_, ...), custom_call_target="tpu_custom_call" | custom-call | tf_op jit(solution)/shard_map/relay/pallas_call | solution.py:304
  55.5 1.4 collective-permute-start.7
  56.9 1.4 all-to-all-done.refs_0_
  58.3 2.3 %transform.2.refs_4_ = bf16[8,52,16,128]{3,2,1,0:T(8,128)(2,1)} custom-call(bf16[8,52,16,128]{3,2,1,0:T(8,128)(2,1)S(1)} %all-to-all-done.refs_0_, bf16[8,28,16,128]{3,2,1,0:T(8,128)(2,1)} %get-tuple-element.34.refs_1_), custom_call_target="tpu_custom_call" | custom-call | flops 999999995904 | tf_op jit(solution)/shard_map/transform/pallas_call | solution.py:304
  60.6 4.3 %all-to-all-start.1 = ((bf16[8,52,16,128]{3,2,1,0:T(8,128)(2,1)}), bf16[8,52,16,128]{3,2,1,0:T(8,128)(2,1)}, u32[]{:S(2)}, u32[]{:S(2)}) async-start(bf16[8,52,16,128]{3,2,1,0:T(8,128)(2,1)} %transform.2.refs_4_), calls=%async_computation.1 | async-start | bytes 3407872 | tf_op jit(solution)/shard_map/all_to_all | solution.py:376
  64.9 2.6 %relay.3 = (bf16[8,24,16,128]{3,2,1,0:T(8,128)(2,1)}, bf16[8,24,16,128]{3,2,1,0:T(8,128)(2,1)}) custom-call(bf16[8,24,16,128]{3,2,1,0:T(8,128)(2,1)} %get-tuple-element.36.refs_0_, bf16[8,24,16,128]{3,2,1,0:T(8,128)(2,1)} %get-tuple-element.37.refs_1_, bf16[4,24,16,128]{3,2,1,0:T(8,128)(2,1)} %collective-permute-done.8.refs_2_, ...), custom_call_target="tpu_custom_call" | custom-call | flops 999999995904 | tf_op jit(solution)/shard_map/relay/pallas_call | solution.py:304
  67.6 1.5 collective-permute-start.10
  69.1 1.5 collective-permute-start.11
  70.6 11.7 %collective-permute-done.6.refs_1_ = bf16[8,28,16,128]{3,2,1,0:T(8,128)(2,1)} collective-permute-done((bf16[8,28,16,128]{3,2,1,0:T(8,128)(2,1)}, bf16[8,28,16,128]{3,2,1,0:T(8,128)(2,1)}, u32[]{:S(2)}, u32[]{:S(2)}) %collective-permute-start.6) | collective-permute-done | bytes 917536 | tf_op jit(solution)/shard_map/ppermute | solution.py:381
  83.3 14.6 %collective-permute-done.10.refs_4_ = bf16[8,24,16,128]{3,2,1,0:T(8,128)(2,1)S(1)} collective-permute-done((bf16[8,24,16,128]{3,2,1,0:T(8,128)(2,1)}, bf16[8,24,16,128]{3,2,1,0:T(8,128)(2,1)S(1)}, u32[]{:S(2)}, u32[]{:S(2)}) %collective-permute-start.10) | collective-permute-done | bytes 786464 | tf_op jit(solution)/shard_map/ppermute | solution.py:381
  98.3 4.3 %total.1.refs_0_ = bf16[8,52,16,128]{3,2,1,0:T(8,128)(2,1)} custom-call(bf16[8,28,16,128]{3,2,1,0:T(8,128)(2,1)} %get-tuple-element.28.refs_3_.refs_0_, bf16[8,28,16,128]{3,2,1,0:T(8,128)(2,1)} %collective-permute-done.6.refs_1_, bf16[8,28,16,128]{3,2,1,0:T(8,128)(2,1)} %collective-permute-done.7.refs_2_, ...), custom_call_target="tpu_custom_call" | custom-call | tf_op jit(solution)/shard_map/total/pallas_call | solution.py:445
  102.6 2.9 %all-to-all-done.1.refs_1_.refs_0_ = bf16[8,52,16,128]{3,2,1,0:T(8,128)(2,1)} async-done(((bf16[8,52,16,128]{3,2,1,0:T(8,128)(2,1)}), bf16[8,52,16,128]{3,2,1,0:T(8,128)(2,1)}, u32[]{:S(2)}, u32[]{:S(2)}) %all-to-all-start.1) | async-done | bytes 1703968 | tf_op jit(solution)/shard_map/all_to_all | solution.py:376
  105.6 3.7 %all-to-all-start.2 = ((bf16[8,52,16,128]{3,2,1,0:T(8,128)(2,1)}), bf16[8,52,16,128]{3,2,1,0:T(8,128)(2,1)S(1)}, u32[]{:S(2)}, u32[]{:S(2)}) async-start(bf16[8,52,16,128]{3,2,1,0:T(8,128)(2,1)} %gate.1), calls=%async_computation.2 | async-start | bytes 3407872 | tf_op jit(solution)/shard_map/all_to_all | solution.py:376
  109.3 1.6 collective-permute-start.12
  110.8 1.5 collective-permute-start.13
  112.4 1.4 backward_matrices.1
  113.8 35.2 %collective-permute-done.12.refs_0_.refs_1_ = bf16[8,52,16,128]{3,2,1,0:T(8,128)(2,1)S(1)} collective-permute-done((bf16[8,52,16,128]{3,2,1,0:T(8,128)(2,1)}, bf16[8,52,16,128]{3,2,1,0:T(8,128)(2,1)S(1)}, u32[]{:S(2)}, u32[]{:S(2)}) %collective-permute-start.12) | collective-permute-done | bytes 1703968 | tf_op jit(solution)/shard_map/ppermute | solution.py:381
  152.5 1.5 collective-permute-start.17
  154.0 2.3 %transform.3.refs_2_.refs_9_ = bf16[8,52,16,128]{3,2,1,0:T(8,128)(2,1)} custom-call(bf16[8,52,16,128]{3,2,1,0:T(8,128)(2,1)S(1)} %all-to-all-done.2.refs_0_), custom_call_target="tpu_custom_call" | custom-call | flops 999999995904 | tf_op jit(solution)/shard_map/transform/pallas_call | solution.py:304
  156.3 5.0 %all-to-all-start.3 = ((bf16[8,52,16,128]{3,2,1,0:T(8,128)(2,1)}), bf16[8,52,16,128]{3,2,1,0:T(8,128)(2,1)}, u32[]{:S(2)}, u32[]{:S(2)}) async-start(bf16[8,52,16,128]{3,2,1,0:T(8,128)(2,1)} %transform.3.refs_2_.refs_9_), calls=%async_computation.3 | async-start | bytes 3407872 | tf_op jit(solution)/shard_map/all_to_all | solution.py:376
  164.5 16.3 %weight_grads.2 = (bf16[6656,2048]{1,0:T(8,128)(2,1)}, f32[28,2048]{1,0:T(8,128)S(1)}) custom-call(bf16[8,52,16,128]{3,2,1,0:T(8,128)(2,1)} %all-to-all-done.1.refs_1_.refs_0_, bf16[8,52,16,128]{3,2,1,0:T(8,128)(2,1)S(1)} %copy-done.3, bf16[8,52,16,128]{3,2,1,0:T(8,128)(2,1)S(1)} %copy-done.5, bf16[4,28,16,128]{3,2,1,0:T(8,128)(2,1)} %collective-permute-done.16.refs_3_, ...), custom_call_target="tpu_custom_call" | custom-call | flops 999999995904 | tf_op jit(solution)/shard_map/weight_grads/pallas_call | solution.py:278
  180.9 14.1 %weight_grads.3 = (bf16[6656,2048]{1,0:T(8,128)(2,1)}, f32[24,2048]{1,0:T(8,128)S(1)}) custom-call(bf16[8,52,16,128]{3,2,1,0:T(8,128)(2,1)} %all-to-all-done.1.refs_1_.refs_0_, bf16[8,52,16,128]{3,2,1,0:T(8,128)(2,1)S(1)} %copy-done.3, bf16[8,52,16,128]{3,2,1,0:T(8,128)(2,1)S(1)} %copy-done.5, ...), custom_call_target="tpu_custom_call", output_to_operand_aliasing={{0}: (9, {})} | custom-call | flops 999999995904 | tf_op jit(solution)/shard_map/weight_grads/pallas_call | solution.py:278
  196.5 5.6 %all-to-all-done.3.refs_0_ = bf16[8,52,16,128]{3,2,1,0:T(8,128)(2,1)} async-done(((bf16[8,52,16,128]{3,2,1,0:T(8,128)(2,1)}), bf16[8,52,16,128]{3,2,1,0:T(8,128)(2,1)}, u32[]{:S(2)}, u32[]{:S(2)}) %all-to-all-start.3) | async-done | bytes 1703968 | tf_op jit(solution)/shard_map/all_to_all | solution.py:376
  202.1 5.6 %local_backward.1 = bf16[128,6656]{1,0:T(8,128)(2,1)} custom-call(bf16[8,52,16,128]{3,2,1,0:T(8,128)(2,1)} %all-to-all-done.3.refs_0_, bf16[416,416]{1,0:T(8,128)(2,1)} %get-tuple-element.42.refs_1_, bf16[416,416]{1,0:T(8,128)(2,1)} %get-tuple-element.43.refs_2_, bf16[128,128]{1,0:T(8,128)(2,1)} %get-tuple-element.44.refs_3_, f32[24,2048]{1,0:T(8,128)} %copy-done.6), custom_call_target="tpu_custom_call" | custom-call | tf_op jit(solution)/shard_map/local_backward/pallas_call | solution.py:173
  (52 shorter events, 17.9 us)
Async XLA Ops:
  1.8 15.9 %collective-permute-start = (bf16[64,2048]{1,0:T(8,128)(2,1)S(1)}, bf16[64,2048]{1,0:T(8,128)(2,1)S(1)}, u32[]{:S(2)}, u32[]{:S(2)}) collective-permute-start(bf16[64,2048]{1,0:T(8,128)(2,1)S(1)} %get-tuple-element.53), channel_id=1, source_target_pairs={{0,8},{8,0},{16,24},{24,16},{1,9},{9,1},{17,25},{25,17},{2,10},{10... | collective-permute-start | bytes 786440 | tf_op jit(solution)/shard_map/ppermute | solution.py:381
  4.8 13.4 %collective-permute-start.1 = (bf16[64,2048]{1,0:T(8,128)(2,1)S(1)}, bf16[64,2048]{1,0:T(8,128)(2,1)S(1)}, u32[]{:S(2)}, u32[]{:S(2)}) collective-permute-start(bf16[64,2048]{1,0:T(8,128)(2,1)S(1)} %get-tuple-element.55), channel_id=1, source_target_pairs={{0,16},{8,24},{16,0},{24,8},{1,17},{9,25},{17,1},{25,9},{2,18},{10... | collective-permute-start | bytes 786440 | tf_op jit(solution)/shard_map/ppermute | solution.py:381
  6.4 11.9 %collective-permute-start.2 = (bf16[64,2048]{1,0:T(8,128)(2,1)S(1)}, bf16[64,2048]{1,0:T(8,128)(2,1)S(1)}, u32[]{:S(2)}, u32[]{:S(2)}) collective-permute-start(bf16[64,2048]{1,0:T(8,128)(2,1)S(1)} %get-tuple-element.54), channel_id=1, source_target_pairs={{0,24},{8,16},{16,8},{24,0},{1,25},{9,17},{17,9},{25,1},{2,26},{10... | collective-permute-start | bytes 786440 | tf_op jit(solution)/shard_map/ppermute | solution.py:381
  12.3 46.0 %all-to-all-start = ((bf16[8,52,16,128]{3,2,1,0:T(8,128)(2,1)}), bf16[8,52,16,128]{3,2,1,0:T(8,128)(2,1)S(1)}, u32[]{:S(2)}, u32[]{:S(2)}) async-start(bf16[8,52,16,128]{3,2,1,0:T(8,128)(2,1)} %local_forward.1.refs_3_), calls=%async_computation | async-start | bytes 3407872 | tf_op jit(solution)/shard_map/all_to_all | solution.py:376
  18.3 2.5 %collective-permute-start.3 = (bf16[3,64,2048]{2,1,0:T(8,128)(2,1)S(1)}, bf16[3,64,2048]{2,1,0:T(8,128)(2,1)}, u32[]{:S(2)}, u32[]{:S(2)}) collective-permute-start(bf16[3,64,2048]{2,1,0:T(8,128)(2,1)S(1)} %pad_maximum_fusion.2), channel_id=1, source_target_pairs={{0,1},{1,0},{2,3},{3,2},{4,5},{5,4},{6,7},{7,6},{8,9},{9,8},{10,11... | collective-permute-start | bytes 2359304 | tf_op jit(solution)/shard_map/ppermute | solution.py:381
  22.4 16.5 %copy-start = (bf16[512,2048]{1,0:T(8,128)(2,1)}, bf16[512,2048]{1,0:T(8,128)(2,1)S(1)}, u32[]{:S(2)}) copy-start(bf16[512,2048]{1,0:T(8,128)(2,1)S(1)} %pad_maximum_fusion.refs_0_.refs_5_) | copy-start | bytes 6291460
  36.2 15.6 %collective-permute-start.4 = (bf16[4,28,16,128]{3,2,1,0:T(8,128)(2,1)}, bf16[4,28,16,128]{3,2,1,0:T(8,128)(2,1)S(1)}, u32[]{:S(2)}, u32[]{:S(2)}) collective-permute-start(bf16[4,28,16,128]{3,2,1,0:T(8,128)(2,1)} %get-tuple-element.31), channel_id=1, source_target_pairs={{0,8},{8,0},{16,24},{24,16},{1,9},{9,1},{17,25},{25,17},{2,10},{10... | collective-permute-start | bytes 1376264 | tf_op jit(solution)/shard_map/ppermute | solution.py:381
  37.4 14.3 %collective-permute-start.5 = (bf16[4,28,16,128]{3,2,1,0:T(8,128)(2,1)}, bf16[4,28,16,128]{3,2,1,0:T(8,128)(2,1)S(1)}, u32[]{:S(2)}, u32[]{:S(2)}) collective-permute-start(bf16[4,28,16,128]{3,2,1,0:T(8,128)(2,1)} %get-tuple-element.32), channel_id=1, source_target_pairs={{0,16},{8,24},{16,0},{24,8},{1,17},{9,25},{17,1},{25,9},{2,18},{10... | collective-permute-start | bytes 1376264 | tf_op jit(solution)/shard_map/ppermute | solution.py:381
  50.4 14.6 %collective-permute-start.8 = (bf16[4,24,16,128]{3,2,1,0:T(8,128)(2,1)}, bf16[4,24,16,128]{3,2,1,0:T(8,128)(2,1)}, u32[]{:S(2)}, u32[]{:S(2)}) collective-permute-start(bf16[4,24,16,128]{3,2,1,0:T(8,128)(2,1)} %get-tuple-element.38), channel_id=1, source_target_pairs={{0,8},{8,0},{16,24},{24,16},{1,9},{9,1},{17,25},{25,17},{2,10},{10... | collective-permute-start | bytes 1179656 | tf_op jit(solution)/shard_map/ppermute | solution.py:381
  51.3 13.7 %collective-permute-start.9 = (bf16[4,24,16,128]{3,2,1,0:T(8,128)(2,1)}, bf16[4,24,16,128]{3,2,1,0:T(8,128)(2,1)}, u32[]{:S(2)}, u32[]{:S(2)}) collective-permute-start(bf16[4,24,16,128]{3,2,1,0:T(8,128)(2,1)} %get-tuple-element.39), channel_id=1, source_target_pairs={{0,16},{8,24},{16,0},{24,8},{1,17},{9,25},{17,1},{25,9},{2,18},{10... | collective-permute-start | bytes 1179656 | tf_op jit(solution)/shard_map/ppermute | solution.py:381
  54.3 28.1 %collective-permute-start.6 = (bf16[8,28,16,128]{3,2,1,0:T(8,128)(2,1)}, bf16[8,28,16,128]{3,2,1,0:T(8,128)(2,1)}, u32[]{:S(2)}, u32[]{:S(2)}) collective-permute-start(bf16[8,28,16,128]{3,2,1,0:T(8,128)(2,1)} %get-tuple-element.34.refs_1_), channel_id=1, source_target_pairs={{0,8},{8,0},{16,24},{24,16},{1,9},{9,1},{17,25},{25,17},{2,10},{10... | collective-permute-start | bytes 2752520 | tf_op jit(solution)/shard_map/ppermute | solution.py:381
  55.5 27.8 %collective-permute-start.7 = (bf16[8,28,16,128]{3,2,1,0:T(8,128)(2,1)}, bf16[8,28,16,128]{3,2,1,0:T(8,128)(2,1)}, u32[]{:S(2)}, u32[]{:S(2)}) collective-permute-start(bf16[8,28,16,128]{3,2,1,0:T(8,128)(2,1)} %get-tuple-element.35), channel_id=1, source_target_pairs={{0,16},{8,24},{16,0},{24,8},{1,17},{9,25},{17,1},{25,9},{2,18},{10... | collective-permute-start | bytes 2752520 | tf_op jit(solution)/shard_map/ppermute | solution.py:381
  60.6 45.0 %all-to-all-start.1 = ((bf16[8,52,16,128]{3,2,1,0:T(8,128)(2,1)}), bf16[8,52,16,128]{3,2,1,0:T(8,128)(2,1)}, u32[]{:S(2)}, u32[]{:S(2)}) async-start(bf16[8,52,16,128]{3,2,1,0:T(8,128)(2,1)} %transform.2.refs_4_), calls=%async_computation.1 | async-start | bytes 3407872 | tf_op jit(solution)/shard_map/all_to_all | solution.py:376
  67.6 30.3 %collective-permute-start.10 = (bf16[8,24,16,128]{3,2,1,0:T(8,128)(2,1)}, bf16[8,24,16,128]{3,2,1,0:T(8,128)(2,1)S(1)}, u32[]{:S(2)}, u32[]{:S(2)}) collective-permute-start(bf16[8,24,16,128]{3,2,1,0:T(8,128)(2,1)} %get-tuple-element.40.refs_1_), channel_id=1, source_target_pairs={{0,8},{8,0},{16,24},{24,16},{1,9},{9,1},{17,25},{25,17},{2,10},{10... | collective-permute-start | bytes 2359304 | tf_op jit(solution)/shard_map/ppermute | solution.py:381
  69.1 29.2 %collective-permute-start.11 = (bf16[8,24,16,128]{3,2,1,0:T(8,128)(2,1)}, bf16[8,24,16,128]{3,2,1,0:T(8,128)(2,1)S(1)}, u32[]{:S(2)}, u32[]{:S(2)}) collective-permute-start(bf16[8,24,16,128]{3,2,1,0:T(8,128)(2,1)} %get-tuple-element.41), channel_id=1, source_target_pairs={{0,16},{8,24},{16,0},{24,8},{1,17},{9,25},{17,1},{25,9},{2,18},{10... | collective-permute-start | bytes 2359304 | tf_op jit(solution)/shard_map/ppermute | solution.py:381
  105.6 6.8 %copy-start.7 = (bf16[8,24,16,128]{3,2,1,0:T(8,128)(2,1)S(1)}, bf16[8,24,16,128]{3,2,1,0:T(8,128)(2,1)}, u32[]{:S(2)}) copy-start(bf16[8,24,16,128]{3,2,1,0:T(8,128)(2,1)} %get-tuple-element.40.refs_1_) | copy-start | bytes 2359300
  105.6 6.8 %copy-start.8 = (f32[52,52]{1,0:T(8,128)S(1)}, f32[52,52]{1,0:T(8,128)}, u32[]{:S(2)}) copy-start(f32[52,52]{1,0:T(8,128)} %refs_0_.1) | copy-start | bytes 32452
  105.6 48.5 %all-to-all-start.2 = ((bf16[8,52,16,128]{3,2,1,0:T(8,128)(2,1)}), bf16[8,52,16,128]{3,2,1,0:T(8,128)(2,1)S(1)}, u32[]{:S(2)}, u32[]{:S(2)}) async-start(bf16[8,52,16,128]{3,2,1,0:T(8,128)(2,1)} %gate.1), calls=%async_computation.2 | async-start | bytes 3407872 | tf_op jit(solution)/shard_map/all_to_all | solution.py:376
  109.3 39.7 %collective-permute-start.12 = (bf16[8,52,16,128]{3,2,1,0:T(8,128)(2,1)}, bf16[8,52,16,128]{3,2,1,0:T(8,128)(2,1)S(1)}, u32[]{:S(2)}, u32[]{:S(2)}) collective-permute-start(bf16[8,52,16,128]{3,2,1,0:T(8,128)(2,1)} %all-to-all-done.1.refs_1_.refs_0_), channel_id=1, source_target_pairs={{0,8},{8,0},{16,24},{24,16},{1,9},{9,1},{17,25},{25,17},{2,10},{10... | collective-permute-start | bytes 5111816 | tf_op jit(solution)/shard_map/ppermute | solution.py:381
  110.8 39.4 %collective-permute-start.13 = (bf16[8,52,16,128]{3,2,1,0:T(8,128)(2,1)}, bf16[8,52,16,128]{3,2,1,0:T(8,128)(2,1)S(1)}, u32[]{:S(2)}, u32[]{:S(2)}) collective-permute-start(bf16[8,52,16,128]{3,2,1,0:T(8,128)(2,1)} %all-to-all-done.1.refs_1_.refs_0_), channel_id=1, source_target_pairs={{0,16},{8,24},{16,0},{24,8},{1,17},{9,25},{17,1},{25,9},{2,18},{10... | collective-permute-start | bytes 5111816 | tf_op jit(solution)/shard_map/ppermute | solution.py:381
  149.0 2.2 %copy-start.2 = (bf16[8,52,16,128]{3,2,1,0:T(8,128)(2,1)}, bf16[8,52,16,128]{3,2,1,0:T(8,128)(2,1)S(1)}, u32[]{:S(2)}) copy-start(bf16[8,52,16,128]{3,2,1,0:T(8,128)(2,1)S(1)} %collective-permute-done.12.refs_0_.refs_1_) | copy-start | bytes 5111812
  150.2 1.5 copy-start.4
  151.7 12.4 %collective-permute-start.16 = (bf16[4,28,16,128]{3,2,1,0:T(8,128)(2,1)}, bf16[4,28,16,128]{3,2,1,0:T(8,128)(2,1)}, u32[]{:S(2)}, u32[]{:S(2)}) collective-permute-start(bf16[4,28,16,128]{3,2,1,0:T(8,128)(2,1)} %get-tuple-element.47), channel_id=1, source_target_pairs={{0,8},{8,0},{16,24},{24,16},{1,9},{9,1},{17,25},{25,17},{2,10},{10... | collective-permute-start | bytes 1376264 | tf_op jit(solution)/shard_map/ppermute | solution.py:381
  152.5 12.0 %collective-permute-start.17 = (bf16[4,28,16,128]{3,2,1,0:T(8,128)(2,1)}, bf16[4,28,16,128]{3,2,1,0:T(8,128)(2,1)}, u32[]{:S(2)}, u32[]{:S(2)}) collective-permute-start(bf16[4,28,16,128]{3,2,1,0:T(8,128)(2,1)} %get-tuple-element.48), channel_id=1, source_target_pairs={{0,16},{8,24},{16,0},{24,8},{1,17},{9,25},{17,1},{25,9},{2,18},{10... | collective-permute-start | bytes 1376264 | tf_op jit(solution)/shard_map/ppermute | solution.py:381
  156.3 5.0 %copy-start.3 = (bf16[8,52,16,128]{3,2,1,0:T(8,128)(2,1)S(1)}, bf16[8,52,16,128]{3,2,1,0:T(8,128)(2,1)}, u32[]{:S(2)}) copy-start(bf16[8,52,16,128]{3,2,1,0:T(8,128)(2,1)} %copy-done.2) | copy-start | bytes 5111812
  156.3 5.0 %copy-start.5 = (bf16[8,52,16,128]{3,2,1,0:T(8,128)(2,1)S(1)}, bf16[8,52,16,128]{3,2,1,0:T(8,128)(2,1)}, u32[]{:S(2)}) copy-start(bf16[8,52,16,128]{3,2,1,0:T(8,128)(2,1)} %copy-done.4) | copy-start | bytes 5111812
  156.3 45.8 %all-to-all-start.3 = ((bf16[8,52,16,128]{3,2,1,0:T(8,128)(2,1)}), bf16[8,52,16,128]{3,2,1,0:T(8,128)(2,1)}, u32[]{:S(2)}, u32[]{:S(2)}) async-start(bf16[8,52,16,128]{3,2,1,0:T(8,128)(2,1)} %transform.3.refs_2_.refs_9_), calls=%async_computation.3 | async-start | bytes 3407872 | tf_op jit(solution)/shard_map/all_to_all | solution.py:376
  161.3 3.2 %copy-start.1 = (bf16[512,2048]{1,0:T(8,128)(2,1)S(1)}, bf16[512,2048]{1,0:T(8,128)(2,1)}, u32[]{:S(2)}) copy-start(bf16[512,2048]{1,0:T(8,128)(2,1)} %copy-done) | copy-start | bytes 6291460
  162.3 18.6 %collective-permute-start.14 = (bf16[4,24,16,128]{3,2,1,0:T(8,128)(2,1)}, bf16[4,24,16,128]{3,2,1,0:T(8,128)(2,1)}, u32[]{:S(2)}, u32[]{:S(2)}) collective-permute-start(bf16[4,24,16,128]{3,2,1,0:T(8,128)(2,1)} %get-tuple-element.45), channel_id=1, source_target_pairs={{0,8},{8,0},{16,24},{24,16},{1,9},{9,1},{17,25},{25,17},{2,10},{10... | collective-permute-start | bytes 1179656 | tf_op jit(solution)/shard_map/ppermute | solution.py:381
  163.6 17.3 %collective-permute-start.15 = (bf16[4,24,16,128]{3,2,1,0:T(8,128)(2,1)}, bf16[4,24,16,128]{3,2,1,0:T(8,128)(2,1)}, u32[]{:S(2)}, u32[]{:S(2)}) collective-permute-start(bf16[4,24,16,128]{3,2,1,0:T(8,128)(2,1)} %get-tuple-element.46), channel_id=1, source_target_pairs={{0,16},{8,24},{16,0},{24,8},{1,17},{9,25},{17,1},{25,9},{2,18},{10... | collective-permute-start | bytes 1179656 | tf_op jit(solution)/shard_map/ppermute | solution.py:381
  195.0 0.7 copy-start.6

commit v9 on v8

--- a/solution.py
+++ b/solution.py
@@ -38,7 +38,7 @@
     return (1 - 2 * parity).astype(F32).astype(BF16)
 
 
-def build_mixing(rot_ref, high_ref, low_ref, sign_ref, transposed):
+def build_mixing(rot_ref, mix_ref, sign_ref, transposed):
     blocks = rot_ref.shape[0]
     size = blocks * ROWS
     row = lax.broadcasted_iota(jnp.int32, (size, blocks), 0)
@@ -47,36 +47,40 @@
     rows = lax.broadcasted_iota(jnp.int32, (size, size), 0)
     cols = lax.broadcasted_iota(jnp.int32, (size, size), 1)
     same = (rows & (ROWS - 1)) == (cols & (ROWS - 1))
-    for part, out_ref in zip(split2(rot_ref[...]), (high_ref, low_ref)):
-        spread = nt_dot(pick, part) if transposed else nn_dot(pick, part)
-        full = nt_dot(spread.astype(BF16), pick)
-        out_ref[...] = jnp.where(same, full, 0.0).astype(BF16)
+    spread = [
+        nt_dot(pick, part) if transposed else nn_dot(pick, part) for part in split2(rot_ref[...])
+    ]
+    for half, value in enumerate(spread):
+        full = nt_dot(value.astype(BF16), pick)
+        mix_ref[half * size : (half + 1) * size, :] = jnp.where(same, full, 0.0).astype(BF16)
     sign_ref[...] = sign_matrix(HB)
 
 
-def mix_rows(tiles, high_ref, low_ref, sign_ref):
+def mix_rows(tiles, mix_ref, sign_ref):
     blocks = len(tiles[0])
+    size = blocks * ROWS
     stacked = jnp.concatenate([jnp.concatenate(one, axis=0).astype(BF16) for one in tiles], axis=1)
-    mixed = nn_dot(high_ref[...], stacked) + nn_dot(low_ref[...], stacked)
+    halves = nn_dot(mix_ref[...], stacked)
+    mixed = (halves[:size] + halves[size:]).astype(BF16)
     results = []
     for j in range(len(tiles)):
-        part = nn_dot(mixed[:, j * HB : (j + 1) * HB].astype(BF16), sign_ref[...])
+        part = nn_dot(mixed[:, j * HB : (j + 1) * HB], sign_ref[...])
         results.append((part * HB ** (-0.5)).reshape(blocks, ROWS, HB))
     return results
 
 
 def forward_kernel(sizes, x_ref, rot_ref, *refs):
-    outs, (high_ref, low_ref, sign_ref) = refs[: len(sizes)], refs[len(sizes) :]
+    outs, (mix_ref, sign_ref) = refs[: len(sizes)], refs[len(sizes) :]
     blocks = rot_ref.shape[0]
 
     @pl.when(pl.program_id(0) == 0)
     def _():
-        build_mixing(rot_ref, high_ref, low_ref, sign_ref, True)
+        build_mixing(rot_ref, mix_ref, sign_ref, True)
 
     rows = x_ref.shape[0]
     wide = [x_ref[:, k * HB : (k + 1) * HB].astype(F32) for k in range(blocks)]
     tiles = [[one[j : j + ROWS] for one in wide] for j in range(0, rows, ROWS)]
-    results = mix_rows(tiles, high_ref, low_ref, sign_ref)
+    results = mix_rows(tiles, mix_ref, sign_ref)
     for j in range(rows // SUB):
         both = jnp.concatenate([results[2 * j], results[2 * j + 1]], axis=1).astype(BF16)
         start = 0
@@ -86,7 +90,7 @@
 
 
 def backward_kernel(sizes, *refs):
-    ins, (high_ref, low_ref, sign_ref, out_ref) = refs[: len(sizes)], refs[len(sizes) :]
+    ins, (mix_ref, sign_ref, out_ref) = refs[: len(sizes)], refs[len(sizes) :]
     blocks = sum(sizes)
     rows = out_ref.shape[0]
     tiles = []
@@ -95,7 +99,7 @@
             in_ref[j, c].astype(F32) for size, in_ref in zip(sizes, ins) for c in range(size)
         ]
         tiles += [[one[:ROWS] for one in wide], [one[ROWS:] for one in wide]]
-    results = mix_rows(tiles, high_ref, low_ref, sign_ref)
+    results = mix_rows(tiles, mix_ref, sign_ref)
     for j in range(rows // SUB):
         both = jnp.concatenate([results[2 * j], results[2 * j + 1]], axis=1).astype(BF16)
         for k in range(blocks):
@@ -104,8 +108,7 @@
 
 def local_scratch(blocks):
     return [
-        pltpu.VMEM((blocks * ROWS, blocks * ROWS), BF16),
-        pltpu.VMEM((blocks * ROWS, blocks * ROWS), BF16),
+        pltpu.VMEM((2 * blocks * ROWS, blocks * ROWS), BF16),
         pltpu.VMEM((HB, HB), BF16),
     ]
 
@@ -151,13 +154,13 @@
 
 def backward_matrices(rot_block, after=()):
     size = rot_block.shape[0] * ROWS
-    shapes = [(size, size), (size, size), (HB, HB)]
+    shapes = [(2 * size, size), (HB, HB)]
     return pl.pallas_call(
         drop_inputs(
             lambda rot_ref, *refs: build_mixing(rot_ref, *refs, False), 1, len(after)
         ),
         in_specs=[pl.BlockSpec(memory_space=pltpu.VMEM)] + [ANYWHERE] * len(after),
-        out_specs=[pl.BlockSpec(memory_space=pltpu.VMEM)] * 3,
+        out_specs=[pl.BlockSpec(memory_space=pltpu.VMEM)] * 2,
         out_shape=[pltpu.HBM(shape, BF16) for shape in shapes],
         compiler_params=pltpu.CompilerParams(vmem_limit_bytes=SMALL),
         cost_estimate=FREE,
@@ -171,7 +174,7 @@
     blocks = sum(sizes)
     parts = 2
     return pl.pallas_call(
-        drop_inputs(functools.partial(backward_kernel, sizes), len(sizes) + 3, len(after)),
+        drop_inputs(functools.partial(backward_kernel, sizes), len(sizes) + 2, len(after)),
         grid=(count // parts,),
         in_specs=[pl.BlockSpec((parts, size, SUB, HB), lambda i: (i, 0, 0, 0)) for size in sizes]
         + [pl.BlockSpec(value.shape, lambda i: (0, 0)) for value in matrices]
@@ -184,39 +187,52 @@
     )(*mixed, *in_hbm(*matrices, *after))
 
 
+def weight_spec(first, per, cols):
+    return pl.BlockSpec(
+        (pl.Element(per * GROUP), pl.Element(cols)), lambda i: ((first + i * per) * GROUP, 0)
+    )
+
+
 def units_kernel(first, per, up_ref, w_ref, s_ref, *refs):
-    outs, quant_ref = refs[:-1], refs[-1]
+    outs, (turned_ref, quant_ref) = refs[:-2], refs[-2:]
     base = first + pl.program_id(0) * per
+
+    @pl.when(pl.program_id(0) == 0)
+    def _():
+        tile = 256
+        for e in range(0, up_ref.shape[1], tile):
+            turned_ref[e : e + tile, :] = up_ref[:, e : e + tile].T
+
     for g in range(per):
         rows = slice(g * GROUP, (g + 1) * GROUP)
         quant_ref[rows, :] = (w_ref[rows, :].astype(F32) * s_ref[pl.ds(base + g, 1), :]).astype(
             BF16
         )
-    result = nt_dot(up_ref[...], quant_ref[...]).astype(BF16)
-    token = 0
-    for out_ref in outs:
-        for q in range(out_ref.shape[0]):
-            for g in range(per):
-                out_ref[q, g] = result[token : token + SUB, g * GROUP : (g + 1) * GROUP]
-            token += SUB
+    result = nn_dot(quant_ref[...], turned_ref[...]).astype(BF16)
+    for g in range(per):
+        turned = result[g * GROUP : (g + 1) * GROUP, :].T
+        token = 0
+        for out_ref in outs:
+            for q in range(out_ref.shape[0]):
+                out_ref[q, g] = turned[token : token + SUB, :]
+                token += SUB
 
 
 def unit_grads(up, weight, scales, first, size, per, counts, after=(), cost=FREE):
     tokens, cols = up.shape
-    offset = first // per
     return pl.pallas_call(
         drop_inputs(functools.partial(units_kernel, first, per), 3, len(after)),
         grid=(size // per,),
         in_specs=[
             pl.BlockSpec((tokens, cols), lambda i: (0, 0)),
-            pl.BlockSpec((per * GROUP, cols), lambda i: (offset + i, 0)),
+            weight_spec(first, per, cols),
             pl.BlockSpec(scales.shape, lambda i: (0, 0)),
         ]
         + [ANYWHERE] * len(after),
         out_specs=[pl.BlockSpec((count, per, SUB, HB), lambda i: (0, i, 0, 0)) for count in counts],
         out_shape=[pltpu.HBM((count, size, SUB, HB), BF16) for count in counts],
-        scratch_shapes=[pltpu.VMEM((per * GROUP, cols), BF16)],
-        compiler_params=pltpu.CompilerParams(vmem_limit_bytes=26 << 20),
+        scratch_shapes=[pltpu.VMEM((cols, tokens), BF16), pltpu.VMEM((per * GROUP, cols), BF16)],
+        compiler_params=pltpu.CompilerParams(vmem_limit_bytes=40 << 20),
         cost_estimate=cost,
         name="unit_grads",
     )(up, *in_hbm(weight, scales), *in_hbm(*after))
@@ -255,17 +271,16 @@
 
 def weight_grads(rotated, up, weight, scales, mask, buffer, first, size, per, after=()):
     tokens, cols = up.shape
-    offset = first // per
     specs = [
         pl.BlockSpec(
-            (piece.shape[0], per, SUB, HB),
-            functools.partial(lambda place, i: (0, place + i, 0, 0), place),
+            tuple(map(pl.Element, (piece.shape[0], per, SUB, HB))),
+            functools.partial(lambda place, i: (0, place + i * per, 0, 0), place),
         )
         for piece in rotated
-        for place in ((0 if piece.shape[1] == size else offset),)
+        for place in ((0 if piece.shape[1] == size else first),)
     ] + [
         pl.BlockSpec((tokens, cols), lambda i: (0, 0)),
-        pl.BlockSpec((per * GROUP, cols), lambda i: (offset + i, 0)),
+        weight_spec(first, per, cols),
         pl.BlockSpec(scales.shape, lambda i: (0, 0)),
         pl.BlockSpec(scales.shape, lambda i: (0, 0)),
     ]
@@ -280,7 +295,7 @@
         grid=(size // per,),
         in_specs=specs + [ANYWHERE] * len(after),
         out_specs=[
-            pl.BlockSpec((per * GROUP, cols), lambda i: (offset + i, 0)),
+            weight_spec(first, per, cols),
             pl.BlockSpec((size, cols), lambda i: (0, 0)),
         ],
         out_shape=[
@@ -288,7 +303,7 @@
             jax.ShapeDtypeStruct((size, cols), F32),
         ],
         input_output_aliases=aliases,
-        compiler_params=pltpu.CompilerParams(vmem_limit_bytes=26 << 20),
+        compiler_params=pltpu.CompilerParams(vmem_limit_bytes=40 << 20),
         cost_estimate=LONG,
         name="weight_grads",
     )(*args, *in_hbm(*after))
@@ -512,11 +527,14 @@
     up = gather_upstream(upstream)
     (local,) = local_forward(hidden, rot_block, (groups,))
     forth = exchange(local)
+    pers = [size // 4 for size in sizes]
     unit0 = unit_grads(
-        up, weight, scales, starts[0], sizes[0], per, counts, after=(local,), cost=SOME
+        up, weight, scales, starts[0], sizes[0], pers[0], counts, after=(local,), cost=SOME
     )
     first0 = scatter_first(unit0)
-    unit1 = unit_grads(up, weight, scales, starts[1], sizes[1], per, counts, after=(unit0[0],))
+    unit1 = unit_grads(
+        up, weight, scales, starts[1], sizes[1], pers[1], counts, after=(unit0[0],)
+    )
     first1 = scatter_first(unit1)
     relayed0, *second0 = scatter_second(unit0, first0, after=(unit1[0],))
     turned = transform(forth, after=(relayed0,), cost=LONG)
@@ -531,10 +549,10 @@
     final = exchange(mixed)
     gathered1 = gather_rest(near, 1, (mixed,))
     buffer, scale0 = weight_grads(
-        gathered0, up, weight, scales, clip_mask, None, starts[0], sizes[0], per, after=(mixed,)
+        gathered0, up, weight, scales, clip_mask, None, starts[0], sizes[0], pers[0], after=(mixed,)
     )
     buffer, scale1 = weight_grads(
-        gathered1, up, weight, scales, clip_mask, buffer, starts[1], sizes[1], per
+        gathered1, up, weight, scales, clip_mask, buffer, starts[1], sizes[1], pers[1]
     )
     grad_hidden = local_backward([final], matrices, (groups,), after=(scale1,))
     return grad_hidden, buffer, jnp.concatenate([scale0, scale1], axis=0)

time: 209 us -> 209 us (level)
  waiting for transfers between devices: 76.3 us -> 78.4 us
  Pallas kernels: 84.8 us -> 82.7 us
    all_to_all x4, waiting for transfers between devices: 9.88 us -> 12.2 us  [exchange(): lax.all_to_all(value, 'tensor', split_axis=0, concat_axis=0, tiled=True)]
  transfers between devices with their start and end apart: 22 -> 22, of which waited for: 12 -> 12; matrix products, arithmetic and copies ran while one was open for 2% -> 2% of each run, Pallas kernels for 38% -> 37%
where the time goes in v9:
time: 209 us; the launch traced here: 208 us
  Pallas kernels  82.7 us (40%)
  waiting for transfers between devices  78.4 us (38%)
  starting transfers between devices  39.7 us (19%)
  local copies, waits for them, and re-layouts  3.43 us (2%)
  other arithmetic  2.56 us (1%)
    ppermute x18, waiting for transfers between devices, partner(): return lax.ppermute(value, axis, [(i, i ^ mask) for i in range(size)])  66.2 us
    pallas_call x2, Pallas kernels, weight_grads(): pl.pallas_call(functools.partial(weights_kernel, first, per, len(rotated)...  29.1 us
    pallas_call x2, Pallas kernels, unit_grads(): pl.pallas_call(drop_inputs(functools.partial(units_kernel, first, per), 3...  24.7 us
    ppermute x18, starting transfers between devices, partner(): return lax.ppermute(value, axis, [(i, i ^ mask) for i in range(size)])  21.3 us
    all_to_all x4, starting transfers between devices, exchange(): lax.all_to_all(value, 'tensor', split_axis=0, concat_axis=0, tiled=True)  18.4 us
    all_to_all x4, waiting for transfers between devices, exchange(): lax.all_to_all(value, 'tensor', split_axis=0, concat_axis=0, tiled=True)  12.2 us
    pallas_call x4, Pallas kernels, small_call(): pl.pallas_call(drop_inputs(kernel, len(ins), len(after)), grid=(steps,),...  9.71 us
    pallas_call x1, Pallas kernels, local_forward(): pl.pallas_call(functools.partial(forward_kernel, sizes), grid=(rows // (S...  5.83 us
  transfers between devices with their start and end apart: 22, of which 12 were waited for; matrix products, arithmetic and copies ran while one was open for 2% of the time, Pallas kernels for 37%

profile of v9, /device:TPU:0, one launch (start us, length us, event | category | flops | bytes accessed | tf_op | source)
XLA Modules:
  0.0 207.6 jit_solution(4617257713330318494)
XLA Ops:
  1.8 3.0 %collective-permute-start = (bf16[64,2048]{1,0:T(8,128)(2,1)S(1)}, bf16[64,2048]{1,0:T(8,128)(2,1)S(1)}, u32[]{:S(2)}, u32[]{:S(2)}) collective-permute-start(bf16[64,2048]{1,0:T(8,128)(2,1)S(1)} %get-tuple-element.51), channel_id=1, source_target_pairs={{0,8},{8,0},{16,24},{24,16},{1,9},{9,1},{17,25},{25,17},{2,10},{10... | collective-permute-start | bytes 786440 | tf_op jit(solution)/shard_map/ppermute | solution.py:396
  4.8 1.5 collective-permute-start.1
  6.4 5.8 %local_forward.1.refs_3_ = bf16[8,52,16,128]{3,2,1,0:T(8,128)(2,1)} custom-call(bf16[128,6656]{1,0:T(8,128)(2,1)} %x_ref.1, f32[52,52]{1,0:T(8,128)} %refs_0_.1), custom_call_target="tpu_custom_call" | custom-call | tf_op jit(solution)/shard_map/local_forward/pallas_call | solution.py:139
  12.2 5.3 %all-to-all-start = ((bf16[8,52,16,128]{3,2,1,0:T(8,128)(2,1)}), bf16[8,52,16,128]{3,2,1,0:T(8,128)(2,1)S(1)}, u32[]{:S(2)}, u32[]{:S(2)}) async-start(bf16[8,52,16,128]{3,2,1,0:T(8,128)(2,1)} %local_forward.1.refs_3_), calls=%async_computation | async-start | bytes 3407872 | tf_op jit(solution)/shard_map/all_to_all | solution.py:391
  19.5 1.3 collective-permute-done.3
  20.8 1.3 broadcast_select_fusion.1
  22.5 13.3 %unit_grads.2 = (bf16[8,28,16,128]{3,2,1,0:T(8,128)(2,1)}, bf16[8,28,16,128]{3,2,1,0:T(8,128)(2,1)}, bf16[8,28,16,128]{3,2,1,0:T(8,128)(2,1)}, bf16[4,28,16,128]{3,2,1,0:T(8,128)(2,1)}, bf16[4,28,16,128]{3,2,1,0:T(8,128)(2,1)}) custom-call(bf16[512,2048]{1,0:T(8,128)(2,1)S(1)} %pad_maximum_fusion.refs_0_.refs_5_, bf16[6656,2048]{1,0:T(8,128)(2,1)} %refs_6_.3, ...), custom_call_target="tpu_custom_call" | custom-call | flops 5000000000 | tf_op jit(solution)/shard_map/unit_grads/pallas_call | solution.py:223
  37.0 1.3 collective-permute-start.5
  38.3 11.4 %unit_grads.3 = (bf16[8,24,16,128]{3,2,1,0:T(8,128)(2,1)}, bf16[8,24,16,128]{3,2,1,0:T(8,128)(2,1)}, bf16[8,24,16,128]{3,2,1,0:T(8,128)(2,1)}, bf16[4,24,16,128]{3,2,1,0:T(8,128)(2,1)}, bf16[4,24,16,128]{3,2,1,0:T(8,128)(2,1)}) custom-call(bf16[512,2048]{1,0:T(8,128)(2,1)S(1)} %pad_maximum_fusion.refs_0_.refs_5_, bf16[6656,2048]{1,0:T(8,128)(2,1)} %refs_6_.3, ...), custom_call_target="tpu_custom_call" | custom-call | tf_op jit(solution)/shard_map/unit_grads/pallas_call | solution.py:223
  51.2 2.5 %relay.2 = (bf16[8,28,16,128]{3,2,1,0:T(8,128)(2,1)}, bf16[8,28,16,128]{3,2,1,0:T(8,128)(2,1)}) custom-call(bf16[8,28,16,128]{3,2,1,0:T(8,128)(2,1)} %get-tuple-element.28.refs_0_, bf16[8,28,16,128]{3,2,1,0:T(8,128)(2,1)} %get-tuple-element.29.refs_1_, bf16[4,28,16,128]{3,2,1,0:T(8,128)(2,1)S(1)} %collective-permute-done.4.refs_2_, ...), custom_call_target="tpu_custom_call" | custom-call | tf_op jit(solution)/shard_map/relay/pallas_call | solution.py:319
  56.3 1.9 all-to-all-done.refs_0_
  58.2 2.3 %transform.2.refs_4_ = bf16[8,52,16,128]{3,2,1,0:T(8,128)(2,1)} custom-call(bf16[8,52,16,128]{3,2,1,0:T(8,128)(2,1)S(1)} %all-to-all-done.refs_0_, bf16[8,28,16,128]{3,2,1,0:T(8,128)(2,1)} %get-tuple-element.33.refs_1_), custom_call_target="tpu_custom_call" | custom-call | flops 999999995904 | tf_op jit(solution)/shard_map/transform/pallas_call | solution.py:319
  60.5 4.3 %all-to-all-start.1 = ((bf16[8,52,16,128]{3,2,1,0:T(8,128)(2,1)}), bf16[8,52,16,128]{3,2,1,0:T(8,128)(2,1)}, u32[]{:S(2)}, u32[]{:S(2)}) async-start(bf16[8,52,16,128]{3,2,1,0:T(8,128)(2,1)} %transform.2.refs_4_), calls=%async_computation.1 | async-start | bytes 3407872 | tf_op jit(solution)/shard_map/all_to_all | solution.py:391
  64.8 2.6 %relay.3 = (bf16[8,24,16,128]{3,2,1,0:T(8,128)(2,1)}, bf16[8,24,16,128]{3,2,1,0:T(8,128)(2,1)}) custom-call(bf16[8,24,16,128]{3,2,1,0:T(8,128)(2,1)} %get-tuple-element.35.refs_0_, bf16[8,24,16,128]{3,2,1,0:T(8,128)(2,1)} %get-tuple-element.36.refs_1_, bf16[4,24,16,128]{3,2,1,0:T(8,128)(2,1)} %collective-permute-done.8.refs_2_, ...), custom_call_target="tpu_custom_call" | custom-call | flops 999999995904 | tf_op jit(solution)/shard_map/relay/pallas_call | solution.py:319
  67.4 1.5 collective-permute-start.10
  68.9 1.5 collective-permute-start.11
  70.5 11.2 %collective-permute-done.6.refs_1_ = bf16[8,28,16,128]{3,2,1,0:T(8,128)(2,1)} collective-permute-done((bf16[8,28,16,128]{3,2,1,0:T(8,128)(2,1)}, bf16[8,28,16,128]{3,2,1,0:T(8,128)(2,1)}, u32[]{:S(2)}, u32[]{:S(2)}) %collective-permute-start.6) | collective-permute-done | bytes 917536 | tf_op jit(solution)/shard_map/ppermute | solution.py:396
  82.8 14.5 %collective-permute-done.10.refs_4_ = bf16[8,24,16,128]{3,2,1,0:T(8,128)(2,1)S(1)} collective-permute-done((bf16[8,24,16,128]{3,2,1,0:T(8,128)(2,1)}, bf16[8,24,16,128]{3,2,1,0:T(8,128)(2,1)S(1)}, u32[]{:S(2)}, u32[]{:S(2)}) %collective-permute-start.10) | collective-permute-done | bytes 786464 | tf_op jit(solution)/shard_map/ppermute | solution.py:396
  97.8 4.3 %total.1.refs_0_ = bf16[8,52,16,128]{3,2,1,0:T(8,128)(2,1)} custom-call(bf16[8,28,16,128]{3,2,1,0:T(8,128)(2,1)} %get-tuple-element.27.refs_3_.refs_0_, bf16[8,28,16,128]{3,2,1,0:T(8,128)(2,1)} %collective-permute-done.6.refs_1_, bf16[8,28,16,128]{3,2,1,0:T(8,128)(2,1)} %collective-permute-done.7.refs_2_, ...), custom_call_target="tpu_custom_call" | custom-call | tf_op jit(solution)/shard_map/total/pallas_call | solution.py:460
  102.1 3.3 %all-to-all-done.1.refs_1_.refs_0_ = bf16[8,52,16,128]{3,2,1,0:T(8,128)(2,1)} async-done(((bf16[8,52,16,128]{3,2,1,0:T(8,128)(2,1)}), bf16[8,52,16,128]{3,2,1,0:T(8,128)(2,1)}, u32[]{:S(2)}, u32[]{:S(2)}) %all-to-all-start.1) | async-done | bytes 1703968 | tf_op jit(solution)/shard_map/all_to_all | solution.py:391
  105.4 3.7 %all-to-all-start.2 = ((bf16[8,52,16,128]{3,2,1,0:T(8,128)(2,1)}), bf16[8,52,16,128]{3,2,1,0:T(8,128)(2,1)S(1)}, u32[]{:S(2)}, u32[]{:S(2)}) async-start(bf16[8,52,16,128]{3,2,1,0:T(8,128)(2,1)} %gate.1), calls=%async_computation.2 | async-start | bytes 3407872 | tf_op jit(solution)/shard_map/all_to_all | solution.py:391
  109.1 1.6 collective-permute-start.12
  110.7 1.5 collective-permute-start.13
  112.2 1.4 backward_matrices.1
  113.6 35.2 %collective-permute-done.12.refs_0_.refs_1_ = bf16[8,52,16,128]{3,2,1,0:T(8,128)(2,1)S(1)} collective-permute-done((bf16[8,52,16,128]{3,2,1,0:T(8,128)(2,1)}, bf16[8,52,16,128]{3,2,1,0:T(8,128)(2,1)S(1)}, u32[]{:S(2)}, u32[]{:S(2)}) %collective-permute-start.12) | collective-permute-done | bytes 1703968 | tf_op jit(solution)/shard_map/ppermute | solution.py:396
  152.4 1.5 collective-permute-start.17
  153.9 2.3 %transform.3.refs_2_.refs_9_ = bf16[8,52,16,128]{3,2,1,0:T(8,128)(2,1)} custom-call(bf16[8,52,16,128]{3,2,1,0:T(8,128)(2,1)S(1)} %all-to-all-done.2.refs_0_), custom_call_target="tpu_custom_call" | custom-call | flops 999999995904 | tf_op jit(solution)/shard_map/transform/pallas_call | solution.py:319
  156.2 5.0 %all-to-all-start.3 = ((bf16[8,52,16,128]{3,2,1,0:T(8,128)(2,1)}), bf16[8,52,16,128]{3,2,1,0:T(8,128)(2,1)}, u32[]{:S(2)}, u32[]{:S(2)}) async-start(bf16[8,52,16,128]{3,2,1,0:T(8,128)(2,1)} %transform.3.refs_2_.refs_9_), calls=%async_computation.3 | async-start | bytes 3407872 | tf_op jit(solution)/shard_map/all_to_all | solution.py:391
  164.4 15.5 %weight_grads.2 = (bf16[6656,2048]{1,0:T(8,128)(2,1)}, f32[28,2048]{1,0:T(8,128)S(1)}) custom-call(bf16[8,52,16,128]{3,2,1,0:T(8,128)(2,1)} %all-to-all-done.1.refs_1_.refs_0_, bf16[8,52,16,128]{3,2,1,0:T(8,128)(2,1)S(1)} %copy-done.3, bf16[8,52,16,128]{3,2,1,0:T(8,128)(2,1)S(1)} %copy-done.5, bf16[4,28,16,128]{3,2,1,0:T(8,128)(2,1)} %collective-permute-done.16.refs_3_, ...), custom_call_target="tpu_custom_call" | custom-call | flops 999999995904 | tf_op jit(solution)/shard_map/weight_grads/pallas_call | solution.py:293
  179.9 13.7 %weight_grads.3 = (bf16[6656,2048]{1,0:T(8,128)(2,1)}, f32[24,2048]{1,0:T(8,128)S(1)}) custom-call(bf16[8,52,16,128]{3,2,1,0:T(8,128)(2,1)} %all-to-all-done.1.refs_1_.refs_0_, bf16[8,52,16,128]{3,2,1,0:T(8,128)(2,1)S(1)} %copy-done.3, bf16[8,52,16,128]{3,2,1,0:T(8,128)(2,1)S(1)} %copy-done.5, ...), custom_call_target="tpu_custom_call", output_to_operand_aliasing={{0}: (9, {})} | custom-call | flops 999999995904 | tf_op jit(solution)/shard_map/weight_grads/pallas_call | solution.py:293
  195.0 7.0 %all-to-all-done.3.refs_0_ = bf16[8,52,16,128]{3,2,1,0:T(8,128)(2,1)} async-done(((bf16[8,52,16,128]{3,2,1,0:T(8,128)(2,1)}), bf16[8,52,16,128]{3,2,1,0:T(8,128)(2,1)}, u32[]{:S(2)}, u32[]{:S(2)}) %all-to-all-start.3) | async-done | bytes 1703968 | tf_op jit(solution)/shard_map/all_to_all | solution.py:391
  202.0 5.6 %local_backward.1 = bf16[128,6656]{1,0:T(8,128)(2,1)} custom-call(bf16[8,52,16,128]{3,2,1,0:T(8,128)(2,1)} %all-to-all-done.3.refs_0_, bf16[832,416]{1,0:T(8,128)(2,1)} %get-tuple-element.41.refs_1_, bf16[128,128]{1,0:T(8,128)(2,1)} %get-tuple-element.42.refs_2_, f32[24,2048]{1,0:T(8,128)} %copy-done.6), custom_call_target="tpu_custom_call" | custom-call | tf_op jit(solution)/shard_map/local_backward/pallas_call | solution.py:176
  (52 shorter events, 18.6 us)
Async XLA Ops:
  1.8 15.7 %collective-permute-start = (bf16[64,2048]{1,0:T(8,128)(2,1)S(1)}, bf16[64,2048]{1,0:T(8,128)(2,1)S(1)}, u32[]{:S(2)}, u32[]{:S(2)}) collective-permute-start(bf16[64,2048]{1,0:T(8,128)(2,1)S(1)} %get-tuple-element.51), channel_id=1, source_target_pairs={{0,8},{8,0},{16,24},{24,16},{1,9},{9,1},{17,25},{25,17},{2,10},{10... | collective-permute-start | bytes 786440 | tf_op jit(solution)/shard_map/ppermute | solution.py:396
  4.8 13.4 %collective-permute-start.1 = (bf16[64,2048]{1,0:T(8,128)(2,1)S(1)}, bf16[64,2048]{1,0:T(8,128)(2,1)S(1)}, u32[]{:S(2)}, u32[]{:S(2)}) collective-permute-start(bf16[64,2048]{1,0:T(8,128)(2,1)S(1)} %get-tuple-element.53), channel_id=1, source_target_pairs={{0,16},{8,24},{16,0},{24,8},{1,17},{9,25},{17,1},{25,9},{2,18},{10... | collective-permute-start | bytes 786440 | tf_op jit(solution)/shard_map/ppermute | solution.py:396
  6.4 11.9 %collective-permute-start.2 = (bf16[64,2048]{1,0:T(8,128)(2,1)S(1)}, bf16[64,2048]{1,0:T(8,128)(2,1)S(1)}, u32[]{:S(2)}, u32[]{:S(2)}) collective-permute-start(bf16[64,2048]{1,0:T(8,128)(2,1)S(1)} %get-tuple-element.52), channel_id=1, source_target_pairs={{0,24},{8,16},{16,8},{24,0},{1,25},{9,17},{17,9},{25,1},{2,26},{10... | collective-permute-start | bytes 786440 | tf_op jit(solution)/shard_map/ppermute | solution.py:396
  12.2 46.0 %all-to-all-start = ((bf16[8,52,16,128]{3,2,1,0:T(8,128)(2,1)}), bf16[8,52,16,128]{3,2,1,0:T(8,128)(2,1)S(1)}, u32[]{:S(2)}, u32[]{:S(2)}) async-start(bf16[8,52,16,128]{3,2,1,0:T(8,128)(2,1)} %local_forward.1.refs_3_), calls=%async_computation | async-start | bytes 3407872 | tf_op jit(solution)/shard_map/all_to_all | solution.py:391
  18.3 2.5 %collective-permute-start.3 = (bf16[3,64,2048]{2,1,0:T(8,128)(2,1)S(1)}, bf16[3,64,2048]{2,1,0:T(8,128)(2,1)}, u32[]{:S(2)}, u32[]{:S(2)}) collective-permute-start(bf16[3,64,2048]{2,1,0:T(8,128)(2,1)S(1)} %pad_maximum_fusion.2), channel_id=1, source_target_pairs={{0,1},{1,0},{2,3},{3,2},{4,5},{5,4},{6,7},{7,6},{8,9},{9,8},{10,11... | collective-permute-start | bytes 2359304 | tf_op jit(solution)/shard_map/ppermute | solution.py:396
  22.5 15.8 %copy-start = (bf16[512,2048]{1,0:T(8,128)(2,1)}, bf16[512,2048]{1,0:T(8,128)(2,1)S(1)}, u32[]{:S(2)}) copy-start(bf16[512,2048]{1,0:T(8,128)(2,1)S(1)} %pad_maximum_fusion.refs_0_.refs_5_) | copy-start | bytes 6291460
  35.8 15.5 %collective-permute-start.4 = (bf16[4,28,16,128]{3,2,1,0:T(8,128)(2,1)}, bf16[4,28,16,128]{3,2,1,0:T(8,128)(2,1)S(1)}, u32[]{:S(2)}, u32[]{:S(2)}) collective-permute-start(bf16[4,28,16,128]{3,2,1,0:T(8,128)(2,1)} %get-tuple-element.30), channel_id=1, source_target_pairs={{0,8},{8,0},{16,24},{24,16},{1,9},{9,1},{17,25},{25,17},{2,10},{10... | collective-permute-start | bytes 1376264 | tf_op jit(solution)/shard_map/ppermute | solution.py:396
  37.0 14.2 %collective-permute-start.5 = (bf16[4,28,16,128]{3,2,1,0:T(8,128)(2,1)}, bf16[4,28,16,128]{3,2,1,0:T(8,128)(2,1)S(1)}, u32[]{:S(2)}, u32[]{:S(2)}) collective-permute-start(bf16[4,28,16,128]{3,2,1,0:T(8,128)(2,1)} %get-tuple-element.31), channel_id=1, source_target_pairs={{0,16},{8,24},{16,0},{24,8},{1,17},{9,25},{17,1},{25,9},{2,18},{10... | collective-permute-start | bytes 1376264 | tf_op jit(solution)/shard_map/ppermute | solution.py:396
  49.7 15.1 %collective-permute-start.8 = (bf16[4,24,16,128]{3,2,1,0:T(8,128)(2,1)}, bf16[4,24,16,128]{3,2,1,0:T(8,128)(2,1)}, u32[]{:S(2)}, u32[]{:S(2)}) collective-permute-start(bf16[4,24,16,128]{3,2,1,0:T(8,128)(2,1)} %get-tuple-element.37), channel_id=1, source_target_pairs={{0,8},{8,0},{16,24},{24,16},{1,9},{9,1},{17,25},{25,17},{2,10},{10... | collective-permute-start | bytes 1179656 | tf_op jit(solution)/shard_map/ppermute | solution.py:396
  50.7 14.1 %collective-permute-start.9 = (bf16[4,24,16,128]{3,2,1,0:T(8,128)(2,1)}, bf16[4,24,16,128]{3,2,1,0:T(8,128)(2,1)}, u32[]{:S(2)}, u32[]{:S(2)}) collective-permute-start(bf16[4,24,16,128]{3,2,1,0:T(8,128)(2,1)} %get-tuple-element.38), channel_id=1, source_target_pairs={{0,16},{8,24},{16,0},{24,8},{1,17},{9,25},{17,1},{25,9},{2,18},{10... | collective-permute-start | bytes 1179656 | tf_op jit(solution)/shard_map/ppermute | solution.py:396
  53.7 27.9 %collective-permute-start.6 = (bf16[8,28,16,128]{3,2,1,0:T(8,128)(2,1)}, bf16[8,28,16,128]{3,2,1,0:T(8,128)(2,1)}, u32[]{:S(2)}, u32[]{:S(2)}) collective-permute-start(bf16[8,28,16,128]{3,2,1,0:T(8,128)(2,1)} %get-tuple-element.33.refs_1_), channel_id=1, source_target_pairs={{0,8},{8,0},{16,24},{24,16},{1,9},{9,1},{17,25},{25,17},{2,10},{10... | collective-permute-start | bytes 2752520 | tf_op jit(solution)/shard_map/ppermute | solution.py:396
  55.0 27.8 %collective-permute-start.7 = (bf16[8,28,16,128]{3,2,1,0:T(8,128)(2,1)}, bf16[8,28,16,128]{3,2,1,0:T(8,128)(2,1)}, u32[]{:S(2)}, u32[]{:S(2)}) collective-permute-start(bf16[8,28,16,128]{3,2,1,0:T(8,128)(2,1)} %get-tuple-element.34), channel_id=1, source_target_pairs={{0,16},{8,24},{16,0},{24,8},{1,17},{9,25},{17,1},{25,9},{2,18},{10... | collective-permute-start | bytes 2752520 | tf_op jit(solution)/shard_map/ppermute | solution.py:396
  60.5 45.0 %all-to-all-start.1 = ((bf16[8,52,16,128]{3,2,1,0:T(8,128)(2,1)}), bf16[8,52,16,128]{3,2,1,0:T(8,128)(2,1)}, u32[]{:S(2)}, u32[]{:S(2)}) async-start(bf16[8,52,16,128]{3,2,1,0:T(8,128)(2,1)} %transform.2.refs_4_), calls=%async_computation.1 | async-start | bytes 3407872 | tf_op jit(solution)/shard_map/all_to_all | solution.py:391
  67.4 29.8 %collective-permute-start.10 = (bf16[8,24,16,128]{3,2,1,0:T(8,128)(2,1)}, bf16[8,24,16,128]{3,2,1,0:T(8,128)(2,1)S(1)}, u32[]{:S(2)}, u32[]{:S(2)}) collective-permute-start(bf16[8,24,16,128]{3,2,1,0:T(8,128)(2,1)} %get-tuple-element.39.refs_1_), channel_id=1, source_target_pairs={{0,8},{8,0},{16,24},{24,16},{1,9},{9,1},{17,25},{25,17},{2,10},{10... | collective-permute-start | bytes 2359304 | tf_op jit(solution)/shard_map/ppermute | solution.py:396
  68.9 28.8 %collective-permute-start.11 = (bf16[8,24,16,128]{3,2,1,0:T(8,128)(2,1)}, bf16[8,24,16,128]{3,2,1,0:T(8,128)(2,1)S(1)}, u32[]{:S(2)}, u32[]{:S(2)}) collective-permute-start(bf16[8,24,16,128]{3,2,1,0:T(8,128)(2,1)} %get-tuple-element.40), channel_id=1, source_target_pairs={{0,16},{8,24},{16,0},{24,8},{1,17},{9,25},{17,1},{25,9},{2,18},{10... | collective-permute-start | bytes 2359304 | tf_op jit(solution)/shard_map/ppermute | solution.py:396
  105.4 6.8 %copy-start.7 = (bf16[8,24,16,128]{3,2,1,0:T(8,128)(2,1)S(1)}, bf16[8,24,16,128]{3,2,1,0:T(8,128)(2,1)}, u32[]{:S(2)}) copy-start(bf16[8,24,16,128]{3,2,1,0:T(8,128)(2,1)} %get-tuple-element.39.refs_1_) | copy-start | bytes 2359300
  105.4 6.8 %copy-start.8 = (f32[52,52]{1,0:T(8,128)S(1)}, f32[52,52]{1,0:T(8,128)}, u32[]{:S(2)}) copy-start(f32[52,52]{1,0:T(8,128)} %refs_0_.1) | copy-start | bytes 32452
  105.4 48.5 %all-to-all-start.2 = ((bf16[8,52,16,128]{3,2,1,0:T(8,128)(2,1)}), bf16[8,52,16,128]{3,2,1,0:T(8,128)(2,1)S(1)}, u32[]{:S(2)}, u32[]{:S(2)}) async-start(bf16[8,52,16,128]{3,2,1,0:T(8,128)(2,1)} %gate.1), calls=%async_computation.2 | async-start | bytes 3407872 | tf_op jit(solution)/shard_map/all_to_all | solution.py:391
  109.1 39.7 %collective-permute-start.12 = (bf16[8,52,16,128]{3,2,1,0:T(8,128)(2,1)}, bf16[8,52,16,128]{3,2,1,0:T(8,128)(2,1)S(1)}, u32[]{:S(2)}, u32[]{:S(2)}) collective-permute-start(bf16[8,52,16,128]{3,2,1,0:T(8,128)(2,1)} %all-to-all-done.1.refs_1_.refs_0_), channel_id=1, source_target_pairs={{0,8},{8,0},{16,24},{24,16},{1,9},{9,1},{17,25},{25,17},{2,10},{10... | collective-permute-start | bytes 5111816 | tf_op jit(solution)/shard_map/ppermute | solution.py:396
  110.7 39.4 %collective-permute-start.13 = (bf16[8,52,16,128]{3,2,1,0:T(8,128)(2,1)}, bf16[8,52,16,128]{3,2,1,0:T(8,128)(2,1)S(1)}, u32[]{:S(2)}, u32[]{:S(2)}) collective-permute-start(bf16[8,52,16,128]{3,2,1,0:T(8,128)(2,1)} %all-to-all-done.1.refs_1_.refs_0_), channel_id=1, source_target_pairs={{0,16},{8,24},{16,0},{24,8},{1,17},{9,25},{17,1},{25,9},{2,18},{10... | collective-permute-start | bytes 5111816 | tf_op jit(solution)/shard_map/ppermute | solution.py:396
  148.9 2.2 %copy-start.2 = (bf16[8,52,16,128]{3,2,1,0:T(8,128)(2,1)}, bf16[8,52,16,128]{3,2,1,0:T(8,128)(2,1)S(1)}, u32[]{:S(2)}) copy-start(bf16[8,52,16,128]{3,2,1,0:T(8,128)(2,1)S(1)} %collective-permute-done.12.refs_0_.refs_1_) | copy-start | bytes 5111812
  150.1 1.5 copy-start.4
  151.6 12.4 %collective-permute-start.16 = (bf16[4,28,16,128]{3,2,1,0:T(8,128)(2,1)}, bf16[4,28,16,128]{3,2,1,0:T(8,128)(2,1)}, u32[]{:S(2)}, u32[]{:S(2)}) collective-permute-start(bf16[4,28,16,128]{3,2,1,0:T(8,128)(2,1)} %get-tuple-element.45), channel_id=1, source_target_pairs={{0,8},{8,0},{16,24},{24,16},{1,9},{9,1},{17,25},{25,17},{2,10},{10... | collective-permute-start | bytes 1376264 | tf_op jit(solution)/shard_map/ppermute | solution.py:396
  152.4 12.0 %collective-permute-start.17 = (bf16[4,28,16,128]{3,2,1,0:T(8,128)(2,1)}, bf16[4,28,16,128]{3,2,1,0:T(8,128)(2,1)}, u32[]{:S(2)}, u32[]{:S(2)}) collective-permute-start(bf16[4,28,16,128]{3,2,1,0:T(8,128)(2,1)} %get-tuple-element.46), channel_id=1, source_target_pairs={{0,16},{8,24},{16,0},{24,8},{1,17},{9,25},{17,1},{25,9},{2,18},{10... | collective-permute-start | bytes 1376264 | tf_op jit(solution)/shard_map/ppermute | solution.py:396
  156.2 5.0 %copy-start.3 = (bf16[8,52,16,128]{3,2,1,0:T(8,128)(2,1)S(1)}, bf16[8,52,16,128]{3,2,1,0:T(8,128)(2,1)}, u32[]{:S(2)}) copy-start(bf16[8,52,16,128]{3,2,1,0:T(8,128)(2,1)} %copy-done.2) | copy-start | bytes 5111812
  156.2 5.0 %copy-start.5 = (bf16[8,52,16,128]{3,2,1,0:T(8,128)(2,1)S(1)}, bf16[8,52,16,128]{3,2,1,0:T(8,128)(2,1)}, u32[]{:S(2)}) copy-start(bf16[8,52,16,128]{3,2,1,0:T(8,128)(2,1)} %copy-done.4) | copy-start | bytes 5111812
  156.2 45.8 %all-to-all-start.3 = ((bf16[8,52,16,128]{3,2,1,0:T(8,128)(2,1)}), bf16[8,52,16,128]{3,2,1,0:T(8,128)(2,1)}, u32[]{:S(2)}, u32[]{:S(2)}) async-start(bf16[8,52,16,128]{3,2,1,0:T(8,128)(2,1)} %transform.3.refs_2_.refs_9_), calls=%async_computation.3 | async-start | bytes 3407872 | tf_op jit(solution)/shard_map/all_to_all | solution.py:391
  161.2 3.1 %copy-start.1 = (bf16[512,2048]{1,0:T(8,128)(2,1)S(1)}, bf16[512,2048]{1,0:T(8,128)(2,1)}, u32[]{:S(2)}) copy-start(bf16[512,2048]{1,0:T(8,128)(2,1)} %copy-done) | copy-start | bytes 6291460
  162.2 17.6 %collective-permute-start.14 = (bf16[4,24,16,128]{3,2,1,0:T(8,128)(2,1)}, bf16[4,24,16,128]{3,2,1,0:T(8,128)(2,1)}, u32[]{:S(2)}, u32[]{:S(2)}) collective-permute-start(bf16[4,24,16,128]{3,2,1,0:T(8,128)(2,1)} %get-tuple-element.43), channel_id=1, source_target_pairs={{0,8},{8,0},{16,24},{24,16},{1,9},{9,1},{17,25},{25,17},{2,10},{10... | collective-permute-start | bytes 1179656 | tf_op jit(solution)/shard_map/ppermute | solution.py:396
  163.4 16.4 %collective-permute-start.15 = (bf16[4,24,16,128]{3,2,1,0:T(8,128)(2,1)}, bf16[4,24,16,128]{3,2,1,0:T(8,128)(2,1)}, u32[]{:S(2)}, u32[]{:S(2)}) collective-permute-start(bf16[4,24,16,128]{3,2,1,0:T(8,128)(2,1)} %get-tuple-element.44), channel_id=1, source_target_pairs={{0,16},{8,24},{16,0},{24,8},{1,17},{9,25},{17,1},{25,9},{2,18},{10... | collective-permute-start | bytes 1179656 | tf_op jit(solution)/shard_map/ppermute | solution.py:396
  193.5 0.7 copy-start.6

commit v10 on v9

--- a/solution.py
+++ b/solution.py
@@ -28,14 +28,15 @@
     return high, (value - high.astype(F32)).astype(BF16)
 
 
-def sign_matrix(size):
-    both = lax.broadcasted_iota(jnp.int32, (size, size), 0) & lax.broadcasted_iota(
-        jnp.int32, (size, size), 1
-    )
+def sign_matrix():
+    size = 2 * HB
+    row = lax.broadcasted_iota(jnp.int32, (size, size), 0)
+    col = lax.broadcasted_iota(jnp.int32, (size, size), 1)
+    both = row & col
     parity = jnp.zeros((size, size), jnp.int32)
-    for bit in range(size.bit_length() - 1):
+    for bit in range(HB.bit_length() - 1):
         parity = parity ^ ((both >> bit) & 1)
-    return (1 - 2 * parity).astype(F32).astype(BF16)
+    return jnp.where((row ^ col) < HB, (1 - 2 * parity).astype(F32), 0.0).astype(BF16)
 
 
 def build_mixing(rot_ref, mix_ref, sign_ref, transposed):
@@ -53,7 +54,7 @@
     for half, value in enumerate(spread):
         full = nt_dot(value.astype(BF16), pick)
         mix_ref[half * size : (half + 1) * size, :] = jnp.where(same, full, 0.0).astype(BF16)
-    sign_ref[...] = sign_matrix(HB)
+    sign_ref[...] = sign_matrix()
 
 
 def mix_rows(tiles, mix_ref, sign_ref):
@@ -63,9 +64,9 @@
     halves = nn_dot(mix_ref[...], stacked)
     mixed = (halves[:size] + halves[size:]).astype(BF16)
     results = []
-    for j in range(len(tiles)):
-        part = nn_dot(mixed[:, j * HB : (j + 1) * HB], sign_ref[...])
-        results.append((part * HB ** (-0.5)).reshape(blocks, ROWS, HB))
+    for j in range(0, len(tiles), 2):
+        part = nn_dot(mixed[:, j * HB : (j + 2) * HB], sign_ref[...]) * HB ** (-0.5)
+        results += [part[:, :HB].reshape(blocks, ROWS, HB), part[:, HB:].reshape(blocks, ROWS, HB)]
     return results
 
 
@@ -94,9 +95,12 @@
     blocks = sum(sizes)
     rows = out_ref.shape[0]
     tiles = []
+    start = pl.program_id(0) * (rows // SUB)
     for j in range(rows // SUB):
         wide = [
-            in_ref[j, c].astype(F32) for size, in_ref in zip(sizes, ins) for c in range(size)
+            in_ref[start + j, c].astype(F32)
+            for size, in_ref in zip(sizes, ins)
+            for c in range(size)
         ]
         tiles += [[one[:ROWS] for one in wide], [one[ROWS:] for one in wide]]
     results = mix_rows(tiles, mix_ref, sign_ref)
@@ -109,7 +113,7 @@
 def local_scratch(blocks):
     return [
         pltpu.VMEM((2 * blocks * ROWS, blocks * ROWS), BF16),
-        pltpu.VMEM((HB, HB), BF16),
+        pltpu.VMEM((2 * HB, 2 * HB), BF16),
     ]
 
 
@@ -154,7 +158,7 @@
 
 def backward_matrices(rot_block, after=()):
     size = rot_block.shape[0] * ROWS
-    shapes = [(2 * size, size), (HB, HB)]
+    shapes = [(2 * size, size), (2 * HB, 2 * HB)]
     return pl.pallas_call(
         drop_inputs(
             lambda rot_ref, *refs: build_mixing(rot_ref, *refs, False), 1, len(after)
@@ -176,7 +180,7 @@
     return pl.pallas_call(
         drop_inputs(functools.partial(backward_kernel, sizes), len(sizes) + 2, len(after)),
         grid=(count // parts,),
-        in_specs=[pl.BlockSpec((parts, size, SUB, HB), lambda i: (i, 0, 0, 0)) for size in sizes]
+        in_specs=[pl.BlockSpec(memory_space=pltpu.VMEM)] * len(sizes)
         + [pl.BlockSpec(value.shape, lambda i: (0, 0)) for value in matrices]
         + [ANYWHERE] * len(after),
         out_specs=pl.BlockSpec((parts * SUB, blocks * HB), lambda i: (i, 0)),
@@ -367,8 +371,9 @@
 
 
 def transform_kernel(x_ref, out_ref):
-    count = x_ref.shape[0]
-    values = [x_ref[t].astype(F32) for t in range(count)]
+    count, size = out_ref.shape[:2]
+    start = pl.program_id(0) * size
+    values = [x_ref[t, pl.ds(start, size)].astype(F32) for t in range(count)]
     stride = 1
     while stride < count:
         for t in range(count):
@@ -381,10 +386,18 @@
 
 
 def transform(value, after=(), cost=FREE):
-    steps = 4 if value.shape[1] % 4 == 0 else 1
-    return small_call(
-        transform_kernel, "transform", [value], [value.shape], steps, after, cost
-    )[0]
+    count, groups = value.shape[:2]
+    steps = 4 if groups % 4 == 0 else 1
+    return pl.pallas_call(
+        drop_inputs(transform_kernel, 1, len(after)),
+        grid=(steps,),
+        in_specs=[pl.BlockSpec(memory_space=pltpu.VMEM)] + [ANYWHERE] * len(after),
+        out_specs=pl.BlockSpec((count, groups // steps, SUB, HB), lambda i: (0, i, 0, 0)),
+        out_shape=pltpu.HBM(value.shape, BF16),
+        compiler_params=pltpu.CompilerParams(vmem_limit_bytes=SMALL),
+        cost_estimate=cost,
+        name="transform",
+    )(value, *in_hbm(*after))
 
 
 def exchange(value):

time: 209 us -> 208 us (level)
    pallas_call x4 -> x2, Pallas kernels: 9.71 us -> 5.16 us  [small_call(): pl.pallas_call(drop_inputs(kernel, len(ins), len(after)), grid=(steps,),...]
    pallas_call x0 -> x2, Pallas kernels: none -> 4.32 us  [transform(): pl.pallas_call(drop_inputs(transform_kernel, 1, len(after)), grid=(steps,...]
where the time goes in v10:
time: 208 us; the launch traced here: 207 us
  Pallas kernels  82.2 us (40%)
  waiting for transfers between devices  78.5 us (38%)
  starting transfers between devices  39.6 us (19%)
  local copies, waits for them, and re-layouts  3.43 us (2%)
  other arithmetic  2.56 us (1%)
    ppermute x18, waiting for transfers between devices, partner(): return lax.ppermute(value, axis, [(i, i ^ mask) for i in range(size)])  66.6 us
    pallas_call x2, Pallas kernels, weight_grads(): pl.pallas_call(functools.partial(weights_kernel, first, per, len(rotated)...  29.1 us
    pallas_call x2, Pallas kernels, unit_grads(): pl.pallas_call(drop_inputs(functools.partial(units_kernel, first, per), 3...  24.7 us
    ppermute x18, starting transfers between devices, partner(): return lax.ppermute(value, axis, [(i, i ^ mask) for i in range(size)])  21.2 us
    all_to_all x4, starting transfers between devices, exchange(): lax.all_to_all(value, 'tensor', split_axis=0, concat_axis=0, tiled=True)  18.4 us
    all_to_all x4, waiting for transfers between devices, exchange(): lax.all_to_all(value, 'tensor', split_axis=0, concat_axis=0, tiled=True)  11.9 us
    pallas_call x1, Pallas kernels, local_forward(): pl.pallas_call(functools.partial(forward_kernel, sizes), grid=(rows // (S...  5.71 us
    pallas_call x1, Pallas kernels, local_backward(): pl.pallas_call(drop_inputs(functools.partial(backward_kernel, sizes), len...  5.45 us
  transfers between devices with their start and end apart: 22, of which 12 were waited for; matrix products, arithmetic and copies ran while one was open for 2% of the time, Pallas kernels for 37%

profile of v10, /device:TPU:0, one launch (start us, length us, event | category | flops | bytes accessed | tf_op | source)
XLA Modules:
  0.0 207.1 jit_solution(4043989578436473423)
XLA Ops:
  1.8 3.0 %collective-permute-start = (bf16[64,2048]{1,0:T(8,128)(2,1)S(1)}, bf16[64,2048]{1,0:T(8,128)(2,1)S(1)}, u32[]{:S(2)}, u32[]{:S(2)}) collective-permute-start(bf16[64,2048]{1,0:T(8,128)(2,1)S(1)} %get-tuple-element.51), channel_id=1, source_target_pairs={{0,8},{8,0},{16,24},{24,16},{1,9},{9,1},{17,25},{25,17},{2,10},{10... | collective-permute-start | bytes 786440 | tf_op jit(solution)/shard_map/ppermute | solution.py:409
  4.8 1.5 collective-permute-start.1
  6.4 5.7 %local_forward.1.refs_3_ = bf16[8,52,16,128]{3,2,1,0:T(8,128)(2,1)} custom-call(bf16[128,6656]{1,0:T(8,128)(2,1)} %x_ref.1, f32[52,52]{1,0:T(8,128)} %refs_0_.1), custom_call_target="tpu_custom_call" | custom-call | tf_op jit(solution)/shard_map/local_forward/pallas_call | solution.py:143
  12.1 5.3 %all-to-all-start = ((bf16[8,52,16,128]{3,2,1,0:T(8,128)(2,1)}), bf16[8,52,16,128]{3,2,1,0:T(8,128)(2,1)S(1)}, u32[]{:S(2)}, u32[]{:S(2)}) async-start(bf16[8,52,16,128]{3,2,1,0:T(8,128)(2,1)} %local_forward.1.refs_3_), calls=%async_computation | async-start | bytes 3407872 | tf_op jit(solution)/shard_map/all_to_all | solution.py:404
  19.5 1.3 collective-permute-done.3
  20.8 1.3 broadcast_select_fusion.1
  22.5 13.3 %unit_grads.2 = (bf16[8,28,16,128]{3,2,1,0:T(8,128)(2,1)}, bf16[8,28,16,128]{3,2,1,0:T(8,128)(2,1)}, bf16[8,28,16,128]{3,2,1,0:T(8,128)(2,1)}, bf16[4,28,16,128]{3,2,1,0:T(8,128)(2,1)}, bf16[4,28,16,128]{3,2,1,0:T(8,128)(2,1)}) custom-call(bf16[512,2048]{1,0:T(8,128)(2,1)S(1)} %pad_maximum_fusion.refs_0_.refs_5_, bf16[6656,2048]{1,0:T(8,128)(2,1)} %refs_6_.3, ...), custom_call_target="tpu_custom_call" | custom-call | flops 5000000000 | tf_op jit(solution)/shard_map/unit_grads/pallas_call | solution.py:227
  35.8 1.2 collective-permute-start.4
  38.2 11.4 %unit_grads.3 = (bf16[8,24,16,128]{3,2,1,0:T(8,128)(2,1)}, bf16[8,24,16,128]{3,2,1,0:T(8,128)(2,1)}, bf16[8,24,16,128]{3,2,1,0:T(8,128)(2,1)}, bf16[4,24,16,128]{3,2,1,0:T(8,128)(2,1)}, bf16[4,24,16,128]{3,2,1,0:T(8,128)(2,1)}) custom-call(bf16[512,2048]{1,0:T(8,128)(2,1)S(1)} %pad_maximum_fusion.refs_0_.refs_5_, bf16[6656,2048]{1,0:T(8,128)(2,1)} %refs_6_.3, ...), custom_call_target="tpu_custom_call" | custom-call | tf_op jit(solution)/shard_map/unit_grads/pallas_call | solution.py:227
  51.2 2.5 %relay.2 = (bf16[8,28,16,128]{3,2,1,0:T(8,128)(2,1)}, bf16[8,28,16,128]{3,2,1,0:T(8,128)(2,1)}) custom-call(bf16[8,28,16,128]{3,2,1,0:T(8,128)(2,1)} %get-tuple-element.28.refs_0_, bf16[8,28,16,128]{3,2,1,0:T(8,128)(2,1)} %get-tuple-element.29.refs_1_, bf16[4,28,16,128]{3,2,1,0:T(8,128)(2,1)S(1)} %collective-permute-done.4.refs_2_, ...), custom_call_target="tpu_custom_call" | custom-call | tf_op jit(solution)/shard_map/relay/pallas_call | solution.py:323
  56.1 1.9 all-to-all-done.refs_0_
  58.1 2.2 %transform.2.refs_4_ = bf16[8,52,16,128]{3,2,1,0:T(8,128)(2,1)} custom-call(bf16[8,52,16,128]{3,2,1,0:T(8,128)(2,1)S(1)} %all-to-all-done.refs_0_, bf16[8,28,16,128]{3,2,1,0:T(8,128)(2,1)} %get-tuple-element.33.refs_1_), custom_call_target="tpu_custom_call" | custom-call | flops 999999995904 | tf_op jit(solution)/shard_map/transform/pallas_call | solution.py:391
  60.2 4.3 %all-to-all-start.1 = ((bf16[8,52,16,128]{3,2,1,0:T(8,128)(2,1)}), bf16[8,52,16,128]{3,2,1,0:T(8,128)(2,1)}, u32[]{:S(2)}, u32[]{:S(2)}) async-start(bf16[8,52,16,128]{3,2,1,0:T(8,128)(2,1)} %transform.2.refs_4_), calls=%async_computation.1 | async-start | bytes 3407872 | tf_op jit(solution)/shard_map/all_to_all | solution.py:404
  64.6 2.6 %relay.3 = (bf16[8,24,16,128]{3,2,1,0:T(8,128)(2,1)}, bf16[8,24,16,128]{3,2,1,0:T(8,128)(2,1)}) custom-call(bf16[8,24,16,128]{3,2,1,0:T(8,128)(2,1)} %get-tuple-element.35.refs_0_, bf16[8,24,16,128]{3,2,1,0:T(8,128)(2,1)} %get-tuple-element.36.refs_1_, bf16[4,24,16,128]{3,2,1,0:T(8,128)(2,1)} %collective-permute-done.8.refs_2_, ...), custom_call_target="tpu_custom_call" | custom-call | flops 999999995904 | tf_op jit(solution)/shard_map/relay/pallas_call | solution.py:323
  67.2 1.5 collective-permute-start.10
  68.7 1.5 collective-permute-start.11
  70.2 11.3 %collective-permute-done.6.refs_1_ = bf16[8,28,16,128]{3,2,1,0:T(8,128)(2,1)} collective-permute-done((bf16[8,28,16,128]{3,2,1,0:T(8,128)(2,1)}, bf16[8,28,16,128]{3,2,1,0:T(8,128)(2,1)}, u32[]{:S(2)}, u32[]{:S(2)}) %collective-permute-start.6) | collective-permute-done | bytes 917536 | tf_op jit(solution)/shard_map/ppermute | solution.py:409
  82.8 14.3 %collective-permute-done.10.refs_4_ = bf16[8,24,16,128]{3,2,1,0:T(8,128)(2,1)S(1)} collective-permute-done((bf16[8,24,16,128]{3,2,1,0:T(8,128)(2,1)}, bf16[8,24,16,128]{3,2,1,0:T(8,128)(2,1)S(1)}, u32[]{:S(2)}, u32[]{:S(2)}) %collective-permute-start.10) | collective-permute-done | bytes 786464 | tf_op jit(solution)/shard_map/ppermute | solution.py:409
  97.8 4.3 %total.1.refs_0_ = bf16[8,52,16,128]{3,2,1,0:T(8,128)(2,1)} custom-call(bf16[8,28,16,128]{3,2,1,0:T(8,128)(2,1)} %get-tuple-element.27.refs_3_.refs_0_, bf16[8,28,16,128]{3,2,1,0:T(8,128)(2,1)} %collective-permute-done.6.refs_1_, bf16[8,28,16,128]{3,2,1,0:T(8,128)(2,1)} %collective-permute-done.7.refs_2_, ...), custom_call_target="tpu_custom_call" | custom-call | tf_op jit(solution)/shard_map/total/pallas_call | solution.py:473
  102.1 3.1 %all-to-all-done.1.refs_1_.refs_0_ = bf16[8,52,16,128]{3,2,1,0:T(8,128)(2,1)} async-done(((bf16[8,52,16,128]{3,2,1,0:T(8,128)(2,1)}), bf16[8,52,16,128]{3,2,1,0:T(8,128)(2,1)}, u32[]{:S(2)}, u32[]{:S(2)}) %all-to-all-start.1) | async-done | bytes 1703968 | tf_op jit(solution)/shard_map/all_to_all | solution.py:404
  105.2 3.7 %all-to-all-start.2 = ((bf16[8,52,16,128]{3,2,1,0:T(8,128)(2,1)}), bf16[8,52,16,128]{3,2,1,0:T(8,128)(2,1)S(1)}, u32[]{:S(2)}, u32[]{:S(2)}) async-start(bf16[8,52,16,128]{3,2,1,0:T(8,128)(2,1)} %gate.1), calls=%async_computation.2 | async-start | bytes 3407872 | tf_op jit(solution)/shard_map/all_to_all | solution.py:404
  108.9 1.6 collective-permute-start.12
  110.5 1.5 collective-permute-start.13
  112.0 1.4 backward_matrices.1
  113.4 35.2 %collective-permute-done.12.refs_0_.refs_1_ = bf16[8,52,16,128]{3,2,1,0:T(8,128)(2,1)S(1)} collective-permute-done((bf16[8,52,16,128]{3,2,1,0:T(8,128)(2,1)}, bf16[8,52,16,128]{3,2,1,0:T(8,128)(2,1)S(1)}, u32[]{:S(2)}, u32[]{:S(2)}) %collective-permute-start.12) | collective-permute-done | bytes 1703968 | tf_op jit(solution)/shard_map/ppermute | solution.py:409
  152.1 1.5 collective-permute-start.17
  153.7 2.2 %transform.3.refs_2_.refs_9_ = bf16[8,52,16,128]{3,2,1,0:T(8,128)(2,1)} custom-call(bf16[8,52,16,128]{3,2,1,0:T(8,128)(2,1)S(1)} %all-to-all-done.2.refs_0_), custom_call_target="tpu_custom_call" | custom-call | flops 999999995904 | tf_op jit(solution)/shard_map/transform/pallas_call | solution.py:391
  155.8 5.0 %all-to-all-start.3 = ((bf16[8,52,16,128]{3,2,1,0:T(8,128)(2,1)}), bf16[8,52,16,128]{3,2,1,0:T(8,128)(2,1)}, u32[]{:S(2)}, u32[]{:S(2)}) async-start(bf16[8,52,16,128]{3,2,1,0:T(8,128)(2,1)} %transform.3.refs_2_.refs_9_), calls=%async_computation.3 | async-start | bytes 3407872 | tf_op jit(solution)/shard_map/all_to_all | solution.py:404
  164.1 15.5 %weight_grads.2 = (bf16[6656,2048]{1,0:T(8,128)(2,1)}, f32[28,2048]{1,0:T(8,128)S(1)}) custom-call(bf16[8,52,16,128]{3,2,1,0:T(8,128)(2,1)} %all-to-all-done.1.refs_1_.refs_0_, bf16[8,52,16,128]{3,2,1,0:T(8,128)(2,1)S(1)} %copy-done.3, bf16[8,52,16,128]{3,2,1,0:T(8,128)(2,1)S(1)} %copy-done.5, bf16[4,28,16,128]{3,2,1,0:T(8,128)(2,1)} %collective-permute-done.16.refs_3_, ...), custom_call_target="tpu_custom_call" | custom-call | flops 999999995904 | tf_op jit(solution)/shard_map/weight_grads/pallas_call | solution.py:297
  179.6 13.6 %weight_grads.3 = (bf16[6656,2048]{1,0:T(8,128)(2,1)}, f32[24,2048]{1,0:T(8,128)S(1)}) custom-call(bf16[8,52,16,128]{3,2,1,0:T(8,128)(2,1)} %all-to-all-done.1.refs_1_.refs_0_, bf16[8,52,16,128]{3,2,1,0:T(8,128)(2,1)S(1)} %copy-done.3, bf16[8,52,16,128]{3,2,1,0:T(8,128)(2,1)S(1)} %copy-done.5, ...), custom_call_target="tpu_custom_call", output_to_operand_aliasing={{0}: (9, {})} | custom-call | flops 999999995904 | tf_op jit(solution)/shard_map/weight_grads/pallas_call | solution.py:297
  194.7 6.9 %all-to-all-done.3.refs_0_ = bf16[8,52,16,128]{3,2,1,0:T(8,128)(2,1)} async-done(((bf16[8,52,16,128]{3,2,1,0:T(8,128)(2,1)}), bf16[8,52,16,128]{3,2,1,0:T(8,128)(2,1)}, u32[]{:S(2)}, u32[]{:S(2)}) %all-to-all-start.3) | async-done | bytes 1703968 | tf_op jit(solution)/shard_map/all_to_all | solution.py:404
  201.6 5.5 %local_backward.1 = bf16[128,6656]{1,0:T(8,128)(2,1)} custom-call(bf16[8,52,16,128]{3,2,1,0:T(8,128)(2,1)} %all-to-all-done.3.refs_0_, bf16[832,416]{1,0:T(8,128)(2,1)} %get-tuple-element.41.refs_1_, bf16[256,256]{1,0:T(8,128)(2,1)} %get-tuple-element.42.refs_2_, f32[24,2048]{1,0:T(8,128)} %copy-done.6), custom_call_target="tpu_custom_call" | custom-call | tf_op jit(solution)/shard_map/local_backward/pallas_call | solution.py:180
  (52 shorter events, 19.0 us)
Async XLA Ops:
  1.8 15.6 %collective-permute-start = (bf16[64,2048]{1,0:T(8,128)(2,1)S(1)}, bf16[64,2048]{1,0:T(8,128)(2,1)S(1)}, u32[]{:S(2)}, u32[]{:S(2)}) collective-permute-start(bf16[64,2048]{1,0:T(8,128)(2,1)S(1)} %get-tuple-element.51), channel_id=1, source_target_pairs={{0,8},{8,0},{16,24},{24,16},{1,9},{9,1},{17,25},{25,17},{2,10},{10... | collective-permute-start | bytes 786440 | tf_op jit(solution)/shard_map/ppermute | solution.py:409
  4.8 13.4 %collective-permute-start.1 = (bf16[64,2048]{1,0:T(8,128)(2,1)S(1)}, bf16[64,2048]{1,0:T(8,128)(2,1)S(1)}, u32[]{:S(2)}, u32[]{:S(2)}) collective-permute-start(bf16[64,2048]{1,0:T(8,128)(2,1)S(1)} %get-tuple-element.53), channel_id=1, source_target_pairs={{0,16},{8,24},{16,0},{24,8},{1,17},{9,25},{17,1},{25,9},{2,18},{10... | collective-permute-start | bytes 786440 | tf_op jit(solution)/shard_map/ppermute | solution.py:409
  6.4 11.9 %collective-permute-start.2 = (bf16[64,2048]{1,0:T(8,128)(2,1)S(1)}, bf16[64,2048]{1,0:T(8,128)(2,1)S(1)}, u32[]{:S(2)}, u32[]{:S(2)}) collective-permute-start(bf16[64,2048]{1,0:T(8,128)(2,1)S(1)} %get-tuple-element.52), channel_id=1, source_target_pairs={{0,24},{8,16},{16,8},{24,0},{1,25},{9,17},{17,9},{25,1},{2,26},{10... | collective-permute-start | bytes 786440 | tf_op jit(solution)/shard_map/ppermute | solution.py:409
  12.1 46.0 %all-to-all-start = ((bf16[8,52,16,128]{3,2,1,0:T(8,128)(2,1)}), bf16[8,52,16,128]{3,2,1,0:T(8,128)(2,1)S(1)}, u32[]{:S(2)}, u32[]{:S(2)}) async-start(bf16[8,52,16,128]{3,2,1,0:T(8,128)(2,1)} %local_forward.1.refs_3_), calls=%async_computation | async-start | bytes 3407872 | tf_op jit(solution)/shard_map/all_to_all | solution.py:404
  18.3 2.5 %collective-permute-start.3 = (bf16[3,64,2048]{2,1,0:T(8,128)(2,1)S(1)}, bf16[3,64,2048]{2,1,0:T(8,128)(2,1)}, u32[]{:S(2)}, u32[]{:S(2)}) collective-permute-start(bf16[3,64,2048]{2,1,0:T(8,128)(2,1)S(1)} %pad_maximum_fusion.2), channel_id=1, source_target_pairs={{0,1},{1,0},{2,3},{3,2},{4,5},{5,4},{6,7},{7,6},{8,9},{9,8},{10,11... | collective-permute-start | bytes 2359304 | tf_op jit(solution)/shard_map/ppermute | solution.py:409
  22.5 15.7 %copy-start = (bf16[512,2048]{1,0:T(8,128)(2,1)}, bf16[512,2048]{1,0:T(8,128)(2,1)S(1)}, u32[]{:S(2)}) copy-start(bf16[512,2048]{1,0:T(8,128)(2,1)S(1)} %pad_maximum_fusion.refs_0_.refs_5_) | copy-start | bytes 6291460
  35.8 15.5 %collective-permute-start.4 = (bf16[4,28,16,128]{3,2,1,0:T(8,128)(2,1)}, bf16[4,28,16,128]{3,2,1,0:T(8,128)(2,1)S(1)}, u32[]{:S(2)}, u32[]{:S(2)}) collective-permute-start(bf16[4,28,16,128]{3,2,1,0:T(8,128)(2,1)} %get-tuple-element.30), channel_id=1, source_target_pairs={{0,8},{8,0},{16,24},{24,16},{1,9},{9,1},{17,25},{25,17},{2,10},{10... | collective-permute-start | bytes 1376264 | tf_op jit(solution)/shard_map/ppermute | solution.py:409
  37.0 14.2 %collective-permute-start.5 = (bf16[4,28,16,128]{3,2,1,0:T(8,128)(2,1)}, bf16[4,28,16,128]{3,2,1,0:T(8,128)(2,1)S(1)}, u32[]{:S(2)}, u32[]{:S(2)}) collective-permute-start(bf16[4,28,16,128]{3,2,1,0:T(8,128)(2,1)} %get-tuple-element.31), channel_id=1, source_target_pairs={{0,16},{8,24},{16,0},{24,8},{1,17},{9,25},{17,1},{25,9},{2,18},{10... | collective-permute-start | bytes 1376264 | tf_op jit(solution)/shard_map/ppermute | solution.py:409
  49.5 15.0 %collective-permute-start.8 = (bf16[4,24,16,128]{3,2,1,0:T(8,128)(2,1)}, bf16[4,24,16,128]{3,2,1,0:T(8,128)(2,1)}, u32[]{:S(2)}, u32[]{:S(2)}) collective-permute-start(bf16[4,24,16,128]{3,2,1,0:T(8,128)(2,1)} %get-tuple-element.37), channel_id=1, source_target_pairs={{0,8},{8,0},{16,24},{24,16},{1,9},{9,1},{17,25},{25,17},{2,10},{10... | collective-permute-start | bytes 1179656 | tf_op jit(solution)/shard_map/ppermute | solution.py:409
  50.7 13.8 %collective-permute-start.9 = (bf16[4,24,16,128]{3,2,1,0:T(8,128)(2,1)}, bf16[4,24,16,128]{3,2,1,0:T(8,128)(2,1)}, u32[]{:S(2)}, u32[]{:S(2)}) collective-permute-start(bf16[4,24,16,128]{3,2,1,0:T(8,128)(2,1)} %get-tuple-element.38), channel_id=1, source_target_pairs={{0,16},{8,24},{16,0},{24,8},{1,17},{9,25},{17,1},{25,9},{2,18},{10... | collective-permute-start | bytes 1179656 | tf_op jit(solution)/shard_map/ppermute | solution.py:409
  53.7 27.8 %collective-permute-start.6 = (bf16[8,28,16,128]{3,2,1,0:T(8,128)(2,1)}, bf16[8,28,16,128]{3,2,1,0:T(8,128)(2,1)}, u32[]{:S(2)}, u32[]{:S(2)}) collective-permute-start(bf16[8,28,16,128]{3,2,1,0:T(8,128)(2,1)} %get-tuple-element.33.refs_1_), channel_id=1, source_target_pairs={{0,8},{8,0},{16,24},{24,16},{1,9},{9,1},{17,25},{25,17},{2,10},{10... | collective-permute-start | bytes 2752520 | tf_op jit(solution)/shard_map/ppermute | solution.py:409
  55.0 27.8 %collective-permute-start.7 = (bf16[8,28,16,128]{3,2,1,0:T(8,128)(2,1)}, bf16[8,28,16,128]{3,2,1,0:T(8,128)(2,1)}, u32[]{:S(2)}, u32[]{:S(2)}) collective-permute-start(bf16[8,28,16,128]{3,2,1,0:T(8,128)(2,1)} %get-tuple-element.34), channel_id=1, source_target_pairs={{0,16},{8,24},{16,0},{24,8},{1,17},{9,25},{17,1},{25,9},{2,18},{10... | collective-permute-start | bytes 2752520 | tf_op jit(solution)/shard_map/ppermute | solution.py:409
  60.2 45.0 %all-to-all-start.1 = ((bf16[8,52,16,128]{3,2,1,0:T(8,128)(2,1)}), bf16[8,52,16,128]{3,2,1,0:T(8,128)(2,1)}, u32[]{:S(2)}, u32[]{:S(2)}) async-start(bf16[8,52,16,128]{3,2,1,0:T(8,128)(2,1)} %transform.2.refs_4_), calls=%async_computation.1 | async-start | bytes 3407872 | tf_op jit(solution)/shard_map/all_to_all | solution.py:404
  67.2 29.9 %collective-permute-start.10 = (bf16[8,24,16,128]{3,2,1,0:T(8,128)(2,1)}, bf16[8,24,16,128]{3,2,1,0:T(8,128)(2,1)S(1)}, u32[]{:S(2)}, u32[]{:S(2)}) collective-permute-start(bf16[8,24,16,128]{3,2,1,0:T(8,128)(2,1)} %get-tuple-element.39.refs_1_), channel_id=1, source_target_pairs={{0,8},{8,0},{16,24},{24,16},{1,9},{9,1},{17,25},{25,17},{2,10},{10... | collective-permute-start | bytes 2359304 | tf_op jit(solution)/shard_map/ppermute | solution.py:409
  68.7 29.1 %collective-permute-start.11 = (bf16[8,24,16,128]{3,2,1,0:T(8,128)(2,1)}, bf16[8,24,16,128]{3,2,1,0:T(8,128)(2,1)S(1)}, u32[]{:S(2)}, u32[]{:S(2)}) collective-permute-start(bf16[8,24,16,128]{3,2,1,0:T(8,128)(2,1)} %get-tuple-element.40), channel_id=1, source_target_pairs={{0,16},{8,24},{16,0},{24,8},{1,17},{9,25},{17,1},{25,9},{2,18},{10... | collective-permute-start | bytes 2359304 | tf_op jit(solution)/shard_map/ppermute | solution.py:409
  105.2 6.8 %copy-start.7 = (bf16[8,24,16,128]{3,2,1,0:T(8,128)(2,1)S(1)}, bf16[8,24,16,128]{3,2,1,0:T(8,128)(2,1)}, u32[]{:S(2)}) copy-start(bf16[8,24,16,128]{3,2,1,0:T(8,128)(2,1)} %get-tuple-element.39.refs_1_) | copy-start | bytes 2359300
  105.2 6.8 %copy-start.8 = (f32[52,52]{1,0:T(8,128)S(1)}, f32[52,52]{1,0:T(8,128)}, u32[]{:S(2)}) copy-start(f32[52,52]{1,0:T(8,128)} %refs_0_.1) | copy-start | bytes 32452
  105.2 48.5 %all-to-all-start.2 = ((bf16[8,52,16,128]{3,2,1,0:T(8,128)(2,1)}), bf16[8,52,16,128]{3,2,1,0:T(8,128)(2,1)S(1)}, u32[]{:S(2)}, u32[]{:S(2)}) async-start(bf16[8,52,16,128]{3,2,1,0:T(8,128)(2,1)} %gate.1), calls=%async_computation.2 | async-start | bytes 3407872 | tf_op jit(solution)/shard_map/all_to_all | solution.py:404
  108.9 39.7 %collective-permute-start.12 = (bf16[8,52,16,128]{3,2,1,0:T(8,128)(2,1)}, bf16[8,52,16,128]{3,2,1,0:T(8,128)(2,1)S(1)}, u32[]{:S(2)}, u32[]{:S(2)}) collective-permute-start(bf16[8,52,16,128]{3,2,1,0:T(8,128)(2,1)} %all-to-all-done.1.refs_1_.refs_0_), channel_id=1, source_target_pairs={{0,8},{8,0},{16,24},{24,16},{1,9},{9,1},{17,25},{25,17},{2,10},{10... | collective-permute-start | bytes 5111816 | tf_op jit(solution)/shard_map/ppermute | solution.py:409
  110.5 39.4 %collective-permute-start.13 = (bf16[8,52,16,128]{3,2,1,0:T(8,128)(2,1)}, bf16[8,52,16,128]{3,2,1,0:T(8,128)(2,1)S(1)}, u32[]{:S(2)}, u32[]{:S(2)}) collective-permute-start(bf16[8,52,16,128]{3,2,1,0:T(8,128)(2,1)} %all-to-all-done.1.refs_1_.refs_0_), channel_id=1, source_target_pairs={{0,16},{8,24},{16,0},{24,8},{1,17},{9,25},{17,1},{25,9},{2,18},{10... | collective-permute-start | bytes 5111816 | tf_op jit(solution)/shard_map/ppermute | solution.py:409
  148.6 2.2 %copy-start.2 = (bf16[8,52,16,128]{3,2,1,0:T(8,128)(2,1)}, bf16[8,52,16,128]{3,2,1,0:T(8,128)(2,1)S(1)}, u32[]{:S(2)}) copy-start(bf16[8,52,16,128]{3,2,1,0:T(8,128)(2,1)S(1)} %collective-permute-done.12.refs_0_.refs_1_) | copy-start | bytes 5111812
  149.8 1.5 copy-start.4
  151.3 12.3 %collective-permute-start.16 = (bf16[4,28,16,128]{3,2,1,0:T(8,128)(2,1)}, bf16[4,28,16,128]{3,2,1,0:T(8,128)(2,1)}, u32[]{:S(2)}, u32[]{:S(2)}) collective-permute-start(bf16[4,28,16,128]{3,2,1,0:T(8,128)(2,1)} %get-tuple-element.45), channel_id=1, source_target_pairs={{0,8},{8,0},{16,24},{24,16},{1,9},{9,1},{17,25},{25,17},{2,10},{10... | collective-permute-start | bytes 1376264 | tf_op jit(solution)/shard_map/ppermute | solution.py:409
  152.1 12.0 %collective-permute-start.17 = (bf16[4,28,16,128]{3,2,1,0:T(8,128)(2,1)}, bf16[4,28,16,128]{3,2,1,0:T(8,128)(2,1)}, u32[]{:S(2)}, u32[]{:S(2)}) collective-permute-start(bf16[4,28,16,128]{3,2,1,0:T(8,128)(2,1)} %get-tuple-element.46), channel_id=1, source_target_pairs={{0,16},{8,24},{16,0},{24,8},{1,17},{9,25},{17,1},{25,9},{2,18},{10... | collective-permute-start | bytes 1376264 | tf_op jit(solution)/shard_map/ppermute | solution.py:409
  155.8 5.0 %copy-start.3 = (bf16[8,52,16,128]{3,2,1,0:T(8,128)(2,1)S(1)}, bf16[8,52,16,128]{3,2,1,0:T(8,128)(2,1)}, u32[]{:S(2)}) copy-start(bf16[8,52,16,128]{3,2,1,0:T(8,128)(2,1)} %copy-done.2) | copy-start | bytes 5111812
  155.8 5.0 %copy-start.5 = (bf16[8,52,16,128]{3,2,1,0:T(8,128)(2,1)S(1)}, bf16[8,52,16,128]{3,2,1,0:T(8,128)(2,1)}, u32[]{:S(2)}) copy-start(bf16[8,52,16,128]{3,2,1,0:T(8,128)(2,1)} %copy-done.4) | copy-start | bytes 5111812
  155.8 45.8 %all-to-all-start.3 = ((bf16[8,52,16,128]{3,2,1,0:T(8,128)(2,1)}), bf16[8,52,16,128]{3,2,1,0:T(8,128)(2,1)}, u32[]{:S(2)}, u32[]{:S(2)}) async-start(bf16[8,52,16,128]{3,2,1,0:T(8,128)(2,1)} %transform.3.refs_2_.refs_9_), calls=%async_computation.3 | async-start | bytes 3407872 | tf_op jit(solution)/shard_map/all_to_all | solution.py:404
  160.9 3.3 %copy-start.1 = (bf16[512,2048]{1,0:T(8,128)(2,1)S(1)}, bf16[512,2048]{1,0:T(8,128)(2,1)}, u32[]{:S(2)}) copy-start(bf16[512,2048]{1,0:T(8,128)(2,1)} %copy-done) | copy-start | bytes 6291460
  161.9 17.7 %collective-permute-start.14 = (bf16[4,24,16,128]{3,2,1,0:T(8,128)(2,1)}, bf16[4,24,16,128]{3,2,1,0:T(8,128)(2,1)}, u32[]{:S(2)}, u32[]{:S(2)}) collective-permute-start(bf16[4,24,16,128]{3,2,1,0:T(8,128)(2,1)} %get-tuple-element.43), channel_id=1, source_target_pairs={{0,8},{8,0},{16,24},{24,16},{1,9},{9,1},{17,25},{25,17},{2,10},{10... | collective-permute-start | bytes 1179656 | tf_op jit(solution)/shard_map/ppermute | solution.py:409
  163.1 16.5 %collective-permute-start.15 = (bf16[4,24,16,128]{3,2,1,0:T(8,128)(2,1)}, bf16[4,24,16,128]{3,2,1,0:T(8,128)(2,1)}, u32[]{:S(2)}, u32[]{:S(2)}) collective-permute-start(bf16[4,24,16,128]{3,2,1,0:T(8,128)(2,1)} %get-tuple-element.44), channel_id=1, source_target_pairs={{0,16},{8,24},{16,0},{24,8},{1,17},{9,25},{17,1},{25,9},{2,18},{10... | collective-permute-start | bytes 1179656 | tf_op jit(solution)/shard_map/ppermute | solution.py:409
  193.3 0.7 copy-start.6

commit v11 on v10

--- a/solution.py
+++ b/solution.py
@@ -57,7 +57,7 @@
     sign_ref[...] = sign_matrix()
 
 
-def mix_rows(tiles, mix_ref, sign_ref):
+def mix_rows(tiles, mix_ref, sign_ref, scale):
     blocks = len(tiles[0])
     size = blocks * ROWS
     stacked = jnp.concatenate([jnp.concatenate(one, axis=0).astype(BF16) for one in tiles], axis=1)
@@ -65,12 +65,12 @@
     mixed = (halves[:size] + halves[size:]).astype(BF16)
     results = []
     for j in range(0, len(tiles), 2):
-        part = nn_dot(mixed[:, j * HB : (j + 2) * HB], sign_ref[...]) * HB ** (-0.5)
+        part = nn_dot(mixed[:, j * HB : (j + 2) * HB], sign_ref[...]) * scale
         results += [part[:, :HB].reshape(blocks, ROWS, HB), part[:, HB:].reshape(blocks, ROWS, HB)]
     return results
 
 
-def forward_kernel(sizes, x_ref, rot_ref, *refs):
+def forward_kernel(sizes, scale, x_ref, rot_ref, *refs):
     outs, (mix_ref, sign_ref) = refs[: len(sizes)], refs[len(sizes) :]
     blocks = rot_ref.shape[0]
 
@@ -81,7 +81,7 @@
     rows = x_ref.shape[0]
     wide = [x_ref[:, k * HB : (k + 1) * HB].astype(F32) for k in range(blocks)]
     tiles = [[one[j : j + ROWS] for one in wide] for j in range(0, rows, ROWS)]
-    results = mix_rows(tiles, mix_ref, sign_ref)
+    results = mix_rows(tiles, mix_ref, sign_ref, scale)
     for j in range(rows // SUB):
         both = jnp.concatenate([results[2 * j], results[2 * j + 1]], axis=1).astype(BF16)
         start = 0
@@ -90,7 +90,7 @@
             start += size
 
 
-def backward_kernel(sizes, *refs):
+def backward_kernel(sizes, scale, *refs):
     ins, (mix_ref, sign_ref, out_ref) = refs[: len(sizes)], refs[len(sizes) :]
     blocks = sum(sizes)
     rows = out_ref.shape[0]
@@ -103,7 +103,7 @@
             for c in range(size)
         ]
         tiles += [[one[:ROWS] for one in wide], [one[ROWS:] for one in wide]]
-    results = mix_rows(tiles, mix_ref, sign_ref)
+    results = mix_rows(tiles, mix_ref, sign_ref, scale)
     for j in range(rows // SUB):
         both = jnp.concatenate([results[2 * j], results[2 * j + 1]], axis=1).astype(BF16)
         for k in range(blocks):
@@ -136,12 +136,12 @@
     return run
 
 
-def local_forward(hidden, rot_block, sizes):
+def local_forward(hidden, rot_block, sizes, scale=HB ** (-0.5)):
     rows, width = hidden.shape
     blocks = width // HB
-    parts = 2
-    return pl.pallas_call(
-        functools.partial(forward_kernel, sizes),
+    parts = 4
+    return pl.pallas_call(
+        functools.partial(forward_kernel, sizes, scale),
         grid=(rows // (SUB * parts),),
         in_specs=[
             pl.BlockSpec((SUB * parts, width), lambda i: (i, 0)),
@@ -172,13 +172,13 @@
     )(rot_block, *after)
 
 
-def local_backward(mixed, matrices, sizes, after=()):
+def local_backward(mixed, matrices, sizes, after=(), scale=HB ** (-0.5)):
     count = mixed[0].shape[0]
     rows = count * SUB
     blocks = sum(sizes)
-    parts = 2
-    return pl.pallas_call(
-        drop_inputs(functools.partial(backward_kernel, sizes), len(sizes) + 2, len(after)),
+    parts = 4
+    return pl.pallas_call(
+        drop_inputs(functools.partial(backward_kernel, sizes, scale), len(sizes) + 2, len(after)),
         grid=(count // parts,),
         in_specs=[pl.BlockSpec(memory_space=pltpu.VMEM)] * len(sizes)
         + [pl.BlockSpec(value.shape, lambda i: (0, 0)) for value in matrices]
@@ -382,7 +382,7 @@
                 values[t], values[t | stride] = a + b, a - b
         stride *= 2
     for t in range(count):
-        out_ref[t] = (values[t] * count ** (-0.5)).astype(BF16)
+        out_ref[t] = values[t].astype(BF16)
 
 
 def transform(value, after=(), cost=FREE):
@@ -538,7 +538,8 @@
         return *near, partner(y_half, "dp", 1), partner(x_half, "dp", 2)
 
     up = gather_upstream(upstream)
-    (local,) = local_forward(hidden, rot_block, (groups,))
+    scale = (HB * subs) ** (-0.5)
+    (local,) = local_forward(hidden, rot_block, (groups,), scale)
     forth = exchange(local)
     pers = [size // 4 for size in sizes]
     unit0 = unit_grads(
@@ -567,7 +568,9 @@
     buffer, scale1 = weight_grads(
         gathered1, up, weight, scales, clip_mask, buffer, starts[1], sizes[1], pers[1]
     )
-    grad_hidden = local_backward([final], matrices, (groups,), after=(scale1,))
+    grad_hidden = local_backward(
+        [final], matrices, (groups,), after=(scale1,), scale=scale
+    )
     return grad_hidden, buffer, jnp.concatenate([scale0, scale1], axis=0)
 
 

time: 208 us -> 207 us (level)
  no operation moved by 1% of the time
where the time goes in v11:
time: 207 us; the launch traced here: 206 us
  Pallas kernels  81.2 us (39%)
  waiting for transfers between devices  78.8 us (38%)
  starting transfers between devices  39.3 us (19%)
  local copies, waits for them, and re-layouts  3.43 us (2%)
  other arithmetic  2.56 us (1%)
    ppermute x18, waiting for transfers between devices, partner(): return lax.ppermute(value, axis, [(i, i ^ mask) for i in range(size)])  67.9 us
    pallas_call x2, Pallas kernels, weight_grads(): pl.pallas_call(functools.partial(weights_kernel, first, per, len(rotated)...  29.1 us
    pallas_call x2, Pallas kernels, unit_grads(): pl.pallas_call(drop_inputs(functools.partial(units_kernel, first, per), 3...  24.7 us
    ppermute x18, starting transfers between devices, partner(): return lax.ppermute(value, axis, [(i, i ^ mask) for i in range(size)])  20.9 us
    all_to_all x4, starting transfers between devices, exchange(): lax.all_to_all(value, 'tensor', split_axis=0, concat_axis=0, tiled=True)  18.4 us
    all_to_all x4, waiting for transfers between devices, exchange(): lax.all_to_all(value, 'tensor', split_axis=0, concat_axis=0, tiled=True)  10.9 us
    pallas_call x1, Pallas kernels, local_backward(): pl.pallas_call(drop_inputs(functools.partial(backward_kernel, sizes, scal...  5.18 us
    pallas_call x2, Pallas kernels, small_call(): pl.pallas_call(drop_inputs(kernel, len(ins), len(after)), grid=(steps,),...  5.16 us
  transfers between devices with their start and end apart: 22, of which 12 were waited for; matrix products, arithmetic and copies ran while one was open for 2% of the time, Pallas kernels for 37%

profile of v11, /device:TPU:0, one launch (start us, length us, event | category | flops | bytes accessed | tf_op | source)
XLA Modules:
  0.0 206.1 jit_solution(9345755819027823904)
XLA Ops:
  1.8 3.0 %collective-permute-start = (bf16[64,2048]{1,0:T(8,128)(2,1)S(1)}, bf16[64,2048]{1,0:T(8,128)(2,1)S(1)}, u32[]{:S(2)}, u32[]{:S(2)}) collective-permute-start(bf16[64,2048]{1,0:T(8,128)(2,1)S(1)} %get-tuple-element.51), channel_id=1, source_target_pairs={{0,8},{8,0},{16,24},{24,16},{1,9},{9,1},{17,25},{25,17},{2,10},{10... | collective-permute-start | bytes 786440 | tf_op jit(solution)/shard_map/ppermute | solution.py:409
  4.8 1.5 collective-permute-start.1
  6.4 5.1 %local_forward.1.refs_3_ = bf16[8,52,16,128]{3,2,1,0:T(8,128)(2,1)} custom-call(bf16[128,6656]{1,0:T(8,128)(2,1)} %x_ref.1, f32[52,52]{1,0:T(8,128)} %refs_0_.1), custom_call_target="tpu_custom_call" | custom-call | tf_op jit(solution)/shard_map/local_forward/pallas_call | solution.py:143
  11.5 5.3 %all-to-all-start = ((bf16[8,52,16,128]{3,2,1,0:T(8,128)(2,1)}), bf16[8,52,16,128]{3,2,1,0:T(8,128)(2,1)S(1)}, u32[]{:S(2)}, u32[]{:S(2)}) async-start(bf16[8,52,16,128]{3,2,1,0:T(8,128)(2,1)} %local_forward.1.refs_3_), calls=%async_computation | async-start | bytes 3407872 | tf_op jit(solution)/shard_map/all_to_all | solution.py:404
  16.9 1.4 collective-permute-done.1
  22.5 13.3 %unit_grads.2 = (bf16[8,28,16,128]{3,2,1,0:T(8,128)(2,1)}, bf16[8,28,16,128]{3,2,1,0:T(8,128)(2,1)}, bf16[8,28,16,128]{3,2,1,0:T(8,128)(2,1)}, bf16[4,28,16,128]{3,2,1,0:T(8,128)(2,1)}, bf16[4,28,16,128]{3,2,1,0:T(8,128)(2,1)}) custom-call(bf16[512,2048]{1,0:T(8,128)(2,1)S(1)} %pad_maximum_fusion.refs_0_.refs_5_, bf16[6656,2048]{1,0:T(8,128)(2,1)} %refs_6_.3, ...), custom_call_target="tpu_custom_call" | custom-call | flops 5000000000 | tf_op jit(solution)/shard_map/unit_grads/pallas_call | solution.py:227
  37.8 11.4 %unit_grads.3 = (bf16[8,24,16,128]{3,2,1,0:T(8,128)(2,1)}, bf16[8,24,16,128]{3,2,1,0:T(8,128)(2,1)}, bf16[8,24,16,128]{3,2,1,0:T(8,128)(2,1)}, bf16[4,24,16,128]{3,2,1,0:T(8,128)(2,1)}, bf16[4,24,16,128]{3,2,1,0:T(8,128)(2,1)}) custom-call(bf16[512,2048]{1,0:T(8,128)(2,1)S(1)} %pad_maximum_fusion.refs_0_.refs_5_, bf16[6656,2048]{1,0:T(8,128)(2,1)} %refs_6_.3, ...), custom_call_target="tpu_custom_call" | custom-call | tf_op jit(solution)/shard_map/unit_grads/pallas_call | solution.py:227
  49.2 1.5 collective-permute-start.8
  51.2 2.5 %relay.2 = (bf16[8,28,16,128]{3,2,1,0:T(8,128)(2,1)}, bf16[8,28,16,128]{3,2,1,0:T(8,128)(2,1)}) custom-call(bf16[8,28,16,128]{3,2,1,0:T(8,128)(2,1)} %get-tuple-element.28.refs_0_, bf16[8,28,16,128]{3,2,1,0:T(8,128)(2,1)} %get-tuple-element.29.refs_1_, bf16[4,28,16,128]{3,2,1,0:T(8,128)(2,1)S(1)} %collective-permute-done.4.refs_2_, ...), custom_call_target="tpu_custom_call" | custom-call | tf_op jit(solution)/shard_map/relay/pallas_call | solution.py:323
  55.8 1.7 all-to-all-done.refs_0_
  57.5 2.1 %transform.2.refs_4_ = bf16[8,52,16,128]{3,2,1,0:T(8,128)(2,1)} custom-call(bf16[8,52,16,128]{3,2,1,0:T(8,128)(2,1)S(1)} %all-to-all-done.refs_0_, bf16[8,28,16,128]{3,2,1,0:T(8,128)(2,1)} %get-tuple-element.33.refs_1_), custom_call_target="tpu_custom_call" | custom-call | flops 999999995904 | tf_op jit(solution)/shard_map/transform/pallas_call | solution.py:391
  59.6 4.3 %all-to-all-start.1 = ((bf16[8,52,16,128]{3,2,1,0:T(8,128)(2,1)}), bf16[8,52,16,128]{3,2,1,0:T(8,128)(2,1)}, u32[]{:S(2)}, u32[]{:S(2)}) async-start(bf16[8,52,16,128]{3,2,1,0:T(8,128)(2,1)} %transform.2.refs_4_), calls=%async_computation.1 | async-start | bytes 3407872 | tf_op jit(solution)/shard_map/all_to_all | solution.py:404
  63.9 2.6 %relay.3 = (bf16[8,24,16,128]{3,2,1,0:T(8,128)(2,1)}, bf16[8,24,16,128]{3,2,1,0:T(8,128)(2,1)}) custom-call(bf16[8,24,16,128]{3,2,1,0:T(8,128)(2,1)} %get-tuple-element.35.refs_0_, bf16[8,24,16,128]{3,2,1,0:T(8,128)(2,1)} %get-tuple-element.36.refs_1_, bf16[4,24,16,128]{3,2,1,0:T(8,128)(2,1)} %collective-permute-done.8.refs_2_, ...), custom_call_target="tpu_custom_call" | custom-call | flops 999999995904 | tf_op jit(solution)/shard_map/relay/pallas_call | solution.py:323
  66.6 1.5 collective-permute-start.10
  68.1 1.5 collective-permute-start.11
  69.6 11.6 %collective-permute-done.6.refs_1_ = bf16[8,28,16,128]{3,2,1,0:T(8,128)(2,1)} collective-permute-done((bf16[8,28,16,128]{3,2,1,0:T(8,128)(2,1)}, bf16[8,28,16,128]{3,2,1,0:T(8,128)(2,1)}, u32[]{:S(2)}, u32[]{:S(2)}) %collective-permute-start.6) | collective-permute-done | bytes 917536 | tf_op jit(solution)/shard_map/ppermute | solution.py:409
  81.2 1.5 collective-permute-done.7.refs_2_
  82.8 13.8 %collective-permute-done.10.refs_4_ = bf16[8,24,16,128]{3,2,1,0:T(8,128)(2,1)S(1)} collective-permute-done((bf16[8,24,16,128]{3,2,1,0:T(8,128)(2,1)}, bf16[8,24,16,128]{3,2,1,0:T(8,128)(2,1)S(1)}, u32[]{:S(2)}, u32[]{:S(2)}) %collective-permute-start.10) | collective-permute-done | bytes 786464 | tf_op jit(solution)/shard_map/ppermute | solution.py:409
  97.8 4.3 %total.1.refs_0_ = bf16[8,52,16,128]{3,2,1,0:T(8,128)(2,1)} custom-call(bf16[8,28,16,128]{3,2,1,0:T(8,128)(2,1)} %get-tuple-element.27.refs_3_.refs_0_, bf16[8,28,16,128]{3,2,1,0:T(8,128)(2,1)} %collective-permute-done.6.refs_1_, bf16[8,28,16,128]{3,2,1,0:T(8,128)(2,1)} %collective-permute-done.7.refs_2_, ...), custom_call_target="tpu_custom_call" | custom-call | tf_op jit(solution)/shard_map/total/pallas_call | solution.py:473
  102.1 2.5 %all-to-all-done.1.refs_1_.refs_0_ = bf16[8,52,16,128]{3,2,1,0:T(8,128)(2,1)} async-done(((bf16[8,52,16,128]{3,2,1,0:T(8,128)(2,1)}), bf16[8,52,16,128]{3,2,1,0:T(8,128)(2,1)}, u32[]{:S(2)}, u32[]{:S(2)}) %all-to-all-start.1) | async-done | bytes 1703968 | tf_op jit(solution)/shard_map/all_to_all | solution.py:404
  104.5 3.7 %all-to-all-start.2 = ((bf16[8,52,16,128]{3,2,1,0:T(8,128)(2,1)}), bf16[8,52,16,128]{3,2,1,0:T(8,128)(2,1)S(1)}, u32[]{:S(2)}, u32[]{:S(2)}) async-start(bf16[8,52,16,128]{3,2,1,0:T(8,128)(2,1)} %gate.1), calls=%async_computation.2 | async-start | bytes 3407872 | tf_op jit(solution)/shard_map/all_to_all | solution.py:404
  108.3 1.6 collective-permute-start.12
  109.8 1.5 collective-permute-start.13
  111.4 1.4 backward_matrices.1
  112.8 35.2 %collective-permute-done.12.refs_0_.refs_1_ = bf16[8,52,16,128]{3,2,1,0:T(8,128)(2,1)S(1)} collective-permute-done((bf16[8,52,16,128]{3,2,1,0:T(8,128)(2,1)}, bf16[8,52,16,128]{3,2,1,0:T(8,128)(2,1)S(1)}, u32[]{:S(2)}, u32[]{:S(2)}) %collective-permute-start.12) | collective-permute-done | bytes 1703968 | tf_op jit(solution)/shard_map/ppermute | solution.py:409
  151.5 1.5 collective-permute-start.17
  153.0 2.1 %transform.3.refs_2_.refs_9_ = bf16[8,52,16,128]{3,2,1,0:T(8,128)(2,1)} custom-call(bf16[8,52,16,128]{3,2,1,0:T(8,128)(2,1)S(1)} %all-to-all-done.2.refs_0_), custom_call_target="tpu_custom_call" | custom-call | flops 999999995904 | tf_op jit(solution)/shard_map/transform/pallas_call | solution.py:391
  155.1 5.0 %all-to-all-start.3 = ((bf16[8,52,16,128]{3,2,1,0:T(8,128)(2,1)}), bf16[8,52,16,128]{3,2,1,0:T(8,128)(2,1)}, u32[]{:S(2)}, u32[]{:S(2)}) async-start(bf16[8,52,16,128]{3,2,1,0:T(8,128)(2,1)} %transform.3.refs_2_.refs_9_), calls=%async_computation.3 | async-start | bytes 3407872 | tf_op jit(solution)/shard_map/all_to_all | solution.py:404
  163.5 15.5 %weight_grads.2 = (bf16[6656,2048]{1,0:T(8,128)(2,1)}, f32[28,2048]{1,0:T(8,128)S(1)}) custom-call(bf16[8,52,16,128]{3,2,1,0:T(8,128)(2,1)} %all-to-all-done.1.refs_1_.refs_0_, bf16[8,52,16,128]{3,2,1,0:T(8,128)(2,1)S(1)} %copy-done.3, bf16[8,52,16,128]{3,2,1,0:T(8,128)(2,1)S(1)} %copy-done.5, bf16[4,28,16,128]{3,2,1,0:T(8,128)(2,1)} %collective-permute-done.16.refs_3_, ...), custom_call_target="tpu_custom_call" | custom-call | flops 999999995904 | tf_op jit(solution)/shard_map/weight_grads/pallas_call | solution.py:297
  179.0 13.7 %weight_grads.3 = (bf16[6656,2048]{1,0:T(8,128)(2,1)}, f32[24,2048]{1,0:T(8,128)S(1)}) custom-call(bf16[8,52,16,128]{3,2,1,0:T(8,128)(2,1)} %all-to-all-done.1.refs_1_.refs_0_, bf16[8,52,16,128]{3,2,1,0:T(8,128)(2,1)S(1)} %copy-done.3, bf16[8,52,16,128]{3,2,1,0:T(8,128)(2,1)S(1)} %copy-done.5, ...), custom_call_target="tpu_custom_call", output_to_operand_aliasing={{0}: (9, {})} | custom-call | flops 999999995904 | tf_op jit(solution)/shard_map/weight_grads/pallas_call | solution.py:297
  194.1 6.8 %all-to-all-done.3.refs_0_ = bf16[8,52,16,128]{3,2,1,0:T(8,128)(2,1)} async-done(((bf16[8,52,16,128]{3,2,1,0:T(8,128)(2,1)}), bf16[8,52,16,128]{3,2,1,0:T(8,128)(2,1)}, u32[]{:S(2)}, u32[]{:S(2)}) %all-to-all-start.3) | async-done | bytes 1703968 | tf_op jit(solution)/shard_map/all_to_all | solution.py:404
  200.9 5.2 %local_backward.1 = bf16[128,6656]{1,0:T(8,128)(2,1)} custom-call(bf16[8,52,16,128]{3,2,1,0:T(8,128)(2,1)} %all-to-all-done.3.refs_0_, bf16[832,416]{1,0:T(8,128)(2,1)} %get-tuple-element.41.refs_1_, bf16[256,256]{1,0:T(8,128)(2,1)} %get-tuple-element.42.refs_2_, f32[24,2048]{1,0:T(8,128)} %copy-done.6), custom_call_target="tpu_custom_call" | custom-call | tf_op jit(solution)/shard_map/local_backward/pallas_call | solution.py:180
  (52 shorter events, 19.6 us)
Async XLA Ops:
  1.8 15.0 %collective-permute-start = (bf16[64,2048]{1,0:T(8,128)(2,1)S(1)}, bf16[64,2048]{1,0:T(8,128)(2,1)S(1)}, u32[]{:S(2)}, u32[]{:S(2)}) collective-permute-start(bf16[64,2048]{1,0:T(8,128)(2,1)S(1)} %get-tuple-element.51), channel_id=1, source_target_pairs={{0,8},{8,0},{16,24},{24,16},{1,9},{9,1},{17,25},{25,17},{2,10},{10... | collective-permute-start | bytes 786440 | tf_op jit(solution)/shard_map/ppermute | solution.py:409
  4.8 13.4 %collective-permute-start.1 = (bf16[64,2048]{1,0:T(8,128)(2,1)S(1)}, bf16[64,2048]{1,0:T(8,128)(2,1)S(1)}, u32[]{:S(2)}, u32[]{:S(2)}) collective-permute-start(bf16[64,2048]{1,0:T(8,128)(2,1)S(1)} %get-tuple-element.53), channel_id=1, source_target_pairs={{0,16},{8,24},{16,0},{24,8},{1,17},{9,25},{17,1},{25,9},{2,18},{10... | collective-permute-start | bytes 786440 | tf_op jit(solution)/shard_map/ppermute | solution.py:409
  6.4 11.9 %collective-permute-start.2 = (bf16[64,2048]{1,0:T(8,128)(2,1)S(1)}, bf16[64,2048]{1,0:T(8,128)(2,1)S(1)}, u32[]{:S(2)}, u32[]{:S(2)}) collective-permute-start(bf16[64,2048]{1,0:T(8,128)(2,1)S(1)} %get-tuple-element.52), channel_id=1, source_target_pairs={{0,24},{8,16},{16,8},{24,0},{1,25},{9,17},{17,9},{25,1},{2,26},{10... | collective-permute-start | bytes 786440 | tf_op jit(solution)/shard_map/ppermute | solution.py:409
  11.5 46.0 %all-to-all-start = ((bf16[8,52,16,128]{3,2,1,0:T(8,128)(2,1)}), bf16[8,52,16,128]{3,2,1,0:T(8,128)(2,1)S(1)}, u32[]{:S(2)}, u32[]{:S(2)}) async-start(bf16[8,52,16,128]{3,2,1,0:T(8,128)(2,1)} %local_forward.1.refs_3_), calls=%async_computation | async-start | bytes 3407872 | tf_op jit(solution)/shard_map/all_to_all | solution.py:404
  18.3 2.5 %collective-permute-start.3 = (bf16[3,64,2048]{2,1,0:T(8,128)(2,1)S(1)}, bf16[3,64,2048]{2,1,0:T(8,128)(2,1)}, u32[]{:S(2)}, u32[]{:S(2)}) collective-permute-start(bf16[3,64,2048]{2,1,0:T(8,128)(2,1)S(1)} %pad_maximum_fusion.2), channel_id=1, source_target_pairs={{0,1},{1,0},{2,3},{3,2},{4,5},{5,4},{6,7},{7,6},{8,9},{9,8},{10,11... | collective-permute-start | bytes 2359304 | tf_op jit(solution)/shard_map/ppermute | solution.py:409
  22.5 15.4 %copy-start = (bf16[512,2048]{1,0:T(8,128)(2,1)}, bf16[512,2048]{1,0:T(8,128)(2,1)S(1)}, u32[]{:S(2)}) copy-start(bf16[512,2048]{1,0:T(8,128)(2,1)S(1)} %pad_maximum_fusion.refs_0_.refs_5_) | copy-start | bytes 6291460
  35.8 15.5 %collective-permute-start.4 = (bf16[4,28,16,128]{3,2,1,0:T(8,128)(2,1)}, bf16[4,28,16,128]{3,2,1,0:T(8,128)(2,1)S(1)}, u32[]{:S(2)}, u32[]{:S(2)}) collective-permute-start(bf16[4,28,16,128]{3,2,1,0:T(8,128)(2,1)} %get-tuple-element.30), channel_id=1, source_target_pairs={{0,8},{8,0},{16,24},{24,16},{1,9},{9,1},{17,25},{25,17},{2,10},{10... | collective-permute-start | bytes 1376264 | tf_op jit(solution)/shard_map/ppermute | solution.py:409
  37.0 14.2 %collective-permute-start.5 = (bf16[4,28,16,128]{3,2,1,0:T(8,128)(2,1)}, bf16[4,28,16,128]{3,2,1,0:T(8,128)(2,1)S(1)}, u32[]{:S(2)}, u32[]{:S(2)}) collective-permute-start(bf16[4,28,16,128]{3,2,1,0:T(8,128)(2,1)} %get-tuple-element.31), channel_id=1, source_target_pairs={{0,16},{8,24},{16,0},{24,8},{1,17},{9,25},{17,1},{25,9},{2,18},{10... | collective-permute-start | bytes 1376264 | tf_op jit(solution)/shard_map/ppermute | solution.py:409
  49.2 14.7 %collective-permute-start.8 = (bf16[4,24,16,128]{3,2,1,0:T(8,128)(2,1)}, bf16[4,24,16,128]{3,2,1,0:T(8,128)(2,1)}, u32[]{:S(2)}, u32[]{:S(2)}) collective-permute-start(bf16[4,24,16,128]{3,2,1,0:T(8,128)(2,1)} %get-tuple-element.37), channel_id=1, source_target_pairs={{0,8},{8,0},{16,24},{24,16},{1,9},{9,1},{17,25},{25,17},{2,10},{10... | collective-permute-start | bytes 1179656 | tf_op jit(solution)/shard_map/ppermute | solution.py:409
  50.7 13.2 %collective-permute-start.9 = (bf16[4,24,16,128]{3,2,1,0:T(8,128)(2,1)}, bf16[4,24,16,128]{3,2,1,0:T(8,128)(2,1)}, u32[]{:S(2)}, u32[]{:S(2)}) collective-permute-start(bf16[4,24,16,128]{3,2,1,0:T(8,128)(2,1)} %get-tuple-element.38), channel_id=1, source_target_pairs={{0,16},{8,24},{16,0},{24,8},{1,17},{9,25},{17,1},{25,9},{2,18},{10... | collective-permute-start | bytes 1179656 | tf_op jit(solution)/shard_map/ppermute | solution.py:409
  53.7 27.5 %collective-permute-start.6 = (bf16[8,28,16,128]{3,2,1,0:T(8,128)(2,1)}, bf16[8,28,16,128]{3,2,1,0:T(8,128)(2,1)}, u32[]{:S(2)}, u32[]{:S(2)}) collective-permute-start(bf16[8,28,16,128]{3,2,1,0:T(8,128)(2,1)} %get-tuple-element.33.refs_1_), channel_id=1, source_target_pairs={{0,8},{8,0},{16,24},{24,16},{1,9},{9,1},{17,25},{25,17},{2,10},{10... | collective-permute-start | bytes 2752520 | tf_op jit(solution)/shard_map/ppermute | solution.py:409
  55.0 27.8 %collective-permute-start.7 = (bf16[8,28,16,128]{3,2,1,0:T(8,128)(2,1)}, bf16[8,28,16,128]{3,2,1,0:T(8,128)(2,1)}, u32[]{:S(2)}, u32[]{:S(2)}) collective-permute-start(bf16[8,28,16,128]{3,2,1,0:T(8,128)(2,1)} %get-tuple-element.34), channel_id=1, source_target_pairs={{0,16},{8,24},{16,0},{24,8},{1,17},{9,25},{17,1},{25,9},{2,18},{10... | collective-permute-start | bytes 2752520 | tf_op jit(solution)/shard_map/ppermute | solution.py:409
  59.6 45.0 %all-to-all-start.1 = ((bf16[8,52,16,128]{3,2,1,0:T(8,128)(2,1)}), bf16[8,52,16,128]{3,2,1,0:T(8,128)(2,1)}, u32[]{:S(2)}, u32[]{:S(2)}) async-start(bf16[8,52,16,128]{3,2,1,0:T(8,128)(2,1)} %transform.2.refs_4_), calls=%async_computation.1 | async-start | bytes 3407872 | tf_op jit(solution)/shard_map/all_to_all | solution.py:404
  66.6 30.0 %collective-permute-start.10 = (bf16[8,24,16,128]{3,2,1,0:T(8,128)(2,1)}, bf16[8,24,16,128]{3,2,1,0:T(8,128)(2,1)S(1)}, u32[]{:S(2)}, u32[]{:S(2)}) collective-permute-start(bf16[8,24,16,128]{3,2,1,0:T(8,128)(2,1)} %get-tuple-element.39.refs_1_), channel_id=1, source_target_pairs={{0,8},{8,0},{16,24},{24,16},{1,9},{9,1},{17,25},{25,17},{2,10},{10... | collective-permute-start | bytes 2359304 | tf_op jit(solution)/shard_map/ppermute | solution.py:409
  68.1 29.7 %collective-permute-start.11 = (bf16[8,24,16,128]{3,2,1,0:T(8,128)(2,1)}, bf16[8,24,16,128]{3,2,1,0:T(8,128)(2,1)S(1)}, u32[]{:S(2)}, u32[]{:S(2)}) collective-permute-start(bf16[8,24,16,128]{3,2,1,0:T(8,128)(2,1)} %get-tuple-element.40), channel_id=1, source_target_pairs={{0,16},{8,24},{16,0},{24,8},{1,17},{9,25},{17,1},{25,9},{2,18},{10... | collective-permute-start | bytes 2359304 | tf_op jit(solution)/shard_map/ppermute | solution.py:409
  104.5 6.8 %copy-start.7 = (bf16[8,24,16,128]{3,2,1,0:T(8,128)(2,1)S(1)}, bf16[8,24,16,128]{3,2,1,0:T(8,128)(2,1)}, u32[]{:S(2)}) copy-start(bf16[8,24,16,128]{3,2,1,0:T(8,128)(2,1)} %get-tuple-element.39.refs_1_) | copy-start | bytes 2359300
  104.5 6.8 %copy-start.8 = (f32[52,52]{1,0:T(8,128)S(1)}, f32[52,52]{1,0:T(8,128)}, u32[]{:S(2)}) copy-start(f32[52,52]{1,0:T(8,128)} %refs_0_.1) | copy-start | bytes 32452
  104.5 48.5 %all-to-all-start.2 = ((bf16[8,52,16,128]{3,2,1,0:T(8,128)(2,1)}), bf16[8,52,16,128]{3,2,1,0:T(8,128)(2,1)S(1)}, u32[]{:S(2)}, u32[]{:S(2)}) async-start(bf16[8,52,16,128]{3,2,1,0:T(8,128)(2,1)} %gate.1), calls=%async_computation.2 | async-start | bytes 3407872 | tf_op jit(solution)/shard_map/all_to_all | solution.py:404
  108.3 39.7 %collective-permute-start.12 = (bf16[8,52,16,128]{3,2,1,0:T(8,128)(2,1)}, bf16[8,52,16,128]{3,2,1,0:T(8,128)(2,1)S(1)}, u32[]{:S(2)}, u32[]{:S(2)}) collective-permute-start(bf16[8,52,16,128]{3,2,1,0:T(8,128)(2,1)} %all-to-all-done.1.refs_1_.refs_0_), channel_id=1, source_target_pairs={{0,8},{8,0},{16,24},{24,16},{1,9},{9,1},{17,25},{25,17},{2,10},{10... | collective-permute-start | bytes 5111816 | tf_op jit(solution)/shard_map/ppermute | solution.py:409
  109.8 39.4 %collective-permute-start.13 = (bf16[8,52,16,128]{3,2,1,0:T(8,128)(2,1)}, bf16[8,52,16,128]{3,2,1,0:T(8,128)(2,1)S(1)}, u32[]{:S(2)}, u32[]{:S(2)}) collective-permute-start(bf16[8,52,16,128]{3,2,1,0:T(8,128)(2,1)} %all-to-all-done.1.refs_1_.refs_0_), channel_id=1, source_target_pairs={{0,16},{8,24},{16,0},{24,8},{1,17},{9,25},{17,1},{25,9},{2,18},{10... | collective-permute-start | bytes 5111816 | tf_op jit(solution)/shard_map/ppermute | solution.py:409
  148.0 2.2 %copy-start.2 = (bf16[8,52,16,128]{3,2,1,0:T(8,128)(2,1)}, bf16[8,52,16,128]{3,2,1,0:T(8,128)(2,1)S(1)}, u32[]{:S(2)}) copy-start(bf16[8,52,16,128]{3,2,1,0:T(8,128)(2,1)S(1)} %collective-permute-done.12.refs_0_.refs_1_) | copy-start | bytes 5111812
  149.2 1.5 copy-start.4
  150.7 12.2 %collective-permute-start.16 = (bf16[4,28,16,128]{3,2,1,0:T(8,128)(2,1)}, bf16[4,28,16,128]{3,2,1,0:T(8,128)(2,1)}, u32[]{:S(2)}, u32[]{:S(2)}) collective-permute-start(bf16[4,28,16,128]{3,2,1,0:T(8,128)(2,1)} %get-tuple-element.45), channel_id=1, source_target_pairs={{0,8},{8,0},{16,24},{24,16},{1,9},{9,1},{17,25},{25,17},{2,10},{10... | collective-permute-start | bytes 1376264 | tf_op jit(solution)/shard_map/ppermute | solution.py:409
  151.5 12.0 %collective-permute-start.17 = (bf16[4,28,16,128]{3,2,1,0:T(8,128)(2,1)}, bf16[4,28,16,128]{3,2,1,0:T(8,128)(2,1)}, u32[]{:S(2)}, u32[]{:S(2)}) collective-permute-start(bf16[4,28,16,128]{3,2,1,0:T(8,128)(2,1)} %get-tuple-element.46), channel_id=1, source_target_pairs={{0,16},{8,24},{16,0},{24,8},{1,17},{9,25},{17,1},{25,9},{2,18},{10... | collective-permute-start | bytes 1376264 | tf_op jit(solution)/shard_map/ppermute | solution.py:409
  155.1 5.0 %copy-start.3 = (bf16[8,52,16,128]{3,2,1,0:T(8,128)(2,1)S(1)}, bf16[8,52,16,128]{3,2,1,0:T(8,128)(2,1)}, u32[]{:S(2)}) copy-start(bf16[8,52,16,128]{3,2,1,0:T(8,128)(2,1)} %copy-done.2) | copy-start | bytes 5111812
  155.1 5.0 %copy-start.5 = (bf16[8,52,16,128]{3,2,1,0:T(8,128)(2,1)S(1)}, bf16[8,52,16,128]{3,2,1,0:T(8,128)(2,1)}, u32[]{:S(2)}) copy-start(bf16[8,52,16,128]{3,2,1,0:T(8,128)(2,1)} %copy-done.4) | copy-start | bytes 5111812
  155.1 45.8 %all-to-all-start.3 = ((bf16[8,52,16,128]{3,2,1,0:T(8,128)(2,1)}), bf16[8,52,16,128]{3,2,1,0:T(8,128)(2,1)}, u32[]{:S(2)}, u32[]{:S(2)}) async-start(bf16[8,52,16,128]{3,2,1,0:T(8,128)(2,1)} %transform.3.refs_2_.refs_9_), calls=%async_computation.3 | async-start | bytes 3407872 | tf_op jit(solution)/shard_map/all_to_all | solution.py:404
  160.2 3.3 %copy-start.1 = (bf16[512,2048]{1,0:T(8,128)(2,1)S(1)}, bf16[512,2048]{1,0:T(8,128)(2,1)}, u32[]{:S(2)}) copy-start(bf16[512,2048]{1,0:T(8,128)(2,1)} %copy-done) | copy-start | bytes 6291460
  161.2 17.8 %collective-permute-start.14 = (bf16[4,24,16,128]{3,2,1,0:T(8,128)(2,1)}, bf16[4,24,16,128]{3,2,1,0:T(8,128)(2,1)}, u32[]{:S(2)}, u32[]{:S(2)}) collective-permute-start(bf16[4,24,16,128]{3,2,1,0:T(8,128)(2,1)} %get-tuple-element.43), channel_id=1, source_target_pairs={{0,8},{8,0},{16,24},{24,16},{1,9},{9,1},{17,25},{25,17},{2,10},{10... | collective-permute-start | bytes 1179656 | tf_op jit(solution)/shard_map/ppermute | solution.py:409
  162.4 16.6 %collective-permute-start.15 = (bf16[4,24,16,128]{3,2,1,0:T(8,128)(2,1)}, bf16[4,24,16,128]{3,2,1,0:T(8,128)(2,1)}, u32[]{:S(2)}, u32[]{:S(2)}) collective-permute-start(bf16[4,24,16,128]{3,2,1,0:T(8,128)(2,1)} %get-tuple-element.44), channel_id=1, source_target_pairs={{0,16},{8,24},{16,0},{24,8},{1,17},{9,25},{17,1},{25,9},{2,18},{10... | collective-permute-start | bytes 1179656 | tf_op jit(solution)/shard_map/ppermute | solution.py:409
  192.7 0.7 copy-start.6

commit v12 on v11

--- a/solution.py
+++ b/solution.py
@@ -90,23 +90,22 @@
             start += size
 
 
-def backward_kernel(sizes, scale, *refs):
-    ins, (mix_ref, sign_ref, out_ref) = refs[: len(sizes)], refs[len(sizes) :]
-    blocks = sum(sizes)
+def backward_kernel(counts, scale, *refs):
+    ins, (mix_ref, sign_ref, out_ref) = refs[: sum(counts)], refs[sum(counts) :]
+    chunks = [ins[sum(counts[:i]) : sum(counts[: i + 1])] for i in range(len(counts))]
     rows = out_ref.shape[0]
     tiles = []
-    start = pl.program_id(0) * (rows // SUB)
     for j in range(rows // SUB):
         wide = [
-            in_ref[start + j, c].astype(F32)
-            for size, in_ref in zip(sizes, ins)
-            for c in range(size)
+            sum(term[j, c].astype(F32) for term in terms)
+            for terms in chunks
+            for c in range(terms[0].shape[1])
         ]
         tiles += [[one[:ROWS] for one in wide], [one[ROWS:] for one in wide]]
     results = mix_rows(tiles, mix_ref, sign_ref, scale)
     for j in range(rows // SUB):
         both = jnp.concatenate([results[2 * j], results[2 * j + 1]], axis=1).astype(BF16)
-        for k in range(blocks):
+        for k in range(both.shape[0]):
             out_ref[j * SUB : (j + 1) * SUB, k * HB : (k + 1) * HB] = both[k]
 
 
@@ -172,23 +171,22 @@
     )(rot_block, *after)
 
 
-def local_backward(mixed, matrices, sizes, after=(), scale=HB ** (-0.5)):
-    count = mixed[0].shape[0]
-    rows = count * SUB
-    blocks = sum(sizes)
+def local_backward(chunks, matrices, scale=HB ** (-0.5)):
+    ins = [value for own, *far in chunks for value in (*in_hbm(own), *far)]
+    count = ins[0].shape[0]
+    width = sum(chunk[0].shape[1] for chunk in chunks) * HB
     parts = 4
     return pl.pallas_call(
-        drop_inputs(functools.partial(backward_kernel, sizes, scale), len(sizes) + 2, len(after)),
+        functools.partial(backward_kernel, [len(chunk) for chunk in chunks], scale),
         grid=(count // parts,),
-        in_specs=[pl.BlockSpec(memory_space=pltpu.VMEM)] * len(sizes)
-        + [pl.BlockSpec(value.shape, lambda i: (0, 0)) for value in matrices]
-        + [ANYWHERE] * len(after),
-        out_specs=pl.BlockSpec((parts * SUB, blocks * HB), lambda i: (i, 0)),
-        out_shape=pltpu.HBM((rows, blocks * HB), BF16),
-        compiler_params=pltpu.CompilerParams(vmem_limit_bytes=24 << 20),
+        in_specs=[pl.BlockSpec((parts,) + v.shape[1:], lambda i: (i, 0, 0, 0)) for v in ins]
+        + [pl.BlockSpec(value.shape, lambda i: (0, 0)) for value in matrices],
+        out_specs=pl.BlockSpec((parts * SUB, width), lambda i: (i, 0)),
+        out_shape=pltpu.HBM((count * SUB, width), BF16),
+        compiler_params=pltpu.CompilerParams(vmem_limit_bytes=32 << 20),
         cost_estimate=FREE,
         name="local_backward",
-    )(*mixed, *in_hbm(*matrices, *after))
+    )(*ins, *in_hbm(*matrices))
 
 
 def weight_spec(first, per, cols):
@@ -371,9 +369,9 @@
 
 
 def transform_kernel(x_ref, out_ref):
-    count, size = out_ref.shape[:2]
-    start = pl.program_id(0) * size
-    values = [x_ref[t, pl.ds(start, size)].astype(F32) for t in range(count)]
+    count, _, size = out_ref.shape
+    start = pl.multiple_of(pl.program_id(0) * size, HB)
+    values = [x_ref[t, :, pl.ds(start, size)].astype(F32) for t in range(count)]
     stride = 1
     while stride < count:
         for t in range(count):
@@ -386,13 +384,13 @@
 
 
 def transform(value, after=(), cost=FREE):
-    count, groups = value.shape[:2]
-    steps = 4 if groups % 4 == 0 else 1
+    count, rows, width = value.shape
+    steps = 4
     return pl.pallas_call(
         drop_inputs(transform_kernel, 1, len(after)),
         grid=(steps,),
         in_specs=[pl.BlockSpec(memory_space=pltpu.VMEM)] + [ANYWHERE] * len(after),
-        out_specs=pl.BlockSpec((count, groups // steps, SUB, HB), lambda i: (0, i, 0, 0)),
+        out_specs=pl.BlockSpec((count, rows, width // steps), lambda i: (0, 0, i)),
         out_shape=pltpu.HBM(value.shape, BF16),
         compiler_params=pltpu.CompilerParams(vmem_limit_bytes=SMALL),
         cost_estimate=cost,
@@ -453,36 +451,6 @@
     y_out[half:] = y_ref[half:]
 
 
-def total_kernel(count, *refs):
-    out_ref = refs[-1]
-    start = 0
-    for i in range(count):
-        own_ref, x_ref, y_ref = refs[3 * i : 3 * i + 3]
-        size = own_ref.shape[1]
-        out_ref[:, start : start + size] = (
-            own_ref[...].astype(F32) + x_ref[...].astype(F32) + y_ref[...].astype(F32)
-        ).astype(BF16)
-        start += size
-
-
-def total(chunks, after=()):
-    ins = [value for own, *far in chunks for value in (*in_hbm(own), *far)]
-    subs = ins[0].shape[0]
-    groups = sum(chunk[0].shape[1] for chunk in chunks)
-    step = 2
-    return pl.pallas_call(
-        drop_inputs(functools.partial(total_kernel, len(chunks)), len(ins), len(after)),
-        grid=(subs // step,),
-        in_specs=[pl.BlockSpec((step,) + v.shape[1:], lambda i: (i, 0, 0, 0)) for v in ins]
-        + [ANYWHERE] * len(after),
-        out_specs=pl.BlockSpec((step, groups, SUB, HB), lambda i: (i, 0, 0, 0)),
-        out_shape=pltpu.HBM((subs, groups, SUB, HB), BF16),
-        compiler_params=pltpu.CompilerParams(vmem_limit_bytes=SMALL),
-        cost_estimate=FREE,
-        name="total",
-    )(*ins, *in_hbm(*after))
-
-
 def general_shards(hidden, upstream, weight, scales, clip_mask, rot_block):
     groups = scales.shape[0]
     rows = hidden.shape[0]
@@ -502,7 +470,7 @@
     grad_weight, grad_scales = weight_grads(
         [rotated], up, weight, scales, clip_mask, None, 0, groups, per
     )
-    grad_hidden = local_backward([mixed], backward_matrices(rot_block), (groups,))
+    grad_hidden = local_backward([[mixed]], backward_matrices(rot_block))
     return grad_hidden, grad_weight, grad_scales
 
 
@@ -539,12 +507,10 @@
 
     up = gather_upstream(upstream)
     scale = (HB * subs) ** (-0.5)
-    (local,) = local_forward(hidden, rot_block, (groups,), scale)
-    forth = exchange(local)
+    rows, width = hidden.shape
+    forth = exchange(hidden.reshape(subs, SUB, width))
     pers = [size // 4 for size in sizes]
-    unit0 = unit_grads(
-        up, weight, scales, starts[0], sizes[0], pers[0], counts, after=(local,), cost=SOME
-    )
+    unit0 = unit_grads(up, weight, scales, starts[0], sizes[0], pers[0], counts, cost=SOME)
     first0 = scatter_first(unit0)
     unit1 = unit_grads(
         up, weight, scales, starts[1], sizes[1], pers[1], counts, after=(unit0[0],)
@@ -554,22 +520,21 @@
     turned = transform(forth, after=(relayed0,), cost=LONG)
     rotated = exchange(turned)
     relayed1, *second1 = scatter_second(unit1, first1, after=(turned,), cost=LONG)
-    summed = gate(total(((unit0[0], *second0), (unit1[0], *second1))), after=(rotated,))
     matrices = backward_matrices(rot_block, after=(relayed1,))
-    back = exchange(summed)
+    summed = local_backward(((unit0[0], *second0), (unit1[0], *second1)), matrices, scale)
+    summed = gate(summed, after=(rotated,))
+    back = exchange(summed.reshape(subs, SUB, width))
+    (rotated,) = local_forward(rotated.reshape(rows, width), rot_block, (groups,), scale)
     near = (rotated, partner(rotated, "dp", 1), partner(rotated, "dp", 2))
-    gathered0 = gather_rest(near, 0, ())
     mixed = transform(back, cost=LONG)
-    final = exchange(mixed)
+    grad_hidden = exchange(mixed).reshape(rows, width)
+    gathered0 = gather_rest(near, 0, (mixed,))
     gathered1 = gather_rest(near, 1, (mixed,))
     buffer, scale0 = weight_grads(
         gathered0, up, weight, scales, clip_mask, None, starts[0], sizes[0], pers[0], after=(mixed,)
     )
     buffer, scale1 = weight_grads(
         gathered1, up, weight, scales, clip_mask, buffer, starts[1], sizes[1], pers[1]
-    )
-    grad_hidden = local_backward(
-        [final], matrices, (groups,), after=(scale1,), scale=scale
     )
     return grad_hidden, buffer, jnp.concatenate([scale0, scale1], axis=0)
 

time: 207 us -> 208 us (level)
  local copies, waits for them, and re-layouts: 3.43 us -> 6.19 us
    ppermute x18, waiting for transfers between devices: 67.9 us -> 41.5 us  [partner(): return lax.ppermute(value, axis, [(i, i ^ mask) for i in range(size)])]
    all_to_all x4, waiting for transfers between devices: 10.9 us -> 37.2 us  [exchange(): lax.all_to_all(value, 'tensor', split_axis=0, concat_axis=0, tiled=True)]
    pallas_call x2 -> x1, Pallas kernels: 9.5 us -> 5.51 us  [local_backward(): pl.pallas_call(functools.partial(backward_kernel, [len(chunk) for chunk i...]
    unnamed x18 -> x11, local copies, waits for them, and re-layouts: 1.17 us -> 3.93 us
    pallas_call x2, Pallas kernels: 2 us -> 4.54 us  [cut(): pl.pallas_call(drop_inputs(functools.partial(cut_kernel, start), 2, len(a...]
  transfers between devices with their start and end apart: 22 -> 22, of which waited for: 12 -> 13; matrix products, arithmetic and copies ran while one was open for 2% -> 2% of each run, Pallas kernels for 37% -> 38%
where the time goes in v12:
time: 208 us; the launch traced here: 207 us
  Pallas kernels  80.4 us (39%)
  waiting for transfers between devices  78.7 us (38%)
  starting transfers between devices  38.6 us (19%)
  local copies, waits for them, and re-layouts  6.19 us (3%)
  other arithmetic  2.56 us (1%)
    ppermute x18, waiting for transfers between devices, partner(): return lax.ppermute(value, axis, [(i, i ^ mask) for i in range(size)])  41.5 us
    all_to_all x4, waiting for transfers between devices, exchange(): lax.all_to_all(value, 'tensor', split_axis=0, concat_axis=0, tiled=True)  37.2 us
    pallas_call x2, Pallas kernels, weight_grads(): pl.pallas_call(functools.partial(weights_kernel, first, per, len(rotated)...  29.6 us
    pallas_call x2, Pallas kernels, unit_grads(): pl.pallas_call(drop_inputs(functools.partial(units_kernel, first, per), 3...  24.7 us
    ppermute x18, starting transfers between devices, partner(): return lax.ppermute(value, axis, [(i, i ^ mask) for i in range(size)])  20 us
    all_to_all x4, starting transfers between devices, exchange(): lax.all_to_all(value, 'tensor', split_axis=0, concat_axis=0, tiled=True)  18.6 us
    pallas_call x1, Pallas kernels, local_backward(): pl.pallas_call(functools.partial(backward_kernel, [len(chunk) for chunk i...  5.51 us
    pallas_call x2, Pallas kernels, small_call(): pl.pallas_call(drop_inputs(kernel, len(ins), len(after)), grid=(steps,),...  5.22 us
  transfers between devices with their start and end apart: 22, of which 13 were waited for; matrix products, arithmetic and copies ran while one was open for 2% of the time, Pallas kernels for 38%

profile of v12, /device:TPU:0, one launch (start us, length us, event | category | flops | bytes accessed | tf_op | source)
XLA Modules:
  0.0 207.2 jit_solution(17767060817623368756)
XLA Ops:
  1.8 3.0 %collective-permute-start = (bf16[64,2048]{1,0:T(8,128)(2,1)S(1)}, bf16[64,2048]{1,0:T(8,128)(2,1)S(1)}, u32[]{:S(2)}, u32[]{:S(2)}) collective-permute-start(bf16[64,2048]{1,0:T(8,128)(2,1)S(1)} %get-tuple-element.51), channel_id=1, source_target_pairs={{0,8},{8,0},{16,24},{24,16},{1,9},{9,1},{17,25},{25,17},{2,10},{10... | collective-permute-start | bytes 786440 | tf_op jit(solution)/shard_map/ppermute | solution.py:407
  6.4 5.3 %all-to-all-start = ((bf16[8,16,6656]{2,1,0:T(8,128)(2,1)}), bf16[8,16,6656]{2,1,0:T(8,128)(2,1)S(1)}, u32[]{:S(2)}, u32[]{:S(2)}) async-start(bf16[8,16,6656]{2,1,0:T(8,128)(2,1)} %bitcast.10), calls=%async_computation | async-start | bytes 3407872 | tf_op jit(solution)/shard_map/all_to_all | solution.py:402
  12.0 6.1 %collective-permute-done.2 = bf16[64,2048]{1,0:T(8,128)(2,1)S(1)} collective-permute-done((bf16[64,2048]{1,0:T(8,128)(2,1)S(1)}, bf16[64,2048]{1,0:T(8,128)(2,1)S(1)}, u32[]{:S(2)}, u32[]{:S(2)}) %collective-permute-start.2) | collective-permute-done | bytes 262176 | tf_op jit(solution)/shard_map/ppermute | solution.py:407
  23.7 13.3 %unit_grads.2 = (bf16[8,28,16,128]{3,2,1,0:T(8,128)(2,1)}, bf16[8,28,16,128]{3,2,1,0:T(8,128)(2,1)}, bf16[8,28,16,128]{3,2,1,0:T(8,128)(2,1)}, bf16[4,28,16,128]{3,2,1,0:T(8,128)(2,1)}, bf16[4,28,16,128]{3,2,1,0:T(8,128)(2,1)}) custom-call(bf16[512,2048]{1,0:T(8,128)(2,1)S(1)} %pad_maximum_fusion.refs_0_.refs_5_, bf16[6656,2048]{1,0:T(8,128)(2,1)} %refs_6_.3, ...), custom_call_target="tpu_custom_call" | custom-call | flops 5000000000 | tf_op jit(solution)/shard_map/unit_grads/pallas_call | solution.py:225
  39.0 11.4 %unit_grads.3 = (bf16[8,24,16,128]{3,2,1,0:T(8,128)(2,1)}, bf16[8,24,16,128]{3,2,1,0:T(8,128)(2,1)}, bf16[8,24,16,128]{3,2,1,0:T(8,128)(2,1)}, bf16[4,24,16,128]{3,2,1,0:T(8,128)(2,1)}, bf16[4,24,16,128]{3,2,1,0:T(8,128)(2,1)}) custom-call(bf16[512,2048]{1,0:T(8,128)(2,1)S(1)} %pad_maximum_fusion.refs_0_.refs_5_, bf16[6656,2048]{1,0:T(8,128)(2,1)} %refs_6_.3, ...), custom_call_target="tpu_custom_call" | custom-call | tf_op jit(solution)/shard_map/unit_grads/pallas_call | solution.py:225
  50.7 1.7 collective-permute-start.9
  52.5 2.6 %relay.2 = (bf16[8,28,16,128]{3,2,1,0:T(8,128)(2,1)}, bf16[8,28,16,128]{3,2,1,0:T(8,128)(2,1)}) custom-call(bf16[8,28,16,128]{3,2,1,0:T(8,128)(2,1)} %get-tuple-element.28.refs_0_, bf16[8,28,16,128]{3,2,1,0:T(8,128)(2,1)} %get-tuple-element.29.refs_1_, bf16[4,28,16,128]{3,2,1,0:T(8,128)(2,1)S(1)} %collective-permute-done.4.refs_2_, ...), custom_call_target="tpu_custom_call" | custom-call | tf_op jit(solution)/shard_map/relay/pallas_call | solution.py:321
  55.4 1.7 collective-permute-start.6
  57.0 2.1 %transform.2.refs_4_ = bf16[8,16,6656]{2,1,0:T(8,128)(2,1)} custom-call(bf16[8,16,6656]{2,1,0:T(8,128)(2,1)S(1)} %all-to-all-done.refs_0_, bf16[8,28,16,128]{3,2,1,0:T(8,128)(2,1)} %get-tuple-element.33.refs_1_), custom_call_target="tpu_custom_call" | custom-call | flops 999999995904 | tf_op jit(solution)/shard_map/transform/pallas_call | solution.py:389
  59.1 4.9 %all-to-all-start.1 = ((bf16[8,16,6656]{2,1,0:T(8,128)(2,1)}), bf16[8,16,6656]{2,1,0:T(8,128)(2,1)}, u32[]{:S(2)}, u32[]{:S(2)}) async-start(bf16[8,16,6656]{2,1,0:T(8,128)(2,1)} %transform.2.refs_4_), calls=%async_computation.1 | async-start | bytes 3407872 | tf_op jit(solution)/shard_map/all_to_all | solution.py:402
  64.0 2.6 %relay.3 = (bf16[8,24,16,128]{3,2,1,0:T(8,128)(2,1)}, bf16[8,24,16,128]{3,2,1,0:T(8,128)(2,1)}) custom-call(bf16[8,24,16,128]{3,2,1,0:T(8,128)(2,1)} %get-tuple-element.35.refs_0_, bf16[8,24,16,128]{3,2,1,0:T(8,128)(2,1)} %get-tuple-element.36.refs_1_, bf16[4,24,16,128]{3,2,1,0:T(8,128)(2,1)} %collective-permute-done.8.refs_2_, ...), custom_call_target="tpu_custom_call" | custom-call | flops 999999995904 | tf_op jit(solution)/shard_map/relay/pallas_call | solution.py:321
  66.7 1.5 collective-permute-start.11
  71.5 11.2 %collective-permute-done.7.refs_2_ = bf16[8,28,16,128]{3,2,1,0:T(8,128)(2,1)} collective-permute-done((bf16[8,28,16,128]{3,2,1,0:T(8,128)(2,1)}, bf16[8,28,16,128]{3,2,1,0:T(8,128)(2,1)}, u32[]{:S(2)}, u32[]{:S(2)}) %collective-permute-start.7) | collective-permute-done | bytes 917536 | tf_op jit(solution)/shard_map/ppermute | solution.py:407
  82.8 15.0 %collective-permute-done.11.refs_5_ = bf16[8,24,16,128]{3,2,1,0:T(8,128)(2,1)S(1)} collective-permute-done((bf16[8,24,16,128]{3,2,1,0:T(8,128)(2,1)}, bf16[8,24,16,128]{3,2,1,0:T(8,128)(2,1)S(1)}, u32[]{:S(2)}, u32[]{:S(2)}) %collective-permute-start.11) | collective-permute-done | bytes 786464 | tf_op jit(solution)/shard_map/ppermute | solution.py:407
  97.8 5.5 %local_backward.1.refs_0_ = bf16[128,6656]{1,0:T(8,128)(2,1)} custom-call(bf16[8,28,16,128]{3,2,1,0:T(8,128)(2,1)} %get-tuple-element.27.refs_3_.refs_0_, bf16[8,28,16,128]{3,2,1,0:T(8,128)(2,1)} %collective-permute-done.6.refs_1_, bf16[8,28,16,128]{3,2,1,0:T(8,128)(2,1)} %collective-permute-done.7.refs_2_, ...), custom_call_target="tpu_custom_call" | custom-call | tf_op jit(solution)/shard_map/local_backward/pallas_call | solution.py:179
  104.7 3.6 %all-to-all-start.2 = ((bf16[8,16,6656]{2,1,0:T(8,128)(2,1)}), bf16[8,16,6656]{2,1,0:T(8,128)(2,1)S(1)}, u32[]{:S(2)}, u32[]{:S(2)}) async-start(bf16[8,16,6656]{2,1,0:T(8,128)(2,1)} %bitcast.8), calls=%async_computation.2 | async-start | bytes 3407872 | tf_op jit(solution)/shard_map/all_to_all | solution.py:402
  108.4 5.2 %local_forward.1.refs_0_ = bf16[8,52,16,128]{3,2,1,0:T(8,128)(2,1)} custom-call(bf16[128,6656]{1,0:T(8,128)(2,1)} %bitcast.7.x_ref, f32[52,52]{1,0:T(8,128)} %rot_ref.1), custom_call_target="tpu_custom_call" | custom-call | tf_op jit(solution)/shard_map/local_forward/pallas_call | solution.py:142
  113.6 1.5 collective-permute-start.13
  115.1 1.5 collective-permute-start.12
  116.6 32.4 %all-to-all-done.2.refs_0_ = bf16[8,16,6656]{2,1,0:T(8,128)(2,1)S(1)} async-done(((bf16[8,16,6656]{2,1,0:T(8,128)(2,1)}), bf16[8,16,6656]{2,1,0:T(8,128)(2,1)S(1)}, u32[]{:S(2)}, u32[]{:S(2)}) %all-to-all-start.2) | async-done | bytes 1703968 | tf_op jit(solution)/shard_map/all_to_all | solution.py:402
  149.0 2.1 %transform.3.refs_2_.refs_9_ = bf16[8,16,6656]{2,1,0:T(8,128)(2,1)} custom-call(bf16[8,16,6656]{2,1,0:T(8,128)(2,1)S(1)} %all-to-all-done.2.refs_0_), custom_call_target="tpu_custom_call" | custom-call | flops 999999995904 | tf_op jit(solution)/shard_map/transform/pallas_call | solution.py:389
  151.1 2.4 %collective-permute-done.13.refs_1_.refs_2_ = bf16[8,52,16,128]{3,2,1,0:T(8,128)(2,1)} collective-permute-done((bf16[8,52,16,128]{3,2,1,0:T(8,128)(2,1)}, bf16[8,52,16,128]{3,2,1,0:T(8,128)(2,1)}, u32[]{:S(2)}, u32[]{:S(2)}) %collective-permute-start.13) | collective-permute-done | bytes 1703968 | tf_op jit(solution)/shard_map/ppermute | solution.py:407
  154.7 2.2 %cut.3 = (bf16[4,28,16,128]{3,2,1,0:T(8,128)(2,1)}, bf16[4,28,16,128]{3,2,1,0:T(8,128)(2,1)}) custom-call(bf16[8,52,16,128]{3,2,1,0:T(8,128)(2,1)} %collective-permute-done.12.refs_0_.refs_1_, bf16[8,52,16,128]{3,2,1,0:T(8,128)(2,1)} %collective-permute-done.13.refs_1_.refs_2_, bf16[8,16,6656]{2,1,0:T(8,128)(2,1)} %transform.3.refs_2_.refs_9_), custom_call_target="tpu_custom_call" | custom-call | tf_op jit(solution)/shard_map/cut/pallas_call | solution.py:343
  156.9 1.5 collective-permute-start.16
  158.9 4.7 %all-to-all-start.3 = ((bf16[8,16,6656]{2,1,0:T(8,128)(2,1)}), bf16[8,16,6656]{2,1,0:T(8,128)(2,1)}, u32[]{:S(2)}, u32[]{:S(2)}) async-start(bf16[8,16,6656]{2,1,0:T(8,128)(2,1)} %transform.3.refs_2_.refs_9_), calls=%async_computation.3 | async-start | bytes 3407872 | tf_op jit(solution)/shard_map/all_to_all | solution.py:402
  163.7 2.3 %cut.2 = (bf16[4,24,16,128]{3,2,1,0:T(8,128)(2,1)}, bf16[4,24,16,128]{3,2,1,0:T(8,128)(2,1)}) custom-call(bf16[8,52,16,128]{3,2,1,0:T(8,128)(2,1)} %collective-permute-done.12.refs_0_.refs_1_, bf16[8,52,16,128]{3,2,1,0:T(8,128)(2,1)} %collective-permute-done.13.refs_1_.refs_2_, bf16[8,16,6656]{2,1,0:T(8,128)(2,1)} %transform.3.refs_2_.refs_9_), custom_call_target="tpu_custom_call" | custom-call | tf_op jit(solution)/shard_map/cut/pallas_call | solution.py:343
  166.6 1.5 collective-permute-start.15
  169.0 1.7 collective-permute-done.17.refs_4_
  170.7 15.5 %weight_grads.2 = (bf16[6656,2048]{1,0:T(8,128)(2,1)}, f32[28,2048]{1,0:T(8,128)S(1)}) custom-call(bf16[8,52,16,128]{3,2,1,0:T(8,128)(2,1)S(1)} %copy-done.2, bf16[8,52,16,128]{3,2,1,0:T(8,128)(2,1)} %collective-permute-done.12.refs_0_.refs_1_, bf16[8,52,16,128]{3,2,1,0:T(8,128)(2,1)} %collective-permute-done.13.refs_1_.refs_2_, ...), custom_call_target="tpu_custom_call" | custom-call | flops 999999995904 | tf_op jit(solution)/shard_map/weight_grads/pallas_call | solution.py:295
  186.2 14.1 %weight_grads.3 = (bf16[6656,2048]{1,0:T(8,128)(2,1)}, f32[24,2048]{1,0:T(8,128)S(1)}) custom-call(bf16[8,52,16,128]{3,2,1,0:T(8,128)(2,1)S(1)} %copy-done.2, bf16[8,52,16,128]{3,2,1,0:T(8,128)(2,1)} %collective-permute-done.12.refs_0_.refs_1_, bf16[8,52,16,128]{3,2,1,0:T(8,128)(2,1)} %collective-permute-done.13.refs_1_.refs_2_, ...), custom_call_target="tpu_custom_call", output_to_operand_aliasing={{0}: (9, {})} | custom-call | flops 999999995904 | tf_op jit(solution)/shard_map/weight_grads/pallas_call | solution.py:295
  201.1 3.3 %all-to-all-done.3 = bf16[8,16,6656]{2,1,0:T(8,128)(2,1)} async-done(((bf16[8,16,6656]{2,1,0:T(8,128)(2,1)}), bf16[8,16,6656]{2,1,0:T(8,128)(2,1)}, u32[]{:S(2)}, u32[]{:S(2)}) %all-to-all-start.3) | async-done | bytes 1703968 | tf_op jit(solution)/shard_map/all_to_all | solution.py:402
  204.4 2.7 %copy.14 = bf16[128,6656]{1,0:T(8,128)(2,1)} copy(bf16[128,6656]{1,0:T(8,128)(2,1)} %bitcast.6) | data formatting | bytes 3407872
  (44 shorter events, 20.0 us)
Async XLA Ops:
  1.8 10.1 %collective-permute-start = (bf16[64,2048]{1,0:T(8,128)(2,1)S(1)}, bf16[64,2048]{1,0:T(8,128)(2,1)S(1)}, u32[]{:S(2)}, u32[]{:S(2)}) collective-permute-start(bf16[64,2048]{1,0:T(8,128)(2,1)S(1)} %get-tuple-element.51), channel_id=1, source_target_pairs={{0,8},{8,0},{16,24},{24,16},{1,9},{9,1},{17,25},{25,17},{2,10},{10... | collective-permute-start | bytes 786440 | tf_op jit(solution)/shard_map/ppermute | solution.py:407
  4.8 13.2 %collective-permute-start.2 = (bf16[64,2048]{1,0:T(8,128)(2,1)S(1)}, bf16[64,2048]{1,0:T(8,128)(2,1)S(1)}, u32[]{:S(2)}, u32[]{:S(2)}) collective-permute-start(bf16[64,2048]{1,0:T(8,128)(2,1)S(1)} %get-tuple-element.52), channel_id=1, source_target_pairs={{0,24},{8,16},{16,8},{24,0},{1,25},{9,17},{17,9},{25,1},{2,26},{10... | collective-permute-start | bytes 786440 | tf_op jit(solution)/shard_map/ppermute | solution.py:407
  6.3 13.1 %collective-permute-start.1 = (bf16[64,2048]{1,0:T(8,128)(2,1)S(1)}, bf16[64,2048]{1,0:T(8,128)(2,1)S(1)}, u32[]{:S(2)}, u32[]{:S(2)}) collective-permute-start(bf16[64,2048]{1,0:T(8,128)(2,1)S(1)} %get-tuple-element.53), channel_id=1, source_target_pairs={{0,16},{8,24},{16,0},{24,8},{1,17},{9,25},{17,1},{25,9},{2,18},{10... | collective-permute-start | bytes 786440 | tf_op jit(solution)/shard_map/ppermute | solution.py:407
  6.4 50.7 %all-to-all-start = ((bf16[8,16,6656]{2,1,0:T(8,128)(2,1)}), bf16[8,16,6656]{2,1,0:T(8,128)(2,1)S(1)}, u32[]{:S(2)}, u32[]{:S(2)}) async-start(bf16[8,16,6656]{2,1,0:T(8,128)(2,1)} %bitcast.10), calls=%async_computation | async-start | bytes 3407872 | tf_op jit(solution)/shard_map/all_to_all | solution.py:402
  19.5 2.5 %collective-permute-start.3 = (bf16[3,64,2048]{2,1,0:T(8,128)(2,1)S(1)}, bf16[3,64,2048]{2,1,0:T(8,128)(2,1)}, u32[]{:S(2)}, u32[]{:S(2)}) collective-permute-start(bf16[3,64,2048]{2,1,0:T(8,128)(2,1)S(1)} %pad_maximum_fusion.2), channel_id=1, source_target_pairs={{0,1},{1,0},{2,3},{3,2},{4,5},{5,4},{6,7},{7,6},{8,9},{9,8},{10,11... | collective-permute-start | bytes 2359304 | tf_op jit(solution)/shard_map/ppermute | solution.py:407
  23.7 15.3 %copy-start = (bf16[512,2048]{1,0:T(8,128)(2,1)}, bf16[512,2048]{1,0:T(8,128)(2,1)S(1)}, u32[]{:S(2)}) copy-start(bf16[512,2048]{1,0:T(8,128)(2,1)S(1)} %pad_maximum_fusion.refs_0_.refs_5_) | copy-start | bytes 6291460
  37.0 15.4 %collective-permute-start.4 = (bf16[4,28,16,128]{3,2,1,0:T(8,128)(2,1)}, bf16[4,28,16,128]{3,2,1,0:T(8,128)(2,1)S(1)}, u32[]{:S(2)}, u32[]{:S(2)}) collective-permute-start(bf16[4,28,16,128]{3,2,1,0:T(8,128)(2,1)} %get-tuple-element.30), channel_id=1, source_target_pairs={{0,8},{8,0},{16,24},{24,16},{1,9},{9,1},{17,25},{25,17},{2,10},{10... | collective-permute-start | bytes 1376264 | tf_op jit(solution)/shard_map/ppermute | solution.py:407
  38.5 14.0 %collective-permute-start.5 = (bf16[4,28,16,128]{3,2,1,0:T(8,128)(2,1)}, bf16[4,28,16,128]{3,2,1,0:T(8,128)(2,1)S(1)}, u32[]{:S(2)}, u32[]{:S(2)}) collective-permute-start(bf16[4,28,16,128]{3,2,1,0:T(8,128)(2,1)} %get-tuple-element.31), channel_id=1, source_target_pairs={{0,16},{8,24},{16,0},{24,8},{1,17},{9,25},{17,1},{25,9},{2,18},{10... | collective-permute-start | bytes 1376264 | tf_op jit(solution)/shard_map/ppermute | solution.py:407
  50.4 13.6 %collective-permute-start.8 = (bf16[4,24,16,128]{3,2,1,0:T(8,128)(2,1)}, bf16[4,24,16,128]{3,2,1,0:T(8,128)(2,1)}, u32[]{:S(2)}, u32[]{:S(2)}) collective-permute-start(bf16[4,24,16,128]{3,2,1,0:T(8,128)(2,1)} %get-tuple-element.37), channel_id=1, source_target_pairs={{0,8},{8,0},{16,24},{24,16},{1,9},{9,1},{17,25},{25,17},{2,10},{10... | collective-permute-start | bytes 1179656 | tf_op jit(solution)/shard_map/ppermute | solution.py:407
  50.7 13.3 %collective-permute-start.9 = (bf16[4,24,16,128]{3,2,1,0:T(8,128)(2,1)}, bf16[4,24,16,128]{3,2,1,0:T(8,128)(2,1)}, u32[]{:S(2)}, u32[]{:S(2)}) collective-permute-start(bf16[4,24,16,128]{3,2,1,0:T(8,128)(2,1)} %get-tuple-element.38), channel_id=1, source_target_pairs={{0,16},{8,24},{16,0},{24,8},{1,17},{9,25},{17,1},{25,9},{2,18},{10... | collective-permute-start | bytes 1179656 | tf_op jit(solution)/shard_map/ppermute | solution.py:407
  55.0 27.7 %collective-permute-start.7 = (bf16[8,28,16,128]{3,2,1,0:T(8,128)(2,1)}, bf16[8,28,16,128]{3,2,1,0:T(8,128)(2,1)}, u32[]{:S(2)}, u32[]{:S(2)}) collective-permute-start(bf16[8,28,16,128]{3,2,1,0:T(8,128)(2,1)} %get-tuple-element.34), channel_id=1, source_target_pairs={{0,16},{8,24},{16,0},{24,8},{1,17},{9,25},{17,1},{25,9},{2,18},{10... | collective-permute-start | bytes 2752520 | tf_op jit(solution)/shard_map/ppermute | solution.py:407
  55.4 27.4 %collective-permute-start.6 = (bf16[8,28,16,128]{3,2,1,0:T(8,128)(2,1)}, bf16[8,28,16,128]{3,2,1,0:T(8,128)(2,1)}, u32[]{:S(2)}, u32[]{:S(2)}) collective-permute-start(bf16[8,28,16,128]{3,2,1,0:T(8,128)(2,1)} %get-tuple-element.33.refs_1_), channel_id=1, source_target_pairs={{0,8},{8,0},{16,24},{24,16},{1,9},{9,1},{17,25},{25,17},{2,10},{10... | collective-permute-start | bytes 2752520 | tf_op jit(solution)/shard_map/ppermute | solution.py:407
  59.1 45.6 %all-to-all-start.1 = ((bf16[8,16,6656]{2,1,0:T(8,128)(2,1)}), bf16[8,16,6656]{2,1,0:T(8,128)(2,1)}, u32[]{:S(2)}, u32[]{:S(2)}) async-start(bf16[8,16,6656]{2,1,0:T(8,128)(2,1)} %transform.2.refs_4_), calls=%async_computation.1 | async-start | bytes 3407872 | tf_op jit(solution)/shard_map/all_to_all | solution.py:402
  64.0 4.9 %copy-start.4 = (f32[52,52]{1,0:T(8,128)S(1)}, f32[52,52]{1,0:T(8,128)}, u32[]{:S(2)}) copy-start(f32[52,52]{1,0:T(8,128)} %rot_ref.1) | copy-start | bytes 32452
  66.7 31.1 %collective-permute-start.11 = (bf16[8,24,16,128]{3,2,1,0:T(8,128)(2,1)}, bf16[8,24,16,128]{3,2,1,0:T(8,128)(2,1)S(1)}, u32[]{:S(2)}, u32[]{:S(2)}) collective-permute-start(bf16[8,24,16,128]{3,2,1,0:T(8,128)(2,1)} %get-tuple-element.40), channel_id=1, source_target_pairs={{0,16},{8,24},{16,0},{24,8},{1,17},{9,25},{17,1},{25,9},{2,18},{10... | collective-permute-start | bytes 2359304 | tf_op jit(solution)/shard_map/ppermute | solution.py:407
  68.2 29.6 %collective-permute-start.10 = (bf16[8,24,16,128]{3,2,1,0:T(8,128)(2,1)}, bf16[8,24,16,128]{3,2,1,0:T(8,128)(2,1)S(1)}, u32[]{:S(2)}, u32[]{:S(2)}) collective-permute-start(bf16[8,24,16,128]{3,2,1,0:T(8,128)(2,1)} %get-tuple-element.39.refs_1_), channel_id=1, source_target_pairs={{0,8},{8,0},{16,24},{24,16},{1,9},{9,1},{17,25},{25,17},{2,10},{10... | collective-permute-start | bytes 2359304 | tf_op jit(solution)/shard_map/ppermute | solution.py:407
  68.9 1.2 copy-start.3
  104.7 44.3 %all-to-all-start.2 = ((bf16[8,16,6656]{2,1,0:T(8,128)(2,1)}), bf16[8,16,6656]{2,1,0:T(8,128)(2,1)S(1)}, u32[]{:S(2)}, u32[]{:S(2)}) async-start(bf16[8,16,6656]{2,1,0:T(8,128)(2,1)} %bitcast.8), calls=%async_computation.2 | async-start | bytes 3407872 | tf_op jit(solution)/shard_map/all_to_all | solution.py:402
  113.6 39.9 %collective-permute-start.13 = (bf16[8,52,16,128]{3,2,1,0:T(8,128)(2,1)}, bf16[8,52,16,128]{3,2,1,0:T(8,128)(2,1)}, u32[]{:S(2)}, u32[]{:S(2)}) collective-permute-start(bf16[8,52,16,128]{3,2,1,0:T(8,128)(2,1)} %local_forward.1.refs_0_), channel_id=1, source_target_pairs={{0,16},{8,24},{16,0},{24,8},{1,17},{9,25},{17,1},{25,9},{2,18},{10... | collective-permute-start | bytes 5111816 | tf_op jit(solution)/shard_map/ppermute | solution.py:407
  115.1 39.6 %collective-permute-start.12 = (bf16[8,52,16,128]{3,2,1,0:T(8,128)(2,1)}, bf16[8,52,16,128]{3,2,1,0:T(8,128)(2,1)}, u32[]{:S(2)}, u32[]{:S(2)}) collective-permute-start(bf16[8,52,16,128]{3,2,1,0:T(8,128)(2,1)} %local_forward.1.refs_0_), channel_id=1, source_target_pairs={{0,8},{8,0},{16,24},{24,16},{1,9},{9,1},{17,25},{25,17},{2,10},{10... | collective-permute-start | bytes 5111816 | tf_op jit(solution)/shard_map/ppermute | solution.py:407
  156.9 12.0 %collective-permute-start.16 = (bf16[4,28,16,128]{3,2,1,0:T(8,128)(2,1)}, bf16[4,28,16,128]{3,2,1,0:T(8,128)(2,1)S(1)}, u32[]{:S(2)}, u32[]{:S(2)}) collective-permute-start(bf16[4,28,16,128]{3,2,1,0:T(8,128)(2,1)} %get-tuple-element.45), channel_id=1, source_target_pairs={{0,8},{8,0},{16,24},{24,16},{1,9},{9,1},{17,25},{25,17},{2,10},{10... | collective-permute-start | bytes 1376264 | tf_op jit(solution)/shard_map/ppermute | solution.py:407
  158.4 12.3 %collective-permute-start.17 = (bf16[4,28,16,128]{3,2,1,0:T(8,128)(2,1)}, bf16[4,28,16,128]{3,2,1,0:T(8,128)(2,1)S(1)}, u32[]{:S(2)}, u32[]{:S(2)}) collective-permute-start(bf16[4,28,16,128]{3,2,1,0:T(8,128)(2,1)} %get-tuple-element.46), channel_id=1, source_target_pairs={{0,16},{8,24},{16,0},{24,8},{1,17},{9,25},{17,1},{25,9},{2,18},{10... | collective-permute-start | bytes 1376264 | tf_op jit(solution)/shard_map/ppermute | solution.py:407
  158.9 45.5 %all-to-all-start.3 = ((bf16[8,16,6656]{2,1,0:T(8,128)(2,1)}), bf16[8,16,6656]{2,1,0:T(8,128)(2,1)}, u32[]{:S(2)}, u32[]{:S(2)}) async-start(bf16[8,16,6656]{2,1,0:T(8,128)(2,1)} %transform.3.refs_2_.refs_9_), calls=%async_computation.3 | async-start | bytes 3407872 | tf_op jit(solution)/shard_map/all_to_all | solution.py:402
  163.7 7.0 %copy-start.1 = (bf16[512,2048]{1,0:T(8,128)(2,1)S(1)}, bf16[512,2048]{1,0:T(8,128)(2,1)}, u32[]{:S(2)}) copy-start(bf16[512,2048]{1,0:T(8,128)(2,1)} %copy-done) | copy-start | bytes 6291460
  163.7 7.0 %copy-start.2 = (bf16[8,52,16,128]{3,2,1,0:T(8,128)(2,1)S(1)}, bf16[8,52,16,128]{3,2,1,0:T(8,128)(2,1)}, u32[]{:S(2)}) copy-start(bf16[8,52,16,128]{3,2,1,0:T(8,128)(2,1)} %local_forward.1.refs_0_) | copy-start | bytes 5111812
  166.0 20.2 %collective-permute-start.14 = (bf16[4,24,16,128]{3,2,1,0:T(8,128)(2,1)}, bf16[4,24,16,128]{3,2,1,0:T(8,128)(2,1)}, u32[]{:S(2)}, u32[]{:S(2)}) collective-permute-start(bf16[4,24,16,128]{3,2,1,0:T(8,128)(2,1)} %get-tuple-element.43), channel_id=1, source_target_pairs={{0,8},{8,0},{16,24},{24,16},{1,9},{9,1},{17,25},{25,17},{2,10},{10... | collective-permute-start | bytes 1179656 | tf_op jit(solution)/shard_map/ppermute | solution.py:407
  166.6 19.6 %collective-permute-start.15 = (bf16[4,24,16,128]{3,2,1,0:T(8,128)(2,1)}, bf16[4,24,16,128]{3,2,1,0:T(8,128)(2,1)}, u32[]{:S(2)}, u32[]{:S(2)}) collective-permute-start(bf16[4,24,16,128]{3,2,1,0:T(8,128)(2,1)} %get-tuple-element.44), channel_id=1, source_target_pairs={{0,16},{8,24},{16,0},{24,8},{1,17},{9,25},{17,1},{25,9},{2,18},{10... | collective-permute-start | bytes 1179656 | tf_op jit(solution)/shard_map/ppermute | solution.py:407

commit v13 on v12

--- a/solution.py
+++ b/solution.py
@@ -368,10 +368,42 @@
     )(*in_hbm(value, *after))
 
 
+def land_kernel(x_ref, out_ref, sems):
+    size = x_ref.shape[0] // 4
+    copies = [
+        pltpu.make_async_copy(
+            x_ref.at[pl.ds(i * size, size)], out_ref.at[pl.ds(i * size, size)], sems.at[i]
+        )
+        for i in range(4)
+    ]
+    for copy in copies:
+        copy.start()
+    for copy in copies:
+        copy.wait()
+
+
+def land(value):
+    return pl.pallas_call(
+        land_kernel,
+        in_specs=[ANYWHERE],
+        out_specs=ANYWHERE,
+        out_shape=pltpu.HBM(value.shape, value.dtype),
+        scratch_shapes=[pltpu.SemaphoreType.DMA((4,))],
+        compiler_params=pltpu.CompilerParams(vmem_limit_bytes=SMALL),
+        cost_estimate=FREE,
+        name="land",
+    )(value)
+
+
 def transform_kernel(x_ref, out_ref):
-    count, _, size = out_ref.shape
-    start = pl.multiple_of(pl.program_id(0) * size, HB)
-    values = [x_ref[t, :, pl.ds(start, size)].astype(F32) for t in range(count)]
+    count = x_ref.shape[0]
+    if len(x_ref.shape) == 4:
+        size = out_ref.shape[1]
+        span = (pl.ds(pl.program_id(0) * size, size),)
+    else:
+        size = out_ref.shape[2]
+        span = (slice(None), pl.ds(pl.multiple_of(pl.program_id(0) * size, HB), size))
+    values = [x_ref[(t, *span)].astype(F32) for t in range(count)]
     stride = 1
     while stride < count:
         for t in range(count):
@@ -384,13 +416,18 @@
 
 
 def transform(value, after=(), cost=FREE):
-    count, rows, width = value.shape
     steps = 4
+    if value.ndim == 4:
+        count, groups = value.shape[:2]
+        out = pl.BlockSpec((count, groups // steps, SUB, HB), lambda i: (0, i, 0, 0))
+    else:
+        count, rows, width = value.shape
+        out = pl.BlockSpec((count, rows, width // steps), lambda i: (0, 0, i))
     return pl.pallas_call(
         drop_inputs(transform_kernel, 1, len(after)),
         grid=(steps,),
         in_specs=[pl.BlockSpec(memory_space=pltpu.VMEM)] + [ANYWHERE] * len(after),
-        out_specs=pl.BlockSpec((count, rows, width // steps), lambda i: (0, 0, i)),
+        out_specs=out,
         out_shape=pltpu.HBM(value.shape, BF16),
         compiler_params=pltpu.CompilerParams(vmem_limit_bytes=SMALL),
         cost_estimate=cost,
@@ -508,9 +545,10 @@
     up = gather_upstream(upstream)
     scale = (HB * subs) ** (-0.5)
     rows, width = hidden.shape
-    forth = exchange(hidden.reshape(subs, SUB, width))
+    (local,) = local_forward(hidden, rot_block, (groups,), scale)
+    forth = exchange(local)
     pers = [size // 4 for size in sizes]
-    unit0 = unit_grads(up, weight, scales, starts[0], sizes[0], pers[0], counts, cost=SOME)
+    unit0 = unit_grads(up, weight, scales, starts[0], sizes[0], pers[0], counts, (local,), SOME)
     first0 = scatter_first(unit0)
     unit1 = unit_grads(
         up, weight, scales, starts[1], sizes[1], pers[1], counts, after=(unit0[0],)
@@ -523,12 +561,11 @@
     matrices = backward_matrices(rot_block, after=(relayed1,))
     summed = local_backward(((unit0[0], *second0), (unit1[0], *second1)), matrices, scale)
     summed = gate(summed, after=(rotated,))
-    back = exchange(summed.reshape(subs, SUB, width))
-    (rotated,) = local_forward(rotated.reshape(rows, width), rot_block, (groups,), scale)
+    back = exchange(summed).reshape(subs, SUB, width)
     near = (rotated, partner(rotated, "dp", 1), partner(rotated, "dp", 2))
+    gathered0 = gather_rest(near, 0, ())
     mixed = transform(back, cost=LONG)
-    grad_hidden = exchange(mixed).reshape(rows, width)
-    gathered0 = gather_rest(near, 0, (mixed,))
+    grad_hidden = land(exchange(mixed.reshape(rows, width)))
     gathered1 = gather_rest(near, 1, (mixed,))
     buffer, scale0 = weight_grads(
         gathered0, up, weight, scales, clip_mask, None, starts[0], sizes[0], pers[0], after=(mixed,)

time: 208 us -> 255 us (1.23)
  Pallas kernels: 80.4 us -> 130 us
    pallas_call x0 -> x1, Pallas kernels: none -> 52.8 us  [land(): pl.pallas_call(land_kernel, in_specs=[ANYWHERE], out_specs=ANYWHERE, out_...]
    all_to_all x4, waiting for transfers between devices: 37.2 us -> 8.72 us  [exchange(): lax.all_to_all(value, 'tensor', split_axis=0, concat_axis=0, tiled=True)]
    ppermute x18, waiting for transfers between devices: 41.5 us -> 68.6 us  [partner(): return lax.ppermute(value, axis, [(i, i ^ mask) for i in range(size)])]
    pallas_call x2, Pallas kernels: 4.54 us -> 1.98 us  [cut(): pl.pallas_call(drop_inputs(functools.partial(cut_kernel, start), 2, len(a...]
  transfers between devices with their start and end apart: 22 -> 22, of which waited for: 13 -> 11; matrix products, arithmetic and copies ran while one was open for 2% -> 1% of each run, Pallas kernels for 38% -> 30%
where the time goes in v13:
time: 255 us; the launch traced here: 254 us
  Pallas kernels  130 us (51%)
  waiting for transfers between devices  77.4 us (30%)
  starting transfers between devices  39.1 us (15%)
  local copies, waits for them, and re-layouts  3.95 us (2%)
  other arithmetic  2.56 us (1%)
    ppermute x18, waiting for transfers between devices, partner(): return lax.ppermute(value, axis, [(i, i ^ mask) for i in range(size)])  68.6 us
    pallas_call x1, Pallas kernels, land(): pl.pallas_call(land_kernel, in_specs=[ANYWHERE], out_specs=ANYWHERE, out_...  52.8 us
    pallas_call x2, Pallas kernels, weight_grads(): pl.pallas_call(functools.partial(weights_kernel, first, per, len(rotated)...  29.1 us
    pallas_call x2, Pallas kernels, unit_grads(): pl.pallas_call(drop_inputs(functools.partial(units_kernel, first, per), 3...  24.7 us
    ppermute x18, starting transfers between devices, partner(): return lax.ppermute(value, axis, [(i, i ^ mask) for i in range(size)])  20.7 us
    all_to_all x4, starting transfers between devices, exchange(): lax.all_to_all(value, 'tensor', split_axis=0, concat_axis=0, tiled=True)  18.4 us
    all_to_all x4, waiting for transfers between devices, exchange(): lax.all_to_all(value, 'tensor', split_axis=0, concat_axis=0, tiled=True)  8.72 us
    pallas_call x1, Pallas kernels, local_backward(): pl.pallas_call(functools.partial(backward_kernel, [len(chunk) for chunk i...  5.53 us
  transfers between devices with their start and end apart: 22, of which 11 were waited for; matrix products, arithmetic and copies ran while one was open for 1% of the time, Pallas kernels for 30%

profile of v13, /device:TPU:0, one launch (start us, length us, event | category | flops | bytes accessed | tf_op | source)
XLA Modules:
  0.0 254.0 jit_solution(2501124635703659153)
XLA Ops:
  1.8 3.0 %collective-permute-start = (bf16[64,2048]{1,0:T(8,128)(2,1)S(1)}, bf16[64,2048]{1,0:T(8,128)(2,1)S(1)}, u32[]{:S(2)}, u32[]{:S(2)}) collective-permute-start(bf16[64,2048]{1,0:T(8,128)(2,1)S(1)} %get-tuple-element.51), channel_id=1, source_target_pairs={{0,8},{8,0},{16,24},{24,16},{1,9},{9,1},{17,25},{25,17},{2,10},{10... | collective-permute-start | bytes 786440 | tf_op jit(solution)/shard_map/ppermute | solution.py:444
  4.8 1.5 collective-permute-start.2
  6.4 5.1 %local_forward.1.refs_3_ = bf16[8,52,16,128]{3,2,1,0:T(8,128)(2,1)} custom-call(bf16[128,6656]{1,0:T(8,128)(2,1)} %x_ref.1, f32[52,52]{1,0:T(8,128)} %refs_0_.1), custom_call_target="tpu_custom_call" | custom-call | tf_op jit(solution)/shard_map/local_forward/pallas_call | solution.py:142
  11.5 5.3 %all-to-all-start = ((bf16[8,52,16,128]{3,2,1,0:T(8,128)(2,1)}), bf16[8,52,16,128]{3,2,1,0:T(8,128)(2,1)S(1)}, u32[]{:S(2)}, u32[]{:S(2)}) async-start(bf16[8,52,16,128]{3,2,1,0:T(8,128)(2,1)} %local_forward.1.refs_3_), calls=%async_computation | async-start | bytes 3407872 | tf_op jit(solution)/shard_map/all_to_all | solution.py:439
  18.1 1.4 collective-permute-done.1
  23.7 13.3 %unit_grads.2 = (bf16[8,28,16,128]{3,2,1,0:T(8,128)(2,1)}, bf16[8,28,16,128]{3,2,1,0:T(8,128)(2,1)}, bf16[8,28,16,128]{3,2,1,0:T(8,128)(2,1)}, bf16[4,28,16,128]{3,2,1,0:T(8,128)(2,1)}, bf16[4,28,16,128]{3,2,1,0:T(8,128)(2,1)}) custom-call(bf16[512,2048]{1,0:T(8,128)(2,1)S(1)} %pad_maximum_fusion.refs_0_.refs_5_, bf16[6656,2048]{1,0:T(8,128)(2,1)} %refs_6_.3, ...), custom_call_target="tpu_custom_call" | custom-call | flops 5000000000 | tf_op jit(solution)/shard_map/unit_grads/pallas_call | solution.py:225
  37.0 1.5 collective-permute-start.4
  39.0 11.4 %unit_grads.3 = (bf16[8,24,16,128]{3,2,1,0:T(8,128)(2,1)}, bf16[8,24,16,128]{3,2,1,0:T(8,128)(2,1)}, bf16[8,24,16,128]{3,2,1,0:T(8,128)(2,1)}, bf16[4,24,16,128]{3,2,1,0:T(8,128)(2,1)}, bf16[4,24,16,128]{3,2,1,0:T(8,128)(2,1)}) custom-call(bf16[512,2048]{1,0:T(8,128)(2,1)S(1)} %pad_maximum_fusion.refs_0_.refs_5_, bf16[6656,2048]{1,0:T(8,128)(2,1)} %refs_6_.3, ...), custom_call_target="tpu_custom_call" | custom-call | tf_op jit(solution)/shard_map/unit_grads/pallas_call | solution.py:225
  50.7 1.7 collective-permute-start.9
  52.5 2.5 %relay.2 = (bf16[8,28,16,128]{3,2,1,0:T(8,128)(2,1)}, bf16[8,28,16,128]{3,2,1,0:T(8,128)(2,1)}) custom-call(bf16[8,28,16,128]{3,2,1,0:T(8,128)(2,1)} %get-tuple-element.28.refs_0_, bf16[8,28,16,128]{3,2,1,0:T(8,128)(2,1)} %get-tuple-element.29.refs_1_, bf16[4,28,16,128]{3,2,1,0:T(8,128)(2,1)S(1)} %collective-permute-done.4.refs_2_, ...), custom_call_target="tpu_custom_call" | custom-call | tf_op jit(solution)/shard_map/relay/pallas_call | solution.py:321
  55.3 1.7 collective-permute-start.6
  57.5 2.1 transform.2.refs_4_
  59.6 4.4 %all-to-all-start.1 = ((bf16[8,52,16,128]{3,2,1,0:T(8,128)(2,1)}), bf16[8,52,16,128]{3,2,1,0:T(8,128)(2,1)}, u32[]{:S(2)}, u32[]{:S(2)}) async-start(bf16[8,52,16,128]{3,2,1,0:T(8,128)(2,1)} %transform.2.refs_4_), calls=%async_computation.1 | async-start | bytes 3407872 | tf_op jit(solution)/shard_map/all_to_all | solution.py:439
  64.0 2.6 %relay.3 = (bf16[8,24,16,128]{3,2,1,0:T(8,128)(2,1)}, bf16[8,24,16,128]{3,2,1,0:T(8,128)(2,1)}) custom-call(bf16[8,24,16,128]{3,2,1,0:T(8,128)(2,1)} %get-tuple-element.35.refs_0_, bf16[8,24,16,128]{3,2,1,0:T(8,128)(2,1)} %get-tuple-element.36.refs_1_, bf16[4,24,16,128]{3,2,1,0:T(8,128)(2,1)} %collective-permute-done.8.refs_2_, ...), custom_call_target="tpu_custom_call" | custom-call | flops 999999995904 | tf_op jit(solution)/shard_map/relay/pallas_call | solution.py:321
  66.6 1.5 collective-permute-start.11
  68.2 1.4 collective-permute-start.10
  70.8 1.5 backward_matrices.1
  72.3 10.5 %collective-permute-done.7.refs_2_ = bf16[8,28,16,128]{3,2,1,0:T(8,128)(2,1)} collective-permute-done((bf16[8,28,16,128]{3,2,1,0:T(8,128)(2,1)}, bf16[8,28,16,128]{3,2,1,0:T(8,128)(2,1)}, u32[]{:S(2)}, u32[]{:S(2)}) %collective-permute-start.7) | collective-permute-done | bytes 917536 | tf_op jit(solution)/shard_map/ppermute | solution.py:444
  82.8 15.0 %collective-permute-done.11.refs_5_ = bf16[8,24,16,128]{3,2,1,0:T(8,128)(2,1)S(1)} collective-permute-done((bf16[8,24,16,128]{3,2,1,0:T(8,128)(2,1)}, bf16[8,24,16,128]{3,2,1,0:T(8,128)(2,1)S(1)}, u32[]{:S(2)}, u32[]{:S(2)}) %collective-permute-start.11) | collective-permute-done | bytes 786464 | tf_op jit(solution)/shard_map/ppermute | solution.py:444
  97.8 5.5 %local_backward.1.refs_0_ = bf16[128,6656]{1,0:T(8,128)(2,1)} custom-call(bf16[8,28,16,128]{3,2,1,0:T(8,128)(2,1)} %get-tuple-element.27.refs_3_.refs_0_, bf16[8,28,16,128]{3,2,1,0:T(8,128)(2,1)} %collective-permute-done.6.refs_1_, bf16[8,28,16,128]{3,2,1,0:T(8,128)(2,1)} %collective-permute-done.7.refs_2_, ...), custom_call_target="tpu_custom_call" | custom-call | tf_op jit(solution)/shard_map/local_backward/pallas_call | solution.py:179
  103.3 1.4 all-to-all-done.1.refs_1_.refs_0_
  104.7 3.7 %all-to-all-start.2 = ((bf16[8,16,6656]{2,1,0:T(8,128)(2,1)}), bf16[8,16,6656]{2,1,0:T(8,128)(2,1)S(1)}, u32[]{:S(2)}, u32[]{:S(2)}) async-start(bf16[8,16,6656]{2,1,0:T(8,128)(2,1)} %bitcast.6), calls=%async_computation.2 | async-start | bytes 3407872 | tf_op jit(solution)/shard_map/all_to_all | solution.py:439
  108.4 1.5 collective-permute-start.13
  109.9 1.5 collective-permute-start.12
  111.4 36.8 %collective-permute-done.13.refs_1_.refs_2_ = bf16[8,52,16,128]{3,2,1,0:T(8,128)(2,1)S(1)} collective-permute-done((bf16[8,52,16,128]{3,2,1,0:T(8,128)(2,1)}, bf16[8,52,16,128]{3,2,1,0:T(8,128)(2,1)S(1)}, u32[]{:S(2)}, u32[]{:S(2)}) %collective-permute-start.13) | collective-permute-done | bytes 1703968 | tf_op jit(solution)/shard_map/ppermute | solution.py:444
  150.9 1.5 collective-permute-start.16
  153.2 2.1 transform.3.refs_2_.refs_9_
  155.3 5.0 %all-to-all-start.3 = ((bf16[8,16,6656]{2,1,0:T(8,128)(2,1)}), bf16[8,16,6656]{2,1,0:T(8,128)(2,1)}, u32[]{:S(2)}, u32[]{:S(2)}) async-start(bf16[8,16,6656]{2,1,0:T(8,128)(2,1)} %transform.3.refs_2_.refs_9_), calls=%async_computation.3 | async-start | bytes 3407872 | tf_op jit(solution)/shard_map/all_to_all | solution.py:439
  164.3 15.5 %weight_grads.2 = (bf16[6656,2048]{1,0:T(8,128)(2,1)}, f32[28,2048]{1,0:T(8,128)S(1)}) custom-call(bf16[8,52,16,128]{3,2,1,0:T(8,128)(2,1)} %all-to-all-done.1.refs_1_.refs_0_, bf16[8,52,16,128]{3,2,1,0:T(8,128)(2,1)S(1)} %copy-done.5, bf16[8,52,16,128]{3,2,1,0:T(8,128)(2,1)S(1)} %copy-done.3, bf16[4,28,16,128]{3,2,1,0:T(8,128)(2,1)} %collective-permute-done.16.refs_3_, ...), custom_call_target="tpu_custom_call" | custom-call | flops 999999995904 | tf_op jit(solution)/shard_map/weight_grads/pallas_call | solution.py:295
  179.8 13.7 %weight_grads.3 = (bf16[6656,2048]{1,0:T(8,128)(2,1)}, f32[24,2048]{1,0:T(8,128)S(1)}) custom-call(bf16[8,52,16,128]{3,2,1,0:T(8,128)(2,1)} %all-to-all-done.1.refs_1_.refs_0_, bf16[8,52,16,128]{3,2,1,0:T(8,128)(2,1)S(1)} %copy-done.5, bf16[8,52,16,128]{3,2,1,0:T(8,128)(2,1)S(1)} %copy-done.3, ...), custom_call_target="tpu_custom_call", output_to_operand_aliasing={{0}: (9, {})} | custom-call | flops 999999995904 | tf_op jit(solution)/shard_map/weight_grads/pallas_call | solution.py:295
  194.3 6.8 %all-to-all-done.3 = bf16[8,16,6656]{2,1,0:T(8,128)(2,1)} async-done(((bf16[8,16,6656]{2,1,0:T(8,128)(2,1)}), bf16[8,16,6656]{2,1,0:T(8,128)(2,1)}, u32[]{:S(2)}, u32[]{:S(2)}) %all-to-all-start.3) | async-done | bytes 1703968 | tf_op jit(solution)/shard_map/all_to_all | solution.py:439
  201.1 52.8 %land.1 = bf16[128,6656]{1,0:T(8,128)(2,1)} custom-call(bf16[128,6656]{1,0:T(8,128)(2,1)} %bitcast.5.x_ref), custom_call_target="tpu_custom_call" | custom-call | tf_op jit(solution)/shard_map/land/pallas_call | solution.py:386
  (50 shorter events, 17.8 us)
Async XLA Ops:
  1.8 15.0 %collective-permute-start = (bf16[64,2048]{1,0:T(8,128)(2,1)S(1)}, bf16[64,2048]{1,0:T(8,128)(2,1)S(1)}, u32[]{:S(2)}, u32[]{:S(2)}) collective-permute-start(bf16[64,2048]{1,0:T(8,128)(2,1)S(1)} %get-tuple-element.51), channel_id=1, source_target_pairs={{0,8},{8,0},{16,24},{24,16},{1,9},{9,1},{17,25},{25,17},{2,10},{10... | collective-permute-start | bytes 786440 | tf_op jit(solution)/shard_map/ppermute | solution.py:444
  4.8 13.2 %collective-permute-start.2 = (bf16[64,2048]{1,0:T(8,128)(2,1)S(1)}, bf16[64,2048]{1,0:T(8,128)(2,1)S(1)}, u32[]{:S(2)}, u32[]{:S(2)}) collective-permute-start(bf16[64,2048]{1,0:T(8,128)(2,1)S(1)} %get-tuple-element.52), channel_id=1, source_target_pairs={{0,24},{8,16},{16,8},{24,0},{1,25},{9,17},{17,9},{25,1},{2,26},{10... | collective-permute-start | bytes 786440 | tf_op jit(solution)/shard_map/ppermute | solution.py:444
  6.3 13.1 %collective-permute-start.1 = (bf16[64,2048]{1,0:T(8,128)(2,1)S(1)}, bf16[64,2048]{1,0:T(8,128)(2,1)S(1)}, u32[]{:S(2)}, u32[]{:S(2)}) collective-permute-start(bf16[64,2048]{1,0:T(8,128)(2,1)S(1)} %get-tuple-element.53), channel_id=1, source_target_pairs={{0,16},{8,24},{16,0},{24,8},{1,17},{9,25},{17,1},{25,9},{2,18},{10... | collective-permute-start | bytes 786440 | tf_op jit(solution)/shard_map/ppermute | solution.py:444
  11.5 46.0 %all-to-all-start = ((bf16[8,52,16,128]{3,2,1,0:T(8,128)(2,1)}), bf16[8,52,16,128]{3,2,1,0:T(8,128)(2,1)S(1)}, u32[]{:S(2)}, u32[]{:S(2)}) async-start(bf16[8,52,16,128]{3,2,1,0:T(8,128)(2,1)} %local_forward.1.refs_3_), calls=%async_computation | async-start | bytes 3407872 | tf_op jit(solution)/shard_map/all_to_all | solution.py:439
  19.5 2.5 collective-permute-start.3
  23.7 15.3 %copy-start = (bf16[512,2048]{1,0:T(8,128)(2,1)}, bf16[512,2048]{1,0:T(8,128)(2,1)S(1)}, u32[]{:S(2)}) copy-start(bf16[512,2048]{1,0:T(8,128)(2,1)S(1)} %pad_maximum_fusion.refs_0_.refs_5_) | copy-start | bytes 6291460
  37.0 15.5 %collective-permute-start.4 = (bf16[4,28,16,128]{3,2,1,0:T(8,128)(2,1)}, bf16[4,28,16,128]{3,2,1,0:T(8,128)(2,1)S(1)}, u32[]{:S(2)}, u32[]{:S(2)}) collective-permute-start(bf16[4,28,16,128]{3,2,1,0:T(8,128)(2,1)} %get-tuple-element.30), channel_id=1, source_target_pairs={{0,8},{8,0},{16,24},{24,16},{1,9},{9,1},{17,25},{25,17},{2,10},{10... | collective-permute-start | bytes 1376264 | tf_op jit(solution)/shard_map/ppermute | solution.py:444
  38.5 14.0 %collective-permute-start.5 = (bf16[4,28,16,128]{3,2,1,0:T(8,128)(2,1)}, bf16[4,28,16,128]{3,2,1,0:T(8,128)(2,1)S(1)}, u32[]{:S(2)}, u32[]{:S(2)}) collective-permute-start(bf16[4,28,16,128]{3,2,1,0:T(8,128)(2,1)} %get-tuple-element.31), channel_id=1, source_target_pairs={{0,16},{8,24},{16,0},{24,8},{1,17},{9,25},{17,1},{25,9},{2,18},{10... | collective-permute-start | bytes 1376264 | tf_op jit(solution)/shard_map/ppermute | solution.py:444
  50.4 13.6 %collective-permute-start.8 = (bf16[4,24,16,128]{3,2,1,0:T(8,128)(2,1)}, bf16[4,24,16,128]{3,2,1,0:T(8,128)(2,1)}, u32[]{:S(2)}, u32[]{:S(2)}) collective-permute-start(bf16[4,24,16,128]{3,2,1,0:T(8,128)(2,1)} %get-tuple-element.37), channel_id=1, source_target_pairs={{0,8},{8,0},{16,24},{24,16},{1,9},{9,1},{17,25},{25,17},{2,10},{10... | collective-permute-start | bytes 1179656 | tf_op jit(solution)/shard_map/ppermute | solution.py:444
  50.7 13.2 %collective-permute-start.9 = (bf16[4,24,16,128]{3,2,1,0:T(8,128)(2,1)}, bf16[4,24,16,128]{3,2,1,0:T(8,128)(2,1)}, u32[]{:S(2)}, u32[]{:S(2)}) collective-permute-start(bf16[4,24,16,128]{3,2,1,0:T(8,128)(2,1)} %get-tuple-element.38), channel_id=1, source_target_pairs={{0,16},{8,24},{16,0},{24,8},{1,17},{9,25},{17,1},{25,9},{2,18},{10... | collective-permute-start | bytes 1179656 | tf_op jit(solution)/shard_map/ppermute | solution.py:444
  55.0 27.8 %collective-permute-start.7 = (bf16[8,28,16,128]{3,2,1,0:T(8,128)(2,1)}, bf16[8,28,16,128]{3,2,1,0:T(8,128)(2,1)}, u32[]{:S(2)}, u32[]{:S(2)}) collective-permute-start(bf16[8,28,16,128]{3,2,1,0:T(8,128)(2,1)} %get-tuple-element.34), channel_id=1, source_target_pairs={{0,16},{8,24},{16,0},{24,8},{1,17},{9,25},{17,1},{25,9},{2,18},{10... | collective-permute-start | bytes 2752520 | tf_op jit(solution)/shard_map/ppermute | solution.py:444
  55.3 27.5 %collective-permute-start.6 = (bf16[8,28,16,128]{3,2,1,0:T(8,128)(2,1)}, bf16[8,28,16,128]{3,2,1,0:T(8,128)(2,1)}, u32[]{:S(2)}, u32[]{:S(2)}) collective-permute-start(bf16[8,28,16,128]{3,2,1,0:T(8,128)(2,1)} %get-tuple-element.33.refs_1_), channel_id=1, source_target_pairs={{0,8},{8,0},{16,24},{24,16},{1,9},{9,1},{17,25},{25,17},{2,10},{10... | collective-permute-start | bytes 2752520 | tf_op jit(solution)/shard_map/ppermute | solution.py:444
  59.6 45.1 %all-to-all-start.1 = ((bf16[8,52,16,128]{3,2,1,0:T(8,128)(2,1)}), bf16[8,52,16,128]{3,2,1,0:T(8,128)(2,1)}, u32[]{:S(2)}, u32[]{:S(2)}) async-start(bf16[8,52,16,128]{3,2,1,0:T(8,128)(2,1)} %transform.2.refs_4_), calls=%async_computation.1 | async-start | bytes 3407872 | tf_op jit(solution)/shard_map/all_to_all | solution.py:439
  64.0 5.6 %copy-start.7 = (f32[52,52]{1,0:T(8,128)S(1)}, f32[52,52]{1,0:T(8,128)}, u32[]{:S(2)}) copy-start(f32[52,52]{1,0:T(8,128)} %refs_0_.1) | copy-start | bytes 32452
  66.6 31.1 %collective-permute-start.11 = (bf16[8,24,16,128]{3,2,1,0:T(8,128)(2,1)}, bf16[8,24,16,128]{3,2,1,0:T(8,128)(2,1)S(1)}, u32[]{:S(2)}, u32[]{:S(2)}) collective-permute-start(bf16[8,24,16,128]{3,2,1,0:T(8,128)(2,1)} %get-tuple-element.40), channel_id=1, source_target_pairs={{0,16},{8,24},{16,0},{24,8},{1,17},{9,25},{17,1},{25,9},{2,18},{10... | collective-permute-start | bytes 2359304 | tf_op jit(solution)/shard_map/ppermute | solution.py:444
  68.2 29.6 %collective-permute-start.10 = (bf16[8,24,16,128]{3,2,1,0:T(8,128)(2,1)}, bf16[8,24,16,128]{3,2,1,0:T(8,128)(2,1)S(1)}, u32[]{:S(2)}, u32[]{:S(2)}) collective-permute-start(bf16[8,24,16,128]{3,2,1,0:T(8,128)(2,1)} %get-tuple-element.39.refs_1_), channel_id=1, source_target_pairs={{0,8},{8,0},{16,24},{24,16},{1,9},{9,1},{17,25},{25,17},{2,10},{10... | collective-permute-start | bytes 2359304 | tf_op jit(solution)/shard_map/ppermute | solution.py:444
  69.6 1.2 copy-start.6
  104.7 48.5 %all-to-all-start.2 = ((bf16[8,16,6656]{2,1,0:T(8,128)(2,1)}), bf16[8,16,6656]{2,1,0:T(8,128)(2,1)S(1)}, u32[]{:S(2)}, u32[]{:S(2)}) async-start(bf16[8,16,6656]{2,1,0:T(8,128)(2,1)} %bitcast.6), calls=%async_computation.2 | async-start | bytes 3407872 | tf_op jit(solution)/shard_map/all_to_all | solution.py:439
  108.4 39.8 %collective-permute-start.13 = (bf16[8,52,16,128]{3,2,1,0:T(8,128)(2,1)}, bf16[8,52,16,128]{3,2,1,0:T(8,128)(2,1)S(1)}, u32[]{:S(2)}, u32[]{:S(2)}) collective-permute-start(bf16[8,52,16,128]{3,2,1,0:T(8,128)(2,1)} %all-to-all-done.1.refs_1_.refs_0_), channel_id=1, source_target_pairs={{0,16},{8,24},{16,0},{24,8},{1,17},{9,25},{17,1},{25,9},{2,18},{10... | collective-permute-start | bytes 5111816 | tf_op jit(solution)/shard_map/ppermute | solution.py:444
  109.9 39.5 %collective-permute-start.12 = (bf16[8,52,16,128]{3,2,1,0:T(8,128)(2,1)}, bf16[8,52,16,128]{3,2,1,0:T(8,128)(2,1)S(1)}, u32[]{:S(2)}, u32[]{:S(2)}) collective-permute-start(bf16[8,52,16,128]{3,2,1,0:T(8,128)(2,1)} %all-to-all-done.1.refs_1_.refs_0_), channel_id=1, source_target_pairs={{0,8},{8,0},{16,24},{24,16},{1,9},{9,1},{17,25},{25,17},{2,10},{10... | collective-permute-start | bytes 5111816 | tf_op jit(solution)/shard_map/ppermute | solution.py:444
  148.2 2.2 copy-start.2
  149.4 1.5 copy-start.4
  150.9 12.2 %collective-permute-start.16 = (bf16[4,28,16,128]{3,2,1,0:T(8,128)(2,1)}, bf16[4,28,16,128]{3,2,1,0:T(8,128)(2,1)}, u32[]{:S(2)}, u32[]{:S(2)}) collective-permute-start(bf16[4,28,16,128]{3,2,1,0:T(8,128)(2,1)} %get-tuple-element.45), channel_id=1, source_target_pairs={{0,8},{8,0},{16,24},{24,16},{1,9},{9,1},{17,25},{25,17},{2,10},{10... | collective-permute-start | bytes 1376264 | tf_op jit(solution)/shard_map/ppermute | solution.py:444
  152.4 11.9 %collective-permute-start.17 = (bf16[4,28,16,128]{3,2,1,0:T(8,128)(2,1)}, bf16[4,28,16,128]{3,2,1,0:T(8,128)(2,1)}, u32[]{:S(2)}, u32[]{:S(2)}) collective-permute-start(bf16[4,28,16,128]{3,2,1,0:T(8,128)(2,1)} %get-tuple-element.46), channel_id=1, source_target_pairs={{0,16},{8,24},{16,0},{24,8},{1,17},{9,25},{17,1},{25,9},{2,18},{10... | collective-permute-start | bytes 1376264 | tf_op jit(solution)/shard_map/ppermute | solution.py:444
  155.3 5.0 %copy-start.3 = (bf16[8,52,16,128]{3,2,1,0:T(8,128)(2,1)S(1)}, bf16[8,52,16,128]{3,2,1,0:T(8,128)(2,1)}, u32[]{:S(2)}) copy-start(bf16[8,52,16,128]{3,2,1,0:T(8,128)(2,1)} %copy-done.2) | copy-start | bytes 5111812
  155.3 5.0 %copy-start.5 = (bf16[8,52,16,128]{3,2,1,0:T(8,128)(2,1)S(1)}, bf16[8,52,16,128]{3,2,1,0:T(8,128)(2,1)}, u32[]{:S(2)}) copy-start(bf16[8,52,16,128]{3,2,1,0:T(8,128)(2,1)} %copy-done.4) | copy-start | bytes 5111812
  155.3 45.8 %all-to-all-start.3 = ((bf16[8,16,6656]{2,1,0:T(8,128)(2,1)}), bf16[8,16,6656]{2,1,0:T(8,128)(2,1)}, u32[]{:S(2)}, u32[]{:S(2)}) async-start(bf16[8,16,6656]{2,1,0:T(8,128)(2,1)} %transform.3.refs_2_.refs_9_), calls=%async_computation.3 | async-start | bytes 3407872 | tf_op jit(solution)/shard_map/all_to_all | solution.py:439
  160.4 4.0 %copy-start.1 = (bf16[512,2048]{1,0:T(8,128)(2,1)S(1)}, bf16[512,2048]{1,0:T(8,128)(2,1)}, u32[]{:S(2)}) copy-start(bf16[512,2048]{1,0:T(8,128)(2,1)} %copy-done) | copy-start | bytes 6291460
  161.4 18.4 %collective-permute-start.14 = (bf16[4,24,16,128]{3,2,1,0:T(8,128)(2,1)}, bf16[4,24,16,128]{3,2,1,0:T(8,128)(2,1)}, u32[]{:S(2)}, u32[]{:S(2)}) collective-permute-start(bf16[4,24,16,128]{3,2,1,0:T(8,128)(2,1)} %get-tuple-element.43), channel_id=1, source_target_pairs={{0,8},{8,0},{16,24},{24,16},{1,9},{9,1},{17,25},{25,17},{2,10},{10... | collective-permute-start | bytes 1179656 | tf_op jit(solution)/shard_map/ppermute | solution.py:444
  161.9 17.9 %collective-permute-start.15 = (bf16[4,24,16,128]{3,2,1,0:T(8,128)(2,1)}, bf16[4,24,16,128]{3,2,1,0:T(8,128)(2,1)}, u32[]{:S(2)}, u32[]{:S(2)}) collective-permute-start(bf16[4,24,16,128]{3,2,1,0:T(8,128)(2,1)} %get-tuple-element.44), channel_id=1, source_target_pairs={{0,16},{8,24},{16,0},{24,8},{1,17},{9,25},{17,1},{25,9},{2,18},{10... | collective-permute-start | bytes 1179656 | tf_op jit(solution)/shard_map/ppermute | solution.py:444

commit v14 on v13

--- a/solution.py
+++ b/solution.py
@@ -368,27 +368,19 @@
     )(*in_hbm(value, *after))
 
 
-def land_kernel(x_ref, out_ref, sems):
-    size = x_ref.shape[0] // 4
-    copies = [
-        pltpu.make_async_copy(
-            x_ref.at[pl.ds(i * size, size)], out_ref.at[pl.ds(i * size, size)], sems.at[i]
-        )
-        for i in range(4)
-    ]
-    for copy in copies:
-        copy.start()
-    for copy in copies:
-        copy.wait()
+def land_kernel(x_ref, out_ref):
+    out_ref[...] = x_ref[...]
 
 
 def land(value):
+    steps = 4
+    block = pl.BlockSpec((value.shape[0] // steps, value.shape[1]), lambda i: (i, 0))
     return pl.pallas_call(
         land_kernel,
-        in_specs=[ANYWHERE],
-        out_specs=ANYWHERE,
+        grid=(steps,),
+        in_specs=[block],
+        out_specs=block,
         out_shape=pltpu.HBM(value.shape, value.dtype),
-        scratch_shapes=[pltpu.SemaphoreType.DMA((4,))],
         compiler_params=pltpu.CompilerParams(vmem_limit_bytes=SMALL),
         cost_estimate=FREE,
         name="land",

time: 255 us -> 206 us (0.81)
  Pallas kernels: 130 us -> 81 us
    pallas_call x1, Pallas kernels: 52.8 us -> 3.61 us  [land(): pl.pallas_call(land_kernel, grid=(steps,), in_specs=[block], out_specs=bl...]
  transfers between devices with their start and end apart: 22 -> 22, of which waited for: 11 -> 11; matrix products, arithmetic and copies ran while one was open for 1% -> 2% of each run, Pallas kernels for 30% -> 38%
where the time goes in v14:
time: 206 us; the launch traced here: 205 us
  Pallas kernels  81 us (39%)
  waiting for transfers between devices  77.4 us (38%)
  starting transfers between devices  39.1 us (19%)
  local copies, waits for them, and re-layouts  3.95 us (2%)
  other arithmetic  2.56 us (1%)
    ppermute x18, waiting for transfers between devices, partner(): return lax.ppermute(value, axis, [(i, i ^ mask) for i in range(size)])  68.6 us
    pallas_call x2, Pallas kernels, weight_grads(): pl.pallas_call(functools.partial(weights_kernel, first, per, len(rotated)...  29.1 us
    pallas_call x2, Pallas kernels, unit_grads(): pl.pallas_call(drop_inputs(functools.partial(units_kernel, first, per), 3...  24.7 us
    ppermute x18, starting transfers between devices, partner(): return lax.ppermute(value, axis, [(i, i ^ mask) for i in range(size)])  20.7 us
    all_to_all x4, starting transfers between devices, exchange(): lax.all_to_all(value, 'tensor', split_axis=0, concat_axis=0, tiled=True)  18.4 us
    all_to_all x4, waiting for transfers between devices, exchange(): lax.all_to_all(value, 'tensor', split_axis=0, concat_axis=0, tiled=True)  8.72 us
    pallas_call x1, Pallas kernels, local_backward(): pl.pallas_call(functools.partial(backward_kernel, [len(chunk) for chunk i...  5.53 us
    pallas_call x2, Pallas kernels, small_call(): pl.pallas_call(drop_inputs(kernel, len(ins), len(after)), grid=(steps,),...  5.18 us
  transfers between devices with their start and end apart: 22, of which 11 were waited for; matrix products, arithmetic and copies ran while one was open for 2% of the time, Pallas kernels for 38%

profile of v14, /device:TPU:0, one launch (start us, length us, event | category | flops | bytes accessed | tf_op | source)
XLA Modules:
  0.0 204.7 jit_solution(6740461978136314145)
XLA Ops:
  1.8 3.0 %collective-permute-start = (bf16[64,2048]{1,0:T(8,128)(2,1)S(1)}, bf16[64,2048]{1,0:T(8,128)(2,1)S(1)}, u32[]{:S(2)}, u32[]{:S(2)}) collective-permute-start(bf16[64,2048]{1,0:T(8,128)(2,1)S(1)} %get-tuple-element.51), channel_id=1, source_target_pairs={{0,8},{8,0},{16,24},{24,16},{1,9},{9,1},{17,25},{25,17},{2,10},{10... | collective-permute-start | bytes 786440 | tf_op jit(solution)/shard_map/ppermute | solution.py:436
  4.8 1.5 collective-permute-start.2
  6.4 5.1 %local_forward.1.refs_3_ = bf16[8,52,16,128]{3,2,1,0:T(8,128)(2,1)} custom-call(bf16[128,6656]{1,0:T(8,128)(2,1)} %x_ref.1, f32[52,52]{1,0:T(8,128)} %refs_0_.1), custom_call_target="tpu_custom_call" | custom-call | tf_op jit(solution)/shard_map/local_forward/pallas_call | solution.py:142
  11.5 5.3 %all-to-all-start = ((bf16[8,52,16,128]{3,2,1,0:T(8,128)(2,1)}), bf16[8,52,16,128]{3,2,1,0:T(8,128)(2,1)S(1)}, u32[]{:S(2)}, u32[]{:S(2)}) async-start(bf16[8,52,16,128]{3,2,1,0:T(8,128)(2,1)} %local_forward.1.refs_3_), calls=%async_computation | async-start | bytes 3407872 | tf_op jit(solution)/shard_map/all_to_all | solution.py:431
  18.1 1.4 collective-permute-done.1
  23.7 13.3 %unit_grads.2 = (bf16[8,28,16,128]{3,2,1,0:T(8,128)(2,1)}, bf16[8,28,16,128]{3,2,1,0:T(8,128)(2,1)}, bf16[8,28,16,128]{3,2,1,0:T(8,128)(2,1)}, bf16[4,28,16,128]{3,2,1,0:T(8,128)(2,1)}, bf16[4,28,16,128]{3,2,1,0:T(8,128)(2,1)}) custom-call(bf16[512,2048]{1,0:T(8,128)(2,1)S(1)} %pad_maximum_fusion.refs_0_.refs_5_, bf16[6656,2048]{1,0:T(8,128)(2,1)} %refs_6_.3, ...), custom_call_target="tpu_custom_call" | custom-call | flops 5000000000 | tf_op jit(solution)/shard_map/unit_grads/pallas_call | solution.py:225
  37.0 1.5 collective-permute-start.4
  39.0 11.4 %unit_grads.3 = (bf16[8,24,16,128]{3,2,1,0:T(8,128)(2,1)}, bf16[8,24,16,128]{3,2,1,0:T(8,128)(2,1)}, bf16[8,24,16,128]{3,2,1,0:T(8,128)(2,1)}, bf16[4,24,16,128]{3,2,1,0:T(8,128)(2,1)}, bf16[4,24,16,128]{3,2,1,0:T(8,128)(2,1)}) custom-call(bf16[512,2048]{1,0:T(8,128)(2,1)S(1)} %pad_maximum_fusion.refs_0_.refs_5_, bf16[6656,2048]{1,0:T(8,128)(2,1)} %refs_6_.3, ...), custom_call_target="tpu_custom_call" | custom-call | tf_op jit(solution)/shard_map/unit_grads/pallas_call | solution.py:225
  50.7 1.7 collective-permute-start.9
  52.5 2.5 %relay.2 = (bf16[8,28,16,128]{3,2,1,0:T(8,128)(2,1)}, bf16[8,28,16,128]{3,2,1,0:T(8,128)(2,1)}) custom-call(bf16[8,28,16,128]{3,2,1,0:T(8,128)(2,1)} %get-tuple-element.28.refs_0_, bf16[8,28,16,128]{3,2,1,0:T(8,128)(2,1)} %get-tuple-element.29.refs_1_, bf16[4,28,16,128]{3,2,1,0:T(8,128)(2,1)S(1)} %collective-permute-done.4.refs_2_, ...), custom_call_target="tpu_custom_call" | custom-call | tf_op jit(solution)/shard_map/relay/pallas_call | solution.py:321
  55.3 1.7 collective-permute-start.6
  57.5 2.1 %transform.2.refs_4_ = bf16[8,52,16,128]{3,2,1,0:T(8,128)(2,1)} custom-call(bf16[8,52,16,128]{3,2,1,0:T(8,128)(2,1)S(1)} %all-to-all-done.refs_0_, bf16[8,28,16,128]{3,2,1,0:T(8,128)(2,1)} %get-tuple-element.33.refs_1_), custom_call_target="tpu_custom_call" | custom-call | flops 999999995904 | tf_op jit(solution)/shard_map/transform/pallas_call | solution.py:418
  59.6 4.4 %all-to-all-start.1 = ((bf16[8,52,16,128]{3,2,1,0:T(8,128)(2,1)}), bf16[8,52,16,128]{3,2,1,0:T(8,128)(2,1)}, u32[]{:S(2)}, u32[]{:S(2)}) async-start(bf16[8,52,16,128]{3,2,1,0:T(8,128)(2,1)} %transform.2.refs_4_), calls=%async_computation.1 | async-start | bytes 3407872 | tf_op jit(solution)/shard_map/all_to_all | solution.py:431
  64.0 2.6 %relay.3 = (bf16[8,24,16,128]{3,2,1,0:T(8,128)(2,1)}, bf16[8,24,16,128]{3,2,1,0:T(8,128)(2,1)}) custom-call(bf16[8,24,16,128]{3,2,1,0:T(8,128)(2,1)} %get-tuple-element.35.refs_0_, bf16[8,24,16,128]{3,2,1,0:T(8,128)(2,1)} %get-tuple-element.36.refs_1_, bf16[4,24,16,128]{3,2,1,0:T(8,128)(2,1)} %collective-permute-done.8.refs_2_, ...), custom_call_target="tpu_custom_call" | custom-call | flops 999999995904 | tf_op jit(solution)/shard_map/relay/pallas_call | solution.py:321
  66.6 1.5 collective-permute-start.11
  68.2 1.4 collective-permute-start.10
  70.8 1.5 backward_matrices.1
  72.3 10.5 %collective-permute-done.7.refs_2_ = bf16[8,28,16,128]{3,2,1,0:T(8,128)(2,1)} collective-permute-done((bf16[8,28,16,128]{3,2,1,0:T(8,128)(2,1)}, bf16[8,28,16,128]{3,2,1,0:T(8,128)(2,1)}, u32[]{:S(2)}, u32[]{:S(2)}) %collective-permute-start.7) | collective-permute-done | bytes 917536 | tf_op jit(solution)/shard_map/ppermute | solution.py:436
  82.8 15.0 %collective-permute-done.11.refs_5_ = bf16[8,24,16,128]{3,2,1,0:T(8,128)(2,1)S(1)} collective-permute-done((bf16[8,24,16,128]{3,2,1,0:T(8,128)(2,1)}, bf16[8,24,16,128]{3,2,1,0:T(8,128)(2,1)S(1)}, u32[]{:S(2)}, u32[]{:S(2)}) %collective-permute-start.11) | collective-permute-done | bytes 786464 | tf_op jit(solution)/shard_map/ppermute | solution.py:436
  97.8 5.5 %local_backward.1.refs_0_ = bf16[128,6656]{1,0:T(8,128)(2,1)} custom-call(bf16[8,28,16,128]{3,2,1,0:T(8,128)(2,1)} %get-tuple-element.27.refs_3_.refs_0_, bf16[8,28,16,128]{3,2,1,0:T(8,128)(2,1)} %collective-permute-done.6.refs_1_, bf16[8,28,16,128]{3,2,1,0:T(8,128)(2,1)} %collective-permute-done.7.refs_2_, ...), custom_call_target="tpu_custom_call" | custom-call | tf_op jit(solution)/shard_map/local_backward/pallas_call | solution.py:179
  103.3 1.4 all-to-all-done.1.refs_1_.refs_0_
  104.7 3.7 %all-to-all-start.2 = ((bf16[8,16,6656]{2,1,0:T(8,128)(2,1)}), bf16[8,16,6656]{2,1,0:T(8,128)(2,1)S(1)}, u32[]{:S(2)}, u32[]{:S(2)}) async-start(bf16[8,16,6656]{2,1,0:T(8,128)(2,1)} %bitcast.6), calls=%async_computation.2 | async-start | bytes 3407872 | tf_op jit(solution)/shard_map/all_to_all | solution.py:431
  108.4 1.5 collective-permute-start.13
  109.9 1.5 collective-permute-start.12
  111.4 36.8 %collective-permute-done.13.refs_1_.refs_2_ = bf16[8,52,16,128]{3,2,1,0:T(8,128)(2,1)S(1)} collective-permute-done((bf16[8,52,16,128]{3,2,1,0:T(8,128)(2,1)}, bf16[8,52,16,128]{3,2,1,0:T(8,128)(2,1)S(1)}, u32[]{:S(2)}, u32[]{:S(2)}) %collective-permute-start.13) | collective-permute-done | bytes 1703968 | tf_op jit(solution)/shard_map/ppermute | solution.py:436
  150.9 1.5 collective-permute-start.16
  153.2 2.1 %transform.3.refs_2_.refs_9_ = bf16[8,16,6656]{2,1,0:T(8,128)(2,1)} custom-call(bf16[8,16,6656]{2,1,0:T(8,128)(2,1)S(1)} %all-to-all-done.2.refs_0_), custom_call_target="tpu_custom_call" | custom-call | flops 999999995904 | tf_op jit(solution)/shard_map/transform/pallas_call | solution.py:418
  155.3 5.0 %all-to-all-start.3 = ((bf16[8,16,6656]{2,1,0:T(8,128)(2,1)}), bf16[8,16,6656]{2,1,0:T(8,128)(2,1)}, u32[]{:S(2)}, u32[]{:S(2)}) async-start(bf16[8,16,6656]{2,1,0:T(8,128)(2,1)} %transform.3.refs_2_.refs_9_), calls=%async_computation.3 | async-start | bytes 3407872 | tf_op jit(solution)/shard_map/all_to_all | solution.py:431
  164.3 15.5 %weight_grads.2 = (bf16[6656,2048]{1,0:T(8,128)(2,1)}, f32[28,2048]{1,0:T(8,128)S(1)}) custom-call(bf16[8,52,16,128]{3,2,1,0:T(8,128)(2,1)} %all-to-all-done.1.refs_1_.refs_0_, bf16[8,52,16,128]{3,2,1,0:T(8,128)(2,1)S(1)} %copy-done.5, bf16[8,52,16,128]{3,2,1,0:T(8,128)(2,1)S(1)} %copy-done.3, bf16[4,28,16,128]{3,2,1,0:T(8,128)(2,1)} %collective-permute-done.16.refs_3_, ...), custom_call_target="tpu_custom_call" | custom-call | flops 999999995904 | tf_op jit(solution)/shard_map/weight_grads/pallas_call | solution.py:295
  179.8 13.7 %weight_grads.3 = (bf16[6656,2048]{1,0:T(8,128)(2,1)}, f32[24,2048]{1,0:T(8,128)S(1)}) custom-call(bf16[8,52,16,128]{3,2,1,0:T(8,128)(2,1)} %all-to-all-done.1.refs_1_.refs_0_, bf16[8,52,16,128]{3,2,1,0:T(8,128)(2,1)S(1)} %copy-done.5, bf16[8,52,16,128]{3,2,1,0:T(8,128)(2,1)S(1)} %copy-done.3, ...), custom_call_target="tpu_custom_call", output_to_operand_aliasing={{0}: (9, {})} | custom-call | flops 999999995904 | tf_op jit(solution)/shard_map/weight_grads/pallas_call | solution.py:295
  194.3 6.8 %all-to-all-done.3 = bf16[8,16,6656]{2,1,0:T(8,128)(2,1)} async-done(((bf16[8,16,6656]{2,1,0:T(8,128)(2,1)}), bf16[8,16,6656]{2,1,0:T(8,128)(2,1)}, u32[]{:S(2)}, u32[]{:S(2)}) %all-to-all-start.3) | async-done | bytes 1703968 | tf_op jit(solution)/shard_map/all_to_all | solution.py:431
  201.1 3.6 %land.1 = bf16[128,6656]{1,0:T(8,128)(2,1)} custom-call(bf16[128,6656]{1,0:T(8,128)(2,1)} %bitcast.5.x_ref), custom_call_target="tpu_custom_call" | custom-call | tf_op jit(solution)/shard_map/land/pallas_call | solution.py:378
  (50 shorter events, 17.8 us)
Async XLA Ops:
  1.8 15.0 %collective-permute-start = (bf16[64,2048]{1,0:T(8,128)(2,1)S(1)}, bf16[64,2048]{1,0:T(8,128)(2,1)S(1)}, u32[]{:S(2)}, u32[]{:S(2)}) collective-permute-start(bf16[64,2048]{1,0:T(8,128)(2,1)S(1)} %get-tuple-element.51), channel_id=1, source_target_pairs={{0,8},{8,0},{16,24},{24,16},{1,9},{9,1},{17,25},{25,17},{2,10},{10... | collective-permute-start | bytes 786440 | tf_op jit(solution)/shard_map/ppermute | solution.py:436
  4.8 13.2 %collective-permute-start.2 = (bf16[64,2048]{1,0:T(8,128)(2,1)S(1)}, bf16[64,2048]{1,0:T(8,128)(2,1)S(1)}, u32[]{:S(2)}, u32[]{:S(2)}) collective-permute-start(bf16[64,2048]{1,0:T(8,128)(2,1)S(1)} %get-tuple-element.52), channel_id=1, source_target_pairs={{0,24},{8,16},{16,8},{24,0},{1,25},{9,17},{17,9},{25,1},{2,26},{10... | collective-permute-start | bytes 786440 | tf_op jit(solution)/shard_map/ppermute | solution.py:436
  6.3 13.1 %collective-permute-start.1 = (bf16[64,2048]{1,0:T(8,128)(2,1)S(1)}, bf16[64,2048]{1,0:T(8,128)(2,1)S(1)}, u32[]{:S(2)}, u32[]{:S(2)}) collective-permute-start(bf16[64,2048]{1,0:T(8,128)(2,1)S(1)} %get-tuple-element.53), channel_id=1, source_target_pairs={{0,16},{8,24},{16,0},{24,8},{1,17},{9,25},{17,1},{25,9},{2,18},{10... | collective-permute-start | bytes 786440 | tf_op jit(solution)/shard_map/ppermute | solution.py:436
  11.5 46.0 %all-to-all-start = ((bf16[8,52,16,128]{3,2,1,0:T(8,128)(2,1)}), bf16[8,52,16,128]{3,2,1,0:T(8,128)(2,1)S(1)}, u32[]{:S(2)}, u32[]{:S(2)}) async-start(bf16[8,52,16,128]{3,2,1,0:T(8,128)(2,1)} %local_forward.1.refs_3_), calls=%async_computation | async-start | bytes 3407872 | tf_op jit(solution)/shard_map/all_to_all | solution.py:431
  19.5 2.5 %collective-permute-start.3 = (bf16[3,64,2048]{2,1,0:T(8,128)(2,1)S(1)}, bf16[3,64,2048]{2,1,0:T(8,128)(2,1)}, u32[]{:S(2)}, u32[]{:S(2)}) collective-permute-start(bf16[3,64,2048]{2,1,0:T(8,128)(2,1)S(1)} %pad_maximum_fusion.2), channel_id=1, source_target_pairs={{0,1},{1,0},{2,3},{3,2},{4,5},{5,4},{6,7},{7,6},{8,9},{9,8},{10,11... | collective-permute-start | bytes 2359304 | tf_op jit(solution)/shard_map/ppermute | solution.py:436
  23.7 15.3 %copy-start = (bf16[512,2048]{1,0:T(8,128)(2,1)}, bf16[512,2048]{1,0:T(8,128)(2,1)S(1)}, u32[]{:S(2)}) copy-start(bf16[512,2048]{1,0:T(8,128)(2,1)S(1)} %pad_maximum_fusion.refs_0_.refs_5_) | copy-start | bytes 6291460
  37.0 15.5 %collective-permute-start.4 = (bf16[4,28,16,128]{3,2,1,0:T(8,128)(2,1)}, bf16[4,28,16,128]{3,2,1,0:T(8,128)(2,1)S(1)}, u32[]{:S(2)}, u32[]{:S(2)}) collective-permute-start(bf16[4,28,16,128]{3,2,1,0:T(8,128)(2,1)} %get-tuple-element.30), channel_id=1, source_target_pairs={{0,8},{8,0},{16,24},{24,16},{1,9},{9,1},{17,25},{25,17},{2,10},{10... | collective-permute-start | bytes 1376264 | tf_op jit(solution)/shard_map/ppermute | solution.py:436
  38.5 14.0 %collective-permute-start.5 = (bf16[4,28,16,128]{3,2,1,0:T(8,128)(2,1)}, bf16[4,28,16,128]{3,2,1,0:T(8,128)(2,1)S(1)}, u32[]{:S(2)}, u32[]{:S(2)}) collective-permute-start(bf16[4,28,16,128]{3,2,1,0:T(8,128)(2,1)} %get-tuple-element.31), channel_id=1, source_target_pairs={{0,16},{8,24},{16,0},{24,8},{1,17},{9,25},{17,1},{25,9},{2,18},{10... | collective-permute-start | bytes 1376264 | tf_op jit(solution)/shard_map/ppermute | solution.py:436
  50.4 13.6 %collective-permute-start.8 = (bf16[4,24,16,128]{3,2,1,0:T(8,128)(2,1)}, bf16[4,24,16,128]{3,2,1,0:T(8,128)(2,1)}, u32[]{:S(2)}, u32[]{:S(2)}) collective-permute-start(bf16[4,24,16,128]{3,2,1,0:T(8,128)(2,1)} %get-tuple-element.37), channel_id=1, source_target_pairs={{0,8},{8,0},{16,24},{24,16},{1,9},{9,1},{17,25},{25,17},{2,10},{10... | collective-permute-start | bytes 1179656 | tf_op jit(solution)/shard_map/ppermute | solution.py:436
  50.7 13.2 %collective-permute-start.9 = (bf16[4,24,16,128]{3,2,1,0:T(8,128)(2,1)}, bf16[4,24,16,128]{3,2,1,0:T(8,128)(2,1)}, u32[]{:S(2)}, u32[]{:S(2)}) collective-permute-start(bf16[4,24,16,128]{3,2,1,0:T(8,128)(2,1)} %get-tuple-element.38), channel_id=1, source_target_pairs={{0,16},{8,24},{16,0},{24,8},{1,17},{9,25},{17,1},{25,9},{2,18},{10... | collective-permute-start | bytes 1179656 | tf_op jit(solution)/shard_map/ppermute | solution.py:436
  55.0 27.8 %collective-permute-start.7 = (bf16[8,28,16,128]{3,2,1,0:T(8,128)(2,1)}, bf16[8,28,16,128]{3,2,1,0:T(8,128)(2,1)}, u32[]{:S(2)}, u32[]{:S(2)}) collective-permute-start(bf16[8,28,16,128]{3,2,1,0:T(8,128)(2,1)} %get-tuple-element.34), channel_id=1, source_target_pairs={{0,16},{8,24},{16,0},{24,8},{1,17},{9,25},{17,1},{25,9},{2,18},{10... | collective-permute-start | bytes 2752520 | tf_op jit(solution)/shard_map/ppermute | solution.py:436
  55.3 27.5 %collective-permute-start.6 = (bf16[8,28,16,128]{3,2,1,0:T(8,128)(2,1)}, bf16[8,28,16,128]{3,2,1,0:T(8,128)(2,1)}, u32[]{:S(2)}, u32[]{:S(2)}) collective-permute-start(bf16[8,28,16,128]{3,2,1,0:T(8,128)(2,1)} %get-tuple-element.33.refs_1_), channel_id=1, source_target_pairs={{0,8},{8,0},{16,24},{24,16},{1,9},{9,1},{17,25},{25,17},{2,10},{10... | collective-permute-start | bytes 2752520 | tf_op jit(solution)/shard_map/ppermute | solution.py:436
  59.6 45.1 %all-to-all-start.1 = ((bf16[8,52,16,128]{3,2,1,0:T(8,128)(2,1)}), bf16[8,52,16,128]{3,2,1,0:T(8,128)(2,1)}, u32[]{:S(2)}, u32[]{:S(2)}) async-start(bf16[8,52,16,128]{3,2,1,0:T(8,128)(2,1)} %transform.2.refs_4_), calls=%async_computation.1 | async-start | bytes 3407872 | tf_op jit(solution)/shard_map/all_to_all | solution.py:431
  64.0 5.6 %copy-start.7 = (f32[52,52]{1,0:T(8,128)S(1)}, f32[52,52]{1,0:T(8,128)}, u32[]{:S(2)}) copy-start(f32[52,52]{1,0:T(8,128)} %refs_0_.1) | copy-start | bytes 32452
  66.6 31.1 %collective-permute-start.11 = (bf16[8,24,16,128]{3,2,1,0:T(8,128)(2,1)}, bf16[8,24,16,128]{3,2,1,0:T(8,128)(2,1)S(1)}, u32[]{:S(2)}, u32[]{:S(2)}) collective-permute-start(bf16[8,24,16,128]{3,2,1,0:T(8,128)(2,1)} %get-tuple-element.40), channel_id=1, source_target_pairs={{0,16},{8,24},{16,0},{24,8},{1,17},{9,25},{17,1},{25,9},{2,18},{10... | collective-permute-start | bytes 2359304 | tf_op jit(solution)/shard_map/ppermute | solution.py:436
  68.2 29.6 %collective-permute-start.10 = (bf16[8,24,16,128]{3,2,1,0:T(8,128)(2,1)}, bf16[8,24,16,128]{3,2,1,0:T(8,128)(2,1)S(1)}, u32[]{:S(2)}, u32[]{:S(2)}) collective-permute-start(bf16[8,24,16,128]{3,2,1,0:T(8,128)(2,1)} %get-tuple-element.39.refs_1_), channel_id=1, source_target_pairs={{0,8},{8,0},{16,24},{24,16},{1,9},{9,1},{17,25},{25,17},{2,10},{10... | collective-permute-start | bytes 2359304 | tf_op jit(solution)/shard_map/ppermute | solution.py:436
  69.6 1.2 copy-start.6
  104.7 48.5 %all-to-all-start.2 = ((bf16[8,16,6656]{2,1,0:T(8,128)(2,1)}), bf16[8,16,6656]{2,1,0:T(8,128)(2,1)S(1)}, u32[]{:S(2)}, u32[]{:S(2)}) async-start(bf16[8,16,6656]{2,1,0:T(8,128)(2,1)} %bitcast.6), calls=%async_computation.2 | async-start | bytes 3407872 | tf_op jit(solution)/shard_map/all_to_all | solution.py:431
  108.4 39.8 %collective-permute-start.13 = (bf16[8,52,16,128]{3,2,1,0:T(8,128)(2,1)}, bf16[8,52,16,128]{3,2,1,0:T(8,128)(2,1)S(1)}, u32[]{:S(2)}, u32[]{:S(2)}) collective-permute-start(bf16[8,52,16,128]{3,2,1,0:T(8,128)(2,1)} %all-to-all-done.1.refs_1_.refs_0_), channel_id=1, source_target_pairs={{0,16},{8,24},{16,0},{24,8},{1,17},{9,25},{17,1},{25,9},{2,18},{10... | collective-permute-start | bytes 5111816 | tf_op jit(solution)/shard_map/ppermute | solution.py:436
  109.9 39.5 %collective-permute-start.12 = (bf16[8,52,16,128]{3,2,1,0:T(8,128)(2,1)}, bf16[8,52,16,128]{3,2,1,0:T(8,128)(2,1)S(1)}, u32[]{:S(2)}, u32[]{:S(2)}) collective-permute-start(bf16[8,52,16,128]{3,2,1,0:T(8,128)(2,1)} %all-to-all-done.1.refs_1_.refs_0_), channel_id=1, source_target_pairs={{0,8},{8,0},{16,24},{24,16},{1,9},{9,1},{17,25},{25,17},{2,10},{10... | collective-permute-start | bytes 5111816 | tf_op jit(solution)/shard_map/ppermute | solution.py:436
  148.2 2.2 %copy-start.2 = (bf16[8,52,16,128]{3,2,1,0:T(8,128)(2,1)}, bf16[8,52,16,128]{3,2,1,0:T(8,128)(2,1)S(1)}, u32[]{:S(2)}) copy-start(bf16[8,52,16,128]{3,2,1,0:T(8,128)(2,1)S(1)} %collective-permute-done.13.refs_1_.refs_2_) | copy-start | bytes 5111812
  149.4 1.5 copy-start.4
  150.9 12.2 %collective-permute-start.16 = (bf16[4,28,16,128]{3,2,1,0:T(8,128)(2,1)}, bf16[4,28,16,128]{3,2,1,0:T(8,128)(2,1)}, u32[]{:S(2)}, u32[]{:S(2)}) collective-permute-start(bf16[4,28,16,128]{3,2,1,0:T(8,128)(2,1)} %get-tuple-element.45), channel_id=1, source_target_pairs={{0,8},{8,0},{16,24},{24,16},{1,9},{9,1},{17,25},{25,17},{2,10},{10... | collective-permute-start | bytes 1376264 | tf_op jit(solution)/shard_map/ppermute | solution.py:436
  152.4 11.9 %collective-permute-start.17 = (bf16[4,28,16,128]{3,2,1,0:T(8,128)(2,1)}, bf16[4,28,16,128]{3,2,1,0:T(8,128)(2,1)}, u32[]{:S(2)}, u32[]{:S(2)}) collective-permute-start(bf16[4,28,16,128]{3,2,1,0:T(8,128)(2,1)} %get-tuple-element.46), channel_id=1, source_target_pairs={{0,16},{8,24},{16,0},{24,8},{1,17},{9,25},{17,1},{25,9},{2,18},{10... | collective-permute-start | bytes 1376264 | tf_op jit(solution)/shard_map/ppermute | solution.py:436
  155.3 5.0 %copy-start.3 = (bf16[8,52,16,128]{3,2,1,0:T(8,128)(2,1)S(1)}, bf16[8,52,16,128]{3,2,1,0:T(8,128)(2,1)}, u32[]{:S(2)}) copy-start(bf16[8,52,16,128]{3,2,1,0:T(8,128)(2,1)} %copy-done.2) | copy-start | bytes 5111812
  155.3 5.0 %copy-start.5 = (bf16[8,52,16,128]{3,2,1,0:T(8,128)(2,1)S(1)}, bf16[8,52,16,128]{3,2,1,0:T(8,128)(2,1)}, u32[]{:S(2)}) copy-start(bf16[8,52,16,128]{3,2,1,0:T(8,128)(2,1)} %copy-done.4) | copy-start | bytes 5111812
  155.3 45.8 %all-to-all-start.3 = ((bf16[8,16,6656]{2,1,0:T(8,128)(2,1)}), bf16[8,16,6656]{2,1,0:T(8,128)(2,1)}, u32[]{:S(2)}, u32[]{:S(2)}) async-start(bf16[8,16,6656]{2,1,0:T(8,128)(2,1)} %transform.3.refs_2_.refs_9_), calls=%async_computation.3 | async-start | bytes 3407872 | tf_op jit(solution)/shard_map/all_to_all | solution.py:431
  160.4 4.0 %copy-start.1 = (bf16[512,2048]{1,0:T(8,128)(2,1)S(1)}, bf16[512,2048]{1,0:T(8,128)(2,1)}, u32[]{:S(2)}) copy-start(bf16[512,2048]{1,0:T(8,128)(2,1)} %copy-done) | copy-start | bytes 6291460
  161.4 18.4 %collective-permute-start.14 = (bf16[4,24,16,128]{3,2,1,0:T(8,128)(2,1)}, bf16[4,24,16,128]{3,2,1,0:T(8,128)(2,1)}, u32[]{:S(2)}, u32[]{:S(2)}) collective-permute-start(bf16[4,24,16,128]{3,2,1,0:T(8,128)(2,1)} %get-tuple-element.43), channel_id=1, source_target_pairs={{0,8},{8,0},{16,24},{24,16},{1,9},{9,1},{17,25},{25,17},{2,10},{10... | collective-permute-start | bytes 1179656 | tf_op jit(solution)/shard_map/ppermute | solution.py:436
  161.9 17.9 %collective-permute-start.15 = (bf16[4,24,16,128]{3,2,1,0:T(8,128)(2,1)}, bf16[4,24,16,128]{3,2,1,0:T(8,128)(2,1)}, u32[]{:S(2)}, u32[]{:S(2)}) collective-permute-start(bf16[4,24,16,128]{3,2,1,0:T(8,128)(2,1)} %get-tuple-element.44), channel_id=1, source_target_pairs={{0,16},{8,24},{16,0},{24,8},{1,17},{9,25},{17,1},{25,9},{2,18},{10... | collective-permute-start | bytes 1179656 | tf_op jit(solution)/shard_map/ppermute | solution.py:436
